TPU v7x, 32 devices: a whole 2x2x4 slice. The times are simulated.
32 devices in a mesh: row: 4 (over y, core), col: 8 (over z, x).
Axes of the slice: x: 2, y: 2, z: 4, core: 2. Of those that a mesh axis runs over, the one named last changes fastest.
Arguments:
- scores: float32 [32, 24576], P(None, ('row', 'col')), may hold values from -60 to 60
- tile_values: bfloat16 [4, 8, 240, 128, 128], P('row', 'col'), may hold values from 0 to 1
- tile_rows: int32 [4, 8, 240], P('row', 'col'), may hold values from 0 to 47, as said below
- tile_cols: int32 [4, 8, 240], P('row', 'col'), may hold values from 0 to 23, as said below
- tile_count: int32 [4, 8], P('row', 'col'), may hold values from 120 to 240, as said below
Outputs:
- solution: float32 [32, 24576], P(None, ('row', 'col'))
- residual: float32 [32, 24576], P(None, ('row', 'col'))
Inputs may be any that keep to these rules, and one draw needn't show every extreme that they name: `tile_rows`: on every device each local row tile is named by exactly 5 of the 240 slots. `tile_cols`: on every device each local column tile is named by exactly 10 of the slots. Only the first tile_count slots of a device are live; some device has all 240 slots live.
All inputs are finite; a program needn't handle non-finite values.
Results may differ from a plain program's by a relative error of at most 0.0031.
Values may be sent and summed in bfloat16 or wider, within the bound.
No kernel may reach another device: no remote copies, remote signals or barrier semaphores. Data moves between devices by JAX's collectives and lax.ppermute only.
A program may use at most 128 MiB of HBM per device.

v0:
```python
import jax
import jax.numpy as jnp
from jax import lax
from jax.sharding import PartitionSpec as P

PER_ROW = 5
ITERS = 3


coupling = 0.2


def per_device(scores, tile_values, tile_rows, tile_cols, tile_count):
    tile_blocks = tile_values[0, 0]
    row_tile_ids = tile_rows[0, 0]
    col_tile_ids = tile_cols[0, 0]
    live_count = tile_count[0, 0]
    slot_count = tile_blocks.shape[0]
    tile_size = tile_blocks.shape[1]
    task_count = scores.shape[0]
    piece_len = scores.shape[1]
    row_span = piece_len * lax.axis_size("col")
    col_span = piece_len * lax.axis_size("row")
    row_tiles = row_span // tile_size
    col_tiles = col_span // tile_size
    block_slots = slot_count // PER_ROW
    own_start = lax.axis_index("col") * piece_len
    live_mask = (jnp.arange(slot_count, dtype=jnp.int32) < live_count).astype(jnp.float32)
    row_weight = jnp.sum(tile_blocks, axis=2, dtype=jnp.float32) * live_mask[:, None]
    col_weight = jnp.sum(tile_blocks, axis=1, dtype=jnp.float32) * live_mask[:, None]
    row_degree_part = (
        jnp.zeros((row_tiles, tile_size), jnp.float32)
        .at[row_tile_ids]
        .add(row_weight)
        .reshape(1, row_span)
    )
    col_degree_part = (
        jnp.zeros((col_tiles, tile_size), jnp.float32)
        .at[col_tile_ids]
        .add(col_weight)
        .reshape(1, col_span)
    )

    def to_cols(partial_value):
        return lax.psum_scatter(partial_value, "row", scatter_dimension=1, tiled=True)

    def row_total(partial_value):
        return lax.psum(partial_value, "col")

    def row_block(own_field):
        return lax.all_gather(own_field, "col", axis=1, tiled=True)

    degree = 0.5 * (row_total(row_degree_part) + row_block(to_cols(col_degree_part)))
    right_side = row_block(scores)

    def inner_sums(parts):
        return lax.psum(parts, "row")

    solution = jnp.zeros_like(right_side)
    residual = right_side
    direction = right_side
    norm_now = inner_sums(jnp.sum(residual * residual, axis=1))
    for step_index in range(ITERS):
        block_low = direction.astype(jnp.bfloat16)
        graph_own_low = lax.dynamic_slice_in_dim(block_low, own_start, piece_len, 1)
        graph_col_dir = lax.all_gather(graph_own_low, "row", axis=1, tiled=True)
        col_blocks = graph_col_dir.reshape(task_count, col_tiles, tile_size)
        row_blocks = block_low.reshape(task_count, row_tiles, tile_size)
        block_count = (live_count + block_slots - 1) // block_slots

        def one_block(block_index, totals):
            forward_sum, backward_sum = totals
            first_slot = block_index * block_slots
            tiles_here = lax.dynamic_slice_in_dim(tile_blocks, first_slot, block_slots, 0)
            rows_here = lax.dynamic_slice_in_dim(row_tile_ids, first_slot, block_slots, 0)
            cols_here = lax.dynamic_slice_in_dim(col_tile_ids, first_slot, block_slots, 0)
            live_here = (first_slot + jnp.arange(block_slots, dtype=jnp.int32) < live_count).astype(
                jnp.float32
            )
            col_pieces = jnp.take(col_blocks, cols_here, axis=1)
            row_pieces = jnp.take(row_blocks, rows_here, axis=1)
            forward = (
                jnp.einsum(
                    "ksd,sod->kso", col_pieces, tiles_here, preferred_element_type=jnp.float32
                )
                * live_here[None, :, None]
            )
            backward = (
                jnp.einsum(
                    "kso,sod->ksd", row_pieces, tiles_here, preferred_element_type=jnp.float32
                )
                * live_here[None, :, None]
            )
            return (
                forward_sum.at[:, rows_here, :].add(forward),
                backward_sum.at[:, cols_here, :].add(backward),
            )

        empty_sums = (
            jnp.zeros((task_count, row_tiles, tile_size), jnp.float32),
            jnp.zeros((task_count, col_tiles, tile_size), jnp.float32),
        )
        forward_sum, backward_sum = lax.fori_loop(0, block_count, one_block, empty_sums)
        forward_part = forward_sum.reshape(task_count, row_span)
        backward_part = backward_sum.reshape(task_count, col_span)
        image_field = direction + coupling * (
            degree * direction - 0.5 * (row_total(forward_part) + row_block(to_cols(backward_part)))
        )
        curvature = inner_sums(jnp.sum(direction * image_field, axis=1))
        step_size = norm_now / curvature
        solution = solution + step_size[:, None] * direction
        residual = residual - step_size[:, None] * image_field
        if step_index + 1 < ITERS:
            norm_next = inner_sums(jnp.sum(residual * residual, axis=1))
            direction = residual + (norm_next / norm_now)[:, None] * direction
            norm_now = norm_next
    own_solution = lax.dynamic_slice_in_dim(solution, own_start, piece_len, 1)
    own_residual = lax.dynamic_slice_in_dim(residual, own_start, piece_len, 1)
    return (own_solution, own_residual)


def solution(mesh):
    return jax.shard_map(
        per_device,
        mesh=mesh,
        in_specs=(
            P(None, ("row", "col")),
            P("row", "col", None, None, None),
            P("row", "col", None),
            P("row", "col", None),
            P("row", "col"),
        ),
        out_specs=(P(None, ("row", "col")), P(None, ("row", "col"))),
        check_vma=False,
    )
```

profile of v0, /device:TPU:0, one launch (start us, length us, event | category | flops | bytes accessed | tf_op | source)
XLA Modules:
  0.0 569.1 jit_solution(6667456642564971380)
XLA Ops:
  8.7 5.5 convert_reduce_fusion
  17.5 33.8 %all_gather.24 = f32[32,6144]{1,0:T(8,128)S(1)} all-gather(f32[32,768]{1,0:T(8,128)S(1)} %copy-done.6), channel_id=1, replica_groups=mesh['row'=4,'col'=8] {'col'}, dimensions={1}, use_global_device_ids=true | all-gather | bytes 884736 | tf_op jit(solution)/shard_map/all_gather | solution.py:51
  52.2 5.6 all_gather.26
  57.9 62.2 %while.36 = (s32[]{:T(128)}, f32[32,48,128]{2,0,1:T(8,128)S(1)}, f32[32,24,128]{2,0,1:T(8,128)S(1)}, s32[]{:T(128)}, s32[240]{0:T(256)S(1)}, /*index=5*/bf16[240...) while((s32[]{:T(128)}, f32[32,48,128]{2,0,1:T(8,128)S(1)}, ...), condition=%wide.region_11.14_spmd, body=%wide.region_8.13_spmd.sunk | while | flops 101845712 | bytes 11807567 | solution.py:103
  59.4 2.4 fusion.129
  61.7 2.5 scatter_fusion
  67.9 2.5 scatter_fusion.1
  71.8 2.4 fusion.129
  74.2 2.5 scatter_fusion
  80.3 2.5 scatter_fusion.1
  84.2 2.4 fusion.129
  86.6 2.5 scatter_fusion
  92.7 2.5 scatter_fusion.1
  96.7 2.4 fusion.129
  99.0 2.5 scatter_fusion
  105.2 2.5 scatter_fusion.1
  109.1 2.4 fusion.129
  111.5 2.5 scatter_fusion
  117.6 2.5 scatter_fusion.1
  123.5 37.3 %psum.71 = f32[1,6144]{1,0:T(1,128)S(1)} all-reduce(f32[1,6144]{1,0:T(1,128)S(1)} %bitcast.141), channel_id=1, replica_groups=mesh['row'=4,'col'=8] {'col'}, use_global_device_ids=true, to_apply=%region_4.0 | all-reduce | flops 6144 | bytes 49152 | tf_op jit(solution)/shard_map/psum | solution.py:48
  161.9 30.3 %all_gather.25 = f32[1,6144]{1,0:T(1,128)S(1)} all-gather(f32[1,768]{1,0:T(1,128)S(1)} %copy.44), channel_id=1, replica_groups=mesh['row'=4,'col'=8] {'col'}, dimensions={1}, use_global_device_ids=true | all-gather | bytes 27648 | tf_op jit(solution)/shard_map/all_gather | solution.py:51
  192.3 32.6 %all_gather.27 = f32[32,6144]{1,0:T(8,128)S(1)} all-gather(f32[32,768]{1,0:T(8,128)} %reduce-scatter.7.cloned.1.call-done), channel_id=1, replica_groups=mesh['row'=4,'col'=8] {'col'}, dimensions={1}, use_global_device_ids=true | all-gather | bytes 884736 | tf_op jit(solution)/shard_map/all_gather | solution.py:51
  226.4 5.8 %all-reduce = (f32[32]{0:T(128)S(1)}, f32[32]{0:T(128)S(1)}) all-reduce(f32[32]{0:T(128)S(1)} %get-tuple-element.235, f32[32]{0:T(128)S(1)} %get-tuple-element.234), channel_id=1, replica_groups=mesh['row'=4,'col'=8] {'row'}, use_global_device_ids=true, to_apply=%region_1.0 | all-reduce | flops 64 | bytes 512 | tf_op jit(solution)/shard_map/psum | solution.py:57
  233.7 5.8 %psum.74 = f32[32]{0:T(128)S(1)} all-reduce(f32[32]{0:T(128)S(1)} %get-tuple-element.318), channel_id=1, replica_groups=mesh['row'=4,'col'=8] {'row'}, use_global_device_ids=true, to_apply=%region_17.20 | all-reduce | flops 32 | bytes 256 | tf_op jit(solution)/shard_map/psum | solution.py:57
  241.3 5.6 all_gather.28
  247.1 62.4 %while.37 = (s32[]{:T(128)}, f32[32,48,128]{2,0,1:T(8,128)S(1)}, f32[32,24,128]{2,0,1:T(8,128)S(1)}, s32[]{:T(128)}, s32[240]{0:T(256)S(1)}, /*index=5*/bf16[240...) while((s32[]{:T(128)}, f32[32,48,128]{2,0,1:T(8,128)S(1)}, ...), condition=%wide.region_21.24_spmd, body=%wide.region_18.23_spmd.sunk | while | flops 101845712 | bytes 11807567 | solution.py:103
  251.0 2.5 scatter_fusion.2
  257.2 2.5 scatter_fusion.3
  263.5 2.5 scatter_fusion.2
  269.6 2.5 scatter_fusion.3
  273.5 2.4 fusion.135
  275.9 2.5 scatter_fusion.2
  282.1 2.5 scatter_fusion.3
  286.0 2.4 fusion.135
  288.4 2.5 scatter_fusion.2
  294.5 2.5 scatter_fusion.3
  298.4 2.4 fusion.135
  300.8 2.5 scatter_fusion.2
  306.9 2.5 scatter_fusion.3
  311.3 16.6 %reduce-scatter.9.cloned.1.call-done = f32[32,768]{1,0:T(8,128)} async-done(((f32[32,3072]{1,0:T(8,128)}), f32[32,768]{1,0:T(8,128)}) %reduce-scatter.9.cloned.1.call-update) | async-done | bytes 98320 | tf_op jit(solution)/shard_map/reduce_scatter | solution.py:45
  327.9 32.6 %all_gather.29 = f32[32,6144]{1,0:T(8,128)S(1)} all-gather(f32[32,768]{1,0:T(8,128)} %reduce-scatter.9.cloned.1.call-done), channel_id=1, replica_groups=mesh['row'=4,'col'=8] {'col'}, dimensions={1}, use_global_device_ids=true | all-gather | bytes 884736 | tf_op jit(solution)/shard_map/all_gather | solution.py:51
  360.5 26.1 %all-reduce.7.cloned.1.call-done = f32[32,6144]{1,0:T(8,128)} async-done(((f32[32,6144]{1,0:T(8,128)}), f32[32,6144]{1,0:T(8,128)}) %all-reduce.7.cloned.1.call-update) | async-done | bytes 786448 | tf_op jit(solution)/shard_map/psum | solution.py:48
  388.0 5.7 psum.76
  393.7 2.4 multiply_reduce_fusion.1
  396.1 6.6 %psum.77 = f32[32]{0:T(128)S(1)} all-reduce(f32[32]{0:T(128)S(1)} %get-tuple-element.314), channel_id=1, replica_groups=mesh['row'=4,'col'=8] {'row'}, use_global_device_ids=true, to_apply=%region_27.30 | all-reduce | flops 32 | bytes 256 | tf_op jit(solution)/shard_map/psum | solution.py:57
  405.7 5.6 all_gather.30
  411.5 62.2 %while.38 = (s32[]{:T(128)}, f32[32,48,128]{2,0,1:T(8,128)S(1)}, f32[32,24,128]{2,0,1:T(8,128)S(1)}, s32[]{:T(128)}, s32[240]{0:T(256)S(1)}, /*index=5*/bf16[240...) while((s32[]{:T(128)}, f32[32,48,128]{2,0,1:T(8,128)S(1)}, ...), condition=%wide.region_31.34_spmd, body=%wide.region_28.33_spmd.sunk | while | flops 101845712 | bytes 11807567 | solution.py:103
  412.9 2.4 fusion.141
  415.3 2.5 scatter_fusion.4
  421.4 2.5 scatter_fusion.5
  425.4 2.4 fusion.141
  427.7 2.5 scatter_fusion.4
  433.9 2.5 scatter_fusion.5
  437.8 2.4 fusion.141
  440.2 2.5 scatter_fusion.4
  446.3 2.5 scatter_fusion.5
  452.6 2.5 scatter_fusion.4
  458.7 2.5 scatter_fusion.5
  465.0 2.5 scatter_fusion.4
  471.2 2.5 scatter_fusion.5
  475.5 18.5 %reduce-scatter.11.cloned.1.call-done = f32[32,768]{1,0:T(8,128)} async-done(((f32[32,3072]{1,0:T(8,128)}), f32[32,768]{1,0:T(8,128)}) %reduce-scatter.11.cloned.1.call-update) | async-done | bytes 98320 | tf_op jit(solution)/shard_map/reduce_scatter | solution.py:45
  494.0 32.7 %all_gather.31 = f32[32,6144]{1,0:T(8,128)S(1)} all-gather(f32[32,768]{1,0:T(8,128)} %reduce-scatter.11.cloned.1.call-done), channel_id=1, replica_groups=mesh['row'=4,'col'=8] {'col'}, dimensions={1}, use_global_device_ids=true | all-gather | bytes 884736 | tf_op jit(solution)/shard_map/all_gather | solution.py:51
  526.7 26.2 %all-reduce.9.cloned.1.call-done = f32[32,6144]{1,0:T(8,128)} async-done(((f32[32,6144]{1,0:T(8,128)}), f32[32,6144]{1,0:T(8,128)}) %all-reduce.9.cloned.1.call-update) | async-done | bytes 786448 | tf_op jit(solution)/shard_map/psum | solution.py:48
  554.4 5.7 psum.79
  (193 shorter events, 109.4 us)
Async XLA Ops:
  8.0 152.8 %reduce-scatter.13.cloned.1.call-start = ((), (), s32[]{:S(2)}) async-start(), calls=%async_computation.10 | async-start | bytes 1966080
  8.7 5.5 copy-start.7
  8.7 5.5 copy-start.8
  14.2 3.3 copy-start.6
  17.4 174.9 %reduce-scatter.7.cloned.1.call-start = ((), (), s32[]{:S(2)}) async-start(), calls=%async_computation.5 | async-start | bytes 491520 | tf_op jit(solution)/shard_map/reduce_scatter | solution.py:45
  120.9 104.0 %all-reduce.5.cloned.1.call-start = ((), (), s32[]{:S(2)}) async-start(), calls=%async_computation.4 | async-start | bytes 1572864 | tf_op jit(solution)/shard_map/psum | solution.py:48
  122.0 205.9 %reduce-scatter.9.cloned.1.call-start = ((), (), s32[]{:S(2)}) async-start(), calls=%async_computation.7 | async-start | bytes 491520 | tf_op jit(solution)/shard_map/reduce_scatter | solution.py:45
  192.3 41.4 %copy-start.4 = (f32[1,6144]{1,0:T(1,128)}, f32[1,6144]{1,0:T(1,128)S(1)}, u32[]{:S(2)}) copy-start(f32[1,6144]{1,0:T(1,128)S(1)} %add_multiply_fusion) | copy-start | bytes 73732
  233.7 13.2 %copy-start.1 = (f32[32,6144]{1,0:T(8,128)}, f32[32,6144]{1,0:T(8,128)S(1)}, u32[]{:S(2)}) copy-start(f32[32,6144]{1,0:T(8,128)S(1)} %get-tuple-element.319) | copy-start | bytes 2359300
  239.4 1.1 copy-start.9
  309.5 77.1 %copy-start = (f32[32,6144]{1,0:T(8,128)S(1)}, f32[32,6144]{1,0:T(8,128)}, u32[]{:S(2)}) copy-start(f32[32,6144]{1,0:T(8,128)} %get-tuple-element.317) | copy-start | bytes 2359300
  310.2 83.5 %copy-start.10 = (f32[32]{0:T(128)S(1)}, f32[32]{0:T(128)}, u32[]{:S(2)}) copy-start(f32[32]{0:T(128)} %copy-done.9) | copy-start | bytes 388
  310.2 83.5 %copy-start.2 = (f32[32,6144]{1,0:T(8,128)S(1)}, f32[32,6144]{1,0:T(8,128)}, u32[]{:S(2)}) copy-start(f32[32,6144]{1,0:T(8,128)} %copy-done.1) | copy-start | bytes 2359300
  310.2 83.5 %copy-start.5 = (f32[1,6144]{1,0:T(1,128)S(1)}, f32[1,6144]{1,0:T(1,128)}, u32[]{:S(2)}) copy-start(f32[1,6144]{1,0:T(1,128)} %copy-done.4) | copy-start | bytes 73732
  310.3 76.3 %all-reduce.7.cloned.1.call-start = ((), (), s32[]{:S(2)}) async-start(), calls=%async_computation.6 | async-start | bytes 1572864 | tf_op jit(solution)/shard_map/psum | solution.py:48
  311.3 182.7 %reduce-scatter.11.cloned.1.call-start = ((), (), s32[]{:S(2)}) async-start(), calls=%async_computation.9 | async-start | bytes 491520 | tf_op jit(solution)/shard_map/reduce_scatter | solution.py:45
  402.7 8.6 %copy-start.11 = (f32[32]{0:T(128)}, f32[32]{0:T(128)S(1)}, u32[]{:S(2)}) copy-start(f32[32]{0:T(128)S(1)} %psum.77) | copy-start | bytes 388
  473.7 79.2 %copy-start.3 = (f32[32,6144]{1,0:T(8,128)S(1)}, f32[32,6144]{1,0:T(8,128)}, u32[]{:S(2)}) copy-start(f32[32,6144]{1,0:T(8,128)} %get-tuple-element.313) | copy-start | bytes 2359300
  474.5 78.4 %all-reduce.9.cloned.1.call-start = ((), (), s32[]{:S(2)}) async-start(), calls=%async_computation.8 | async-start | bytes 1572864 | tf_op jit(solution)/shard_map/psum | solution.py:48
  474.5 85.5 %copy-start.12 = (f32[32]{0:T(128)S(1)}, f32[32]{0:T(128)}, u32[]{:S(2)}) copy-start(f32[32]{0:T(128)} %copy-done.11) | copy-start | bytes 388
Sparse Core Ops, SparseCore 0:
  17.5 30.8 reduce-scatter.12
  121.1 21.8 reduce-scatter.6
  310.4 17.4 reduce-scatter.8
  474.6 19.3 reduce-scatter.10
Sparse Core Ops, SparseCore 1:
  124.8 77.2 all-reduce.4
  314.2 72.4 all-reduce.6
  478.8 74.1 all-reduce.8
where the time goes:
time: 571 us; the launch traced here: 569 us
  blocking collectives  246 us (43%)
  other arithmetic  109 us (19%)
  waiting for transfers between devices  87.5 us (15%)
  matrix products  65.5 us (11%)
  local copies, waits for them, and re-layouts  43.8 us (8%)
  between operations  16.4 us (3%)
    all_gather x5, blocking collectives, row_block(): return lax.all_gather(own_field, 'col', axis=1, tiled=True)  162 us
    psum x3, waiting for transfers between devices, row_total(): return lax.psum(partial_value, 'col')  52.3 us
    scatter-add x15, other arithmetic, one_block(): backward_sum.at[:, cols_here, :].add(backward)  37.6 us
    scatter-add x15, other arithmetic, one_block(): forward_sum.at[:, rows_here, :].add(forward)  37.5 us
    psum x1, blocking collectives, row_total(): return lax.psum(partial_value, 'col')  37.3 us
    dot_general x15, matrix products, one_block(): jnp.einsum('ksd,sod->kso', col_pieces, tiles_here, preferred_element_type...  35.6 us
    reduce_scatter x3, waiting for transfers between devices, to_cols(): lax.psum_scatter(partial_value, 'row', scatter_dimension=1, tiled=True)  35.1 us
    dot_general x15, matrix products, one_block(): jnp.einsum('kso,sod->ksd', row_pieces, tiles_here, preferred_element_type...  29.9 us
  transfers between devices with their start and end apart: 7, of which 4 were waited for; matrix products, arithmetic and copies ran while one was open for 12% of the time, Pallas kernels for 0%

commit v1 on v0

v1 whole, which is shorter than its diff:
```python
import functools

import jax
import jax.numpy as jnp
import numpy as np
from jax import lax
from jax.experimental import pallas as pl
from jax.experimental.pallas import tpu as pltpu
from jax.sharding import PartitionSpec as P

PER_ROW = 5
ITERS = 3
MESH_AXES = ("row", "col")

coupling = 0.2

NT = (((1,), (1,)), ((), ()))


def products_kernel(
    task_count, unroll, row_slots, row_loads, row_place, col_slots, col_loads, col_place,
    row_field, col_field, tiles, forward, backward, inner,
):
    row_tiles = row_place.shape[0]
    col_tiles = col_place.shape[0]
    per_row = row_slots.shape[0] // row_tiles
    per_col = col_slots.shape[0] // col_tiles
    ratio = row_tiles // col_tiles
    rows_held = row_field.shape[1]
    forward[...] = jnp.zeros_like(forward)
    inner[...] = jnp.zeros_like(inner)

    def one_row(i):
        base = i * per_row
        field = jnp.concatenate([col_field[row_loads[base + j]] for j in range(per_row)], axis=1)
        block = jnp.concatenate([tiles[row_slots[base + j]] for j in range(per_row)], axis=1)
        total = lax.dot_general(field, block, NT, preferred_element_type=jnp.float32)
        place = row_place[i]
        forward[place] = total
        own = row_field[place][:task_count].astype(jnp.float32)
        part = -own * total[:task_count]
        if rows_held > task_count:
            part += 0.5 * (own * own) * total[task_count : task_count + 1]
        return part

    def one_col(i):
        base = i * per_col
        field = jnp.concatenate([row_field[col_loads[base + j]] for j in range(per_col)], axis=1)
        block = jnp.concatenate([tiles[col_slots[base + j]] for j in range(per_col)], axis=0)
        total = jnp.dot(field, block, preferred_element_type=jnp.float32)
        place = col_place[i]
        backward[place] = total
        if rows_held > task_count:
            own = col_field[place][:task_count].astype(jnp.float32)
            return 0.5 * (own * own) * total[task_count : task_count + 1]
        return None

    def step(g, carry):
        parts = []
        for u in range(unroll):
            i = g * unroll + u
            parts.append(one_col(i))
            for k in range(ratio):
                parts.append(one_row(i * ratio + k))
        inner[...] += sum(p for p in parts if p is not None)
        return carry

    lax.fori_loop(0, col_tiles // unroll, step, 0)


def products(lists, row_field, col_field, tiles, task_count, row_pieces, col_tiles):
    rows_held = row_field.shape[1]
    tile_size = row_field.shape[2]
    unroll = next(u for u in (8, 6, 4, 3, 2, 1) if col_tiles % u == 0)
    in_smem = pl.BlockSpec(memory_space=pltpu.SMEM)
    in_vmem = pl.BlockSpec(memory_space=pltpu.VMEM)
    slots = tiles.shape[0]
    return pl.pallas_call(
        functools.partial(products_kernel, task_count, unroll),
        out_shape=(
            jax.ShapeDtypeStruct((row_pieces, rows_held, tile_size), jnp.float32),
            jax.ShapeDtypeStruct((col_tiles, rows_held, tile_size), jnp.float32),
            jax.ShapeDtypeStruct((task_count, tile_size), jnp.float32),
        ),
        in_specs=[in_smem] * 6 + [in_vmem] * 3,
        out_specs=(in_vmem,) * 3,
        compiler_params=pltpu.CompilerParams(vmem_limit_bytes=44 * 2**20),
        cost_estimate=pl.CostEstimate(
            flops=4 * slots * rows_held * tile_size * tile_size,
            bytes_accessed=2 * slots * tile_size * tile_size,
            transcendentals=0,
        ),
    )(*lists, row_field, col_field, tiles)


def sorted_lists(ids, loads, per_id):
    slots = ids.shape[0]
    order = jnp.arange(slots, dtype=jnp.int32)
    before = (ids[:, None] == ids[None, :]) & (order[None, :] < order[:, None])
    place = ids * per_id + jnp.sum(before, axis=1, dtype=jnp.int32)
    chosen = place[None, :] == order[:, None]
    pick = lambda values: jnp.sum(jnp.where(chosen, values[None, :], 0), axis=1, dtype=jnp.int32)
    return pick(order), pick(loads)


def exact_parts(value, count):
    parts = []
    for _ in range(count):
        high = lax.reduce_precision(value, 8, 7)
        parts.append(high.astype(jnp.bfloat16))
        value = value - high
    return parts


class Plan:
    def __init__(self, rows, cols):
        self.rows, self.cols = rows, cols
        chip_rows = rows // 2
        others = [("row", m) for m in range(1, chip_rows)]
        self.row_steps = len(others)
        partners = [("col", k) for k in range(1, cols)]
        self.steps = (len(others) + len(partners) + 1) // 2
        first = others + partners[: self.steps - len(others)]
        second = partners[self.steps - len(others) :]
        second += [None] * (self.steps - len(second))
        self.gather_steps = list(zip(first, second, strict=True))
        self.sum_steps = [
            (None if a is None or a[0] == "row" else a, b) for a, b in self.gather_steps
        ]
        place = np.zeros((2, cols), np.int32)
        for j, pair in enumerate(self.gather_steps):
            for core, partner in enumerate(pair):
                if partner is not None and partner[0] == "col":
                    place[core, partner[1]] = 1 + j
                    place[1 - core, partner[1]] = 1 + self.steps + j
        self.place = place

    def pairs(self, by_core):
        found = []
        for r in range(self.rows):
            partner = by_core[r % 2]
            if partner is None:
                continue
            axis, k = partner
            for c in range(self.cols):
                to = (r ^ (2 * k), c) if axis == "row" else (r, c ^ k)
                found.append((r * self.cols + c, to[0] * self.cols + to[1]))
        return found

    def send(self, value, by_core):
        return lax.ppermute(value, MESH_AXES, self.pairs(by_core))

    def swap(self, value):
        return lax.ppermute(value, "row", [(r, r ^ 1) for r in range(self.rows)])


def per_device(plan, scores, tile_values, tile_rows, tile_cols, tile_count):
    tiles = tile_values[0, 0]
    row_ids = tile_rows[0, 0]
    col_ids = tile_cols[0, 0]
    live = tile_count[0, 0]
    slots, tile_size = tiles.shape[0], tiles.shape[1]
    task_count, piece_len = scores.shape
    own_tiles = piece_len // tile_size
    row_tiles, col_tiles = own_tiles * plan.cols, own_tiles * plan.rows
    steps = plan.steps
    row_pieces = own_tiles * (1 + 2 * steps)
    row_index, col_index = lax.axis_index("row"), lax.axis_index("col")
    core = row_index % 2
    low = jnp.bfloat16

    place_of = jnp.where(core == 0, jnp.asarray(plan.place[0]), jnp.asarray(plan.place[1]))

    def row_place(ids):
        piece = (ids // own_tiles) ^ col_index
        chosen = piece[:, None] == jnp.arange(plan.cols, dtype=jnp.int32)[None, :]
        piece = jnp.sum(jnp.where(chosen, place_of[None, :], 0), axis=1, dtype=jnp.int32)
        return piece * own_tiles + ids % own_tiles

    def col_place(ids):
        return ((ids // own_tiles) ^ row_index) * own_tiles + ids % own_tiles

    is_live = jnp.arange(slots, dtype=jnp.int32) < live
    row_loads_of = jnp.where(is_live, row_place(row_ids), row_pieces)
    col_loads_of = jnp.where(is_live, col_place(col_ids), col_tiles)
    lists = (
        *sorted_lists(row_ids, col_loads_of, slots // row_tiles),
        row_place(jnp.arange(row_tiles, dtype=jnp.int32)),
        *sorted_lists(col_ids, row_loads_of, slots // col_tiles),
        col_place(jnp.arange(col_tiles, dtype=jnp.int32)),
    )

    def gather(own):
        sibling = plan.swap(own)
        pair = jnp.concatenate([own, sibling])
        got = [plan.send(pair, by_core) for by_core in plan.gather_steps]
        mine = [g[:own_tiles] for g in got]
        other = [g[own_tiles:] for g in got]
        swapped = plan.swap(jnp.concatenate(other + mine[: plan.row_steps]))
        swapped = jnp.split(swapped, steps + plan.row_steps)
        empty = jnp.zeros((1,) + own.shape[1:], own.dtype)
        col_pieces = [own, sibling]
        for m in range(plan.row_steps):
            col_pieces.append(jnp.where(core == 0, mine[m], swapped[m]))
            col_pieces.append(jnp.where(core == 0, other[m], swapped[steps + m]))
        row_field = jnp.concatenate([own] + mine + swapped[:steps] + [empty])
        col_field = jnp.concatenate(col_pieces + [empty])
        return row_field, col_field

    def with_ones(field):
        field = jnp.pad(field[:-1], ((0, 0), (0, 16), (0, 0)), constant_values=1)
        return jnp.pad(field, ((0, 1), (0, 0), (0, 0)))

    def split_dots(dots, rows_held):
        parts = jnp.stack(exact_parts(dots, 3), axis=1).reshape(-1, task_count).T
        parts = jnp.pad(parts, ((0, rows_held - task_count), (0, tile_size - parts.shape[1])))
        return parts[None]

    def join_dots(tile, count):
        parts = tile[0, :task_count, : 3 * count].astype(jnp.float32)
        return jnp.sum(parts.reshape(task_count, count, 3), axis=2).T

    def totals(forward, backward, dots):
        rows_held = forward.shape[1]
        count = dots.shape[0]
        low_part = own_tiles * steps
        extra = rows_held > task_count

        def to_low(value):
            if not extra:
                return value.astype(low)
            rounded = lax.reduce_precision(value, 8, 7)
            at = lax.broadcasted_iota(jnp.int32, value.shape, 1)
            return jnp.where(at == task_count + 1, value - rounded, rounded).astype(low)

        forward_own = forward[:own_tiles]
        forward_low = to_low(forward[own_tiles:])
        backward = backward.reshape(plan.rows // 2, 2, own_tiles, rows_held, tile_size)
        out = [forward_low[low_part:], to_low(backward[:, 1].reshape(-1, rows_held, tile_size))]
        got = plan.swap(jnp.concatenate(out + [split_dots(dots, rows_held)]))
        forward_sibling = got[:low_part]
        backward_sibling = got[low_part:-1].reshape(backward[:, 0].shape)
        dots = dots + join_dots(got[-1:], count)
        dots_tile = split_dots(dots, rows_held)

        mine, other, dots_mine = 0, 0, 0
        for j, by_core in enumerate(plan.sum_steps):
            piece = slice(j * own_tiles, (j + 1) * own_tiles)
            message = jnp.concatenate([forward_low[piece], forward_sibling[piece], dots_tile])
            back = plan.send(message, by_core).astype(jnp.float32)
            mine += back[:own_tiles]
            other += back[own_tiles:-1]
            dots_mine += join_dots(back[-1:], count)
        dots_wide = jnp.pad(
            dots_mine.T, ((0, rows_held - task_count), (0, tile_size - count))
        )[None]
        got = plan.swap(jnp.concatenate([other, dots_wide]))
        dots = dots + dots_mine + got[-1, :task_count, :count].T

        def clean(value):
            if not extra:
                return value
            at = lax.broadcasted_iota(jnp.int32, value.shape, 1)
            return jnp.where(at == task_count + 1, 0.0, value)

        own = clean(forward_own) + mine + got[:-1]
        backward_mine = [
            clean(backward[m, 0]) + backward_sibling[m].astype(jnp.float32)
            for m in range(plan.rows // 2)
        ]
        own += backward_mine[0]
        dots_tile = split_dots(dots, rows_held)
        for m in range(1, plan.rows // 2):
            wide = backward_mine[m]
            if extra:
                joined = wide[:, task_count] + wide[:, task_count + 1]
                at = lax.broadcasted_iota(jnp.int32, wide.shape, 1)
                wide = jnp.where(at == task_count, joined[:, None], wide)
                wide = jnp.where(at == task_count + 1, joined[:, None], wide)
            message = jnp.concatenate([to_low(wide), dots_tile])
            back = plan.send(message, (("row", m),) * 2).astype(jnp.float32)
            own += back[:-1]
            dots = dots + join_dots(back[-1:], count)
        return 0.5 * own, dots

    def inner(a, b):
        return jnp.sum(a * b, axis=(0, 2))

    residual = scores.reshape(task_count, own_tiles, tile_size).transpose(1, 0, 2)
    solution = direction = image = None
    norm_before = curve_before = scale = None
    for step_index in range(ITERS):
        own_low = residual.astype(low)
        first = step_index == 0
        row_field, col_field = gather(own_low)
        if first:
            row_field, col_field = with_ones(row_field), with_ones(col_field)
        forward, backward, inner_part = products(
            lists, row_field, col_field, tiles, task_count, row_pieces, col_tiles
        )
        norm = inner(residual, residual)
        weighted = norm if first else inner(scale * residual, residual)
        along = jnp.zeros_like(norm) if first else inner(residual, image)
        curve_part = weighted + coupling * jnp.sum(inner_part, axis=1)
        summed, dots = totals(forward, backward, jnp.stack([norm, curve_part, along]))
        if first:
            degree = summed[:, task_count : task_count + 1] + summed[:, task_count + 1 : task_count + 2]
            scale = 1.0 + coupling * degree
        norm, curve, along = dots
        fresh = scale * residual - coupling * summed[:, :task_count]
        if first:
            direction, image = residual, fresh
        else:
            ratio = norm / norm_before
            curve = curve + 2.0 * ratio * along + ratio * ratio * curve_before
            direction = residual + ratio[:, None] * direction
            image = fresh + ratio[:, None] * image
        norm_before, curve_before = norm, curve
        step_size = (norm / curve)[:, None]
        solution = step_size * direction if first else solution + step_size * direction
        residual = residual - step_size * image

    def to_field(value):
        return value.transpose(1, 0, 2).reshape(task_count, piece_len)

    return to_field(solution), to_field(residual)


def solution(mesh):
    plan = Plan(mesh.shape["row"], mesh.shape["col"])
    return jax.shard_map(
        functools.partial(per_device, plan),
        mesh=mesh,
        in_specs=(
            P(None, ("row", "col")),
            P("row", "col", None, None, None),
            P("row", "col", None),
            P("row", "col", None),
            P("row", "col"),
        ),
        out_specs=(P(None, ("row", "col")), P(None, ("row", "col"))),
        check_vma=False,
    )
```

time: 571 us -> 155 us (0.27)
  blocking collectives: 246 us -> 0 us
  other arithmetic: 109 us -> 12.2 us
  matrix products: 65.5 us -> 0 us
  starting transfers between devices: 0.29 us -> 59.3 us
  waiting for transfers between devices: 87.5 us -> 46.7 us
  local copies, waits for them, and re-layouts: 43.8 us -> 16.7 us
  Pallas kernels: 0 us -> 17.4 us
  between operations: 16.4 us -> 2.37 us
    all_gather x8 -> x0, blocking collectives: 179 us -> none  [the longest x5 162 us: row_block(): return lax.all_gather(own_field, 'col', axis=1, tiled=True)]
    scatter-add x32 -> x0, other arithmetic: 78 us -> none  [the longest x15 37.6 us: one_block(): backward_sum.at[:, cols_here, :].add(backward)]
    psum x6 -> x0, blocking collectives: 66.7 us -> none  [the longest x1 37.3 us: row_total(): return lax.psum(partial_value, 'col')]
    dot_general x30 -> x0, matrix products: 65.5 us -> none  [the longest x15 35.6 us: one_block(): jnp.einsum('ksd,sod->kso', col_pieces, tiles_here, preferred_element_type...]
    ppermute x0 -> x39, starting transfers between devices: none -> 59.3 us  [the longest x27 33 us: send(): return lax.ppermute(value, MESH_AXES, self.pairs(by_core))]
    psum x3 -> x0, waiting for transfers between devices: 52.3 us -> none  [row_total(): return lax.psum(partial_value, 'col')]
    ppermute x0 -> x39, waiting for transfers between devices: none -> 46.7 us  [the longest x27 35 us: send(): return lax.ppermute(value, MESH_AXES, self.pairs(by_core))]
    reduce_scatter x3 -> x0, waiting for transfers between devices: 35.1 us -> none  [to_cols(): lax.psum_scatter(partial_value, 'row', scatter_dimension=1, tiled=True)]
  transfers between devices with their start and end apart: 7 -> 39, of which waited for: 4 -> 25; matrix products, arithmetic and copies ran while one was open for 12% -> 5% of each run, Pallas kernels for 0% -> 0%
where the time goes in v1:
time: 155 us
  starting transfers between devices  59.3 us (38%)
  waiting for transfers between devices  46.7 us (30%)
  Pallas kernels  17.4 us (11%)
  local copies, waits for them, and re-layouts  16.7 us (11%)
  other arithmetic  12.2 us (8%)
  between operations  2.37 us (2%)
    ppermute x27, waiting for transfers between devices, send(): return lax.ppermute(value, MESH_AXES, self.pairs(by_core))  35 us
    ppermute x27, starting transfers between devices, send(): return lax.ppermute(value, MESH_AXES, self.pairs(by_core))  33 us
    ppermute x12, starting transfers between devices, swap(): return lax.ppermute(value, 'row', [(r, r ^ 1) for r in range(self.rows)])  26.3 us
    pallas_call x3, Pallas kernels, products(): pl.pallas_call(functools.partial(products_kernel, task_count, unroll), ou...  17.4 us
    ppermute x12, waiting for transfers between devices, swap(): return lax.ppermute(value, 'row', [(r, r ^ 1) for r in range(self.rows)])  11.7 us
    unnamed x50, local copies, waits for them, and re-layouts  8.66 us
  transfers between devices with their start and end apart: 39, of which 25 were waited for; matrix products, arithmetic and copies ran while one was open for 5% of the time, Pallas kernels for 0%

profile of v1, /device:TPU:0, one launch (start us, length us, event | category | flops | bytes accessed | tf_op | source)
XLA Modules:
  0.0 154.6 jit_solution(17548263647208996836)
XLA Ops:
  0.6 0.9 copy-done
  2.2 0.7 fusion.84
  2.9 0.9 convert_reduce_fusion.1
  4.5 0.9 convert_reduce_fusion
  5.4 0.7 broadcast_select_fusion
  6.2 0.7 fusion.77
  7.3 2.6 %collective-permute-start.1 = (bf16[12,32,128]{2,1,0:T(8,128)(2,1)S(1)}, bf16[12,32,128]{2,1,0:T(8,128)(2,1)S(1)}, u32[]{:S(2)}, u32[]{:S(2)}) collective-permute-start(bf16[12,32,128]{2,1,0:T(8,128)(2,1)S(1)} %pad_maximum_fusion.18), channel_id=1, source_target_pairs={{0,16},{1,17},{2,18},{3,19},{4,20},{5,21},{6,22},{7,23},{8,12},{9,... | collective-permute-start | bytes 294920 | tf_op jit(solution)/shard_map/ppermute | solution.py:151
  9.9 2.5 %collective-permute-start.4 = (bf16[12,32,128]{2,1,0:T(8,128)(2,1)S(1)}, bf16[12,32,128]{2,1,0:T(8,128)(2,1)S(1)}, u32[]{:S(2)}, u32[]{:S(2)}) collective-permute-start(bf16[12,32,128]{2,1,0:T(8,128)(2,1)S(1)} %pad_maximum_fusion.18), channel_id=1, source_target_pairs={{0,3},{1,2},{2,1},{3,0},{4,7},{5,6},{6,5},{7,4},{8,15},{9,14},{10,... | collective-permute-start | bytes 294920 | tf_op jit(solution)/shard_map/ppermute | solution.py:151
  13.4 5.1 %collective-permute-done.2 = bf16[12,32,128]{2,1,0:T(8,128)(2,1)S(1)} collective-permute-done((bf16[12,32,128]{2,1,0:T(8,128)(2,1)S(1)}, bf16[12,32,128]{2,1,0:T(8,128)(2,1)S(1)}, u32[]{:S(2)}, u32[]{:S(2)}) %collective-permute-start.2) | collective-permute-done | bytes 98336 | tf_op jit(solution)/shard_map/ppermute | solution.py:151
  18.6 3.8 %collective-permute-start.5 = (bf16[30,32,128]{2,1,0:T(8,128)(2,1)S(1)}, bf16[30,32,128]{2,1,0:T(8,128)(2,1)S(1)}, u32[]{:S(2)}, u32[]{:S(2)}) collective-permute-start(bf16[30,32,128]{2,1,0:T(8,128)(2,1)S(1)} %constant_dynamic-update-slice_fusion), channel_id=1, source_target_pairs={{0,8},{8,0},{16,24},{24,16},{1,9},{9,1},{17,25},{25,17},{2,10},{10... | collective-permute-start | bytes 737288 | tf_op jit(solution)/shard_map/ppermute | solution.py:154
  22.4 1.0 collective-permute-done.5
  23.7 7.8 %shard_map.86 = (f32[54,48,128]{2,1,0:T(8,128)S(1)}, f32[24,48,128]{2,1,0:T(8,128)S(1)}, f32[32,128]{1,0:T(8,128)S(1)}) custom-call(s32[240]{0:T(256)S(1)} %get-tuple-element.37.row_slots, s32[240]{0:T(256)S(1)} %get-tuple-element.36.row_loads, s32[48]{0:T(128)S(1)} %fusion.88.row_place, s32[240]{0:T(256)S(1)} %get-tuple-element.35.col_slots, ...), custom_call_target="tpu_custom_call" | custom-call | flops 754974720 | bytes 7864320 | tf_op jit(solution)/shard_map/pallas_call | solution.py:78
  33.4 0.9 collective-permute-done.6
  34.5 0.7 copy.294
  35.4 0.8 pad_maximum_fusion.2
  36.2 1.5 collective-permute-start.8
  37.7 2.0 %collective-permute-start.10 = (bf16[13,48,128]{2,1,0:T(8,128)(2,1)}, bf16[13,48,128]{2,1,0:T(8,128)(2,1)S(1)}, u32[]{:S(2)}, u32[]{:S(2)}) collective-permute-start(bf16[13,48,128]{2,1,0:T(8,128)(2,1)} %get-tuple-element.111), channel_id=1, source_target_pairs={{0,3},{1,2},{2,1},{3,0},{4,7},{5,6},{6,5},{7,4},{8,15},{9,14},{10,... | collective-permute-start | bytes 479240 | tf_op jit(solution)/shard_map/ppermute | solution.py:151
  39.7 0.7 collective-permute-start.7
  41.1 0.9 collective-permute-done.9
  42.3 4.4 %collective-permute-done.10 = bf16[13,48,128]{2,1,0:T(8,128)(2,1)S(1)} collective-permute-done((bf16[13,48,128]{2,1,0:T(8,128)(2,1)}, bf16[13,48,128]{2,1,0:T(8,128)(2,1)S(1)}, u32[]{:S(2)}, u32[]{:S(2)}) %collective-permute-start.10) | collective-permute-done | bytes 159776 | tf_op jit(solution)/shard_map/ppermute | solution.py:151
  47.6 0.9 convert_element_type.317
  48.7 6.9 %collective-permute-start.11 = (f32[7,48,128]{2,1,0:T(8,128)S(1)}, f32[7,48,128]{2,1,0:T(8,128)}, u32[]{:S(2)}, u32[]{:S(2)}) collective-permute-start(f32[7,48,128]{2,1,0:T(8,128)S(1)} %pad_maximum_fusion.15), channel_id=1, source_target_pairs={{0,8},{8,0},{16,24},{24,16},{1,9},{9,1},{17,25},{25,17},{2,10},{10... | collective-permute-start | bytes 516104 | tf_op jit(solution)/shard_map/ppermute | solution.py:154
  55.7 1.1 collective-permute-done.11
  56.7 0.7 reduce-precision_convert_fusion.5
  57.9 1.4 collective-permute-start.12
  59.3 3.5 %collective-permute-done.12 = bf16[7,48,128]{2,1,0:T(8,128)(2,1)S(1)} collective-permute-done((bf16[7,48,128]{2,1,0:T(8,128)(2,1)S(1)}, bf16[7,48,128]{2,1,0:T(8,128)(2,1)S(1)}, u32[]{:S(2)}, u32[]{:S(2)}) %collective-permute-start.12) | collective-permute-done | bytes 86048 | tf_op jit(solution)/shard_map/ppermute | solution.py:151
  63.2 1.1 fusion.13
  64.5 1.2 collective-permute-done.13
  65.7 1.3 collective-permute-start.14
  67.1 2.6 %collective-permute-start.16 = (bf16[12,32,128]{2,1,0:T(8,128)(2,1)S(1)}, bf16[12,32,128]{2,1,0:T(8,128)(2,1)S(1)}, u32[]{:S(2)}, u32[]{:S(2)}) collective-permute-start(bf16[12,32,128]{2,1,0:T(8,128)(2,1)S(1)} %pad_maximum_fusion.19), channel_id=1, source_target_pairs={{0,2},{1,3},{2,0},{3,1},{4,6},{5,7},{6,4},{7,5},{8,14},{9,15},{10,... | collective-permute-start | bytes 294920 | tf_op jit(solution)/shard_map/ppermute | solution.py:151
  69.7 0.9 collective-permute-start.15
  70.6 4.3 %collective-permute-done.15 = bf16[12,32,128]{2,1,0:T(8,128)(2,1)S(1)} collective-permute-done((bf16[12,32,128]{2,1,0:T(8,128)(2,1)S(1)}, bf16[12,32,128]{2,1,0:T(8,128)(2,1)S(1)}, u32[]{:S(2)}, u32[]{:S(2)}) %collective-permute-start.15) | collective-permute-done | bytes 98336 | tf_op jit(solution)/shard_map/ppermute | solution.py:151
  75.2 2.3 %collective-permute-start.18 = (bf16[30,32,128]{2,1,0:T(8,128)(2,1)S(1)}, bf16[30,32,128]{2,1,0:T(8,128)(2,1)S(1)}, u32[]{:S(2)}, u32[]{:S(2)}) collective-permute-start(bf16[30,32,128]{2,1,0:T(8,128)(2,1)S(1)} %constant_dynamic-update-slice_fusion.10), channel_id=1, source_target_pairs={{0,8},{8,0},{16,24},{24,16},{1,9},{9,1},{17,25},{25,17},{2,10},{10... | collective-permute-start | bytes 737288 | tf_op jit(solution)/shard_map/ppermute | solution.py:154
  77.7 1.0 collective-permute-done.18
  78.8 3.2 %copy-done.1 = bf16[1,1,240,128,128]{4,3,2,1,0:T(8,128)(2,1)S(1)} copy-done((bf16[1,1,240,128,128]{4,3,2,1,0:T(8,128)(2,1)S(1)}, bf16[1,1,240,128,128]{4,3,2,1,0:T(8,128)(2,1)}, u32[]{:S(2)}) %copy-start.1) | copy-done | bytes 7864344
  82.1 4.8 %shard_map.87 = (f32[54,32,128]{2,1,0:T(8,128)S(1)}, f32[24,32,128]{2,1,0:T(8,128)S(1)}, f32[32,128]{1,0:T(8,128)S(1)}) custom-call(s32[240]{0:T(256)S(1)} %get-tuple-element.37.row_slots, s32[240]{0:T(256)S(1)} %get-tuple-element.36.row_loads, s32[48]{0:T(128)S(1)} %fusion.88.row_place, s32[240]{0:T(256)S(1)} %get-tuple-element.35.col_slots, ...), custom_call_target="tpu_custom_call" | custom-call | flops 503316480 | bytes 7864320 | tf_op jit(solution)/shard_map/pallas_call | solution.py:78
  87.8 1.2 collective-permute-done.19
  89.5 1.2 collective-permute-start.21
  90.7 2.3 %collective-permute-start.23 = (bf16[13,32,128]{2,1,0:T(8,128)(2,1)S(1)}, bf16[13,32,128]{2,1,0:T(8,128)(2,1)S(1)}, u32[]{:S(2)}, u32[]{:S(2)}) collective-permute-start(bf16[13,32,128]{2,1,0:T(8,128)(2,1)S(1)} %get-tuple-element.119), channel_id=1, source_target_pairs={{0,3},{1,2},{2,1},{3,0},{4,7},{5,6},{6,5},{7,4},{8,15},{9,14},{10,... | collective-permute-start | bytes 319496 | tf_op jit(solution)/shard_map/ppermute | solution.py:151
  92.9 0.7 collective-permute-start.20
  94.5 2.7 %collective-permute-done.23 = bf16[13,32,128]{2,1,0:T(8,128)(2,1)S(1)} collective-permute-done((bf16[13,32,128]{2,1,0:T(8,128)(2,1)S(1)}, bf16[13,32,128]{2,1,0:T(8,128)(2,1)S(1)}, u32[]{:S(2)}, u32[]{:S(2)}) %collective-permute-start.23) | collective-permute-done | bytes 106528 | tf_op jit(solution)/shard_map/ppermute | solution.py:151
  97.8 4.7 %collective-permute-start.24 = (f32[7,32,128]{2,1,0:T(8,128)S(1)}, f32[7,32,128]{2,1,0:T(8,128)S(1)}, u32[]{:S(2)}, u32[]{:S(2)}) collective-permute-start(f32[7,32,128]{2,1,0:T(8,128)S(1)} %pad_maximum_fusion.16), channel_id=1, source_target_pairs={{0,8},{8,0},{16,24},{24,16},{1,9},{9,1},{17,25},{25,17},{2,10},{10... | collective-permute-start | bytes 344072 | tf_op jit(solution)/shard_map/ppermute | solution.py:154
  102.5 0.9 collective-permute-done.24
  103.9 1.5 collective-permute-start.25
  105.5 2.7 %collective-permute-done.25 = bf16[7,32,128]{2,1,0:T(8,128)(2,1)S(1)} collective-permute-done((bf16[7,32,128]{2,1,0:T(8,128)(2,1)S(1)}, bf16[7,32,128]{2,1,0:T(8,128)(2,1)S(1)}, u32[]{:S(2)}, u32[]{:S(2)}) %collective-permute-start.25) | collective-permute-done | bytes 57376 | tf_op jit(solution)/shard_map/ppermute | solution.py:151
  108.9 1.2 collective-permute-done.26
  110.1 1.5 collective-permute-start.27
  111.7 2.7 %collective-permute-start.29 = (bf16[12,32,128]{2,1,0:T(8,128)(2,1)S(1)}, bf16[12,32,128]{2,1,0:T(8,128)(2,1)S(1)}, u32[]{:S(2)}, u32[]{:S(2)}) collective-permute-start(bf16[12,32,128]{2,1,0:T(8,128)(2,1)S(1)} %pad_maximum_fusion.20), channel_id=1, source_target_pairs={{0,2},{1,3},{2,0},{3,1},{4,6},{5,7},{6,4},{7,5},{8,14},{9,15},{10,... | collective-permute-start | bytes 294920 | tf_op jit(solution)/shard_map/ppermute | solution.py:151
  114.4 0.8 collective-permute-start.28
  115.1 4.0 %collective-permute-done.28 = bf16[12,32,128]{2,1,0:T(8,128)(2,1)S(1)} collective-permute-done((bf16[12,32,128]{2,1,0:T(8,128)(2,1)S(1)}, bf16[12,32,128]{2,1,0:T(8,128)(2,1)S(1)}, u32[]{:S(2)}, u32[]{:S(2)}) %collective-permute-start.28) | collective-permute-done | bytes 98336 | tf_op jit(solution)/shard_map/ppermute | solution.py:151
  119.1 0.7 collective-permute-done.29
  119.8 2.2 %collective-permute-start.31 = (bf16[30,32,128]{2,1,0:T(8,128)(2,1)S(1)}, bf16[30,32,128]{2,1,0:T(8,128)(2,1)S(1)}, u32[]{:S(2)}, u32[]{:S(2)}) collective-permute-start(bf16[30,32,128]{2,1,0:T(8,128)(2,1)S(1)} %constant_dynamic-update-slice_fusion.26), channel_id=1, source_target_pairs={{0,8},{8,0},{16,24},{24,16},{1,9},{9,1},{17,25},{25,17},{2,10},{10... | collective-permute-start | bytes 737288 | tf_op jit(solution)/shard_map/ppermute | solution.py:154
  122.2 1.0 collective-permute-done.31
  123.3 3.2 %copy-done.2 = bf16[1,1,240,128,128]{4,3,2,1,0:T(8,128)(2,1)S(1)} copy-done((bf16[1,1,240,128,128]{4,3,2,1,0:T(8,128)(2,1)S(1)}, bf16[1,1,240,128,128]{4,3,2,1,0:T(8,128)(2,1)}, u32[]{:S(2)}) %copy-start.2) | copy-done | bytes 7864344
  126.5 4.8 %shard_map.88 = (f32[54,32,128]{2,1,0:T(8,128)S(1)}, f32[24,32,128]{2,1,0:T(8,128)S(1)}, f32[32,128]{1,0:T(8,128)S(1)}) custom-call(s32[240]{0:T(256)S(1)} %get-tuple-element.37.row_slots, s32[240]{0:T(256)S(1)} %get-tuple-element.36.row_loads, s32[48]{0:T(128)S(1)} %fusion.88.row_place, s32[240]{0:T(256)S(1)} %get-tuple-element.35.col_slots, ...), custom_call_target="tpu_custom_call" | custom-call | flops 503316480 | bytes 7864320 | tf_op jit(solution)/shard_map/pallas_call | solution.py:78
  132.3 1.2 collective-permute-done.32
  133.9 1.3 collective-permute-start.34
  135.2 2.2 %collective-permute-start.36 = (bf16[13,32,128]{2,1,0:T(8,128)(2,1)S(1)}, bf16[13,32,128]{2,1,0:T(8,128)(2,1)S(1)}, u32[]{:S(2)}, u32[]{:S(2)}) collective-permute-start(bf16[13,32,128]{2,1,0:T(8,128)(2,1)S(1)} %get-tuple-element.115), channel_id=1, source_target_pairs={{0,3},{1,2},{2,1},{3,0},{4,7},{5,6},{6,5},{7,4},{8,15},{9,14},{10,... | collective-permute-start | bytes 319496 | tf_op jit(solution)/shard_map/ppermute | solution.py:151
  137.4 0.7 collective-permute-start.33
  139.0 2.9 %collective-permute-done.36 = bf16[13,32,128]{2,1,0:T(8,128)(2,1)S(1)} collective-permute-done((bf16[13,32,128]{2,1,0:T(8,128)(2,1)S(1)}, bf16[13,32,128]{2,1,0:T(8,128)(2,1)S(1)}, u32[]{:S(2)}, u32[]{:S(2)}) %collective-permute-start.36) | collective-permute-done | bytes 106528 | tf_op jit(solution)/shard_map/ppermute | solution.py:151
  142.5 4.5 %collective-permute-start.37 = (f32[7,32,128]{2,1,0:T(8,128)S(1)}, f32[7,32,128]{2,1,0:T(8,128)S(1)}, u32[]{:S(2)}, u32[]{:S(2)}) collective-permute-start(f32[7,32,128]{2,1,0:T(8,128)S(1)} %pad_maximum_fusion.17), channel_id=1, source_target_pairs={{0,8},{8,0},{16,24},{24,16},{1,9},{9,1},{17,25},{25,17},{2,10},{10... | collective-permute-start | bytes 344072 | tf_op jit(solution)/shard_map/ppermute | solution.py:154
  147.0 0.9 collective-permute-done.37
  148.4 1.6 %collective-permute-start.38 = (bf16[7,32,128]{2,1,0:T(8,128)(2,1)S(1)}, bf16[7,32,128]{2,1,0:T(8,128)(2,1)S(1)}, u32[]{:S(2)}, u32[]{:S(2)}) collective-permute-start(bf16[7,32,128]{2,1,0:T(8,128)(2,1)S(1)} %pad_maximum_fusion.23), channel_id=1, source_target_pairs={{0,16},{1,17},{2,18},{3,19},{4,20},{5,21},{6,22},{7,23},{8,24},{9,... | collective-permute-start | bytes 172040 | tf_op jit(solution)/shard_map/ppermute | solution.py:151
  150.0 2.7 %collective-permute-done.38 = bf16[7,32,128]{2,1,0:T(8,128)(2,1)S(1)} collective-permute-done((bf16[7,32,128]{2,1,0:T(8,128)(2,1)S(1)}, bf16[7,32,128]{2,1,0:T(8,128)(2,1)S(1)}, u32[]{:S(2)}, u32[]{:S(2)}) %collective-permute-start.38) | collective-permute-done | bytes 57376 | tf_op jit(solution)/shard_map/ppermute | solution.py:151
  (342 shorter events, 17.9 us)
Async XLA Ops:
  0.6 0.9 copy-start
  1.5 5.8 %collective-permute-start = (bf16[6,32,128]{2,1,0:T(8,128)(2,1)S(1)}, bf16[6,32,128]{2,1,0:T(8,128)(2,1)S(1)}, u32[]{:S(2)}, u32[]{:S(2)}) collective-permute-start(bf16[6,32,128]{2,1,0:T(8,128)(2,1)S(1)} %get-tuple-element.69), channel_id=1, source_target_pairs={{0,8},{8,0},{16,24},{24,16},{1,9},{9,1},{17,25},{25,17},{2,10},{10... | collective-permute-start | bytes 147464 | tf_op jit(solution)/shard_map/ppermute | solution.py:154
  7.3 6.1 %collective-permute-start.1 = (bf16[12,32,128]{2,1,0:T(8,128)(2,1)S(1)}, bf16[12,32,128]{2,1,0:T(8,128)(2,1)S(1)}, u32[]{:S(2)}, u32[]{:S(2)}) collective-permute-start(bf16[12,32,128]{2,1,0:T(8,128)(2,1)S(1)} %pad_maximum_fusion.18), channel_id=1, source_target_pairs={{0,16},{1,17},{2,18},{3,19},{4,20},{5,21},{6,22},{7,23},{8,12},{9,... | collective-permute-start | bytes 294920 | tf_op jit(solution)/shard_map/ppermute | solution.py:151
  9.9 30.4 %copy-start.7 = (pred[48]{0:T(512)(128)(4,1)}, pred[48]{0:T(512)(128)(4,1)S(1)}, u32[]{:S(2)}) copy-start(pred[48]{0:T(512)(128)(4,1)S(1)} %iota_compare_fusion.9) | copy-start | bytes 148
  9.9 8.6 %collective-permute-start.4 = (bf16[12,32,128]{2,1,0:T(8,128)(2,1)S(1)}, bf16[12,32,128]{2,1,0:T(8,128)(2,1)S(1)}, u32[]{:S(2)}, u32[]{:S(2)}) collective-permute-start(bf16[12,32,128]{2,1,0:T(8,128)(2,1)S(1)} %pad_maximum_fusion.18), channel_id=1, source_target_pairs={{0,3},{1,2},{2,1},{3,0},{4,7},{5,6},{6,5},{7,4},{8,15},{9,14},{10,... | collective-permute-start | bytes 294920 | tf_op jit(solution)/shard_map/ppermute | solution.py:151
  12.4 6.1 %collective-permute-start.3 = (bf16[12,32,128]{2,1,0:T(8,128)(2,1)S(1)}, bf16[12,32,128]{2,1,0:T(8,128)(2,1)S(1)}, u32[]{:S(2)}, u32[]{:S(2)}) collective-permute-start(bf16[12,32,128]{2,1,0:T(8,128)(2,1)S(1)} %pad_maximum_fusion.18), channel_id=1, source_target_pairs={{0,2},{1,3},{2,0},{3,1},{4,6},{5,7},{6,4},{7,5},{8,14},{9,15},{10,... | collective-permute-start | bytes 294920 | tf_op jit(solution)/shard_map/ppermute | solution.py:151
  12.9 5.6 %collective-permute-start.2 = (bf16[12,32,128]{2,1,0:T(8,128)(2,1)S(1)}, bf16[12,32,128]{2,1,0:T(8,128)(2,1)S(1)}, u32[]{:S(2)}, u32[]{:S(2)}) collective-permute-start(bf16[12,32,128]{2,1,0:T(8,128)(2,1)S(1)} %pad_maximum_fusion.18), channel_id=1, source_target_pairs={{0,1},{1,0},{2,3},{3,2},{4,5},{5,4},{6,7},{7,6},{8,13},{9,12},{10,... | collective-permute-start | bytes 294920 | tf_op jit(solution)/shard_map/ppermute | solution.py:151
  18.6 4.9 %collective-permute-start.5 = (bf16[30,32,128]{2,1,0:T(8,128)(2,1)S(1)}, bf16[30,32,128]{2,1,0:T(8,128)(2,1)S(1)}, u32[]{:S(2)}, u32[]{:S(2)}) collective-permute-start(bf16[30,32,128]{2,1,0:T(8,128)(2,1)S(1)} %constant_dynamic-update-slice_fusion), channel_id=1, source_target_pairs={{0,8},{8,0},{16,24},{24,16},{1,9},{9,1},{17,25},{25,17},{2,10},{10... | collective-permute-start | bytes 737288 | tf_op jit(solution)/shard_map/ppermute | solution.py:154
  32.4 1.9 %collective-permute-start.6 = (bf16[37,48,128]{2,1,0:T(8,128)(2,1)S(1)}, bf16[37,48,128]{2,1,0:T(8,128)(2,1)S(1)}, u32[]{:S(2)}, u32[]{:S(2)}) collective-permute-start(bf16[37,48,128]{2,1,0:T(8,128)(2,1)S(1)} %pad_maximum_fusion), channel_id=1, source_target_pairs={{0,8},{8,0},{16,24},{24,16},{1,9},{9,1},{17,25},{25,17},{2,10},{10... | collective-permute-start | bytes 1363976 | tf_op jit(solution)/shard_map/ppermute | solution.py:154
  34.3 12.8 %copy-start.3 = (bf16[37,48,128]{2,1,0:T(8,128)(2,1)}, bf16[37,48,128]{2,1,0:T(8,128)(2,1)S(1)}, u32[]{:S(2)}) copy-start(bf16[37,48,128]{2,1,0:T(8,128)(2,1)S(1)} %collective-permute-done.6) | copy-start | bytes 1363972
  36.2 5.8 %collective-permute-start.9 = (bf16[13,48,128]{2,1,0:T(8,128)(2,1)S(1)}, bf16[13,48,128]{2,1,0:T(8,128)(2,1)S(1)}, u32[]{:S(2)}, u32[]{:S(2)}) collective-permute-start(bf16[13,48,128]{2,1,0:T(8,128)(2,1)S(1)} %get-tuple-element.109), channel_id=1, source_target_pairs={{0,2},{1,3},{2,0},{3,1},{4,6},{5,7},{6,4},{7,5},{8,14},{9,15},{10,... | collective-permute-start | bytes 479240 | tf_op jit(solution)/shard_map/ppermute | solution.py:151
  36.2 6.0 %collective-permute-start.8 = (bf16[13,48,128]{2,1,0:T(8,128)(2,1)}, bf16[13,48,128]{2,1,0:T(8,128)(2,1)S(1)}, u32[]{:S(2)}, u32[]{:S(2)}) collective-permute-start(bf16[13,48,128]{2,1,0:T(8,128)(2,1)} %get-tuple-element.110), channel_id=1, source_target_pairs={{0,1},{1,0},{2,3},{3,2},{4,5},{5,4},{6,7},{7,6},{8,13},{9,12},{10,... | collective-permute-start | bytes 479240 | tf_op jit(solution)/shard_map/ppermute | solution.py:151
  37.7 9.0 %collective-permute-start.10 = (bf16[13,48,128]{2,1,0:T(8,128)(2,1)}, bf16[13,48,128]{2,1,0:T(8,128)(2,1)S(1)}, u32[]{:S(2)}, u32[]{:S(2)}) collective-permute-start(bf16[13,48,128]{2,1,0:T(8,128)(2,1)} %get-tuple-element.111), channel_id=1, source_target_pairs={{0,3},{1,2},{2,1},{3,0},{4,7},{5,6},{6,5},{7,4},{8,15},{9,14},{10,... | collective-permute-start | bytes 479240 | tf_op jit(solution)/shard_map/ppermute | solution.py:151
  39.7 7.2 %collective-permute-start.7 = (bf16[13,48,128]{2,1,0:T(8,128)(2,1)S(1)}, bf16[13,48,128]{2,1,0:T(8,128)(2,1)S(1)}, u32[]{:S(2)}, u32[]{:S(2)}) collective-permute-start(bf16[13,48,128]{2,1,0:T(8,128)(2,1)S(1)} %get-tuple-element.112), channel_id=1, source_target_pairs={{8,12},{9,13},{10,14},{11,15},{12,8},{13,9},{14,10},{15,11},{24,28... | collective-permute-start | bytes 479240 | tf_op jit(solution)/shard_map/ppermute | solution.py:151
  46.9 0.7 copy-start.4
  47.6 8.0 %copy-start.6 = (f32[6,1,128]{2,0,1:T(8,128)S(1)}, f32[6,1,128]{2,0,1:T(8,128)}, u32[]{:S(2)}) copy-start(f32[6,1,128]{2,0,1:T(8,128)} %copy.377) | copy-start | bytes 9220
  47.6 8.0 %copy-start.8 = (pred[48]{0:T(512)(128)(4,1)S(1)}, pred[48]{0:T(512)(128)(4,1)}, u32[]{:S(2)}) copy-start(pred[48]{0:T(512)(128)(4,1)} %copy-done.7) | copy-start | bytes 148
  47.6 8.0 %copy-start.9 = (pred[48]{0:T(512)(128)(4,1)S(1)}, pred[48]{0:T(512)(128)(4,1)}, u32[]{:S(2)}) copy-start(pred[48]{0:T(512)(128)(4,1)} %iota_compare_fusion.8) | copy-start | bytes 148
  47.6 9.1 %copy-start.5 = (f32[3,32]{0,1:T(8,128)S(1)}, f32[3,32]{0,1:T(8,128)}, u32[]{:S(2)}) copy-start(f32[3,32]{0,1:T(8,128)} %copy.294) | copy-start | bytes 1156
  48.7 8.1 %collective-permute-start.11 = (f32[7,48,128]{2,1,0:T(8,128)S(1)}, f32[7,48,128]{2,1,0:T(8,128)}, u32[]{:S(2)}, u32[]{:S(2)}) collective-permute-start(f32[7,48,128]{2,1,0:T(8,128)S(1)} %pad_maximum_fusion.15), channel_id=1, source_target_pairs={{0,8},{8,0},{16,24},{24,16},{1,9},{9,1},{17,25},{25,17},{2,10},{10... | collective-permute-start | bytes 516104 | tf_op jit(solution)/shard_map/ppermute | solution.py:154
  57.9 4.9 %collective-permute-start.12 = (bf16[7,48,128]{2,1,0:T(8,128)(2,1)S(1)}, bf16[7,48,128]{2,1,0:T(8,128)(2,1)S(1)}, u32[]{:S(2)}, u32[]{:S(2)}) collective-permute-start(bf16[7,48,128]{2,1,0:T(8,128)(2,1)S(1)} %pad_maximum_fusion.21), channel_id=1, source_target_pairs={{0,16},{1,17},{2,18},{3,19},{4,20},{5,21},{6,22},{7,23},{8,24},{9,... | collective-permute-start | bytes 258056 | tf_op jit(solution)/shard_map/ppermute | solution.py:151
  64.4 1.3 collective-permute-start.13
  65.7 4.8 %collective-permute-start.14 = (bf16[12,32,128]{2,1,0:T(8,128)(2,1)S(1)}, bf16[12,32,128]{2,1,0:T(8,128)(2,1)S(1)}, u32[]{:S(2)}, u32[]{:S(2)}) collective-permute-start(bf16[12,32,128]{2,1,0:T(8,128)(2,1)S(1)} %pad_maximum_fusion.19), channel_id=1, source_target_pairs={{0,16},{1,17},{2,18},{3,19},{4,20},{5,21},{6,22},{7,23},{8,12},{9,... | collective-permute-start | bytes 294920 | tf_op jit(solution)/shard_map/ppermute | solution.py:151
  67.1 8.1 %collective-permute-start.17 = (bf16[12,32,128]{2,1,0:T(8,128)(2,1)S(1)}, bf16[12,32,128]{2,1,0:T(8,128)(2,1)S(1)}, u32[]{:S(2)}, u32[]{:S(2)}) collective-permute-start(bf16[12,32,128]{2,1,0:T(8,128)(2,1)S(1)} %pad_maximum_fusion.19), channel_id=1, source_target_pairs={{0,3},{1,2},{2,1},{3,0},{4,7},{5,6},{6,5},{7,4},{8,15},{9,14},{10,... | collective-permute-start | bytes 294920 | tf_op jit(solution)/shard_map/ppermute | solution.py:151
  67.1 8.1 %collective-permute-start.16 = (bf16[12,32,128]{2,1,0:T(8,128)(2,1)S(1)}, bf16[12,32,128]{2,1,0:T(8,128)(2,1)S(1)}, u32[]{:S(2)}, u32[]{:S(2)}) collective-permute-start(bf16[12,32,128]{2,1,0:T(8,128)(2,1)S(1)} %pad_maximum_fusion.19), channel_id=1, source_target_pairs={{0,2},{1,3},{2,0},{3,1},{4,6},{5,7},{6,4},{7,5},{8,14},{9,15},{10,... | collective-permute-start | bytes 294920 | tf_op jit(solution)/shard_map/ppermute | solution.py:151
  69.7 5.1 %collective-permute-start.15 = (bf16[12,32,128]{2,1,0:T(8,128)(2,1)S(1)}, bf16[12,32,128]{2,1,0:T(8,128)(2,1)S(1)}, u32[]{:S(2)}, u32[]{:S(2)}) collective-permute-start(bf16[12,32,128]{2,1,0:T(8,128)(2,1)S(1)} %pad_maximum_fusion.19), channel_id=1, source_target_pairs={{0,1},{1,0},{2,3},{3,2},{4,5},{5,4},{6,7},{7,6},{8,13},{9,12},{10,... | collective-permute-start | bytes 294920 | tf_op jit(solution)/shard_map/ppermute | solution.py:151
  75.2 3.4 %collective-permute-start.18 = (bf16[30,32,128]{2,1,0:T(8,128)(2,1)S(1)}, bf16[30,32,128]{2,1,0:T(8,128)(2,1)S(1)}, u32[]{:S(2)}, u32[]{:S(2)}) collective-permute-start(bf16[30,32,128]{2,1,0:T(8,128)(2,1)S(1)} %constant_dynamic-update-slice_fusion.10), channel_id=1, source_target_pairs={{0,8},{8,0},{16,24},{24,16},{1,9},{9,1},{17,25},{25,17},{2,10},{10... | collective-permute-start | bytes 737288 | tf_op jit(solution)/shard_map/ppermute | solution.py:154
  78.8 3.2 %copy-start.1 = (bf16[1,1,240,128,128]{4,3,2,1,0:T(8,128)(2,1)S(1)}, bf16[1,1,240,128,128]{4,3,2,1,0:T(8,128)(2,1)}, u32[]{:S(2)}) copy-start(bf16[1,1,240,128,128]{4,3,2,1,0:T(8,128)(2,1)} %param.8) | copy-start | bytes 23592964
  87.3 1.7 %collective-permute-start.19 = (bf16[37,32,128]{2,1,0:T(8,128)(2,1)S(1)}, bf16[37,32,128]{2,1,0:T(8,128)(2,1)S(1)}, u32[]{:S(2)}, u32[]{:S(2)}) collective-permute-start(bf16[37,32,128]{2,1,0:T(8,128)(2,1)S(1)} %pad_maximum_fusion.5), channel_id=1, source_target_pairs={{0,8},{8,0},{16,24},{24,16},{1,9},{9,1},{17,25},{25,17},{2,10},{10... | collective-permute-start | bytes 909320 | tf_op jit(solution)/shard_map/ppermute | solution.py:154
  89.4 4.8 %collective-permute-start.22 = (bf16[13,32,128]{2,1,0:T(8,128)(2,1)S(1)}, bf16[13,32,128]{2,1,0:T(8,128)(2,1)S(1)}, u32[]{:S(2)}, u32[]{:S(2)}) collective-permute-start(bf16[13,32,128]{2,1,0:T(8,128)(2,1)S(1)} %get-tuple-element.117), channel_id=1, source_target_pairs={{0,2},{1,3},{2,0},{3,1},{4,6},{5,7},{6,4},{7,5},{8,14},{9,15},{10,... | collective-permute-start | bytes 319496 | tf_op jit(solution)/shard_map/ppermute | solution.py:151
  89.5 4.9 %collective-permute-start.21 = (bf16[13,32,128]{2,1,0:T(8,128)(2,1)S(1)}, bf16[13,32,128]{2,1,0:T(8,128)(2,1)S(1)}, u32[]{:S(2)}, u32[]{:S(2)}) collective-permute-start(bf16[13,32,128]{2,1,0:T(8,128)(2,1)S(1)} %get-tuple-element.118), channel_id=1, source_target_pairs={{0,1},{1,0},{2,3},{3,2},{4,5},{5,4},{6,7},{7,6},{8,13},{9,12},{10,... | collective-permute-start | bytes 319496 | tf_op jit(solution)/shard_map/ppermute | solution.py:151
  90.7 6.5 %collective-permute-start.23 = (bf16[13,32,128]{2,1,0:T(8,128)(2,1)S(1)}, bf16[13,32,128]{2,1,0:T(8,128)(2,1)S(1)}, u32[]{:S(2)}, u32[]{:S(2)}) collective-permute-start(bf16[13,32,128]{2,1,0:T(8,128)(2,1)S(1)} %get-tuple-element.119), channel_id=1, source_target_pairs={{0,3},{1,2},{2,1},{3,0},{4,7},{5,6},{6,5},{7,4},{8,15},{9,14},{10,... | collective-permute-start | bytes 319496 | tf_op jit(solution)/shard_map/ppermute | solution.py:151
  92.9 4.4 %collective-permute-start.20 = (bf16[13,32,128]{2,1,0:T(8,128)(2,1)S(1)}, bf16[13,32,128]{2,1,0:T(8,128)(2,1)S(1)}, u32[]{:S(2)}, u32[]{:S(2)}) collective-permute-start(bf16[13,32,128]{2,1,0:T(8,128)(2,1)S(1)} %get-tuple-element.120), channel_id=1, source_target_pairs={{8,12},{9,13},{10,14},{11,15},{12,8},{13,9},{14,10},{15,11},{24,28... | collective-permute-start | bytes 319496 | tf_op jit(solution)/shard_map/ppermute | solution.py:151
  97.8 5.7 %collective-permute-start.24 = (f32[7,32,128]{2,1,0:T(8,128)S(1)}, f32[7,32,128]{2,1,0:T(8,128)S(1)}, u32[]{:S(2)}, u32[]{:S(2)}) collective-permute-start(f32[7,32,128]{2,1,0:T(8,128)S(1)} %pad_maximum_fusion.16), channel_id=1, source_target_pairs={{0,8},{8,0},{16,24},{24,16},{1,9},{9,1},{17,25},{25,17},{2,10},{10... | collective-permute-start | bytes 344072 | tf_op jit(solution)/shard_map/ppermute | solution.py:154
  103.9 4.3 %collective-permute-start.25 = (bf16[7,32,128]{2,1,0:T(8,128)(2,1)S(1)}, bf16[7,32,128]{2,1,0:T(8,128)(2,1)S(1)}, u32[]{:S(2)}, u32[]{:S(2)}) collective-permute-start(bf16[7,32,128]{2,1,0:T(8,128)(2,1)S(1)} %pad_maximum_fusion.22), channel_id=1, source_target_pairs={{0,16},{1,17},{2,18},{3,19},{4,20},{5,21},{6,22},{7,23},{8,24},{9,... | collective-permute-start | bytes 172040 | tf_op jit(solution)/shard_map/ppermute | solution.py:151
  108.8 1.3 collective-permute-start.26
  110.1 5.0 %collective-permute-start.27 = (bf16[12,32,128]{2,1,0:T(8,128)(2,1)S(1)}, bf16[12,32,128]{2,1,0:T(8,128)(2,1)S(1)}, u32[]{:S(2)}, u32[]{:S(2)}) collective-permute-start(bf16[12,32,128]{2,1,0:T(8,128)(2,1)S(1)} %pad_maximum_fusion.20), channel_id=1, source_target_pairs={{0,16},{1,17},{2,18},{3,19},{4,20},{5,21},{6,22},{7,23},{8,12},{9,... | collective-permute-start | bytes 294920 | tf_op jit(solution)/shard_map/ppermute | solution.py:151
  111.6 8.2 %collective-permute-start.30 = (bf16[12,32,128]{2,1,0:T(8,128)(2,1)S(1)}, bf16[12,32,128]{2,1,0:T(8,128)(2,1)S(1)}, u32[]{:S(2)}, u32[]{:S(2)}) collective-permute-start(bf16[12,32,128]{2,1,0:T(8,128)(2,1)S(1)} %pad_maximum_fusion.20), channel_id=1, source_target_pairs={{0,3},{1,2},{2,1},{3,0},{4,7},{5,6},{6,5},{7,4},{8,15},{9,14},{10,... | collective-permute-start | bytes 294920 | tf_op jit(solution)/shard_map/ppermute | solution.py:151
  111.7 8.1 %collective-permute-start.29 = (bf16[12,32,128]{2,1,0:T(8,128)(2,1)S(1)}, bf16[12,32,128]{2,1,0:T(8,128)(2,1)S(1)}, u32[]{:S(2)}, u32[]{:S(2)}) collective-permute-start(bf16[12,32,128]{2,1,0:T(8,128)(2,1)S(1)} %pad_maximum_fusion.20), channel_id=1, source_target_pairs={{0,2},{1,3},{2,0},{3,1},{4,6},{5,7},{6,4},{7,5},{8,14},{9,15},{10,... | collective-permute-start | bytes 294920 | tf_op jit(solution)/shard_map/ppermute | solution.py:151
  114.4 4.7 %collective-permute-start.28 = (bf16[12,32,128]{2,1,0:T(8,128)(2,1)S(1)}, bf16[12,32,128]{2,1,0:T(8,128)(2,1)S(1)}, u32[]{:S(2)}, u32[]{:S(2)}) collective-permute-start(bf16[12,32,128]{2,1,0:T(8,128)(2,1)S(1)} %pad_maximum_fusion.20), channel_id=1, source_target_pairs={{0,1},{1,0},{2,3},{3,2},{4,5},{5,4},{6,7},{7,6},{8,13},{9,12},{10,... | collective-permute-start | bytes 294920 | tf_op jit(solution)/shard_map/ppermute | solution.py:151
  119.8 3.3 %collective-permute-start.31 = (bf16[30,32,128]{2,1,0:T(8,128)(2,1)S(1)}, bf16[30,32,128]{2,1,0:T(8,128)(2,1)S(1)}, u32[]{:S(2)}, u32[]{:S(2)}) collective-permute-start(bf16[30,32,128]{2,1,0:T(8,128)(2,1)S(1)} %constant_dynamic-update-slice_fusion.26), channel_id=1, source_target_pairs={{0,8},{8,0},{16,24},{24,16},{1,9},{9,1},{17,25},{25,17},{2,10},{10... | collective-permute-start | bytes 737288 | tf_op jit(solution)/shard_map/ppermute | solution.py:154
  123.3 3.2 %copy-start.2 = (bf16[1,1,240,128,128]{4,3,2,1,0:T(8,128)(2,1)S(1)}, bf16[1,1,240,128,128]{4,3,2,1,0:T(8,128)(2,1)}, u32[]{:S(2)}) copy-start(bf16[1,1,240,128,128]{4,3,2,1,0:T(8,128)(2,1)} %param.8) | copy-start | bytes 23592964
  131.8 1.7 %collective-permute-start.32 = (bf16[37,32,128]{2,1,0:T(8,128)(2,1)S(1)}, bf16[37,32,128]{2,1,0:T(8,128)(2,1)S(1)}, u32[]{:S(2)}, u32[]{:S(2)}) collective-permute-start(bf16[37,32,128]{2,1,0:T(8,128)(2,1)S(1)} %pad_maximum_fusion.6), channel_id=1, source_target_pairs={{0,8},{8,0},{16,24},{24,16},{1,9},{9,1},{17,25},{25,17},{2,10},{10... | collective-permute-start | bytes 909320 | tf_op jit(solution)/shard_map/ppermute | solution.py:154
  133.9 4.8 %collective-permute-start.35 = (bf16[13,32,128]{2,1,0:T(8,128)(2,1)S(1)}, bf16[13,32,128]{2,1,0:T(8,128)(2,1)S(1)}, u32[]{:S(2)}, u32[]{:S(2)}) collective-permute-start(bf16[13,32,128]{2,1,0:T(8,128)(2,1)S(1)} %get-tuple-element.113), channel_id=1, source_target_pairs={{0,2},{1,3},{2,0},{3,1},{4,6},{5,7},{6,4},{7,5},{8,14},{9,15},{10,... | collective-permute-start | bytes 319496 | tf_op jit(solution)/shard_map/ppermute | solution.py:151
  133.9 4.9 %collective-permute-start.34 = (bf16[13,32,128]{2,1,0:T(8,128)(2,1)S(1)}, bf16[13,32,128]{2,1,0:T(8,128)(2,1)S(1)}, u32[]{:S(2)}, u32[]{:S(2)}) collective-permute-start(bf16[13,32,128]{2,1,0:T(8,128)(2,1)S(1)} %get-tuple-element.114), channel_id=1, source_target_pairs={{0,1},{1,0},{2,3},{3,2},{4,5},{5,4},{6,7},{7,6},{8,13},{9,12},{10,... | collective-permute-start | bytes 319496 | tf_op jit(solution)/shard_map/ppermute | solution.py:151
  135.2 6.7 %collective-permute-start.36 = (bf16[13,32,128]{2,1,0:T(8,128)(2,1)S(1)}, bf16[13,32,128]{2,1,0:T(8,128)(2,1)S(1)}, u32[]{:S(2)}, u32[]{:S(2)}) collective-permute-start(bf16[13,32,128]{2,1,0:T(8,128)(2,1)S(1)} %get-tuple-element.115), channel_id=1, source_target_pairs={{0,3},{1,2},{2,1},{3,0},{4,7},{5,6},{6,5},{7,4},{8,15},{9,14},{10,... | collective-permute-start | bytes 319496 | tf_op jit(solution)/shard_map/ppermute | solution.py:151
  137.4 4.7 %collective-permute-start.33 = (bf16[13,32,128]{2,1,0:T(8,128)(2,1)S(1)}, bf16[13,32,128]{2,1,0:T(8,128)(2,1)S(1)}, u32[]{:S(2)}, u32[]{:S(2)}) collective-permute-start(bf16[13,32,128]{2,1,0:T(8,128)(2,1)S(1)} %get-tuple-element.116), channel_id=1, source_target_pairs={{8,12},{9,13},{10,14},{11,15},{12,8},{13,9},{14,10},{15,11},{24,28... | collective-permute-start | bytes 319496 | tf_op jit(solution)/shard_map/ppermute | solution.py:151
  142.5 5.5 %collective-permute-start.37 = (f32[7,32,128]{2,1,0:T(8,128)S(1)}, f32[7,32,128]{2,1,0:T(8,128)S(1)}, u32[]{:S(2)}, u32[]{:S(2)}) collective-permute-start(f32[7,32,128]{2,1,0:T(8,128)S(1)} %pad_maximum_fusion.17), channel_id=1, source_target_pairs={{0,8},{8,0},{16,24},{24,16},{1,9},{9,1},{17,25},{25,17},{2,10},{10... | collective-permute-start | bytes 344072 | tf_op jit(solution)/shard_map/ppermute | solution.py:154
  148.4 4.3 %collective-permute-start.38 = (bf16[7,32,128]{2,1,0:T(8,128)(2,1)S(1)}, bf16[7,32,128]{2,1,0:T(8,128)(2,1)S(1)}, u32[]{:S(2)}, u32[]{:S(2)}) collective-permute-start(bf16[7,32,128]{2,1,0:T(8,128)(2,1)S(1)} %pad_maximum_fusion.23), channel_id=1, source_target_pairs={{0,16},{1,17},{2,18},{3,19},{4,20},{5,21},{6,22},{7,23},{8,24},{9,... | collective-permute-start | bytes 172040 | tf_op jit(solution)/shard_map/ppermute | solution.py:151

commit v2 on v0

v2 whole, which is shorter than its diff:
```python
import functools

import jax
import jax.numpy as jnp
import numpy as np
from jax import lax
from jax.experimental import pallas as pl
from jax.experimental.pallas import tpu as pltpu
from jax.sharding import PartitionSpec as P

PER_ROW = 5
ITERS = 3
MESH_AXES = ("row", "col")

coupling = 0.2

def start_copies(source, held, semaphores, to_held=True):
    parts = semaphores.shape[0]
    part = source.shape[0] // parts
    copies = []
    for i in range(parts):
        ends = (source.at[pl.ds(i * part, part)], held.at[pl.ds(i * part, part)])
        copies.append(pltpu.make_async_copy(*(ends if to_held else ends[::-1]), semaphores.at[i]))
    if to_held:
        for copy in copies:
            copy.start()
    return copies


def parts_of(count, wanted):
    return next(n for n in range(wanted, 0, -1) if count % n == 0)


def in_steps(count, unroll, one):
    unroll = parts_of(count, unroll)

    def step(g, carry):
        for u in range(unroll):
            one(g * unroll + u)
        return carry

    lax.fori_loop(0, count // unroll, step, 0)


def gathered(field, loads, base, per):
    return jnp.concatenate([field[loads[base + j]] for j in range(per)], axis=1)


def col_kernel(slots, loads, place, field, source, out, tiles, semaphores):
    copies = start_copies(source, tiles, semaphores)
    count = place.shape[0]
    per = slots.shape[0] // count
    for copy in copies:
        copy.wait()

    def one(i):
        base = i * per
        block = jnp.concatenate([tiles[slots[base + j]] for j in range(per)], axis=0)
        held = gathered(field, loads, base, per)
        out[place[i]] = jnp.dot(held, block, preferred_element_type=jnp.float32)

    in_steps(count, 8, one)


def first_row_kernel(
    slots, loads, place, field, source, out, row_blocks, tiles, blocks, semaphores, back_semaphores
):
    copies = start_copies(source, tiles, semaphores)
    back = start_copies(row_blocks, blocks, back_semaphores, to_held=False)
    count = place.shape[0]
    per = slots.shape[0] // count
    tile_size = tiles.shape[1]
    out[...] = jnp.zeros_like(out)
    for copy in copies:
        copy.wait()

    def one(i):
        base = i * per
        for j in range(per):
            blocks[i, pl.ds(j * tile_size, tile_size)] = tiles[slots[base + j]].T
        held = gathered(field, loads, base, per)
        out[place[i]] = jnp.dot(held, blocks[i], preferred_element_type=jnp.float32)

    part = count // len(back)
    for g, copy in enumerate(back):
        in_steps(part, 8, lambda i, g=g: one(g * part + i))
        copy.start()
    for copy in back:
        copy.wait()


def next_row_kernel(loads, place, field, source, out, blocks, semaphores):
    copies = start_copies(source, blocks, semaphores)
    count = place.shape[0]
    per = loads.shape[0] // count
    out[...] = jnp.zeros_like(out)

    def one(i):
        held = gathered(field, loads, i * per, per)
        total = jnp.dot(held, blocks[i], preferred_element_type=jnp.float32)
        out[place[i]] = total.astype(out.dtype)

    part = count // len(copies)
    for g, copy in enumerate(copies):
        copy.wait()
        in_steps(part, 8, lambda i, g=g: one(g * part + i))


IN_SMEM = pl.BlockSpec(memory_space=pltpu.SMEM)
IN_VMEM = pl.BlockSpec(memory_space=pltpu.VMEM)
IN_HBM = pl.BlockSpec(memory_space=pltpu.HBM)
PARAMS = pltpu.CompilerParams(vmem_limit_bytes=48 * 2**20)


def cost(field, tiles):
    return pl.CostEstimate(
        flops=16 * tiles.size * field.shape[1], bytes_accessed=2 * tiles.size, transcendentals=0
    )


def product(lists, field, tiles, out_tiles):
    parts = parts_of(tiles.shape[0], 8)
    return pl.pallas_call(
        col_kernel,
        out_shape=jax.ShapeDtypeStruct((out_tiles,) + field.shape[1:], jnp.float32),
        in_specs=[IN_SMEM] * 3 + [IN_VMEM, IN_HBM],
        out_specs=IN_VMEM,
        scratch_shapes=[pltpu.VMEM(tiles.shape, tiles.dtype), pltpu.SemaphoreType.DMA((parts,))],
        compiler_params=PARAMS,
        cost_estimate=cost(field, tiles),
    )(*lists, field, tiles)


def first_product(lists, field, tiles, out_tiles):
    count = lists[2].shape[0]
    slots, tile_size = tiles.shape[:2]
    blocks = (count, slots // count * tile_size, tile_size)
    return pl.pallas_call(
        first_row_kernel,
        out_shape=(
            jax.ShapeDtypeStruct((out_tiles,) + field.shape[1:], jnp.float32),
            jax.ShapeDtypeStruct(blocks, tiles.dtype),
        ),
        in_specs=[IN_SMEM] * 3 + [IN_VMEM, IN_HBM],
        out_specs=(IN_VMEM, IN_HBM),
        scratch_shapes=[
            pltpu.VMEM(tiles.shape, tiles.dtype),
            pltpu.VMEM(blocks, tiles.dtype),
            pltpu.SemaphoreType.DMA((parts_of(slots, 8),)),
            pltpu.SemaphoreType.DMA((parts_of(count, 6),)),
        ],
        compiler_params=PARAMS,
        cost_estimate=cost(field, tiles),
    )(*lists, field, tiles)


def next_product(lists, field, blocks, out_tiles):
    return pl.pallas_call(
        next_row_kernel,
        out_shape=jax.ShapeDtypeStruct((out_tiles,) + field.shape[1:], field.dtype),
        in_specs=[IN_SMEM] * 2 + [IN_VMEM, IN_HBM],
        out_specs=IN_VMEM,
        scratch_shapes=[
            pltpu.VMEM(blocks.shape, blocks.dtype),
            pltpu.SemaphoreType.DMA((parts_of(blocks.shape[0], 6),)),
        ],
        compiler_params=PARAMS,
        cost_estimate=cost(field, blocks),
    )(*lists[1:], field, blocks)


def sorted_lists(ids, loads, per_id):
    slots = ids.shape[0]
    order = jnp.arange(slots, dtype=jnp.int32)
    before = (ids[:, None] == ids[None, :]) & (order[None, :] < order[:, None])
    place = ids * per_id + jnp.sum(before, axis=1, dtype=jnp.int32)
    chosen = place[None, :] == order[:, None]
    pick = lambda values: jnp.sum(jnp.where(chosen, values[None, :], 0), axis=1, dtype=jnp.int32)
    return pick(order), pick(loads)


def split(value, rows_held):
    parts = []
    for _ in range(3):
        high = lax.reduce_precision(value, 8, 7)
        parts.append(high)
        value = value - high
    parts = jnp.stack(parts).astype(jnp.bfloat16)
    return jnp.pad(parts, ((0, 0), (0, rows_held - parts.shape[1]), (0, 0)))


def join(parts, rows):
    return jnp.sum(parts[:, :rows].astype(jnp.float32), axis=0)


class Plan:
    def __init__(self, rows, cols):
        self.rows, self.cols = rows, cols
        self.row_steps = [("row", m) for m in range(1, rows // 2)]
        first = self.row_steps + [("col", k) for k in range(2, cols, 2)]
        second = [("col", k) for k in range(1, cols, 2)]
        while len(first) > len(second) + 1:
            second.append(first.pop())
        first += [None] * (len(second) - len(first))
        second += [None] * (len(first) - len(second))
        self.count = len(first)
        self.steps = list(zip(first, second, strict=True))
        self.sum_steps = [(None if a in self.row_steps else a, b) for a, b in self.steps]
        place = np.zeros((2, cols), np.int32)
        for j, pair in enumerate(self.steps):
            for core, partner in enumerate(pair):
                if partner is not None and partner[0] == "col":
                    place[core, partner[1]] = 1 + j
                    place[1 - core, partner[1]] = 1 + self.count + j
        self.place = place

    def pairs(self, by_core):
        found = []
        for r in range(self.rows):
            partner = by_core[r % 2]
            if partner is None:
                continue
            axis, k = partner
            for c in range(self.cols):
                to = (r ^ (2 * k), c) if axis == "row" else (r, c ^ k)
                found.append((r * self.cols + c, to[0] * self.cols + to[1]))
        return found

    def send(self, value, by_core):
        return lax.ppermute(value, MESH_AXES, self.pairs(by_core))

    def swap(self, value):
        return lax.ppermute(value, "row", [(r, r ^ 1) for r in range(self.rows)])


def per_device(plan, scores, tile_values, tile_rows, tile_cols, tile_count):
    tiles = tile_values[0, 0]
    row_ids = tile_rows[0, 0]
    col_ids = tile_cols[0, 0]
    live = tile_count[0, 0]
    slots, tile_size = tiles.shape[:2]
    task_count, piece_len = scores.shape
    own_tiles = piece_len // tile_size
    row_tiles, col_tiles = own_tiles * plan.cols, own_tiles * plan.rows
    low_part = own_tiles * plan.count
    row_pieces = own_tiles + 2 * low_part
    row_index, col_index = lax.axis_index("row"), lax.axis_index("col")
    core = row_index % 2
    low = jnp.bfloat16

    place_of = jnp.where(core == 0, jnp.asarray(plan.place[0]), jnp.asarray(plan.place[1]))

    def row_place(ids):
        piece = (ids // own_tiles) ^ col_index
        chosen = piece[:, None] == jnp.arange(plan.cols, dtype=jnp.int32)[None, :]
        piece = jnp.sum(jnp.where(chosen, place_of[None, :], 0), axis=1, dtype=jnp.int32)
        return piece * own_tiles + ids % own_tiles

    def col_place(ids):
        return ((ids // own_tiles) ^ row_index) * own_tiles + ids % own_tiles

    def make_lists(row_ids, col_ids, live):
        is_live = jnp.arange(slots, dtype=jnp.int32) < live
        row_loads_of = jnp.where(is_live, row_place(row_ids), row_pieces)
        col_loads_of = jnp.where(is_live, col_place(col_ids), col_tiles)
        by_row = (
            *sorted_lists(row_ids, col_loads_of, slots // row_tiles),
            row_place(jnp.arange(row_tiles, dtype=jnp.int32)),
        )
        by_col = (
            *sorted_lists(col_ids, row_loads_of, slots // col_tiles),
            col_place(jnp.arange(col_tiles, dtype=jnp.int32)),
        )
        return by_row, by_col

    def empty_tile(field):
        return jnp.zeros((1,) + field.shape[1:], field.dtype)

    def with_ones(field):
        field = jnp.pad(field[:-1], ((0, 0), (0, 16), (0, 0)), constant_values=1)
        return jnp.pad(field, ((0, 1), (0, 0), (0, 0)))

    def to_low(value):
        if value.shape[1] == task_count:
            return value.astype(low)
        rounded = lax.reduce_precision(value, 8, 7)
        at = lax.broadcasted_iota(jnp.int32, value.shape, 1)
        return jnp.where(at == task_count + 1, value - rounded, rounded).astype(low)

    def one_addend(value):
        if value.shape[1] == task_count:
            return value
        at = lax.broadcasted_iota(jnp.int32, value.shape, 1)
        return jnp.where(at == task_count + 1, 0.0, value)

    def two_addends(value):
        return value[:, task_count : task_count + 1] + value[:, task_count + 1 : task_count + 2]

    def inner(a, b):
        return jnp.sum(a.astype(jnp.float32) * b.astype(jnp.float32), axis=(0, 2))[:, None]

    def as_tile(columns):
        at = lax.broadcasted_iota(jnp.int32, (task_count, tile_size), 1)
        return sum(jnp.where(at == i, column, 0.0) for i, column in enumerate(columns))

    near = len(plan.row_steps)
    chip_rows = plan.rows // 2
    residual = scores.reshape(task_count, own_tiles, tile_size).transpose(1, 0, 2)
    solution = direction = image = None
    norm_before = curve_before = scale = None
    for step_index in range(ITERS):
        first = step_index == 0
        at = slice(0, task_count)

        own_low = residual.astype(low)
        pair = jnp.concatenate([own_low, plan.swap(own_low)])
        if first:
            pair, row_ids, col_ids, live = lax.optimization_barrier((pair, row_ids, col_ids, live))
            by_row, by_col = make_lists(row_ids, col_ids, live)
        got = [plan.send(pair, by_core) for by_core in plan.steps]
        shared = [plan.swap(g) for g in got[:near]]
        col_pieces = [pair]
        for g, other in zip(got, shared):
            col_pieces.append(jnp.where(core == 0, g[:own_tiles], other[own_tiles:]))
            col_pieces.append(jnp.where(core == 0, g[own_tiles:], other[:own_tiles]))
        col_field = jnp.concatenate(col_pieces + [empty_tile(pair)])
        if first:
            col_field = with_ones(col_field)
            forward, row_blocks = first_product(by_row, col_field, tiles, row_pieces)
        else:
            forward = next_product(by_row, col_field, row_blocks, row_pieces)

        far, forward = lax.optimization_barrier((got[near:], forward))
        forward = to_low(forward)
        mine = [g[:own_tiles] for g in got[:near] + far]
        swapped = plan.swap(jnp.concatenate([g[own_tiles:] for g in far]))
        row_field = jnp.concatenate(
            [own_low] + mine + [o[own_tiles:] for o in shared] + [swapped, empty_tile(pair)]
        )
        curve_part = -inner(row_field[:-1], forward[:, at])
        if first:
            backward = product(by_col, with_ones(row_field), tiles, col_tiles)
        norm = inner(residual, residual)
        if first:
            square = lambda value: value.astype(jnp.float32) ** 2
            curve_part += 0.5 * inner(
                square(row_field[:-1]), two_addends(forward.astype(jnp.float32))
            )
            curve_part += 0.5 * inner(
                square(col_field[:-1, at]), backward[:, task_count : task_count + 1]
            )
            dots = as_tile([norm, norm + coupling * curve_part])
        else:
            weighted = inner(scale * residual, residual)
            dots = as_tile([norm, weighted + coupling * curve_part, inner(residual, image)])

        rows_held = forward.shape[1]
        swapped = plan.swap(
            jnp.concatenate([forward[own_tiles + low_part :], split(dots, rows_held)])
        )
        if not first:
            swapped, row_field = lax.optimization_barrier((swapped, row_field))
            backward = product(by_col, row_field, tiles, col_tiles)
        dots = dots + join(swapped[low_part:], task_count)
        dots_low = split(dots, rows_held)
        messages = []
        for j, by_core in enumerate(plan.sum_steps):
            piece = slice(j * own_tiles, (j + 1) * own_tiles)
            message = jnp.concatenate([forward[own_tiles:][piece], swapped[piece], dots_low])
            messages.append(plan.send(message, by_core))
        backward = backward.reshape(chip_rows, 2, own_tiles, rows_held, tile_size)
        back = plan.swap(backward[:, 1].reshape(-1, rows_held, tile_size))
        backward = backward[:, 0] + back.reshape(backward[:, 0].shape)
        total = sum(m.astype(jnp.float32) for m in messages)
        dots_mine = jnp.sum(total[2 * own_tiles :], axis=0)
        back = plan.swap(jnp.concatenate([total[own_tiles : 2 * own_tiles], dots_mine[None]]))
        dots = dots + (dots_mine + back[-1])[at]
        total = total[:own_tiles] + back[:-1] + forward[:own_tiles].astype(jnp.float32)

        total = total + one_addend(backward[0])
        dots_low = split(dots, rows_held)
        for m, by_core in enumerate(plan.row_steps, 1):
            message = jnp.concatenate([to_low(backward[m]), dots_low])
            back = plan.send(message, (by_core,) * 2)
            total = total + back[:own_tiles].astype(jnp.float32)
            dots = dots + join(back[own_tiles:], task_count)
        total = 0.5 * total

        norm, curve, along = dots[:, 0:1], dots[:, 1:2], dots[:, 2:3]
        if first:
            scale = 1.0 + coupling * two_addends(total)
        fresh = scale * residual - coupling * total[:, at]
        if first:
            direction, image = residual, fresh
        else:
            ratio = norm / norm_before
            curve = curve + 2.0 * ratio * along + ratio * ratio * curve_before
            direction = residual + ratio * direction
            image = fresh + ratio * image
        norm_before, curve_before = norm, curve
        step_size = norm / curve
        solution = step_size * direction if first else solution + step_size * direction
        residual = residual - step_size * image

    def to_field(value):
        return value.transpose(1, 0, 2).reshape(task_count, piece_len)

    return to_field(solution), to_field(residual)


def solution(mesh):
    plan = Plan(mesh.shape["row"], mesh.shape["col"])
    return jax.shard_map(
        functools.partial(per_device, plan),
        mesh=mesh,
        in_specs=(
            P(None, ("row", "col")),
            P("row", "col", None, None, None),
            P("row", "col", None),
            P("row", "col", None),
            P("row", "col"),
        ),
        out_specs=(P(None, ("row", "col")), P(None, ("row", "col"))),
        check_vma=False,
    )
```

time: 571 us -> 143 us (0.25)
  blocking collectives: 246 us -> 0 us
  other arithmetic: 109 us -> 9.56 us
  matrix products: 65.5 us -> 0 us
  starting transfers between devices: 0.29 us -> 48.9 us
  waiting for transfers between devices: 87.5 us -> 45.9 us
  local copies, waits for them, and re-layouts: 43.8 us -> 3.06 us
  Pallas kernels: 0 us -> 33.1 us
  between operations: 16.4 us -> 2.17 us
    all_gather x8 -> x0, blocking collectives: 179 us -> none  [the longest x5 162 us: row_block(): return lax.all_gather(own_field, 'col', axis=1, tiled=True)]
    scatter-add x32 -> x0, other arithmetic: 78 us -> none  [the longest x15 37.6 us: one_block(): backward_sum.at[:, cols_here, :].add(backward)]
    psum x6 -> x0, blocking collectives: 66.7 us -> none  [the longest x1 37.3 us: row_total(): return lax.psum(partial_value, 'col')]
    dot_general x30 -> x0, matrix products: 65.5 us -> none  [the longest x15 35.6 us: one_block(): jnp.einsum('ksd,sod->kso', col_pieces, tiles_here, preferred_element_type...]
    psum x3 -> x0, waiting for transfers between devices: 52.3 us -> none  [row_total(): return lax.psum(partial_value, 'col')]
    ppermute x0 -> x45, starting transfers between devices: none -> 48.9 us  [the longest x27 39.7 us: send(): return lax.ppermute(value, MESH_AXES, self.pairs(by_core))]
    ppermute x0 -> x45, waiting for transfers between devices: none -> 45.9 us  [the longest x27 30 us: send(): return lax.ppermute(value, MESH_AXES, self.pairs(by_core))]
    reduce_scatter x3 -> x0, waiting for transfers between devices: 35.1 us -> none  [to_cols(): lax.psum_scatter(partial_value, 'row', scatter_dimension=1, tiled=True)]
  transfers between devices with their start and end apart: 7 -> 45, of which waited for: 4 -> 23; matrix products, arithmetic and copies ran while one was open for 12% -> 4% of each run, Pallas kernels for 0% -> 19%
where the time goes in v2:
time: 143 us
  starting transfers between devices  48.9 us (34%)
  waiting for transfers between devices  45.9 us (32%)
  Pallas kernels  33.1 us (23%)
  other arithmetic  9.56 us (7%)
  local copies, waits for them, and re-layouts  3.06 us (2%)
  between operations  2.17 us (2%)
    ppermute x27, starting transfers between devices, send(): return lax.ppermute(value, MESH_AXES, self.pairs(by_core))  39.7 us
    ppermute x27, waiting for transfers between devices, send(): return lax.ppermute(value, MESH_AXES, self.pairs(by_core))  30 us
    pallas_call x3, Pallas kernels, product(): pl.pallas_call(col_kernel, out_shape=jax.ShapeDtypeStruct((out_tiles,) +...  16.7 us
    ppermute x18, waiting for transfers between devices, swap(): return lax.ppermute(value, 'row', [(r, r ^ 1) for r in range(self.rows)])  15.9 us
    ppermute x18, starting transfers between devices, swap(): return lax.ppermute(value, 'row', [(r, r ^ 1) for r in range(self.rows)])  9.14 us
    pallas_call x2, Pallas kernels, next_product(): pl.pallas_call(next_row_kernel, out_shape=jax.ShapeDtypeStruct((out_tiles...  8.44 us
    pallas_call x1, Pallas kernels, first_product(): pl.pallas_call(first_row_kernel, out_shape=(jax.ShapeDtypeStruct((out_til...  7.9 us
  transfers between devices with their start and end apart: 45, of which 23 were waited for; matrix products, arithmetic and copies ran while one was open for 4% of the time, Pallas kernels for 19%

profile of v2, /device:TPU:0, one launch (start us, length us, event | category | flops | bytes accessed | tf_op | source)
XLA Modules:
  0.0 142.6 jit_solution(17678933673028266523)
XLA Ops:
  0.6 0.9 copy-done
  2.2 0.7 broadcast_select_fusion.1
  3.7 2.6 %collective-permute-start.1 = (bf16[12,32,128]{2,1,0:T(8,128)(2,1)S(1)}, bf16[12,32,128]{2,1,0:T(8,128)(2,1)S(1)}, u32[]{:S(2)}, u32[]{:S(2)}) collective-permute-start(bf16[12,32,128]{2,1,0:T(8,128)(2,1)S(1)} %pad_maximum_fusion.15), channel_id=1, source_target_pairs={{0,16},{1,17},{2,18},{3,19},{4,20},{5,21},{6,22},{7,23},{8,9},{9,8... | collective-permute-start | bytes 294920 | tf_op jit(solution)/shard_map/ppermute | solution.py:230
  6.3 1.6 %collective-permute-start.2 = (bf16[12,32,128]{2,1,0:T(8,128)(2,1)S(1)}, bf16[12,32,128]{2,1,0:T(8,128)(2,1)S(1)}, u32[]{:S(2)}, u32[]{:S(2)}) collective-permute-start(bf16[12,32,128]{2,1,0:T(8,128)(2,1)S(1)} %pad_maximum_fusion.15), channel_id=1, source_target_pairs={{0,2},{1,3},{2,0},{3,1},{4,6},{5,7},{6,4},{7,5},{8,11},{9,10},{10,... | collective-permute-start | bytes 294920 | tf_op jit(solution)/shard_map/ppermute | solution.py:230
  7.9 2.6 %collective-permute-start.3 = (bf16[12,32,128]{2,1,0:T(8,128)(2,1)S(1)}, bf16[12,32,128]{2,1,0:T(8,128)(2,1)S(1)}, u32[]{:S(2)}, u32[]{:S(2)}) collective-permute-start(bf16[12,32,128]{2,1,0:T(8,128)(2,1)S(1)} %pad_maximum_fusion.15), channel_id=1, source_target_pairs={{0,4},{1,5},{2,6},{3,7},{4,0},{5,1},{6,2},{7,3},{8,13},{9,12},{10,... | collective-permute-start | bytes 294920 | tf_op jit(solution)/shard_map/ppermute | solution.py:230
  10.7 0.7 fusion.99
  11.5 1.0 convert_reduce_fusion
  12.5 0.7 fusion.96
  13.2 0.7 multiply_add_fusion.1
  14.5 0.9 collective-permute-done.5
  15.5 7.9 %shard_map.86 = (f32[54,48,128]{2,1,0:T(8,128)S(1)}, bf16[48,640,128]{2,1,0:T(8,128)(2,1)}) custom-call(s32[240]{0:T(256)S(1)} %get-tuple-element.59.slots, s32[240]{0:T(256)S(1)} %get-tuple-element.58.loads, s32[48]{0:T(128)S(1)} %fusion.100.place, bf16[25,48,128]{2,1,0:T(8,128)(2,1)S(1)} %fusion.5.field, bf16[240,128,128]{2,1,0:T(8,128)(2,1)} %bitcast.247), custom_call_target="tpu_custom_call" | custom-call | flops 3019898880 | bytes 7864320 | tf_op jit(solution)/shard_map/pallas_call | solution.py:138
  24.3 0.7 collective-permute-done.6
  25.4 5.7 %shard_map.87 = f32[24,48,128]{2,1,0:T(8,128)S(1)} custom-call(s32[240]{0:T(256)S(1)} %get-tuple-element.61.slots, s32[240]{0:T(256)S(1)} %get-tuple-element.60.loads, s32[24]{0:T(128)S(1)} %fusion.101.place, bf16[55,48,128]{2,1,0:T(8,128)(2,1)S(1)} %fusion.field, bf16[240,128,128]{2,1,0:T(8,128)(2,1)} %bitcast.248), custom_call_target="tpu_custom_call" | custom-call | flops 3019898880 | bytes 7864320 | tf_op jit(solution)/shard_map/pallas_call | solution.py:123
  32.1 1.0 collective-permute-done.7
  33.4 1.8 %collective-permute-start.10 = (bf16[15,48,128]{2,1,0:T(8,128)(2,1)S(1)}, bf16[15,48,128]{2,1,0:T(8,128)(2,1)S(1)}, u32[]{:S(2)}, u32[]{:S(2)}) collective-permute-start(bf16[15,48,128]{2,1,0:T(8,128)(2,1)S(1)} %get-tuple-element.165), channel_id=1, source_target_pairs={{0,4},{1,5},{2,6},{3,7},{4,0},{5,1},{6,2},{7,3},{8,13},{9,12},{10,... | collective-permute-start | bytes 552968 | tf_op jit(solution)/shard_map/ppermute | solution.py:230
  35.2 2.0 %collective-permute-start.11 = (bf16[15,48,128]{2,1,0:T(8,128)(2,1)S(1)}, bf16[15,48,128]{2,1,0:T(8,128)(2,1)S(1)}, u32[]{:S(2)}, u32[]{:S(2)}) collective-permute-start(bf16[15,48,128]{2,1,0:T(8,128)(2,1)S(1)} %get-tuple-element.166), channel_id=1, source_target_pairs={{0,6},{1,7},{2,4},{3,5},{4,2},{5,3},{6,0},{7,1},{8,15},{9,14},{10,... | collective-permute-start | bytes 552968 | tf_op jit(solution)/shard_map/ppermute | solution.py:230
  37.1 0.7 collective-permute-start.8
  38.4 11.3 %collective-permute-done.10 = bf16[15,48,128]{2,1,0:T(8,128)(2,1)S(1)} collective-permute-done((bf16[15,48,128]{2,1,0:T(8,128)(2,1)S(1)}, bf16[15,48,128]{2,1,0:T(8,128)(2,1)S(1)}, u32[]{:S(2)}, u32[]{:S(2)}) %collective-permute-start.10) | collective-permute-done | bytes 184352 | tf_op jit(solution)/shard_map/ppermute | solution.py:230
  49.7 2.2 %collective-permute-done.9 = bf16[15,48,128]{2,1,0:T(8,128)(2,1)S(1)} collective-permute-done((bf16[15,48,128]{2,1,0:T(8,128)(2,1)S(1)}, bf16[15,48,128]{2,1,0:T(8,128)(2,1)S(1)}, u32[]{:S(2)}, u32[]{:S(2)}) %collective-permute-start.9) | collective-permute-done | bytes 184352 | tf_op jit(solution)/shard_map/ppermute | solution.py:230
  52.1 1.2 collective-permute-start.12
  53.4 1.0 collective-permute-done.12
  54.4 1.4 %collective-permute-start.14 = (bf16[9,48,128]{2,1,0:T(8,128)(2,1)S(1)}, bf16[9,48,128]{2,1,0:T(8,128)(2,1)S(1)}, u32[]{:S(2)}, u32[]{:S(2)}) collective-permute-start(bf16[9,48,128]{2,1,0:T(8,128)(2,1)S(1)} %pad_maximum_fusion.14), channel_id=1, source_target_pairs={{0,16},{1,17},{2,18},{3,19},{4,20},{5,21},{6,22},{7,23},{8,24},{9,... | collective-permute-start | bytes 331784 | tf_op jit(solution)/shard_map/ppermute | solution.py:230
  55.9 4.0 %collective-permute-done.14 = bf16[9,48,128]{2,1,0:T(8,128)(2,1)S(1)} collective-permute-done((bf16[9,48,128]{2,1,0:T(8,128)(2,1)S(1)}, bf16[9,48,128]{2,1,0:T(8,128)(2,1)S(1)}, u32[]{:S(2)}, u32[]{:S(2)}) %collective-permute-start.14) | collective-permute-done | bytes 110624 | tf_op jit(solution)/shard_map/ppermute | solution.py:230
  60.5 1.1 collective-permute-done.15
  61.6 1.4 collective-permute-start.16
  63.0 1.4 collective-permute-start.17
  64.4 2.0 %collective-permute-start.18 = (bf16[12,32,128]{2,1,0:T(8,128)(2,1)S(1)}, bf16[12,32,128]{2,1,0:T(8,128)(2,1)S(1)}, u32[]{:S(2)}, u32[]{:S(2)}) collective-permute-start(bf16[12,32,128]{2,1,0:T(8,128)(2,1)S(1)} %pad_maximum_fusion.16), channel_id=1, source_target_pairs={{0,4},{1,5},{2,6},{3,7},{4,0},{5,1},{6,2},{7,3},{8,13},{9,12},{10,... | collective-permute-start | bytes 294920 | tf_op jit(solution)/shard_map/ppermute | solution.py:230
  66.4 1.1 collective-permute-start.19
  67.5 1.2 collective-permute-done.20
  68.9 4.2 %shard_map.88 = bf16[54,32,128]{2,1,0:T(8,128)(2,1)S(1)} custom-call(s32[240]{0:T(256)S(1)} %get-tuple-element.58.loads, s32[48]{0:T(128)S(1)} %fusion.100.place, bf16[25,32,128]{2,1,0:T(8,128)(2,1)S(1)} %constant_dynamic-update-slice_fusion.7.field, bf16[48,640,128]{2,1,0:T(8,128)(2,1)} %get-tuple-element.33.source), custom_call_target="tpu_custom_call" | custom-call | flops 2013265920 | bytes 7864320 | tf_op jit(solution)/shard_map/pallas_call | solution.py:158
  73.1 2.0 %collective-permute-done.18 = bf16[12,32,128]{2,1,0:T(8,128)(2,1)S(1)} collective-permute-done((bf16[12,32,128]{2,1,0:T(8,128)(2,1)S(1)}, bf16[12,32,128]{2,1,0:T(8,128)(2,1)S(1)}, u32[]{:S(2)}, u32[]{:S(2)}) %collective-permute-start.18) | collective-permute-done | bytes 98336 | tf_op jit(solution)/shard_map/ppermute | solution.py:230
  75.3 1.3 collective-permute-done.21
  77.3 1.3 collective-permute-done.22
  79.0 2.3 %collective-permute-start.24 = (bf16[15,32,128]{2,1,0:T(8,128)(2,1)S(1)}, bf16[15,32,128]{2,1,0:T(8,128)(2,1)S(1)}, u32[]{:S(2)}, u32[]{:S(2)}) collective-permute-start(bf16[15,32,128]{2,1,0:T(8,128)(2,1)S(1)} %get-tuple-element.185), channel_id=1, source_target_pairs={{0,2},{1,3},{2,0},{3,1},{4,6},{5,7},{6,4},{7,5},{8,11},{9,10},{10,... | collective-permute-start | bytes 368648 | tf_op jit(solution)/shard_map/ppermute | solution.py:230
  81.3 1.0 collective-permute-start.25
  82.2 1.5 %collective-permute-start.26 = (bf16[15,32,128]{2,1,0:T(8,128)(2,1)S(1)}, bf16[15,32,128]{2,1,0:T(8,128)(2,1)S(1)}, u32[]{:S(2)}, u32[]{:S(2)}) collective-permute-start(bf16[15,32,128]{2,1,0:T(8,128)(2,1)S(1)} %get-tuple-element.187), channel_id=1, source_target_pairs={{0,6},{1,7},{2,4},{3,5},{4,2},{5,3},{6,0},{7,1},{8,15},{9,14},{10,... | collective-permute-start | bytes 368648 | tf_op jit(solution)/shard_map/ppermute | solution.py:230
  83.7 0.8 collective-permute-start.23
  84.6 5.5 %shard_map.89 = f32[24,32,128]{2,1,0:T(8,128)S(1)} custom-call(s32[240]{0:T(256)S(1)} %get-tuple-element.61.slots, s32[240]{0:T(256)S(1)} %get-tuple-element.60.loads, s32[24]{0:T(128)S(1)} %fusion.101.place, bf16[55,32,128]{2,1,0:T(8,128)(2,1)S(1)} %constant_dynamic-update-slice_fusion.19.field, bf16[240,128,128]{2,1,0:T(8,128)(2,1)} %bitcast.249), custom_call_target="tpu_custom_call" | custom-call | flops 2013265920 | bytes 7864320 | tf_op jit(solution)/shard_map/pallas_call | solution.py:123
  90.1 2.5 %collective-permute-start.28 = (f32[12,32,128]{2,1,0:T(8,128)S(1)}, f32[12,32,128]{2,1,0:T(8,128)S(1)}, u32[]{:S(2)}, u32[]{:S(2)}) collective-permute-start(f32[12,32,128]{2,1,0:T(8,128)S(1)} %bitcast.255), channel_id=1, source_target_pairs={{0,8},{8,0},{16,24},{24,16},{1,9},{9,1},{17,25},{25,17},{2,10},{10... | collective-permute-start | bytes 589832 | tf_op jit(solution)/shard_map/ppermute | solution.py:233
  92.6 1.0 collective-permute-done.25
  93.9 1.2 collective-permute-done.27
  95.3 1.1 collective-permute-start.29
  96.4 3.3 %collective-permute-done.29 = bf16[9,32,128]{2,1,0:T(8,128)(2,1)S(1)} collective-permute-done((bf16[9,32,128]{2,1,0:T(8,128)(2,1)S(1)}, bf16[9,32,128]{2,1,0:T(8,128)(2,1)S(1)}, u32[]{:S(2)}, u32[]{:S(2)}) %collective-permute-start.29) | collective-permute-done | bytes 73760 | tf_op jit(solution)/shard_map/ppermute | solution.py:230
  100.3 1.1 collective-permute-done.30
  101.4 1.3 collective-permute-start.31
  102.7 3.3 %collective-permute-start.32 = (bf16[12,32,128]{2,1,0:T(8,128)(2,1)S(1)}, bf16[12,32,128]{2,1,0:T(8,128)(2,1)S(1)}, u32[]{:S(2)}, u32[]{:S(2)}) collective-permute-start(bf16[12,32,128]{2,1,0:T(8,128)(2,1)S(1)} %pad_maximum_fusion.17), channel_id=1, source_target_pairs={{0,2},{1,3},{2,0},{3,1},{4,6},{5,7},{6,4},{7,5},{8,11},{9,10},{10,... | collective-permute-start | bytes 294920 | tf_op jit(solution)/shard_map/ppermute | solution.py:230
  106.0 1.2 collective-permute-start.33
  107.1 1.4 collective-permute-start.34
  108.5 1.3 collective-permute-done.35
  109.9 4.2 %shard_map.90 = bf16[54,32,128]{2,1,0:T(8,128)(2,1)S(1)} custom-call(s32[240]{0:T(256)S(1)} %get-tuple-element.58.loads, s32[48]{0:T(128)S(1)} %fusion.100.place, bf16[25,32,128]{2,1,0:T(8,128)(2,1)S(1)} %constant_dynamic-update-slice_fusion.47.field, bf16[48,640,128]{2,1,0:T(8,128)(2,1)} %get-tuple-element.33.source), custom_call_target="tpu_custom_call" | custom-call | flops 2013265920 | bytes 7864320 | tf_op jit(solution)/shard_map/pallas_call | solution.py:158
  114.1 2.2 %collective-permute-done.33 = bf16[12,32,128]{2,1,0:T(8,128)(2,1)S(1)} collective-permute-done((bf16[12,32,128]{2,1,0:T(8,128)(2,1)S(1)}, bf16[12,32,128]{2,1,0:T(8,128)(2,1)S(1)}, u32[]{:S(2)}, u32[]{:S(2)}) %collective-permute-start.33) | collective-permute-done | bytes 98336 | tf_op jit(solution)/shard_map/ppermute | solution.py:230
  116.6 1.3 collective-permute-done.36
  118.6 1.3 collective-permute-done.37
  120.3 2.1 %collective-permute-start.39 = (bf16[15,32,128]{2,1,0:T(8,128)(2,1)S(1)}, bf16[15,32,128]{2,1,0:T(8,128)(2,1)S(1)}, u32[]{:S(2)}, u32[]{:S(2)}) collective-permute-start(bf16[15,32,128]{2,1,0:T(8,128)(2,1)S(1)} %get-tuple-element.176), channel_id=1, source_target_pairs={{0,2},{1,3},{2,0},{3,1},{4,6},{5,7},{6,4},{7,5},{8,11},{9,10},{10,... | collective-permute-start | bytes 368648 | tf_op jit(solution)/shard_map/ppermute | solution.py:230
  122.4 0.9 collective-permute-start.40
  123.3 1.6 %collective-permute-start.41 = (bf16[15,32,128]{2,1,0:T(8,128)(2,1)S(1)}, bf16[15,32,128]{2,1,0:T(8,128)(2,1)S(1)}, u32[]{:S(2)}, u32[]{:S(2)}) collective-permute-start(bf16[15,32,128]{2,1,0:T(8,128)(2,1)S(1)} %get-tuple-element.178), channel_id=1, source_target_pairs={{0,6},{1,7},{2,4},{3,5},{4,2},{5,3},{6,0},{7,1},{8,15},{9,14},{10,... | collective-permute-start | bytes 368648 | tf_op jit(solution)/shard_map/ppermute | solution.py:230
  124.9 0.7 collective-permute-start.38
  125.5 5.5 %shard_map.91 = f32[24,32,128]{2,1,0:T(8,128)S(1)} custom-call(s32[240]{0:T(256)S(1)} %get-tuple-element.61.slots, s32[240]{0:T(256)S(1)} %get-tuple-element.60.loads, s32[24]{0:T(128)S(1)} %fusion.101.place, bf16[55,32,128]{2,1,0:T(8,128)(2,1)S(1)} %constant_dynamic-update-slice_fusion.59.field, bf16[240,128,128]{2,1,0:T(8,128)(2,1)} %bitcast.250), custom_call_target="tpu_custom_call" | custom-call | flops 2013265920 | bytes 7864320 | tf_op jit(solution)/shard_map/pallas_call | solution.py:123
  131.1 2.6 %collective-permute-start.43 = (f32[12,32,128]{2,1,0:T(8,128)S(1)}, f32[12,32,128]{2,1,0:T(8,128)S(1)}, u32[]{:S(2)}, u32[]{:S(2)}) collective-permute-start(f32[12,32,128]{2,1,0:T(8,128)S(1)} %bitcast.256), channel_id=1, source_target_pairs={{0,8},{8,0},{16,24},{24,16},{1,9},{9,1},{17,25},{25,17},{2,10},{10... | collective-permute-start | bytes 589832 | tf_op jit(solution)/shard_map/ppermute | solution.py:233
  133.7 1.1 collective-permute-done.40
  135.1 1.2 collective-permute-done.42
  136.4 1.5 %collective-permute-start.44 = (bf16[9,32,128]{2,1,0:T(8,128)(2,1)S(1)}, bf16[9,32,128]{2,1,0:T(8,128)(2,1)S(1)}, u32[]{:S(2)}, u32[]{:S(2)}) collective-permute-start(bf16[9,32,128]{2,1,0:T(8,128)(2,1)S(1)} %pad_maximum_fusion.19), channel_id=1, source_target_pairs={{0,16},{1,17},{2,18},{3,19},{4,20},{5,21},{6,22},{7,23},{8,24},{9,... | collective-permute-start | bytes 221192 | tf_op jit(solution)/shard_map/ppermute | solution.py:230
  137.9 2.9 %collective-permute-done.44 = bf16[9,32,128]{2,1,0:T(8,128)(2,1)S(1)} collective-permute-done((bf16[9,32,128]{2,1,0:T(8,128)(2,1)S(1)}, bf16[9,32,128]{2,1,0:T(8,128)(2,1)S(1)}, u32[]{:S(2)}, u32[]{:S(2)}) %collective-permute-start.44) | collective-permute-done | bytes 73760 | tf_op jit(solution)/shard_map/ppermute | solution.py:230
  141.3 0.6 copy.47
  (184 shorter events, 10.9 us)
Async XLA Ops:
  0.6 0.9 copy-start
  1.5 2.1 %collective-permute-start = (bf16[6,32,128]{2,1,0:T(8,128)(2,1)S(1)}, bf16[6,32,128]{2,1,0:T(8,128)(2,1)S(1)}, u32[]{:S(2)}, u32[]{:S(2)}) collective-permute-start(bf16[6,32,128]{2,1,0:T(8,128)(2,1)S(1)} %get-tuple-element.91), channel_id=1, source_target_pairs={{0,8},{8,0},{16,24},{24,16},{1,9},{9,1},{17,25},{25,17},{2,10},{10... | collective-permute-start | bytes 147464 | tf_op jit(solution)/shard_map/ppermute | solution.py:233
  3.7 10.3 %collective-permute-start.1 = (bf16[12,32,128]{2,1,0:T(8,128)(2,1)S(1)}, bf16[12,32,128]{2,1,0:T(8,128)(2,1)S(1)}, u32[]{:S(2)}, u32[]{:S(2)}) collective-permute-start(bf16[12,32,128]{2,1,0:T(8,128)(2,1)S(1)} %pad_maximum_fusion.15), channel_id=1, source_target_pairs={{0,16},{1,17},{2,18},{3,19},{4,20},{5,21},{6,22},{7,23},{8,9},{9,8... | collective-permute-start | bytes 294920 | tf_op jit(solution)/shard_map/ppermute | solution.py:230
  6.3 17.1 %collective-permute-start.2 = (bf16[12,32,128]{2,1,0:T(8,128)(2,1)S(1)}, bf16[12,32,128]{2,1,0:T(8,128)(2,1)S(1)}, u32[]{:S(2)}, u32[]{:S(2)}) collective-permute-start(bf16[12,32,128]{2,1,0:T(8,128)(2,1)S(1)} %pad_maximum_fusion.15), channel_id=1, source_target_pairs={{0,2},{1,3},{2,0},{3,1},{4,6},{5,7},{6,4},{7,5},{8,11},{9,10},{10,... | collective-permute-start | bytes 294920 | tf_op jit(solution)/shard_map/ppermute | solution.py:230
  7.9 15.5 %collective-permute-start.3 = (bf16[12,32,128]{2,1,0:T(8,128)(2,1)S(1)}, bf16[12,32,128]{2,1,0:T(8,128)(2,1)S(1)}, u32[]{:S(2)}, u32[]{:S(2)}) collective-permute-start(bf16[12,32,128]{2,1,0:T(8,128)(2,1)S(1)} %pad_maximum_fusion.15), channel_id=1, source_target_pairs={{0,4},{1,5},{2,6},{3,7},{4,0},{5,1},{6,2},{7,3},{8,13},{9,12},{10,... | collective-permute-start | bytes 294920 | tf_op jit(solution)/shard_map/ppermute | solution.py:230
  10.5 13.0 %collective-permute-start.4 = (bf16[12,32,128]{2,1,0:T(8,128)(2,1)S(1)}, bf16[12,32,128]{2,1,0:T(8,128)(2,1)S(1)}, u32[]{:S(2)}, u32[]{:S(2)}) collective-permute-start(bf16[12,32,128]{2,1,0:T(8,128)(2,1)S(1)} %pad_maximum_fusion.15), channel_id=1, source_target_pairs={{0,6},{1,7},{2,4},{3,5},{4,2},{5,3},{6,0},{7,1},{8,15},{9,14},{10,... | collective-permute-start | bytes 294920 | tf_op jit(solution)/shard_map/ppermute | solution.py:230
  14.0 1.4 collective-permute-start.5
  23.5 1.4 %collective-permute-start.6 = (bf16[18,32,128]{2,1,0:T(8,128)(2,1)S(1)}, bf16[18,32,128]{2,1,0:T(8,128)(2,1)S(1)}, u32[]{:S(2)}, u32[]{:S(2)}) collective-permute-start(bf16[18,32,128]{2,1,0:T(8,128)(2,1)S(1)} %pad_maximum_fusion.9), channel_id=1, source_target_pairs={{0,8},{8,0},{16,24},{24,16},{1,9},{9,1},{17,25},{25,17},{2,10},{10... | collective-permute-start | bytes 442376 | tf_op jit(solution)/shard_map/ppermute | solution.py:233
  31.5 1.7 %collective-permute-start.7 = (bf16[27,48,128]{2,1,0:T(8,128)(2,1)S(1)}, bf16[27,48,128]{2,1,0:T(8,128)(2,1)S(1)}, u32[]{:S(2)}, u32[]{:S(2)}) collective-permute-start(bf16[27,48,128]{2,1,0:T(8,128)(2,1)S(1)} %pad_maximum_fusion.4), channel_id=1, source_target_pairs={{0,8},{8,0},{16,24},{24,16},{1,9},{9,1},{17,25},{25,17},{2,10},{10... | collective-permute-start | bytes 995336 | tf_op jit(solution)/shard_map/ppermute | solution.py:233
  31.9 6.5 %collective-permute-start.13 = (f32[12,48,128]{2,1,0:T(8,128)S(1)}, f32[12,48,128]{2,1,0:T(8,128)S(1)}, u32[]{:S(2)}, u32[]{:S(2)}) collective-permute-start(f32[12,48,128]{2,1,0:T(8,128)S(1)} %bitcast.252), channel_id=1, source_target_pairs={{0,8},{8,0},{16,24},{24,16},{1,9},{9,1},{17,25},{25,17},{2,10},{10... | collective-permute-start | bytes 884744 | tf_op jit(solution)/shard_map/ppermute | solution.py:233
  33.4 16.3 %collective-permute-start.10 = (bf16[15,48,128]{2,1,0:T(8,128)(2,1)S(1)}, bf16[15,48,128]{2,1,0:T(8,128)(2,1)S(1)}, u32[]{:S(2)}, u32[]{:S(2)}) collective-permute-start(bf16[15,48,128]{2,1,0:T(8,128)(2,1)S(1)} %get-tuple-element.165), channel_id=1, source_target_pairs={{0,4},{1,5},{2,6},{3,7},{4,0},{5,1},{6,2},{7,3},{8,13},{9,12},{10,... | collective-permute-start | bytes 552968 | tf_op jit(solution)/shard_map/ppermute | solution.py:230
  35.2 14.6 %collective-permute-start.11 = (bf16[15,48,128]{2,1,0:T(8,128)(2,1)S(1)}, bf16[15,48,128]{2,1,0:T(8,128)(2,1)S(1)}, u32[]{:S(2)}, u32[]{:S(2)}) collective-permute-start(bf16[15,48,128]{2,1,0:T(8,128)(2,1)S(1)} %get-tuple-element.166), channel_id=1, source_target_pairs={{0,6},{1,7},{2,4},{3,5},{4,2},{5,3},{6,0},{7,1},{8,15},{9,14},{10,... | collective-permute-start | bytes 552968 | tf_op jit(solution)/shard_map/ppermute | solution.py:230
  37.1 12.6 %collective-permute-start.8 = (bf16[15,48,128]{2,1,0:T(8,128)(2,1)S(1)}, bf16[15,48,128]{2,1,0:T(8,128)(2,1)S(1)}, u32[]{:S(2)}, u32[]{:S(2)}) collective-permute-start(bf16[15,48,128]{2,1,0:T(8,128)(2,1)S(1)} %get-tuple-element.163), channel_id=1, source_target_pairs={{8,9},{9,8},{10,11},{11,10},{12,13},{13,12},{14,15},{15,14},{24,25... | collective-permute-start | bytes 552968 | tf_op jit(solution)/shard_map/ppermute | solution.py:230
  37.8 14.1 %collective-permute-start.9 = (bf16[15,48,128]{2,1,0:T(8,128)(2,1)S(1)}, bf16[15,48,128]{2,1,0:T(8,128)(2,1)S(1)}, u32[]{:S(2)}, u32[]{:S(2)}) collective-permute-start(bf16[15,48,128]{2,1,0:T(8,128)(2,1)S(1)} %get-tuple-element.164), channel_id=1, source_target_pairs={{0,2},{1,3},{2,0},{3,1},{4,6},{5,7},{6,4},{7,5},{8,11},{9,10},{10,... | collective-permute-start | bytes 552968 | tf_op jit(solution)/shard_map/ppermute | solution.py:230
  52.1 2.2 %collective-permute-start.12 = (f32[7,48,128]{2,1,0:T(8,128)S(1)}, f32[7,48,128]{2,1,0:T(8,128)S(1)}, u32[]{:S(2)}, u32[]{:S(2)}) collective-permute-start(f32[7,48,128]{2,1,0:T(8,128)S(1)} %pad_maximum_fusion.8), channel_id=1, source_target_pairs={{0,8},{8,0},{16,24},{24,16},{1,9},{9,1},{17,25},{25,17},{2,10},{10... | collective-permute-start | bytes 516104 | tf_op jit(solution)/shard_map/ppermute | solution.py:233
  54.4 5.4 %collective-permute-start.14 = (bf16[9,48,128]{2,1,0:T(8,128)(2,1)S(1)}, bf16[9,48,128]{2,1,0:T(8,128)(2,1)S(1)}, u32[]{:S(2)}, u32[]{:S(2)}) collective-permute-start(bf16[9,48,128]{2,1,0:T(8,128)(2,1)S(1)} %pad_maximum_fusion.14), channel_id=1, source_target_pairs={{0,16},{1,17},{2,18},{3,19},{4,20},{5,21},{6,22},{7,23},{8,24},{9,... | collective-permute-start | bytes 331784 | tf_op jit(solution)/shard_map/ppermute | solution.py:230
  60.3 1.3 collective-permute-start.15
  61.6 5.9 %collective-permute-start.16 = (bf16[12,32,128]{2,1,0:T(8,128)(2,1)S(1)}, bf16[12,32,128]{2,1,0:T(8,128)(2,1)S(1)}, u32[]{:S(2)}, u32[]{:S(2)}) collective-permute-start(bf16[12,32,128]{2,1,0:T(8,128)(2,1)S(1)} %pad_maximum_fusion.16), channel_id=1, source_target_pairs={{0,16},{1,17},{2,18},{3,19},{4,20},{5,21},{6,22},{7,23},{8,9},{9,8... | collective-permute-start | bytes 294920 | tf_op jit(solution)/shard_map/ppermute | solution.py:230
  63.0 10.1 %collective-permute-start.17 = (bf16[12,32,128]{2,1,0:T(8,128)(2,1)S(1)}, bf16[12,32,128]{2,1,0:T(8,128)(2,1)S(1)}, u32[]{:S(2)}, u32[]{:S(2)}) collective-permute-start(bf16[12,32,128]{2,1,0:T(8,128)(2,1)S(1)} %pad_maximum_fusion.16), channel_id=1, source_target_pairs={{0,2},{1,3},{2,0},{3,1},{4,6},{5,7},{6,4},{7,5},{8,11},{9,10},{10,... | collective-permute-start | bytes 294920 | tf_op jit(solution)/shard_map/ppermute | solution.py:230
  64.4 10.7 %collective-permute-start.18 = (bf16[12,32,128]{2,1,0:T(8,128)(2,1)S(1)}, bf16[12,32,128]{2,1,0:T(8,128)(2,1)S(1)}, u32[]{:S(2)}, u32[]{:S(2)}) collective-permute-start(bf16[12,32,128]{2,1,0:T(8,128)(2,1)S(1)} %pad_maximum_fusion.16), channel_id=1, source_target_pairs={{0,4},{1,5},{2,6},{3,7},{4,0},{5,1},{6,2},{7,3},{8,13},{9,12},{10,... | collective-permute-start | bytes 294920 | tf_op jit(solution)/shard_map/ppermute | solution.py:230
  66.4 8.7 %collective-permute-start.19 = (bf16[12,32,128]{2,1,0:T(8,128)(2,1)S(1)}, bf16[12,32,128]{2,1,0:T(8,128)(2,1)S(1)}, u32[]{:S(2)}, u32[]{:S(2)}) collective-permute-start(bf16[12,32,128]{2,1,0:T(8,128)(2,1)S(1)} %pad_maximum_fusion.16), channel_id=1, source_target_pairs={{0,6},{1,7},{2,4},{3,5},{4,2},{5,3},{6,0},{7,1},{8,15},{9,14},{10,... | collective-permute-start | bytes 294920 | tf_op jit(solution)/shard_map/ppermute | solution.py:230
  67.5 1.3 collective-permute-start.20
  75.2 1.4 %collective-permute-start.21 = (bf16[18,32,128]{2,1,0:T(8,128)(2,1)S(1)}, bf16[18,32,128]{2,1,0:T(8,128)(2,1)S(1)}, u32[]{:S(2)}, u32[]{:S(2)}) collective-permute-start(bf16[18,32,128]{2,1,0:T(8,128)(2,1)S(1)} %pad_maximum_fusion.10), channel_id=1, source_target_pairs={{0,8},{8,0},{16,24},{24,16},{1,9},{9,1},{17,25},{25,17},{2,10},{10... | collective-permute-start | bytes 442376 | tf_op jit(solution)/shard_map/ppermute | solution.py:233
  77.1 1.5 %collective-permute-start.22 = (bf16[27,32,128]{2,1,0:T(8,128)(2,1)S(1)}, bf16[27,32,128]{2,1,0:T(8,128)(2,1)S(1)}, u32[]{:S(2)}, u32[]{:S(2)}) collective-permute-start(bf16[27,32,128]{2,1,0:T(8,128)(2,1)S(1)} %pad_maximum_fusion.5), channel_id=1, source_target_pairs={{0,8},{8,0},{16,24},{24,16},{1,9},{9,1},{17,25},{25,17},{2,10},{10... | collective-permute-start | bytes 663560 | tf_op jit(solution)/shard_map/ppermute | solution.py:233
  79.0 13.6 %collective-permute-start.24 = (bf16[15,32,128]{2,1,0:T(8,128)(2,1)S(1)}, bf16[15,32,128]{2,1,0:T(8,128)(2,1)S(1)}, u32[]{:S(2)}, u32[]{:S(2)}) collective-permute-start(bf16[15,32,128]{2,1,0:T(8,128)(2,1)S(1)} %get-tuple-element.185), channel_id=1, source_target_pairs={{0,2},{1,3},{2,0},{3,1},{4,6},{5,7},{6,4},{7,5},{8,11},{9,10},{10,... | collective-permute-start | bytes 368648 | tf_op jit(solution)/shard_map/ppermute | solution.py:230
  81.3 12.4 %collective-permute-start.25 = (bf16[15,32,128]{2,1,0:T(8,128)(2,1)S(1)}, bf16[15,32,128]{2,1,0:T(8,128)(2,1)S(1)}, u32[]{:S(2)}, u32[]{:S(2)}) collective-permute-start(bf16[15,32,128]{2,1,0:T(8,128)(2,1)S(1)} %get-tuple-element.186), channel_id=1, source_target_pairs={{0,4},{1,5},{2,6},{3,7},{4,0},{5,1},{6,2},{7,3},{8,13},{9,12},{10,... | collective-permute-start | bytes 368648 | tf_op jit(solution)/shard_map/ppermute | solution.py:230
  82.2 11.4 %collective-permute-start.26 = (bf16[15,32,128]{2,1,0:T(8,128)(2,1)S(1)}, bf16[15,32,128]{2,1,0:T(8,128)(2,1)S(1)}, u32[]{:S(2)}, u32[]{:S(2)}) collective-permute-start(bf16[15,32,128]{2,1,0:T(8,128)(2,1)S(1)} %get-tuple-element.187), channel_id=1, source_target_pairs={{0,6},{1,7},{2,4},{3,5},{4,2},{5,3},{6,0},{7,1},{8,15},{9,14},{10,... | collective-permute-start | bytes 368648 | tf_op jit(solution)/shard_map/ppermute | solution.py:230
  83.7 9.9 %collective-permute-start.23 = (bf16[15,32,128]{2,1,0:T(8,128)(2,1)S(1)}, bf16[15,32,128]{2,1,0:T(8,128)(2,1)S(1)}, u32[]{:S(2)}, u32[]{:S(2)}) collective-permute-start(bf16[15,32,128]{2,1,0:T(8,128)(2,1)S(1)} %get-tuple-element.77), channel_id=1, source_target_pairs={{8,9},{9,8},{10,11},{11,10},{12,13},{13,12},{14,15},{15,14},{24,25... | collective-permute-start | bytes 368648 | tf_op jit(solution)/shard_map/ppermute | solution.py:230
  90.1 3.7 %collective-permute-start.28 = (f32[12,32,128]{2,1,0:T(8,128)S(1)}, f32[12,32,128]{2,1,0:T(8,128)S(1)}, u32[]{:S(2)}, u32[]{:S(2)}) collective-permute-start(f32[12,32,128]{2,1,0:T(8,128)S(1)} %bitcast.255), channel_id=1, source_target_pairs={{0,8},{8,0},{16,24},{24,16},{1,9},{9,1},{17,25},{25,17},{2,10},{10... | collective-permute-start | bytes 589832 | tf_op jit(solution)/shard_map/ppermute | solution.py:233
  93.8 1.4 collective-permute-start.27
  95.3 4.4 %collective-permute-start.29 = (bf16[9,32,128]{2,1,0:T(8,128)(2,1)S(1)}, bf16[9,32,128]{2,1,0:T(8,128)(2,1)S(1)}, u32[]{:S(2)}, u32[]{:S(2)}) collective-permute-start(bf16[9,32,128]{2,1,0:T(8,128)(2,1)S(1)} %pad_maximum_fusion.18), channel_id=1, source_target_pairs={{0,16},{1,17},{2,18},{3,19},{4,20},{5,21},{6,22},{7,23},{8,24},{9,... | collective-permute-start | bytes 221192 | tf_op jit(solution)/shard_map/ppermute | solution.py:230
  100.1 1.3 collective-permute-start.30
  101.4 7.1 %collective-permute-start.31 = (bf16[12,32,128]{2,1,0:T(8,128)(2,1)S(1)}, bf16[12,32,128]{2,1,0:T(8,128)(2,1)S(1)}, u32[]{:S(2)}, u32[]{:S(2)}) collective-permute-start(bf16[12,32,128]{2,1,0:T(8,128)(2,1)S(1)} %pad_maximum_fusion.17), channel_id=1, source_target_pairs={{0,16},{1,17},{2,18},{3,19},{4,20},{5,21},{6,22},{7,23},{8,9},{9,8... | collective-permute-start | bytes 294920 | tf_op jit(solution)/shard_map/ppermute | solution.py:230
  102.7 11.4 %collective-permute-start.32 = (bf16[12,32,128]{2,1,0:T(8,128)(2,1)S(1)}, bf16[12,32,128]{2,1,0:T(8,128)(2,1)S(1)}, u32[]{:S(2)}, u32[]{:S(2)}) collective-permute-start(bf16[12,32,128]{2,1,0:T(8,128)(2,1)S(1)} %pad_maximum_fusion.17), channel_id=1, source_target_pairs={{0,2},{1,3},{2,0},{3,1},{4,6},{5,7},{6,4},{7,5},{8,11},{9,10},{10,... | collective-permute-start | bytes 294920 | tf_op jit(solution)/shard_map/ppermute | solution.py:230
  106.0 10.4 %collective-permute-start.33 = (bf16[12,32,128]{2,1,0:T(8,128)(2,1)S(1)}, bf16[12,32,128]{2,1,0:T(8,128)(2,1)S(1)}, u32[]{:S(2)}, u32[]{:S(2)}) collective-permute-start(bf16[12,32,128]{2,1,0:T(8,128)(2,1)S(1)} %pad_maximum_fusion.17), channel_id=1, source_target_pairs={{0,4},{1,5},{2,6},{3,7},{4,0},{5,1},{6,2},{7,3},{8,13},{9,12},{10,... | collective-permute-start | bytes 294920 | tf_op jit(solution)/shard_map/ppermute | solution.py:230
  107.1 9.2 %collective-permute-start.34 = (bf16[12,32,128]{2,1,0:T(8,128)(2,1)S(1)}, bf16[12,32,128]{2,1,0:T(8,128)(2,1)S(1)}, u32[]{:S(2)}, u32[]{:S(2)}) collective-permute-start(bf16[12,32,128]{2,1,0:T(8,128)(2,1)S(1)} %pad_maximum_fusion.17), channel_id=1, source_target_pairs={{0,6},{1,7},{2,4},{3,5},{4,2},{5,3},{6,0},{7,1},{8,15},{9,14},{10,... | collective-permute-start | bytes 294920 | tf_op jit(solution)/shard_map/ppermute | solution.py:230
  108.5 1.3 collective-permute-start.35
  116.5 1.4 %collective-permute-start.36 = (bf16[18,32,128]{2,1,0:T(8,128)(2,1)S(1)}, bf16[18,32,128]{2,1,0:T(8,128)(2,1)S(1)}, u32[]{:S(2)}, u32[]{:S(2)}) collective-permute-start(bf16[18,32,128]{2,1,0:T(8,128)(2,1)S(1)} %pad_maximum_fusion.11), channel_id=1, source_target_pairs={{0,8},{8,0},{16,24},{24,16},{1,9},{9,1},{17,25},{25,17},{2,10},{10... | collective-permute-start | bytes 442376 | tf_op jit(solution)/shard_map/ppermute | solution.py:233
  118.4 1.5 %collective-permute-start.37 = (bf16[27,32,128]{2,1,0:T(8,128)(2,1)S(1)}, bf16[27,32,128]{2,1,0:T(8,128)(2,1)S(1)}, u32[]{:S(2)}, u32[]{:S(2)}) collective-permute-start(bf16[27,32,128]{2,1,0:T(8,128)(2,1)S(1)} %pad_maximum_fusion.6), channel_id=1, source_target_pairs={{0,8},{8,0},{16,24},{24,16},{1,9},{9,1},{17,25},{25,17},{2,10},{10... | collective-permute-start | bytes 663560 | tf_op jit(solution)/shard_map/ppermute | solution.py:233
  120.3 13.4 %collective-permute-start.39 = (bf16[15,32,128]{2,1,0:T(8,128)(2,1)S(1)}, bf16[15,32,128]{2,1,0:T(8,128)(2,1)S(1)}, u32[]{:S(2)}, u32[]{:S(2)}) collective-permute-start(bf16[15,32,128]{2,1,0:T(8,128)(2,1)S(1)} %get-tuple-element.176), channel_id=1, source_target_pairs={{0,2},{1,3},{2,0},{3,1},{4,6},{5,7},{6,4},{7,5},{8,11},{9,10},{10,... | collective-permute-start | bytes 368648 | tf_op jit(solution)/shard_map/ppermute | solution.py:230
  122.4 12.4 %collective-permute-start.40 = (bf16[15,32,128]{2,1,0:T(8,128)(2,1)S(1)}, bf16[15,32,128]{2,1,0:T(8,128)(2,1)S(1)}, u32[]{:S(2)}, u32[]{:S(2)}) collective-permute-start(bf16[15,32,128]{2,1,0:T(8,128)(2,1)S(1)} %get-tuple-element.177), channel_id=1, source_target_pairs={{0,4},{1,5},{2,6},{3,7},{4,0},{5,1},{6,2},{7,3},{8,13},{9,12},{10,... | collective-permute-start | bytes 368648 | tf_op jit(solution)/shard_map/ppermute | solution.py:230
  123.3 11.5 %collective-permute-start.41 = (bf16[15,32,128]{2,1,0:T(8,128)(2,1)S(1)}, bf16[15,32,128]{2,1,0:T(8,128)(2,1)S(1)}, u32[]{:S(2)}, u32[]{:S(2)}) collective-permute-start(bf16[15,32,128]{2,1,0:T(8,128)(2,1)S(1)} %get-tuple-element.178), channel_id=1, source_target_pairs={{0,6},{1,7},{2,4},{3,5},{4,2},{5,3},{6,0},{7,1},{8,15},{9,14},{10,... | collective-permute-start | bytes 368648 | tf_op jit(solution)/shard_map/ppermute | solution.py:230
  124.9 9.9 %collective-permute-start.38 = (bf16[15,32,128]{2,1,0:T(8,128)(2,1)S(1)}, bf16[15,32,128]{2,1,0:T(8,128)(2,1)S(1)}, u32[]{:S(2)}, u32[]{:S(2)}) collective-permute-start(bf16[15,32,128]{2,1,0:T(8,128)(2,1)S(1)} %get-tuple-element.64), channel_id=1, source_target_pairs={{8,9},{9,8},{10,11},{11,10},{12,13},{13,12},{14,15},{15,14},{24,25... | collective-permute-start | bytes 368648 | tf_op jit(solution)/shard_map/ppermute | solution.py:230
  131.1 3.9 %collective-permute-start.43 = (f32[12,32,128]{2,1,0:T(8,128)S(1)}, f32[12,32,128]{2,1,0:T(8,128)S(1)}, u32[]{:S(2)}, u32[]{:S(2)}) collective-permute-start(f32[12,32,128]{2,1,0:T(8,128)S(1)} %bitcast.256), channel_id=1, source_target_pairs={{0,8},{8,0},{16,24},{24,16},{1,9},{9,1},{17,25},{25,17},{2,10},{10... | collective-permute-start | bytes 589832 | tf_op jit(solution)/shard_map/ppermute | solution.py:233
  134.9 1.4 collective-permute-start.42
  136.4 4.4 %collective-permute-start.44 = (bf16[9,32,128]{2,1,0:T(8,128)(2,1)S(1)}, bf16[9,32,128]{2,1,0:T(8,128)(2,1)S(1)}, u32[]{:S(2)}, u32[]{:S(2)}) collective-permute-start(bf16[9,32,128]{2,1,0:T(8,128)(2,1)S(1)} %pad_maximum_fusion.19), channel_id=1, source_target_pairs={{0,16},{1,17},{2,18},{3,19},{4,20},{5,21},{6,22},{7,23},{8,24},{9,... | collective-permute-start | bytes 221192 | tf_op jit(solution)/shard_map/ppermute | solution.py:230

commit v3 on v2

--- a/solution.py
+++ b/solution.py
@@ -63,23 +63,34 @@
 
 
 def first_row_kernel(
-    slots, loads, place, field, source, out, row_blocks, tiles, blocks, semaphores, back_semaphores
+    slots, loads, place, field, source, out, degree, col_degree, squares, row_blocks, tiles, blocks,
+    semaphores, back_semaphores,
 ):
     copies = start_copies(source, tiles, semaphores)
     back = start_copies(row_blocks, blocks, back_semaphores, to_held=False)
     count = place.shape[0]
     per = slots.shape[0] // count
     tile_size = tiles.shape[1]
+    tasks = out.shape[1]
     out[...] = jnp.zeros_like(out)
+    degree[...] = jnp.zeros_like(degree)
+    squares[...] = jnp.zeros_like(squares)
+    col_degree[...] = jnp.zeros_like(col_degree)
     for copy in copies:
         copy.wait()
 
     def one(i):
         base = i * per
         for j in range(per):
-            blocks[i, pl.ds(j * tile_size, tile_size)] = tiles[slots[base + j]].T
+            tile = tiles[slots[base + j]]
+            blocks[i, pl.ds(j * tile_size, tile_size)] = tile.T
+            addends = tile.astype(jnp.float32).reshape(tile_size // 8, 8, tile_size)
+            col_degree[loads[base + j]] += jnp.sum(addends, axis=0)
         held = gathered(field, loads, base, per)
-        out[place[i]] = jnp.dot(held, blocks[i], preferred_element_type=jnp.float32)
+        total = jnp.dot(held, blocks[i], preferred_element_type=jnp.float32)
+        out[place[i]] = total[:tasks].astype(out.dtype)
+        degree[place[i]] = total[tasks : tasks + 8]
+        squares[...] += total[tasks + 16 :]
 
     part = count // len(back)
     for g, copy in enumerate(back):
@@ -131,18 +142,21 @@
     )(*lists, field, tiles)
 
 
-def first_product(lists, field, tiles, out_tiles):
+def first_product(lists, field, tiles, out_tiles, tasks):
     count = lists[2].shape[0]
     slots, tile_size = tiles.shape[:2]
     blocks = (count, slots // count * tile_size, tile_size)
     return pl.pallas_call(
         first_row_kernel,
         out_shape=(
-            jax.ShapeDtypeStruct((out_tiles,) + field.shape[1:], jnp.float32),
+            jax.ShapeDtypeStruct((out_tiles, tasks, tile_size), field.dtype),
+            jax.ShapeDtypeStruct((out_tiles, 8, tile_size), jnp.float32),
+            jax.ShapeDtypeStruct((field.shape[0], 8, tile_size), jnp.float32),
+            jax.ShapeDtypeStruct((tasks, tile_size), jnp.float32),
             jax.ShapeDtypeStruct(blocks, tiles.dtype),
         ),
         in_specs=[IN_SMEM] * 3 + [IN_VMEM, IN_HBM],
-        out_specs=(IN_VMEM, IN_HBM),
+        out_specs=(IN_VMEM, IN_VMEM, IN_VMEM, IN_VMEM, IN_HBM),
         scratch_shapes=[
             pltpu.VMEM(tiles.shape, tiles.dtype),
             pltpu.VMEM(blocks, tiles.dtype),
@@ -179,26 +193,35 @@
     return pick(order), pick(loads)
 
 
-def split(value, rows_held):
+def addends(value, count):
     parts = []
-    for _ in range(3):
+    for _ in range(count):
         high = lax.reduce_precision(value, 8, 7)
         parts.append(high)
         value = value - high
-    parts = jnp.stack(parts).astype(jnp.bfloat16)
-    return jnp.pad(parts, ((0, 0), (0, rows_held - parts.shape[1]), (0, 0)))
-
-
-def join(parts, rows):
-    return jnp.sum(parts[:, :rows].astype(jnp.float32), axis=0)
+    return jnp.stack(parts).astype(jnp.bfloat16)
+
+
+def join(parts):
+    return jnp.sum(parts.astype(jnp.float32), axis=0)
+
+
+def rows_to_tiles(rows, tile_rows):
+    count = -(-rows.shape[0] // tile_rows)
+    rows = jnp.pad(rows, ((0, count * tile_rows - rows.shape[0]), (0, 0)))
+    return rows.reshape(count, tile_rows, rows.shape[1])
+
+
+def tiles_to_rows(tiles, count):
+    return tiles.reshape(-1, tiles.shape[2])[:count]
 
 
 class Plan:
     def __init__(self, rows, cols):
         self.rows, self.cols = rows, cols
         self.row_steps = [("row", m) for m in range(1, rows // 2)]
-        first = self.row_steps + [("col", k) for k in range(2, cols, 2)]
-        second = [("col", k) for k in range(1, cols, 2)]
+        first = self.row_steps + [("col", k) for k in range(cols - 2, 0, -2)]
+        second = [("col", 1)] + [("col", k) for k in range(cols - 1, 1, -2)]
         while len(first) > len(second) + 1:
             second.append(first.pop())
         first += [None] * (len(second) - len(first))
@@ -276,25 +299,17 @@
     def empty_tile(field):
         return jnp.zeros((1,) + field.shape[1:], field.dtype)
 
-    def with_ones(field):
-        field = jnp.pad(field[:-1], ((0, 0), (0, 16), (0, 0)), constant_values=1)
+    def with_rows(field):
+        ones = jnp.ones((field.shape[0] - 1, 16, tile_size), field.dtype)
+        squares = (field[:-1].astype(jnp.float32) ** 2).astype(field.dtype)
+        field = jnp.concatenate([field[:-1], ones, squares], axis=1)
         return jnp.pad(field, ((0, 1), (0, 0), (0, 0)))
 
-    def to_low(value):
-        if value.shape[1] == task_count:
-            return value.astype(low)
-        rounded = lax.reduce_precision(value, 8, 7)
-        at = lax.broadcasted_iota(jnp.int32, value.shape, 1)
-        return jnp.where(at == task_count + 1, value - rounded, rounded).astype(low)
-
-    def one_addend(value):
-        if value.shape[1] == task_count:
-            return value
-        at = lax.broadcasted_iota(jnp.int32, value.shape, 1)
-        return jnp.where(at == task_count + 1, 0.0, value)
-
-    def two_addends(value):
-        return value[:, task_count : task_count + 1] + value[:, task_count + 1 : task_count + 2]
+    def pack(degree):
+        return rows_to_tiles(addends(degree, 2).reshape(-1, tile_size), task_count)
+
+    def unpack(tiles, count):
+        return join(tiles_to_rows(tiles, 2 * count).reshape(2, count, tile_size))
 
     def inner(a, b):
         return jnp.sum(a.astype(jnp.float32) * b.astype(jnp.float32), axis=(0, 2))[:, None]
@@ -310,7 +325,6 @@
     norm_before = curve_before = scale = None
     for step_index in range(ITERS):
         first = step_index == 0
-        at = slice(0, task_count)
 
         own_low = residual.astype(low)
         pair = jnp.concatenate([own_low, plan.swap(own_low)])
@@ -325,71 +339,87 @@
             col_pieces.append(jnp.where(core == 0, g[own_tiles:], other[:own_tiles]))
         col_field = jnp.concatenate(col_pieces + [empty_tile(pair)])
         if first:
-            col_field = with_ones(col_field)
-            forward, row_blocks = first_product(by_row, col_field, tiles, row_pieces)
+            forward, row_degree, col_degree, squares, row_blocks = first_product(
+                by_row, with_rows(col_field), tiles, row_pieces, task_count
+            )
         else:
             forward = next_product(by_row, col_field, row_blocks, row_pieces)
 
         far, forward = lax.optimization_barrier((got[near:], forward))
-        forward = to_low(forward)
         mine = [g[:own_tiles] for g in got[:near] + far]
         swapped = plan.swap(jnp.concatenate([g[own_tiles:] for g in far]))
         row_field = jnp.concatenate(
             [own_low] + mine + [o[own_tiles:] for o in shared] + [swapped, empty_tile(pair)]
         )
-        curve_part = -inner(row_field[:-1], forward[:, at])
-        if first:
-            backward = product(by_col, with_ones(row_field), tiles, col_tiles)
+        curve_part = -inner(row_field[:-1], forward)
         norm = inner(residual, residual)
         if first:
-            square = lambda value: value.astype(jnp.float32) ** 2
-            curve_part += 0.5 * inner(
-                square(row_field[:-1]), two_addends(forward.astype(jnp.float32))
-            )
-            curve_part += 0.5 * inner(
-                square(col_field[:-1, at]), backward[:, task_count : task_count + 1]
-            )
-            dots = as_tile([norm, norm + coupling * curve_part])
+            row_degree = row_degree[:, 0]
+            weights = 0.5 * coupling * row_degree[:, None]
+            curve_part = coupling * curve_part
+            curve_part += inner(row_field[:-1].astype(jnp.float32) ** 2, weights)
+            curve_part += 0.5 * coupling * jnp.sum(squares, axis=1, keepdims=True)
+            dots = as_tile([norm, norm + curve_part])
         else:
             weighted = inner(scale * residual, residual)
             dots = as_tile([norm, weighted + coupling * curve_part, inner(residual, image)])
 
-        rows_held = forward.shape[1]
-        swapped = plan.swap(
-            jnp.concatenate([forward[own_tiles + low_part :], split(dots, rows_held)])
-        )
-        if not first:
-            swapped, row_field = lax.optimization_barrier((swapped, row_field))
-            backward = product(by_col, row_field, tiles, col_tiles)
-        dots = dots + join(swapped[low_part:], task_count)
-        dots_low = split(dots, rows_held)
+        parts = [forward[own_tiles + low_part :], addends(dots, 3)]
+        if first:
+            col_degree = jnp.sum(col_degree[:-1], axis=1)
+            col_degree = col_degree.reshape(chip_rows, 2, own_tiles, tile_size)
+            sent = [row_degree[own_tiles + low_part :], col_degree[:, 1].reshape(-1, tile_size)]
+            parts.append(pack(jnp.concatenate(sent)))
+        swapped = plan.swap(jnp.concatenate(parts))
+        swapped, row_field = lax.optimization_barrier((swapped, row_field))
+        if first:
+            back = unpack(swapped[low_part + 3 :], low_part + chip_rows * own_tiles)
+            other_degree = back[:low_part]
+            col_degree = col_degree[:, 0] + back[low_part:].reshape(col_degree[:, 0].shape)
+        backward = product(by_col, row_field, tiles, col_tiles)
+        dots = dots + join(swapped[low_part : low_part + 3])
+        dots_low = addends(dots, 3)
         messages = []
         for j, by_core in enumerate(plan.sum_steps):
             piece = slice(j * own_tiles, (j + 1) * own_tiles)
-            message = jnp.concatenate([forward[own_tiles:][piece], swapped[piece], dots_low])
-            messages.append(plan.send(message, by_core))
-        backward = backward.reshape(chip_rows, 2, own_tiles, rows_held, tile_size)
-        back = plan.swap(backward[:, 1].reshape(-1, rows_held, tile_size))
+            message = [forward[own_tiles:][piece], swapped[:low_part][piece], dots_low]
+            if first:
+                degrees = [row_degree[own_tiles:][piece], other_degree[piece]]
+                message.append(pack(jnp.concatenate(degrees)))
+            messages.append(plan.send(jnp.concatenate(message), by_core))
+        backward = backward.reshape(chip_rows, 2, own_tiles, task_count, tile_size)
+        back = plan.swap(backward[:, 1].reshape(-1, task_count, tile_size))
         backward = backward[:, 0] + back.reshape(backward[:, 0].shape)
         total = sum(m.astype(jnp.float32) for m in messages)
-        dots_mine = jnp.sum(total[2 * own_tiles :], axis=0)
-        back = plan.swap(jnp.concatenate([total[own_tiles : 2 * own_tiles], dots_mine[None]]))
-        dots = dots + (dots_mine + back[-1])[at]
-        total = total[:own_tiles] + back[:-1] + forward[:own_tiles].astype(jnp.float32)
-
-        total = total + one_addend(backward[0])
-        dots_low = split(dots, rows_held)
+        dots_mine = jnp.sum(total[2 * own_tiles : 2 * own_tiles + 3], axis=0)
+        message = [total[own_tiles : 2 * own_tiles], dots_mine[None]]
+        if first:
+            degree = unpack(total[2 * own_tiles + 3 :], 2 * own_tiles)
+            message.append(rows_to_tiles(degree[own_tiles:], task_count))
+        back = plan.swap(jnp.concatenate(message))
+        dots = dots + (dots_mine + back[own_tiles])
+        total = total[:own_tiles] + back[:own_tiles] + forward[:own_tiles].astype(jnp.float32)
+        if first:
+            degree = degree[:own_tiles] + tiles_to_rows(back[own_tiles + 1 :], own_tiles)
+            degree += row_degree[:own_tiles] + col_degree[0]
+
+        total = total + backward[0]
+        dots_low = addends(dots, 3)
         for m, by_core in enumerate(plan.row_steps, 1):
-            message = jnp.concatenate([to_low(backward[m]), dots_low])
-            back = plan.send(message, (by_core,) * 2)
+            message = [backward[m].astype(low), dots_low]
+            if first:
+                message.append(pack(col_degree[m]))
+            back = plan.send(jnp.concatenate(message), (by_core,) * 2)
             total = total + back[:own_tiles].astype(jnp.float32)
-            dots = dots + join(back[own_tiles:], task_count)
+            dots = dots + join(back[own_tiles : own_tiles + 3])
+            if first:
+                degree += unpack(back[own_tiles + 3 :], own_tiles)
         total = 0.5 * total
 
         norm, curve, along = dots[:, 0:1], dots[:, 1:2], dots[:, 2:3]
         if first:
-            scale = 1.0 + coupling * two_addends(total)
-        fresh = scale * residual - coupling * total[:, at]
+            scale = 1.0 + 0.5 * coupling * degree[:, None]
+        fresh = scale * residual - coupling * total
         if first:
             direction, image = residual, fresh
         else:

time: 143 us -> 129 us (0.902)
  waiting for transfers between devices: 45.9 us -> 28.7 us
  starting transfers between devices: 48.9 us -> 52 us
    ppermute x27, waiting for transfers between devices: 30 us -> 13.3 us  [send(): return lax.ppermute(value, MESH_AXES, self.pairs(by_core))]
    ppermute x18, starting transfers between devices: 9.14 us -> 13.6 us  [swap(): return lax.ppermute(value, 'row', [(r, r ^ 1) for r in range(self.rows)])]
  transfers between devices with their start and end apart: 45 -> 45, of which waited for: 23 -> 22; matrix products, arithmetic and copies ran while one was open for 4% -> 5% of each run, Pallas kernels for 19% -> 26%
where the time goes in v3:
time: 129 us
  starting transfers between devices  52 us (40%)
  Pallas kernels  33 us (26%)
  waiting for transfers between devices  28.7 us (22%)
  other arithmetic  9.54 us (7%)
  local copies, waits for them, and re-layouts  3.53 us (3%)
  between operations  2.35 us (2%)
    ppermute x27, starting transfers between devices, send(): return lax.ppermute(value, MESH_AXES, self.pairs(by_core))  38.4 us
    pallas_call x3, Pallas kernels, product(): pl.pallas_call(col_kernel, out_shape=jax.ShapeDtypeStruct((out_tiles,) +...  16.5 us
    ppermute x18, waiting for transfers between devices, swap(): return lax.ppermute(value, 'row', [(r, r ^ 1) for r in range(self.rows)])  15.4 us
    ppermute x18, starting transfers between devices, swap(): return lax.ppermute(value, 'row', [(r, r ^ 1) for r in range(self.rows)])  13.6 us
    ppermute x27, waiting for transfers between devices, send(): return lax.ppermute(value, MESH_AXES, self.pairs(by_core))  13.3 us
    pallas_call x2, Pallas kernels, next_product(): pl.pallas_call(next_row_kernel, out_shape=jax.ShapeDtypeStruct((out_tiles...  8.44 us
    pallas_call x1, Pallas kernels, first_product(): pl.pallas_call(first_row_kernel, out_shape=(jax.ShapeDtypeStruct((out_til...  8.05 us
  transfers between devices with their start and end apart: 45, of which 22 were waited for; matrix products, arithmetic and copies ran while one was open for 5% of the time, Pallas kernels for 26%

profile of v3, /device:TPU:0, one launch (start us, length us, event | category | flops | bytes accessed | tf_op | source)
XLA Modules:
  0.0 129.1 jit_solution(9347266408303545576)
XLA Ops:
  0.6 0.9 copy-done
  1.5 0.5 collective-permute-start
  2.2 0.7 broadcast_select_fusion.1
  3.8 2.6 %collective-permute-start.1 = (bf16[12,32,128]{2,1,0:T(8,128)(2,1)S(1)}, bf16[12,32,128]{2,1,0:T(8,128)(2,1)S(1)}, u32[]{:S(2)}, u32[]{:S(2)}) collective-permute-start(bf16[12,32,128]{2,1,0:T(8,128)(2,1)S(1)} %pad_maximum_fusion.9), channel_id=1, source_target_pairs={{0,16},{1,17},{2,18},{3,19},{4,20},{5,21},{6,22},{7,23},{8,9},{9,8... | collective-permute-start | bytes 294920 | tf_op jit(solution)/shard_map/ppermute | solution.py:253
  6.4 3.6 %collective-permute-start.2 = (bf16[12,32,128]{2,1,0:T(8,128)(2,1)S(1)}, bf16[12,32,128]{2,1,0:T(8,128)(2,1)S(1)}, u32[]{:S(2)}, u32[]{:S(2)}) collective-permute-start(bf16[12,32,128]{2,1,0:T(8,128)(2,1)S(1)} %pad_maximum_fusion.9), channel_id=1, source_target_pairs={{0,6},{1,7},{2,4},{3,5},{4,2},{5,3},{6,0},{7,1},{8,15},{9,14},{10,... | collective-permute-start | bytes 294920 | tf_op jit(solution)/shard_map/ppermute | solution.py:253
  10.0 0.8 collective-permute-start.4
  10.8 0.7 fusion.95
  11.5 1.0 convert_reduce_fusion
  12.5 0.7 fusion.92
  13.2 0.7 multiply_add_fusion.1
  14.6 0.9 collective-permute-done.5
  15.8 8.0 %shard_map.86 = (bf16[54,32,128]{2,1,0:T(8,128)(2,1)S(1)}, f32[54,8,128]{2,1,0:T(8,128)S(1)}, f32[25,8,128]{2,1,0:T(8,128)S(1)}, f32[32,128]{1,0:T(8,128)S(1)}, bf16[48,640,128]{2,1,0:T(8,128)(2,1)}) custom-call(s32[240]{0:T(256)S(1)} %get-tuple-element.69.slots, s32[240]{0:T(256)S(1)} %get-tuple-element.68.loads, s32[48]{0:T(128)S(1)} %fusion.96.place, ...), custom_call_target="tpu_custom_call" | custom-call | flops 5033164800 | bytes 7864320 | tf_op jit(solution)/shard_map/pallas_call | solution.py:149
  24.8 0.9 collective-permute-done.6
  25.8 0.4 fusion
  26.8 1.2 collective-permute-done.7
  28.5 0.7 collective-permute-start.8
  29.3 3.7 %collective-permute-start.9 = (bf16[16,32,128]{2,1,0:T(8,128)(2,1)S(1)}, bf16[16,32,128]{2,1,0:T(8,128)(2,1)S(1)}, u32[]{:S(2)}, u32[]{:S(2)}) collective-permute-start(bf16[16,32,128]{2,1,0:T(8,128)(2,1)S(1)} %constant_dynamic-update-slice_fusion.26), channel_id=1, source_target_pairs={{0,6},{1,7},{2,4},{3,5},{4,2},{5,3},{6,0},{7,1},{8,15},{9,14},{10,... | collective-permute-start | bytes 393224 | tf_op jit(solution)/shard_map/ppermute | solution.py:253
  33.2 0.8 collective-permute-start.11
  34.0 5.5 %shard_map.87 = f32[24,32,128]{2,1,0:T(8,128)S(1)} custom-call(s32[240]{0:T(256)S(1)} %get-tuple-element.71.slots, s32[240]{0:T(256)S(1)} %get-tuple-element.70.loads, s32[24]{0:T(128)S(1)} %fusion.97.place, bf16[55,32,128]{2,1,0:T(8,128)(2,1)S(1)} %constant_dynamic-update-slice_fusion.12.field, bf16[240,128,128]{2,1,0:T(8,128)(2,1)} %bitcast.292), custom_call_target="tpu_custom_call" | custom-call | flops 2013265920 | bytes 7864320 | tf_op jit(solution)/shard_map/pallas_call | solution.py:134
  39.5 2.8 %collective-permute-start.13 = (f32[12,32,128]{2,1,0:T(8,128)S(1)}, f32[12,32,128]{2,1,0:T(8,128)S(1)}, u32[]{:S(2)}, u32[]{:S(2)}) collective-permute-start(f32[12,32,128]{2,1,0:T(8,128)S(1)} %bitcast.298), channel_id=1, source_target_pairs={{0,8},{8,0},{16,24},{24,16},{1,9},{9,1},{17,25},{25,17},{2,10},{10... | collective-permute-start | bytes 589832 | tf_op jit(solution)/shard_map/ppermute | solution.py:256
  42.4 1.4 %collective-permute-done.10 = bf16[16,32,128]{2,1,0:T(8,128)(2,1)S(1)} collective-permute-done((bf16[16,32,128]{2,1,0:T(8,128)(2,1)S(1)}, bf16[16,32,128]{2,1,0:T(8,128)(2,1)S(1)}, u32[]{:S(2)}, u32[]{:S(2)}) %collective-permute-start.10) | collective-permute-done | bytes 131104 | tf_op jit(solution)/shard_map/ppermute | solution.py:253
  44.0 1.8 %collective-permute-start.12 = (f32[8,32,128]{2,1,0:T(8,128)S(1)}, f32[8,32,128]{2,1,0:T(8,128)S(1)}, u32[]{:S(2)}, u32[]{:S(2)}) collective-permute-start(f32[8,32,128]{2,1,0:T(8,128)S(1)} %pad_maximum_fusion.6), channel_id=1, source_target_pairs={{0,8},{8,0},{16,24},{24,16},{1,9},{9,1},{17,25},{25,17},{2,10},{10... | collective-permute-start | bytes 393224 | tf_op jit(solution)/shard_map/ppermute | solution.py:256
  45.8 0.9 collective-permute-done.12
  46.9 1.2 collective-permute-start.14
  48.1 3.6 %collective-permute-done.14 = bf16[10,32,128]{2,1,0:T(8,128)(2,1)S(1)} collective-permute-done((bf16[10,32,128]{2,1,0:T(8,128)(2,1)S(1)}, bf16[10,32,128]{2,1,0:T(8,128)(2,1)S(1)}, u32[]{:S(2)}, u32[]{:S(2)}) %collective-permute-start.14) | collective-permute-done | bytes 81952 | tf_op jit(solution)/shard_map/ppermute | solution.py:253
  52.3 1.1 collective-permute-done.15
  53.4 1.2 collective-permute-start.16
  54.6 2.7 %collective-permute-start.17 = (bf16[12,32,128]{2,1,0:T(8,128)(2,1)S(1)}, bf16[12,32,128]{2,1,0:T(8,128)(2,1)S(1)}, u32[]{:S(2)}, u32[]{:S(2)}) collective-permute-start(bf16[12,32,128]{2,1,0:T(8,128)(2,1)S(1)} %pad_maximum_fusion.10), channel_id=1, source_target_pairs={{0,6},{1,7},{2,4},{3,5},{4,2},{5,3},{6,0},{7,1},{8,15},{9,14},{10,... | collective-permute-start | bytes 294920 | tf_op jit(solution)/shard_map/ppermute | solution.py:253
  57.3 1.8 %collective-permute-start.19 = (bf16[12,32,128]{2,1,0:T(8,128)(2,1)S(1)}, bf16[12,32,128]{2,1,0:T(8,128)(2,1)S(1)}, u32[]{:S(2)}, u32[]{:S(2)}) collective-permute-start(bf16[12,32,128]{2,1,0:T(8,128)(2,1)S(1)} %pad_maximum_fusion.10), channel_id=1, source_target_pairs={{0,2},{1,3},{2,0},{3,1},{4,6},{5,7},{6,4},{7,5},{8,11},{9,10},{10,... | collective-permute-start | bytes 294920 | tf_op jit(solution)/shard_map/ppermute | solution.py:253
  59.4 1.0 collective-permute-done.20
  60.4 4.2 %shard_map.88 = bf16[54,32,128]{2,1,0:T(8,128)(2,1)S(1)} custom-call(s32[240]{0:T(256)S(1)} %get-tuple-element.68.loads, s32[48]{0:T(128)S(1)} %fusion.96.place, bf16[25,32,128]{2,1,0:T(8,128)(2,1)S(1)} %constant_dynamic-update-slice_fusion.49.field, bf16[48,640,128]{2,1,0:T(8,128)(2,1)} %get-tuple-element.43.source), custom_call_target="tpu_custom_call" | custom-call | flops 2013265920 | bytes 7864320 | tf_op jit(solution)/shard_map/pallas_call | solution.py:172
  64.7 1.0 collective-permute-done.18
  66.0 1.3 collective-permute-done.21
  67.9 1.3 %collective-permute-done.22 = bf16[27,32,128]{2,1,0:T(8,128)(2,1)S(1)} collective-permute-done((bf16[27,32,128]{2,1,0:T(8,128)(2,1)S(1)}, bf16[27,32,128]{2,1,0:T(8,128)(2,1)S(1)}, u32[]{:S(2)}, u32[]{:S(2)}) %collective-permute-start.22) | collective-permute-done | bytes 221216 | tf_op jit(solution)/shard_map/ppermute | solution.py:256
  69.6 2.8 %collective-permute-start.24 = (bf16[15,32,128]{2,1,0:T(8,128)(2,1)S(1)}, bf16[15,32,128]{2,1,0:T(8,128)(2,1)S(1)}, u32[]{:S(2)}, u32[]{:S(2)}) collective-permute-start(bf16[15,32,128]{2,1,0:T(8,128)(2,1)S(1)} %get-tuple-element.210), channel_id=1, source_target_pairs={{0,6},{1,7},{2,4},{3,5},{4,2},{5,3},{6,0},{7,1},{8,15},{9,14},{10,... | collective-permute-start | bytes 368648 | tf_op jit(solution)/shard_map/ppermute | solution.py:253
  72.4 1.7 %collective-permute-start.26 = (bf16[15,32,128]{2,1,0:T(8,128)(2,1)S(1)}, bf16[15,32,128]{2,1,0:T(8,128)(2,1)S(1)}, u32[]{:S(2)}, u32[]{:S(2)}) collective-permute-start(bf16[15,32,128]{2,1,0:T(8,128)(2,1)S(1)} %get-tuple-element.212), channel_id=1, source_target_pairs={{0,2},{1,3},{2,0},{3,1},{4,6},{5,7},{6,4},{7,5},{8,11},{9,10},{10,... | collective-permute-start | bytes 368648 | tf_op jit(solution)/shard_map/ppermute | solution.py:253
  74.1 0.8 collective-permute-start.23
  74.9 5.5 %shard_map.89 = f32[24,32,128]{2,1,0:T(8,128)S(1)} custom-call(s32[240]{0:T(256)S(1)} %get-tuple-element.71.slots, s32[240]{0:T(256)S(1)} %get-tuple-element.70.loads, s32[24]{0:T(128)S(1)} %fusion.97.place, bf16[55,32,128]{2,1,0:T(8,128)(2,1)S(1)} %constant_dynamic-update-slice_fusion.61.field, bf16[240,128,128]{2,1,0:T(8,128)(2,1)} %bitcast.293), custom_call_target="tpu_custom_call" | custom-call | flops 2013265920 | bytes 7864320 | tf_op jit(solution)/shard_map/pallas_call | solution.py:134
  80.4 2.7 %collective-permute-start.28 = (f32[12,32,128]{2,1,0:T(8,128)S(1)}, f32[12,32,128]{2,1,0:T(8,128)S(1)}, u32[]{:S(2)}, u32[]{:S(2)}) collective-permute-start(f32[12,32,128]{2,1,0:T(8,128)S(1)} %bitcast.299), channel_id=1, source_target_pairs={{0,8},{8,0},{16,24},{24,16},{1,9},{9,1},{17,25},{25,17},{2,10},{10... | collective-permute-start | bytes 589832 | tf_op jit(solution)/shard_map/ppermute | solution.py:256
  83.1 0.7 collective-permute-done.25
  83.9 0.4 collective-permute-start.27
  84.4 0.9 collective-permute-done.27
  85.5 1.6 %collective-permute-start.29 = (bf16[9,32,128]{2,1,0:T(8,128)(2,1)S(1)}, bf16[9,32,128]{2,1,0:T(8,128)(2,1)S(1)}, u32[]{:S(2)}, u32[]{:S(2)}) collective-permute-start(bf16[9,32,128]{2,1,0:T(8,128)(2,1)S(1)} %pad_maximum_fusion.12), channel_id=1, source_target_pairs={{0,16},{1,17},{2,18},{3,19},{4,20},{5,21},{6,22},{7,23},{8,24},{9,... | collective-permute-start | bytes 221192 | tf_op jit(solution)/shard_map/ppermute | solution.py:253
  87.1 3.0 %collective-permute-done.29 = bf16[9,32,128]{2,1,0:T(8,128)(2,1)S(1)} collective-permute-done((bf16[9,32,128]{2,1,0:T(8,128)(2,1)S(1)}, bf16[9,32,128]{2,1,0:T(8,128)(2,1)S(1)}, u32[]{:S(2)}, u32[]{:S(2)}) %collective-permute-start.29) | collective-permute-done | bytes 73760 | tf_op jit(solution)/shard_map/ppermute | solution.py:253
  90.7 1.1 collective-permute-done.30
  91.7 1.5 %collective-permute-start.31 = (bf16[12,32,128]{2,1,0:T(8,128)(2,1)S(1)}, bf16[12,32,128]{2,1,0:T(8,128)(2,1)S(1)}, u32[]{:S(2)}, u32[]{:S(2)}) collective-permute-start(bf16[12,32,128]{2,1,0:T(8,128)(2,1)S(1)} %pad_maximum_fusion.11), channel_id=1, source_target_pairs={{0,16},{1,17},{2,18},{3,19},{4,20},{5,21},{6,22},{7,23},{8,9},{9,8... | collective-permute-start | bytes 294920 | tf_op jit(solution)/shard_map/ppermute | solution.py:253
  93.2 2.1 %collective-permute-start.32 = (bf16[12,32,128]{2,1,0:T(8,128)(2,1)S(1)}, bf16[12,32,128]{2,1,0:T(8,128)(2,1)S(1)}, u32[]{:S(2)}, u32[]{:S(2)}) collective-permute-start(bf16[12,32,128]{2,1,0:T(8,128)(2,1)S(1)} %pad_maximum_fusion.11), channel_id=1, source_target_pairs={{0,6},{1,7},{2,4},{3,5},{4,2},{5,3},{6,0},{7,1},{8,15},{9,14},{10,... | collective-permute-start | bytes 294920 | tf_op jit(solution)/shard_map/ppermute | solution.py:253
  95.3 2.4 %collective-permute-start.34 = (bf16[12,32,128]{2,1,0:T(8,128)(2,1)S(1)}, bf16[12,32,128]{2,1,0:T(8,128)(2,1)S(1)}, u32[]{:S(2)}, u32[]{:S(2)}) collective-permute-start(bf16[12,32,128]{2,1,0:T(8,128)(2,1)S(1)} %pad_maximum_fusion.11), channel_id=1, source_target_pairs={{0,2},{1,3},{2,0},{3,1},{4,6},{5,7},{6,4},{7,5},{8,11},{9,10},{10,... | collective-permute-start | bytes 294920 | tf_op jit(solution)/shard_map/ppermute | solution.py:253
  97.7 1.3 collective-permute-done.35
  99.1 4.2 %shard_map.90 = bf16[54,32,128]{2,1,0:T(8,128)(2,1)S(1)} custom-call(s32[240]{0:T(256)S(1)} %get-tuple-element.68.loads, s32[48]{0:T(128)S(1)} %fusion.96.place, bf16[25,32,128]{2,1,0:T(8,128)(2,1)S(1)} %constant_dynamic-update-slice_fusion.89.field, bf16[48,640,128]{2,1,0:T(8,128)(2,1)} %get-tuple-element.43.source), custom_call_target="tpu_custom_call" | custom-call | flops 2013265920 | bytes 7864320 | tf_op jit(solution)/shard_map/pallas_call | solution.py:172
  103.3 0.7 collective-permute-done.33
  104.4 1.1 collective-permute-done.36
  106.3 1.2 collective-permute-done.37
  107.9 2.0 %collective-permute-start.39 = (bf16[15,32,128]{2,1,0:T(8,128)(2,1)S(1)}, bf16[15,32,128]{2,1,0:T(8,128)(2,1)S(1)}, u32[]{:S(2)}, u32[]{:S(2)}) collective-permute-start(bf16[15,32,128]{2,1,0:T(8,128)(2,1)S(1)} %get-tuple-element.201), channel_id=1, source_target_pairs={{0,6},{1,7},{2,4},{3,5},{4,2},{5,3},{6,0},{7,1},{8,15},{9,14},{10,... | collective-permute-start | bytes 368648 | tf_op jit(solution)/shard_map/ppermute | solution.py:253
  109.9 2.4 %collective-permute-start.41 = (bf16[15,32,128]{2,1,0:T(8,128)(2,1)S(1)}, bf16[15,32,128]{2,1,0:T(8,128)(2,1)S(1)}, u32[]{:S(2)}, u32[]{:S(2)}) collective-permute-start(bf16[15,32,128]{2,1,0:T(8,128)(2,1)S(1)} %get-tuple-element.203), channel_id=1, source_target_pairs={{0,2},{1,3},{2,0},{3,1},{4,6},{5,7},{6,4},{7,5},{8,11},{9,10},{10,... | collective-permute-start | bytes 368648 | tf_op jit(solution)/shard_map/ppermute | solution.py:253
  112.3 0.7 collective-permute-start.38
  113.0 5.5 %shard_map.91 = f32[24,32,128]{2,1,0:T(8,128)S(1)} custom-call(s32[240]{0:T(256)S(1)} %get-tuple-element.71.slots, s32[240]{0:T(256)S(1)} %get-tuple-element.70.loads, s32[24]{0:T(128)S(1)} %fusion.97.place, bf16[55,32,128]{2,1,0:T(8,128)(2,1)S(1)} %constant_dynamic-update-slice_fusion.101.field, bf16[240,128,128]{2,1,0:T(8,128)(2,1)} %bitcast.294), custom_call_target="tpu_custom_call" | custom-call | flops 2013265920 | bytes 7864320 | tf_op jit(solution)/shard_map/pallas_call | solution.py:134
  118.6 2.8 %collective-permute-start.43 = (f32[12,32,128]{2,1,0:T(8,128)S(1)}, f32[12,32,128]{2,1,0:T(8,128)S(1)}, u32[]{:S(2)}, u32[]{:S(2)}) collective-permute-start(f32[12,32,128]{2,1,0:T(8,128)S(1)} %bitcast.300), channel_id=1, source_target_pairs={{0,8},{8,0},{16,24},{24,16},{1,9},{9,1},{17,25},{25,17},{2,10},{10... | collective-permute-start | bytes 589832 | tf_op jit(solution)/shard_map/ppermute | solution.py:256
  121.6 0.8 collective-permute-done.43
  122.4 0.4 collective-permute-done.42
  123.0 1.5 %collective-permute-start.44 = (bf16[9,32,128]{2,1,0:T(8,128)(2,1)S(1)}, bf16[9,32,128]{2,1,0:T(8,128)(2,1)S(1)}, u32[]{:S(2)}, u32[]{:S(2)}) collective-permute-start(bf16[9,32,128]{2,1,0:T(8,128)(2,1)S(1)} %pad_maximum_fusion.13), channel_id=1, source_target_pairs={{0,16},{1,17},{2,18},{3,19},{4,20},{5,21},{6,22},{7,23},{8,24},{9,... | collective-permute-start | bytes 221192 | tf_op jit(solution)/shard_map/ppermute | solution.py:253
  124.5 2.9 %collective-permute-done.44 = bf16[9,32,128]{2,1,0:T(8,128)(2,1)S(1)} collective-permute-done((bf16[9,32,128]{2,1,0:T(8,128)(2,1)S(1)}, bf16[9,32,128]{2,1,0:T(8,128)(2,1)S(1)}, u32[]{:S(2)}, u32[]{:S(2)}) %collective-permute-start.44) | collective-permute-done | bytes 73760 | tf_op jit(solution)/shard_map/ppermute | solution.py:253
  127.8 0.6 copy.59
  128.5 0.6 copy.60
  (235 shorter events, 9.5 us)
Async XLA Ops:
  0.6 0.9 copy-start
  1.5 2.2 %collective-permute-start = (bf16[6,32,128]{2,1,0:T(8,128)(2,1)S(1)}, bf16[6,32,128]{2,1,0:T(8,128)(2,1)S(1)}, u32[]{:S(2)}, u32[]{:S(2)}) collective-permute-start(bf16[6,32,128]{2,1,0:T(8,128)(2,1)S(1)} %get-tuple-element.106), channel_id=1, source_target_pairs={{0,8},{8,0},{16,24},{24,16},{1,9},{9,1},{17,25},{25,17},{2,10},{10... | collective-permute-start | bytes 147464 | tf_op jit(solution)/shard_map/ppermute | solution.py:256
  3.8 10.3 %collective-permute-start.1 = (bf16[12,32,128]{2,1,0:T(8,128)(2,1)S(1)}, bf16[12,32,128]{2,1,0:T(8,128)(2,1)S(1)}, u32[]{:S(2)}, u32[]{:S(2)}) collective-permute-start(bf16[12,32,128]{2,1,0:T(8,128)(2,1)S(1)} %pad_maximum_fusion.9), channel_id=1, source_target_pairs={{0,16},{1,17},{2,18},{3,19},{4,20},{5,21},{6,22},{7,23},{8,9},{9,8... | collective-permute-start | bytes 294920 | tf_op jit(solution)/shard_map/ppermute | solution.py:253
  6.4 17.6 %collective-permute-start.2 = (bf16[12,32,128]{2,1,0:T(8,128)(2,1)S(1)}, bf16[12,32,128]{2,1,0:T(8,128)(2,1)S(1)}, u32[]{:S(2)}, u32[]{:S(2)}) collective-permute-start(bf16[12,32,128]{2,1,0:T(8,128)(2,1)S(1)} %pad_maximum_fusion.9), channel_id=1, source_target_pairs={{0,6},{1,7},{2,4},{3,5},{4,2},{5,3},{6,0},{7,1},{8,15},{9,14},{10,... | collective-permute-start | bytes 294920 | tf_op jit(solution)/shard_map/ppermute | solution.py:253
  10.0 14.0 %collective-permute-start.3 = (bf16[12,32,128]{2,1,0:T(8,128)(2,1)S(1)}, bf16[12,32,128]{2,1,0:T(8,128)(2,1)S(1)}, u32[]{:S(2)}, u32[]{:S(2)}) collective-permute-start(bf16[12,32,128]{2,1,0:T(8,128)(2,1)S(1)} %pad_maximum_fusion.9), channel_id=1, source_target_pairs={{0,4},{1,5},{2,6},{3,7},{4,0},{5,1},{6,2},{7,3},{8,13},{9,12},{10,... | collective-permute-start | bytes 294920 | tf_op jit(solution)/shard_map/ppermute | solution.py:253
  10.0 14.0 %collective-permute-start.4 = (bf16[12,32,128]{2,1,0:T(8,128)(2,1)S(1)}, bf16[12,32,128]{2,1,0:T(8,128)(2,1)S(1)}, u32[]{:S(2)}, u32[]{:S(2)}) collective-permute-start(bf16[12,32,128]{2,1,0:T(8,128)(2,1)S(1)} %pad_maximum_fusion.9), channel_id=1, source_target_pairs={{0,2},{1,3},{2,0},{3,1},{4,6},{5,7},{6,4},{7,5},{8,11},{9,10},{10,... | collective-permute-start | bytes 294920 | tf_op jit(solution)/shard_map/ppermute | solution.py:253
  14.1 1.4 %collective-permute-start.5 = (bf16[12,32,128]{2,1,0:T(8,128)(2,1)S(1)}, bf16[12,32,128]{2,1,0:T(8,128)(2,1)S(1)}, u32[]{:S(2)}, u32[]{:S(2)}) collective-permute-start(bf16[12,32,128]{2,1,0:T(8,128)(2,1)S(1)} %collective-permute-done.1), channel_id=1, source_target_pairs={{0,8},{8,0},{16,24},{24,16},{1,9},{9,1},{17,25},{25,17},{2,10},{10... | collective-permute-start | bytes 294920 | tf_op jit(solution)/shard_map/ppermute | solution.py:256
  24.3 1.4 %collective-permute-start.6 = (bf16[18,32,128]{2,1,0:T(8,128)(2,1)S(1)}, bf16[18,32,128]{2,1,0:T(8,128)(2,1)S(1)}, u32[]{:S(2)}, u32[]{:S(2)}) collective-permute-start(bf16[18,32,128]{2,1,0:T(8,128)(2,1)S(1)} %pad_maximum_fusion.3), channel_id=1, source_target_pairs={{0,8},{8,0},{16,24},{24,16},{1,9},{9,1},{17,25},{25,17},{2,10},{10... | collective-permute-start | bytes 442376 | tf_op jit(solution)/shard_map/ppermute | solution.py:256
  26.4 1.6 %collective-permute-start.7 = (bf16[30,32,128]{2,1,0:T(8,128)(2,1)S(1)}, bf16[30,32,128]{2,1,0:T(8,128)(2,1)S(1)}, u32[]{:S(2)}, u32[]{:S(2)}) collective-permute-start(bf16[30,32,128]{2,1,0:T(8,128)(2,1)S(1)} %constant_dynamic-update-slice_fusion.7), channel_id=1, source_target_pairs={{0,8},{8,0},{16,24},{24,16},{1,9},{9,1},{17,25},{25,17},{2,10},{10... | collective-permute-start | bytes 737288 | tf_op jit(solution)/shard_map/ppermute | solution.py:256
  28.5 13.9 %collective-permute-start.8 = (bf16[16,32,128]{2,1,0:T(8,128)(2,1)S(1)}, bf16[16,32,128]{2,1,0:T(8,128)(2,1)S(1)}, u32[]{:S(2)}, u32[]{:S(2)}) collective-permute-start(bf16[16,32,128]{2,1,0:T(8,128)(2,1)S(1)} %constant_dynamic-update-slice_fusion.20), channel_id=1, source_target_pairs={{8,9},{9,8},{10,11},{11,10},{12,13},{13,12},{14,15},{15,14},{24,25... | collective-permute-start | bytes 393224 | tf_op jit(solution)/shard_map/ppermute | solution.py:253
  29.3 13.1 %collective-permute-start.9 = (bf16[16,32,128]{2,1,0:T(8,128)(2,1)S(1)}, bf16[16,32,128]{2,1,0:T(8,128)(2,1)S(1)}, u32[]{:S(2)}, u32[]{:S(2)}) collective-permute-start(bf16[16,32,128]{2,1,0:T(8,128)(2,1)S(1)} %constant_dynamic-update-slice_fusion.26), channel_id=1, source_target_pairs={{0,6},{1,7},{2,4},{3,5},{4,2},{5,3},{6,0},{7,1},{8,15},{9,14},{10,... | collective-permute-start | bytes 393224 | tf_op jit(solution)/shard_map/ppermute | solution.py:253
  33.0 10.8 %collective-permute-start.10 = (bf16[16,32,128]{2,1,0:T(8,128)(2,1)S(1)}, bf16[16,32,128]{2,1,0:T(8,128)(2,1)S(1)}, u32[]{:S(2)}, u32[]{:S(2)}) collective-permute-start(bf16[16,32,128]{2,1,0:T(8,128)(2,1)S(1)} %constant_dynamic-update-slice_fusion.32), channel_id=1, source_target_pairs={{0,4},{1,5},{2,6},{3,7},{4,0},{5,1},{6,2},{7,3},{8,13},{9,12},{10,... | collective-permute-start | bytes 393224 | tf_op jit(solution)/shard_map/ppermute | solution.py:253
  33.2 10.6 %collective-permute-start.11 = (bf16[16,32,128]{2,1,0:T(8,128)(2,1)S(1)}, bf16[16,32,128]{2,1,0:T(8,128)(2,1)S(1)}, u32[]{:S(2)}, u32[]{:S(2)}) collective-permute-start(bf16[16,32,128]{2,1,0:T(8,128)(2,1)S(1)} %constant_dynamic-update-slice_fusion.38), channel_id=1, source_target_pairs={{0,2},{1,3},{2,0},{3,1},{4,6},{5,7},{6,4},{7,5},{8,11},{9,10},{10,... | collective-permute-start | bytes 393224 | tf_op jit(solution)/shard_map/ppermute | solution.py:253
  39.5 6.3 %collective-permute-start.13 = (f32[12,32,128]{2,1,0:T(8,128)S(1)}, f32[12,32,128]{2,1,0:T(8,128)S(1)}, u32[]{:S(2)}, u32[]{:S(2)}) collective-permute-start(f32[12,32,128]{2,1,0:T(8,128)S(1)} %bitcast.298), channel_id=1, source_target_pairs={{0,8},{8,0},{16,24},{24,16},{1,9},{9,1},{17,25},{25,17},{2,10},{10... | collective-permute-start | bytes 589832 | tf_op jit(solution)/shard_map/ppermute | solution.py:256
  44.0 2.8 %collective-permute-start.12 = (f32[8,32,128]{2,1,0:T(8,128)S(1)}, f32[8,32,128]{2,1,0:T(8,128)S(1)}, u32[]{:S(2)}, u32[]{:S(2)}) collective-permute-start(f32[8,32,128]{2,1,0:T(8,128)S(1)} %pad_maximum_fusion.6), channel_id=1, source_target_pairs={{0,8},{8,0},{16,24},{24,16},{1,9},{9,1},{17,25},{25,17},{2,10},{10... | collective-permute-start | bytes 393224 | tf_op jit(solution)/shard_map/ppermute | solution.py:256
  46.9 4.8 %collective-permute-start.14 = (bf16[10,32,128]{2,1,0:T(8,128)(2,1)S(1)}, bf16[10,32,128]{2,1,0:T(8,128)(2,1)S(1)}, u32[]{:S(2)}, u32[]{:S(2)}) collective-permute-start(bf16[10,32,128]{2,1,0:T(8,128)(2,1)S(1)} %constant_dynamic-update-slice_fusion.44), channel_id=1, source_target_pairs={{0,16},{1,17},{2,18},{3,19},{4,20},{5,21},{6,22},{7,23},{8,24},{9,... | collective-permute-start | bytes 245768 | tf_op jit(solution)/shard_map/ppermute | solution.py:253
  52.1 1.3 %collective-permute-start.15 = (bf16[6,32,128]{2,1,0:T(8,128)(2,1)S(1)}, bf16[6,32,128]{2,1,0:T(8,128)(2,1)S(1)}, u32[]{:S(2)}, u32[]{:S(2)}) collective-permute-start(bf16[6,32,128]{2,1,0:T(8,128)(2,1)S(1)} %get-tuple-element.94), channel_id=1, source_target_pairs={{0,8},{8,0},{16,24},{24,16},{1,9},{9,1},{17,25},{25,17},{2,10},{10... | collective-permute-start | bytes 147464 | tf_op jit(solution)/shard_map/ppermute | solution.py:256
  53.4 5.6 %collective-permute-start.16 = (bf16[12,32,128]{2,1,0:T(8,128)(2,1)S(1)}, bf16[12,32,128]{2,1,0:T(8,128)(2,1)S(1)}, u32[]{:S(2)}, u32[]{:S(2)}) collective-permute-start(bf16[12,32,128]{2,1,0:T(8,128)(2,1)S(1)} %pad_maximum_fusion.10), channel_id=1, source_target_pairs={{0,16},{1,17},{2,18},{3,19},{4,20},{5,21},{6,22},{7,23},{8,9},{9,8... | collective-permute-start | bytes 294920 | tf_op jit(solution)/shard_map/ppermute | solution.py:253
  54.6 10.1 %collective-permute-start.17 = (bf16[12,32,128]{2,1,0:T(8,128)(2,1)S(1)}, bf16[12,32,128]{2,1,0:T(8,128)(2,1)S(1)}, u32[]{:S(2)}, u32[]{:S(2)}) collective-permute-start(bf16[12,32,128]{2,1,0:T(8,128)(2,1)S(1)} %pad_maximum_fusion.10), channel_id=1, source_target_pairs={{0,6},{1,7},{2,4},{3,5},{4,2},{5,3},{6,0},{7,1},{8,15},{9,14},{10,... | collective-permute-start | bytes 294920 | tf_op jit(solution)/shard_map/ppermute | solution.py:253
  57.3 8.4 %collective-permute-start.18 = (bf16[12,32,128]{2,1,0:T(8,128)(2,1)S(1)}, bf16[12,32,128]{2,1,0:T(8,128)(2,1)S(1)}, u32[]{:S(2)}, u32[]{:S(2)}) collective-permute-start(bf16[12,32,128]{2,1,0:T(8,128)(2,1)S(1)} %pad_maximum_fusion.10), channel_id=1, source_target_pairs={{0,4},{1,5},{2,6},{3,7},{4,0},{5,1},{6,2},{7,3},{8,13},{9,12},{10,... | collective-permute-start | bytes 294920 | tf_op jit(solution)/shard_map/ppermute | solution.py:253
  57.3 8.4 %collective-permute-start.19 = (bf16[12,32,128]{2,1,0:T(8,128)(2,1)S(1)}, bf16[12,32,128]{2,1,0:T(8,128)(2,1)S(1)}, u32[]{:S(2)}, u32[]{:S(2)}) collective-permute-start(bf16[12,32,128]{2,1,0:T(8,128)(2,1)S(1)} %pad_maximum_fusion.10), channel_id=1, source_target_pairs={{0,2},{1,3},{2,0},{3,1},{4,6},{5,7},{6,4},{7,5},{8,11},{9,10},{10,... | collective-permute-start | bytes 294920 | tf_op jit(solution)/shard_map/ppermute | solution.py:253
  59.0 1.3 %collective-permute-start.20 = (bf16[12,32,128]{2,1,0:T(8,128)(2,1)S(1)}, bf16[12,32,128]{2,1,0:T(8,128)(2,1)S(1)}, u32[]{:S(2)}, u32[]{:S(2)}) collective-permute-start(bf16[12,32,128]{2,1,0:T(8,128)(2,1)S(1)} %collective-permute-done.16), channel_id=1, source_target_pairs={{0,8},{8,0},{16,24},{24,16},{1,9},{9,1},{17,25},{25,17},{2,10},{10... | collective-permute-start | bytes 294920 | tf_op jit(solution)/shard_map/ppermute | solution.py:256
  65.8 1.4 %collective-permute-start.21 = (bf16[18,32,128]{2,1,0:T(8,128)(2,1)S(1)}, bf16[18,32,128]{2,1,0:T(8,128)(2,1)S(1)}, u32[]{:S(2)}, u32[]{:S(2)}) collective-permute-start(bf16[18,32,128]{2,1,0:T(8,128)(2,1)S(1)} %pad_maximum_fusion.4), channel_id=1, source_target_pairs={{0,8},{8,0},{16,24},{24,16},{1,9},{9,1},{17,25},{25,17},{2,10},{10... | collective-permute-start | bytes 442376 | tf_op jit(solution)/shard_map/ppermute | solution.py:256
  67.7 1.5 %collective-permute-start.22 = (bf16[27,32,128]{2,1,0:T(8,128)(2,1)S(1)}, bf16[27,32,128]{2,1,0:T(8,128)(2,1)S(1)}, u32[]{:S(2)}, u32[]{:S(2)}) collective-permute-start(bf16[27,32,128]{2,1,0:T(8,128)(2,1)S(1)} %pad_maximum_fusion.1), channel_id=1, source_target_pairs={{0,8},{8,0},{16,24},{24,16},{1,9},{9,1},{17,25},{25,17},{2,10},{10... | collective-permute-start | bytes 663560 | tf_op jit(solution)/shard_map/ppermute | solution.py:256
  69.6 13.5 %collective-permute-start.24 = (bf16[15,32,128]{2,1,0:T(8,128)(2,1)S(1)}, bf16[15,32,128]{2,1,0:T(8,128)(2,1)S(1)}, u32[]{:S(2)}, u32[]{:S(2)}) collective-permute-start(bf16[15,32,128]{2,1,0:T(8,128)(2,1)S(1)} %get-tuple-element.210), channel_id=1, source_target_pairs={{0,6},{1,7},{2,4},{3,5},{4,2},{5,3},{6,0},{7,1},{8,15},{9,14},{10,... | collective-permute-start | bytes 368648 | tf_op jit(solution)/shard_map/ppermute | solution.py:253
  72.4 11.4 %collective-permute-start.25 = (bf16[15,32,128]{2,1,0:T(8,128)(2,1)S(1)}, bf16[15,32,128]{2,1,0:T(8,128)(2,1)S(1)}, u32[]{:S(2)}, u32[]{:S(2)}) collective-permute-start(bf16[15,32,128]{2,1,0:T(8,128)(2,1)S(1)} %get-tuple-element.211), channel_id=1, source_target_pairs={{0,4},{1,5},{2,6},{3,7},{4,0},{5,1},{6,2},{7,3},{8,13},{9,12},{10,... | collective-permute-start | bytes 368648 | tf_op jit(solution)/shard_map/ppermute | solution.py:253
  72.4 11.4 %collective-permute-start.26 = (bf16[15,32,128]{2,1,0:T(8,128)(2,1)S(1)}, bf16[15,32,128]{2,1,0:T(8,128)(2,1)S(1)}, u32[]{:S(2)}, u32[]{:S(2)}) collective-permute-start(bf16[15,32,128]{2,1,0:T(8,128)(2,1)S(1)} %get-tuple-element.212), channel_id=1, source_target_pairs={{0,2},{1,3},{2,0},{3,1},{4,6},{5,7},{6,4},{7,5},{8,11},{9,10},{10,... | collective-permute-start | bytes 368648 | tf_op jit(solution)/shard_map/ppermute | solution.py:253
  74.1 9.8 %collective-permute-start.23 = (bf16[15,32,128]{2,1,0:T(8,128)(2,1)S(1)}, bf16[15,32,128]{2,1,0:T(8,128)(2,1)S(1)}, u32[]{:S(2)}, u32[]{:S(2)}) collective-permute-start(bf16[15,32,128]{2,1,0:T(8,128)(2,1)S(1)} %get-tuple-element.87), channel_id=1, source_target_pairs={{8,9},{9,8},{10,11},{11,10},{12,13},{13,12},{14,15},{15,14},{24,25... | collective-permute-start | bytes 368648 | tf_op jit(solution)/shard_map/ppermute | solution.py:253
  80.4 3.9 %collective-permute-start.28 = (f32[12,32,128]{2,1,0:T(8,128)S(1)}, f32[12,32,128]{2,1,0:T(8,128)S(1)}, u32[]{:S(2)}, u32[]{:S(2)}) collective-permute-start(f32[12,32,128]{2,1,0:T(8,128)S(1)} %bitcast.299), channel_id=1, source_target_pairs={{0,8},{8,0},{16,24},{24,16},{1,9},{9,1},{17,25},{25,17},{2,10},{10... | collective-permute-start | bytes 589832 | tf_op jit(solution)/shard_map/ppermute | solution.py:256
  83.9 1.4 %collective-permute-start.27 = (f32[7,32,128]{2,1,0:T(8,128)S(1)}, f32[7,32,128]{2,1,0:T(8,128)S(1)}, u32[]{:S(2)}, u32[]{:S(2)}) collective-permute-start(f32[7,32,128]{2,1,0:T(8,128)S(1)} %pad_maximum_fusion.7), channel_id=1, source_target_pairs={{0,8},{8,0},{16,24},{24,16},{1,9},{9,1},{17,25},{25,17},{2,10},{10... | collective-permute-start | bytes 344072 | tf_op jit(solution)/shard_map/ppermute | solution.py:256
  85.5 4.6 %collective-permute-start.29 = (bf16[9,32,128]{2,1,0:T(8,128)(2,1)S(1)}, bf16[9,32,128]{2,1,0:T(8,128)(2,1)S(1)}, u32[]{:S(2)}, u32[]{:S(2)}) collective-permute-start(bf16[9,32,128]{2,1,0:T(8,128)(2,1)S(1)} %pad_maximum_fusion.12), channel_id=1, source_target_pairs={{0,16},{1,17},{2,18},{3,19},{4,20},{5,21},{6,22},{7,23},{8,24},{9,... | collective-permute-start | bytes 221192 | tf_op jit(solution)/shard_map/ppermute | solution.py:253
  90.4 1.3 %collective-permute-start.30 = (bf16[6,32,128]{2,1,0:T(8,128)(2,1)S(1)}, bf16[6,32,128]{2,1,0:T(8,128)(2,1)S(1)}, u32[]{:S(2)}, u32[]{:S(2)}) collective-permute-start(bf16[6,32,128]{2,1,0:T(8,128)(2,1)S(1)} %get-tuple-element.81), channel_id=1, source_target_pairs={{0,8},{8,0},{16,24},{24,16},{1,9},{9,1},{17,25},{25,17},{2,10},{10... | collective-permute-start | bytes 147464 | tf_op jit(solution)/shard_map/ppermute | solution.py:256
  91.7 5.9 %collective-permute-start.31 = (bf16[12,32,128]{2,1,0:T(8,128)(2,1)S(1)}, bf16[12,32,128]{2,1,0:T(8,128)(2,1)S(1)}, u32[]{:S(2)}, u32[]{:S(2)}) collective-permute-start(bf16[12,32,128]{2,1,0:T(8,128)(2,1)S(1)} %pad_maximum_fusion.11), channel_id=1, source_target_pairs={{0,16},{1,17},{2,18},{3,19},{4,20},{5,21},{6,22},{7,23},{8,9},{9,8... | collective-permute-start | bytes 294920 | tf_op jit(solution)/shard_map/ppermute | solution.py:253
  93.2 10.1 %collective-permute-start.32 = (bf16[12,32,128]{2,1,0:T(8,128)(2,1)S(1)}, bf16[12,32,128]{2,1,0:T(8,128)(2,1)S(1)}, u32[]{:S(2)}, u32[]{:S(2)}) collective-permute-start(bf16[12,32,128]{2,1,0:T(8,128)(2,1)S(1)} %pad_maximum_fusion.11), channel_id=1, source_target_pairs={{0,6},{1,7},{2,4},{3,5},{4,2},{5,3},{6,0},{7,1},{8,15},{9,14},{10,... | collective-permute-start | bytes 294920 | tf_op jit(solution)/shard_map/ppermute | solution.py:253
  95.3 8.6 %collective-permute-start.33 = (bf16[12,32,128]{2,1,0:T(8,128)(2,1)S(1)}, bf16[12,32,128]{2,1,0:T(8,128)(2,1)S(1)}, u32[]{:S(2)}, u32[]{:S(2)}) collective-permute-start(bf16[12,32,128]{2,1,0:T(8,128)(2,1)S(1)} %pad_maximum_fusion.11), channel_id=1, source_target_pairs={{0,4},{1,5},{2,6},{3,7},{4,0},{5,1},{6,2},{7,3},{8,13},{9,12},{10,... | collective-permute-start | bytes 294920 | tf_op jit(solution)/shard_map/ppermute | solution.py:253
  95.3 8.6 %collective-permute-start.34 = (bf16[12,32,128]{2,1,0:T(8,128)(2,1)S(1)}, bf16[12,32,128]{2,1,0:T(8,128)(2,1)S(1)}, u32[]{:S(2)}, u32[]{:S(2)}) collective-permute-start(bf16[12,32,128]{2,1,0:T(8,128)(2,1)S(1)} %pad_maximum_fusion.11), channel_id=1, source_target_pairs={{0,2},{1,3},{2,0},{3,1},{4,6},{5,7},{6,4},{7,5},{8,11},{9,10},{10,... | collective-permute-start | bytes 294920 | tf_op jit(solution)/shard_map/ppermute | solution.py:253
  97.7 1.3 %collective-permute-start.35 = (bf16[12,32,128]{2,1,0:T(8,128)(2,1)S(1)}, bf16[12,32,128]{2,1,0:T(8,128)(2,1)S(1)}, u32[]{:S(2)}, u32[]{:S(2)}) collective-permute-start(bf16[12,32,128]{2,1,0:T(8,128)(2,1)S(1)} %collective-permute-done.31), channel_id=1, source_target_pairs={{0,8},{8,0},{16,24},{24,16},{1,9},{9,1},{17,25},{25,17},{2,10},{10... | collective-permute-start | bytes 294920 | tf_op jit(solution)/shard_map/ppermute | solution.py:256
  104.1 1.4 %collective-permute-start.36 = (bf16[18,32,128]{2,1,0:T(8,128)(2,1)S(1)}, bf16[18,32,128]{2,1,0:T(8,128)(2,1)S(1)}, u32[]{:S(2)}, u32[]{:S(2)}) collective-permute-start(bf16[18,32,128]{2,1,0:T(8,128)(2,1)S(1)} %pad_maximum_fusion.5), channel_id=1, source_target_pairs={{0,8},{8,0},{16,24},{24,16},{1,9},{9,1},{17,25},{25,17},{2,10},{10... | collective-permute-start | bytes 442376 | tf_op jit(solution)/shard_map/ppermute | solution.py:256
  106.0 1.5 %collective-permute-start.37 = (bf16[27,32,128]{2,1,0:T(8,128)(2,1)S(1)}, bf16[27,32,128]{2,1,0:T(8,128)(2,1)S(1)}, u32[]{:S(2)}, u32[]{:S(2)}) collective-permute-start(bf16[27,32,128]{2,1,0:T(8,128)(2,1)S(1)} %pad_maximum_fusion.2), channel_id=1, source_target_pairs={{0,8},{8,0},{16,24},{24,16},{1,9},{9,1},{17,25},{25,17},{2,10},{10... | collective-permute-start | bytes 663560 | tf_op jit(solution)/shard_map/ppermute | solution.py:256
  107.9 13.4 %collective-permute-start.39 = (bf16[15,32,128]{2,1,0:T(8,128)(2,1)S(1)}, bf16[15,32,128]{2,1,0:T(8,128)(2,1)S(1)}, u32[]{:S(2)}, u32[]{:S(2)}) collective-permute-start(bf16[15,32,128]{2,1,0:T(8,128)(2,1)S(1)} %get-tuple-element.201), channel_id=1, source_target_pairs={{0,6},{1,7},{2,4},{3,5},{4,2},{5,3},{6,0},{7,1},{8,15},{9,14},{10,... | collective-permute-start | bytes 368648 | tf_op jit(solution)/shard_map/ppermute | solution.py:253
  109.9 11.4 %collective-permute-start.40 = (bf16[15,32,128]{2,1,0:T(8,128)(2,1)S(1)}, bf16[15,32,128]{2,1,0:T(8,128)(2,1)S(1)}, u32[]{:S(2)}, u32[]{:S(2)}) collective-permute-start(bf16[15,32,128]{2,1,0:T(8,128)(2,1)S(1)} %get-tuple-element.202), channel_id=1, source_target_pairs={{0,4},{1,5},{2,6},{3,7},{4,0},{5,1},{6,2},{7,3},{8,13},{9,12},{10,... | collective-permute-start | bytes 368648 | tf_op jit(solution)/shard_map/ppermute | solution.py:253
  109.9 11.4 %collective-permute-start.41 = (bf16[15,32,128]{2,1,0:T(8,128)(2,1)S(1)}, bf16[15,32,128]{2,1,0:T(8,128)(2,1)S(1)}, u32[]{:S(2)}, u32[]{:S(2)}) collective-permute-start(bf16[15,32,128]{2,1,0:T(8,128)(2,1)S(1)} %get-tuple-element.203), channel_id=1, source_target_pairs={{0,2},{1,3},{2,0},{3,1},{4,6},{5,7},{6,4},{7,5},{8,11},{9,10},{10,... | collective-permute-start | bytes 368648 | tf_op jit(solution)/shard_map/ppermute | solution.py:253
  112.3 9.0 %collective-permute-start.38 = (bf16[15,32,128]{2,1,0:T(8,128)(2,1)S(1)}, bf16[15,32,128]{2,1,0:T(8,128)(2,1)S(1)}, u32[]{:S(2)}, u32[]{:S(2)}) collective-permute-start(bf16[15,32,128]{2,1,0:T(8,128)(2,1)S(1)} %get-tuple-element.74), channel_id=1, source_target_pairs={{8,9},{9,8},{10,11},{11,10},{12,13},{13,12},{14,15},{15,14},{24,25... | collective-permute-start | bytes 368648 | tf_op jit(solution)/shard_map/ppermute | solution.py:253
  118.6 3.8 %collective-permute-start.43 = (f32[12,32,128]{2,1,0:T(8,128)S(1)}, f32[12,32,128]{2,1,0:T(8,128)S(1)}, u32[]{:S(2)}, u32[]{:S(2)}) collective-permute-start(f32[12,32,128]{2,1,0:T(8,128)S(1)} %bitcast.300), channel_id=1, source_target_pairs={{0,8},{8,0},{16,24},{24,16},{1,9},{9,1},{17,25},{25,17},{2,10},{10... | collective-permute-start | bytes 589832 | tf_op jit(solution)/shard_map/ppermute | solution.py:256
  121.5 1.4 %collective-permute-start.42 = (f32[7,32,128]{2,1,0:T(8,128)S(1)}, f32[7,32,128]{2,1,0:T(8,128)S(1)}, u32[]{:S(2)}, u32[]{:S(2)}) collective-permute-start(f32[7,32,128]{2,1,0:T(8,128)S(1)} %pad_maximum_fusion.8), channel_id=1, source_target_pairs={{0,8},{8,0},{16,24},{24,16},{1,9},{9,1},{17,25},{25,17},{2,10},{10... | collective-permute-start | bytes 344072 | tf_op jit(solution)/shard_map/ppermute | solution.py:256
  123.0 4.4 %collective-permute-start.44 = (bf16[9,32,128]{2,1,0:T(8,128)(2,1)S(1)}, bf16[9,32,128]{2,1,0:T(8,128)(2,1)S(1)}, u32[]{:S(2)}, u32[]{:S(2)}) collective-permute-start(bf16[9,32,128]{2,1,0:T(8,128)(2,1)S(1)} %pad_maximum_fusion.13), channel_id=1, source_target_pairs={{0,16},{1,17},{2,18},{3,19},{4,20},{5,21},{6,22},{7,23},{8,24},{9,... | collective-permute-start | bytes 221192 | tf_op jit(solution)/shard_map/ppermute | solution.py:253

commit v4 on v3

--- a/solution.py
+++ b/solution.py
@@ -31,6 +31,25 @@
     return next(n for n in range(wanted, 0, -1) if count % n == 0)
 
 
+def fields_kernel(*refs):
+    half = len(refs) // 2
+    for held, out in zip(refs[:half], refs[half:], strict=True):
+        count, rows, tile_size = held.shape
+        for i in range(count):
+            out[:, pl.ds(i * tile_size, tile_size)] = held[i]
+
+
+def to_fields(*held):
+    count, rows, tile_size = held[0].shape
+    return pl.pallas_call(
+        fields_kernel,
+        out_shape=[jax.ShapeDtypeStruct((rows, count * tile_size), h.dtype) for h in held],
+        in_specs=[IN_VMEM] * len(held),
+        out_specs=[IN_VMEM] * len(held),
+        compiler_params=pltpu.CompilerParams(vmem_limit_bytes=4 * 2**20),
+    )(*held)
+
+
 def in_steps(count, unroll, one):
     unroll = parts_of(count, unroll)
 
@@ -43,49 +62,62 @@
 
 
 def gathered(field, loads, base, per):
-    return jnp.concatenate([field[loads[base + j]] for j in range(per)], axis=1)
-
-
-def col_kernel(slots, loads, place, field, source, out, tiles, semaphores):
+    return jnp.concatenate([field[loads[0, base + j]] for j in range(per)], axis=1)
+
+
+def first_col_kernel(
+    per, slots, loads, place, field, source, out, col_blocks, tiles, blocks, semaphores,
+    back_semaphores,
+):
     copies = start_copies(source, tiles, semaphores)
+    back = start_copies(col_blocks, blocks, back_semaphores, to_held=False)
     count = place.shape[0]
-    per = slots.shape[0] // count
+    tile_size = tiles.shape[1]
     for copy in copies:
         copy.wait()
 
     def one(i):
         base = i * per
-        block = jnp.concatenate([tiles[slots[base + j]] for j in range(per)], axis=0)
+        for j in range(per):
+            blocks[i, pl.ds(j * tile_size, tile_size)] = tiles[slots[0, base + j]]
         held = gathered(field, loads, base, per)
-        out[place[i]] = jnp.dot(held, block, preferred_element_type=jnp.float32)
-
-    in_steps(count, 8, one)
+        out[place[i]] = jnp.dot(held, blocks[i], preferred_element_type=jnp.float32)
+
+    part = count // len(back)
+    for g, copy in enumerate(back):
+        in_steps(part, 4, lambda i, g=g: one(g * part + i))
+        copy.start()
+    for copy in back:
+        copy.wait()
 
 
 def first_row_kernel(
-    slots, loads, place, field, source, out, degree, col_degree, squares, row_blocks, tiles, blocks,
+    per, col_of, slots, loads, place, field, source, out, degree, col_degree, squares, row_blocks, tiles, blocks,
     semaphores, back_semaphores,
 ):
     copies = start_copies(source, tiles, semaphores)
     back = start_copies(row_blocks, blocks, back_semaphores, to_held=False)
     count = place.shape[0]
-    per = slots.shape[0] // count
     tile_size = tiles.shape[1]
     tasks = out.shape[1]
     out[...] = jnp.zeros_like(out)
     degree[...] = jnp.zeros_like(degree)
     squares[...] = jnp.zeros_like(squares)
     col_degree[...] = jnp.zeros_like(col_degree)
-    for copy in copies:
+
+    def add_columns(s):
+        addends = tiles[s].astype(jnp.float32).reshape(tile_size // 8, 8, tile_size)
+        col_degree[col_of[0, s]] += jnp.sum(addends, axis=0)
+
+    part = tiles.shape[0] // len(copies)
+    for g, copy in enumerate(copies):
         copy.wait()
+        in_steps(part, 10, lambda s, g=g: add_columns(g * part + s))
 
     def one(i):
         base = i * per
         for j in range(per):
-            tile = tiles[slots[base + j]]
-            blocks[i, pl.ds(j * tile_size, tile_size)] = tile.T
-            addends = tile.astype(jnp.float32).reshape(tile_size // 8, 8, tile_size)
-            col_degree[loads[base + j]] += jnp.sum(addends, axis=0)
+            blocks[i, pl.ds(j * tile_size, tile_size)] = tiles[slots[0, base + j]].T
         held = gathered(field, loads, base, per)
         total = jnp.dot(held, blocks[i], preferred_element_type=jnp.float32)
         out[place[i]] = total[:tasks].astype(out.dtype)
@@ -100,11 +132,11 @@
         copy.wait()
 
 
-def next_row_kernel(loads, place, field, source, out, blocks, semaphores):
+def next_kernel(per, loads, place, field, source, out, blocks, semaphores):
     copies = start_copies(source, blocks, semaphores)
     count = place.shape[0]
-    per = loads.shape[0] // count
-    out[...] = jnp.zeros_like(out)
+    if out.shape[0] > count:
+        out[...] = jnp.zeros_like(out)
 
     def one(i):
         held = gathered(field, loads, i * per, per)
@@ -129,25 +161,35 @@
     )
 
 
-def product(lists, field, tiles, out_tiles):
-    parts = parts_of(tiles.shape[0], 8)
-    return pl.pallas_call(
-        col_kernel,
-        out_shape=jax.ShapeDtypeStruct((out_tiles,) + field.shape[1:], jnp.float32),
-        in_specs=[IN_SMEM] * 3 + [IN_VMEM, IN_HBM],
-        out_specs=IN_VMEM,
-        scratch_shapes=[pltpu.VMEM(tiles.shape, tiles.dtype), pltpu.SemaphoreType.DMA((parts,))],
-        compiler_params=PARAMS,
-        cost_estimate=cost(field, tiles),
-    )(*lists, field, tiles)
-
-
-def first_product(lists, field, tiles, out_tiles, tasks):
+def first_col_product(lists, field, tiles, out_tiles):
     count = lists[2].shape[0]
     slots, tile_size = tiles.shape[:2]
     blocks = (count, slots // count * tile_size, tile_size)
     return pl.pallas_call(
-        first_row_kernel,
+        functools.partial(first_col_kernel, slots // count),
+        out_shape=(
+            jax.ShapeDtypeStruct((out_tiles,) + field.shape[1:], jnp.float32),
+            jax.ShapeDtypeStruct(blocks, tiles.dtype),
+        ),
+        in_specs=[IN_SMEM] * 3 + [IN_VMEM, IN_HBM],
+        out_specs=(IN_VMEM, IN_HBM),
+        scratch_shapes=[
+            pltpu.VMEM(tiles.shape, tiles.dtype),
+            pltpu.VMEM(blocks, tiles.dtype),
+            pltpu.SemaphoreType.DMA((parts_of(slots, 8),)),
+            pltpu.SemaphoreType.DMA((parts_of(count, 6),)),
+        ],
+        compiler_params=PARAMS,
+        cost_estimate=cost(field, tiles),
+    )(*lists, field, tiles)
+
+
+def first_row_product(col_of, lists, field, tiles, out_tiles, tasks):
+    count = lists[2].shape[0]
+    slots, tile_size = tiles.shape[:2]
+    blocks = (count, slots // count * tile_size, tile_size)
+    return pl.pallas_call(
+        functools.partial(first_row_kernel, slots // count),
         out_shape=(
             jax.ShapeDtypeStruct((out_tiles, tasks, tile_size), field.dtype),
             jax.ShapeDtypeStruct((out_tiles, 8, tile_size), jnp.float32),
@@ -155,7 +197,7 @@
             jax.ShapeDtypeStruct((tasks, tile_size), jnp.float32),
             jax.ShapeDtypeStruct(blocks, tiles.dtype),
         ),
-        in_specs=[IN_SMEM] * 3 + [IN_VMEM, IN_HBM],
+        in_specs=[IN_SMEM] * 4 + [IN_VMEM, IN_HBM],
         out_specs=(IN_VMEM, IN_VMEM, IN_VMEM, IN_VMEM, IN_HBM),
         scratch_shapes=[
             pltpu.VMEM(tiles.shape, tiles.dtype),
@@ -165,13 +207,13 @@
         ],
         compiler_params=PARAMS,
         cost_estimate=cost(field, tiles),
-    )(*lists, field, tiles)
-
-
-def next_product(lists, field, blocks, out_tiles):
+    )(col_of, *lists, field, tiles)
+
+
+def next_product(lists, field, blocks, out_tiles, dtype):
     return pl.pallas_call(
-        next_row_kernel,
-        out_shape=jax.ShapeDtypeStruct((out_tiles,) + field.shape[1:], field.dtype),
+        functools.partial(next_kernel, blocks.shape[1] // blocks.shape[2]),
+        out_shape=jax.ShapeDtypeStruct((out_tiles,) + field.shape[1:], dtype),
         in_specs=[IN_SMEM] * 2 + [IN_VMEM, IN_HBM],
         out_specs=IN_VMEM,
         scratch_shapes=[
@@ -183,14 +225,55 @@
     )(*lists[1:], field, blocks)
 
 
-def sorted_lists(ids, loads, per_id):
-    slots = ids.shape[0]
-    order = jnp.arange(slots, dtype=jnp.int32)
-    before = (ids[:, None] == ids[None, :]) & (order[None, :] < order[:, None])
-    place = ids * per_id + jnp.sum(before, axis=1, dtype=jnp.int32)
-    chosen = place[None, :] == order[:, None]
-    pick = lambda values: jnp.sum(jnp.where(chosen, values[None, :], 0), axis=1, dtype=jnp.int32)
-    return pick(order), pick(loads)
+def lists_kernel(own_tiles, row_per, col_per, empty, here, row_ids, col_ids, *rest):
+    by_row, by_row_loads, by_col, by_col_loads, col_of, ids = rest
+    slots = row_ids.shape[1]
+    size = ids.shape[1]
+    lane = lax.broadcasted_iota(jnp.int32, (1, slots), 1)
+
+    def parts(ids):
+        piece = ((ids.astype(jnp.float32) + 0.5) * (1.0 / own_tiles)).astype(jnp.int32)
+        return piece, ids - piece * own_tiles
+
+    rows, cols = row_ids[...], col_ids[...]
+    piece, inside = parts(rows)
+    distance = piece ^ here[0]
+    place = sum(
+        jnp.where(distance == k, here[3 + k], 0) for k in range(here.shape[0] - 3)
+    )
+    row_loads = jnp.where(lane < here[2], place * own_tiles + inside, empty[0])
+    piece, inside = parts(cols)
+    col_loads = jnp.where(lane < here[2], (piece ^ here[1]) * own_tiles + inside, empty[1])
+    ids[...] = jnp.full(ids.shape, size, jnp.int32)
+    for k, values in enumerate((rows, cols, col_loads, row_loads)):
+        ids[k : k + 1, :slots] = values
+    across = ids[...]
+    col_of[...] = across[2:3]
+    down = across.T
+    first = lax.broadcasted_iota(jnp.int32, (size, size), 0)
+    second = lax.broadcasted_iota(jnp.int32, (size, size), 1)
+    for k, per, order, loads in (
+        (0, row_per, by_row, by_row_loads),
+        (1, col_per, by_col, by_col_loads),
+    ):
+        key = down[:, k : k + 1]
+        before = (key == across[k : k + 1]) & (second < first)
+        rank = jnp.sum(before.astype(jnp.float32), axis=1, keepdims=True).astype(jnp.int32)
+        chosen = key * per + rank == second
+        order[...] = jnp.sum(jnp.where(chosen, first, 0), axis=0, keepdims=True)
+        loads[...] = jnp.sum(jnp.where(chosen, down[:, 2 + k : 3 + k], 0), axis=0, keepdims=True)
+
+
+def sorted_lists(own_tiles, row_per, col_per, empty, here, row_ids, col_ids):
+    size = -(-row_ids.shape[1] // 128) * 128
+    return pl.pallas_call(
+        functools.partial(lists_kernel, own_tiles, row_per, col_per, empty),
+        out_shape=[jax.ShapeDtypeStruct((1, size), jnp.int32)] * 5,
+        in_specs=[IN_SMEM, IN_VMEM, IN_VMEM],
+        out_specs=[IN_VMEM] * 5,
+        scratch_shapes=[pltpu.VMEM((8, size), jnp.int32)],
+        compiler_params=pltpu.CompilerParams(vmem_limit_bytes=4 * 2**20),
+    )(here, row_ids, col_ids)
 
 
 def addends(value, count):
@@ -258,8 +341,8 @@
 
 def per_device(plan, scores, tile_values, tile_rows, tile_cols, tile_count):
     tiles = tile_values[0, 0]
-    row_ids = tile_rows[0, 0]
-    col_ids = tile_cols[0, 0]
+    row_ids = tile_rows[0]
+    col_ids = tile_cols[0]
     live = tile_count[0, 0]
     slots, tile_size = tiles.shape[:2]
     task_count, piece_len = scores.shape
@@ -283,18 +366,14 @@
         return ((ids // own_tiles) ^ row_index) * own_tiles + ids % own_tiles
 
     def make_lists(row_ids, col_ids, live):
-        is_live = jnp.arange(slots, dtype=jnp.int32) < live
-        row_loads_of = jnp.where(is_live, row_place(row_ids), row_pieces)
-        col_loads_of = jnp.where(is_live, col_place(col_ids), col_tiles)
-        by_row = (
-            *sorted_lists(row_ids, col_loads_of, slots // row_tiles),
-            row_place(jnp.arange(row_tiles, dtype=jnp.int32)),
+        here = jnp.concatenate([jnp.stack([col_index, row_index, live]), place_of])
+        by_row, by_row_loads, by_col, by_col_loads, col_of = sorted_lists(
+            own_tiles, slots // row_tiles, slots // col_tiles, (row_pieces, col_tiles), here,
+            row_ids, col_ids,
         )
-        by_col = (
-            *sorted_lists(col_ids, row_loads_of, slots // col_tiles),
-            col_place(jnp.arange(col_tiles, dtype=jnp.int32)),
-        )
-        return by_row, by_col
+        by_row = [by_row, by_row_loads, row_place(jnp.arange(row_tiles, dtype=jnp.int32))]
+        by_col = [by_col, by_col_loads, col_place(jnp.arange(col_tiles, dtype=jnp.int32))]
+        return col_of, by_row, by_col
 
     def empty_tile(field):
         return jnp.zeros((1,) + field.shape[1:], field.dtype)
@@ -320,18 +399,23 @@
 
     near = len(plan.row_steps)
     chip_rows = plan.rows // 2
+    chip = 2 * own_tiles
+    own = slice(0, own_tiles)
     residual = scores.reshape(task_count, own_tiles, tile_size).transpose(1, 0, 2)
+    residual = jnp.concatenate([residual, plan.swap(residual)])
     solution = direction = image = None
     norm_before = curve_before = scale = None
     for step_index in range(ITERS):
         first = step_index == 0
 
-        own_low = residual.astype(low)
-        pair = jnp.concatenate([own_low, plan.swap(own_low)])
+        pair = residual.astype(low)
         if first:
             pair, row_ids, col_ids, live = lax.optimization_barrier((pair, row_ids, col_ids, live))
-            by_row, by_col = make_lists(row_ids, col_ids, live)
+            col_of, by_row, by_col = make_lists(row_ids, col_ids, live)
         got = [plan.send(pair, by_core) for by_core in plan.steps]
+        if first:
+            nearby, by_row = lax.optimization_barrier((got[:near], by_row))
+            got = nearby + got[near:]
         shared = [plan.swap(g) for g in got[:near]]
         col_pieces = [pair]
         for g, other in zip(got, shared):
@@ -339,20 +423,20 @@
             col_pieces.append(jnp.where(core == 0, g[own_tiles:], other[:own_tiles]))
         col_field = jnp.concatenate(col_pieces + [empty_tile(pair)])
         if first:
-            forward, row_degree, col_degree, squares, row_blocks = first_product(
-                by_row, with_rows(col_field), tiles, row_pieces, task_count
+            forward, row_degree, col_degree, squares, row_blocks = first_row_product(
+                col_of, by_row, with_rows(col_field), tiles, row_pieces, task_count
             )
         else:
-            forward = next_product(by_row, col_field, row_blocks, row_pieces)
+            forward = next_product(by_row, col_field, row_blocks, row_pieces, low)
 
         far, forward = lax.optimization_barrier((got[near:], forward))
         mine = [g[:own_tiles] for g in got[:near] + far]
         swapped = plan.swap(jnp.concatenate([g[own_tiles:] for g in far]))
         row_field = jnp.concatenate(
-            [own_low] + mine + [o[own_tiles:] for o in shared] + [swapped, empty_tile(pair)]
+            [pair[own]] + mine + [o[own_tiles:] for o in shared] + [swapped, empty_tile(pair)]
         )
         curve_part = -inner(row_field[:-1], forward)
-        norm = inner(residual, residual)
+        norm = inner(residual[own], residual[own])
         if first:
             row_degree = row_degree[:, 0]
             weights = 0.5 * coupling * row_degree[:, None]
@@ -361,60 +445,66 @@
             curve_part += 0.5 * coupling * jnp.sum(squares, axis=1, keepdims=True)
             dots = as_tile([norm, norm + curve_part])
         else:
-            weighted = inner(scale * residual, residual)
-            dots = as_tile([norm, weighted + coupling * curve_part, inner(residual, image)])
-
-        parts = [forward[own_tiles + low_part :], addends(dots, 3)]
-        if first:
-            col_degree = jnp.sum(col_degree[:-1], axis=1)
-            col_degree = col_degree.reshape(chip_rows, 2, own_tiles, tile_size)
-            sent = [row_degree[own_tiles + low_part :], col_degree[:, 1].reshape(-1, tile_size)]
-            parts.append(pack(jnp.concatenate(sent)))
+            weighted = inner(scale[own] * residual[own], residual[own])
+            along = inner(residual[own], image[own])
+            dots = as_tile([norm, weighted + coupling * curve_part, along])
+
+        parts = [forward[own_tiles + low_part :], addends(dots, 2)]
+        if first:
+            col_degree = jnp.sum(col_degree[:-1], axis=1).reshape(chip_rows, chip, tile_size)
+            parts.append(pack(row_degree[own_tiles + low_part :]))
         swapped = plan.swap(jnp.concatenate(parts))
         swapped, row_field = lax.optimization_barrier((swapped, row_field))
         if first:
-            back = unpack(swapped[low_part + 3 :], low_part + chip_rows * own_tiles)
-            other_degree = back[:low_part]
-            col_degree = col_degree[:, 0] + back[low_part:].reshape(col_degree[:, 0].shape)
-        backward = product(by_col, row_field, tiles, col_tiles)
-        dots = dots + join(swapped[low_part : low_part + 3])
-        dots_low = addends(dots, 3)
+            other_degree = unpack(swapped[low_part + 2 :], low_part)
+        if first:
+            backward, col_blocks = first_col_product(by_col, row_field, tiles, col_tiles)
+        else:
+            backward = next_product(by_col, row_field, col_blocks, col_tiles, jnp.float32)
+        dots = dots + join(swapped[low_part : low_part + 2])
+        dots_low = addends(dots, 2)
+        mine_products = forward[own]
         messages = []
-        for j, by_core in enumerate(plan.sum_steps):
+        order = list(range(plan.count))
+        for j in order[1:] + order[:1]:
+            by_core = plan.sum_steps[j]
             piece = slice(j * own_tiles, (j + 1) * own_tiles)
             message = [forward[own_tiles:][piece], swapped[:low_part][piece], dots_low]
             if first:
                 degrees = [row_degree[own_tiles:][piece], other_degree[piece]]
                 message.append(pack(jnp.concatenate(degrees)))
             messages.append(plan.send(jnp.concatenate(message), by_core))
-        backward = backward.reshape(chip_rows, 2, own_tiles, task_count, tile_size)
-        back = plan.swap(backward[:, 1].reshape(-1, task_count, tile_size))
-        backward = backward[:, 0] + back.reshape(backward[:, 0].shape)
+
+        backward = backward.reshape(chip_rows, chip, task_count, tile_size)
+        returned = []
+        for m, by_core in enumerate(plan.row_steps, 1):
+            returned.append(plan.send(backward[m].astype(low), (by_core,) * 2))
         total = sum(m.astype(jnp.float32) for m in messages)
-        dots_mine = jnp.sum(total[2 * own_tiles : 2 * own_tiles + 3], axis=0)
-        message = [total[own_tiles : 2 * own_tiles], dots_mine[None]]
-        if first:
-            degree = unpack(total[2 * own_tiles + 3 :], 2 * own_tiles)
-            message.append(rows_to_tiles(degree[own_tiles:], task_count))
+        dots = jnp.where(core == 0, dots, 0.0) + jnp.sum(total[chip : chip + 2], axis=0)
+        dots_mine = dots
+        degree_back = col_degree[0] if first else None
+        for m, by_core in enumerate(plan.row_steps, 1):
+            message = jnp.concatenate([dots_mine, col_degree[m]]) if first else dots_mine
+            back = plan.send(message, (by_core,) * 2)
+            dots = dots + back[:task_count]
+            if first:
+                degree_back = degree_back + back[task_count:]
+        if first:
+            degree = unpack(total[chip + 2 :], chip) + degree_back
+            degree += jnp.pad(row_degree[own], ((0, own_tiles), (0, 0)))
+        total = total[:chip] + backward[0]
+        total += jnp.pad(mine_products.astype(jnp.float32), ((0, own_tiles), (0, 0), (0, 0)))
+        total += sum(back.astype(jnp.float32) for back in returned)
+
+        message = [total, dots[None]]
+        if first:
+            message.append(rows_to_tiles(degree, task_count))
         back = plan.swap(jnp.concatenate(message))
-        dots = dots + (dots_mine + back[own_tiles])
-        total = total[:own_tiles] + back[:own_tiles] + forward[:own_tiles].astype(jnp.float32)
-        if first:
-            degree = degree[:own_tiles] + tiles_to_rows(back[own_tiles + 1 :], own_tiles)
-            degree += row_degree[:own_tiles] + col_degree[0]
-
-        total = total + backward[0]
-        dots_low = addends(dots, 3)
-        for m, by_core in enumerate(plan.row_steps, 1):
-            message = [backward[m].astype(low), dots_low]
-            if first:
-                message.append(pack(col_degree[m]))
-            back = plan.send(jnp.concatenate(message), (by_core,) * 2)
-            total = total + back[:own_tiles].astype(jnp.float32)
-            dots = dots + join(back[own_tiles : own_tiles + 3])
-            if first:
-                degree += unpack(back[own_tiles + 3 :], own_tiles)
-        total = 0.5 * total
+        total = 0.5 * (total + jnp.concatenate([back[own_tiles:chip], back[own]]))
+        dots = dots + back[chip]
+        if first:
+            back = tiles_to_rows(back[chip + 1 :], chip)
+            degree = degree + jnp.concatenate([back[own_tiles:], back[own]])
 
         norm, curve, along = dots[:, 0:1], dots[:, 1:2], dots[:, 2:3]
         if first:
@@ -432,10 +522,7 @@
         solution = step_size * direction if first else solution + step_size * direction
         residual = residual - step_size * image
 
-    def to_field(value):
-        return value.transpose(1, 0, 2).reshape(task_count, piece_len)
-
-    return to_field(solution), to_field(residual)
+    return tuple(to_fields(solution[own], residual[own]))
 
 
 def solution(mesh):

time: 129 us -> 121 us (0.938)
  other arithmetic: 9.54 us -> 5.58 us
  starting transfers between devices: 52 us -> 48.4 us
  waiting for transfers between devices: 28.7 us -> 26.6 us
  Pallas kernels: 33 us -> 34.3 us
    ppermute x18 -> x13, starting transfers between devices: 13.6 us -> 6.52 us  [swap(): return lax.ppermute(value, 'row', [(r, r ^ 1) for r in range(self.rows)])]
    ppermute x27 -> x30, starting transfers between devices: 38.4 us -> 41.9 us  [send(): return lax.ppermute(value, MESH_AXES, self.pairs(by_core))]
    ppermute x18 -> x13, waiting for transfers between devices: 15.4 us -> 12 us  [swap(): return lax.ppermute(value, 'row', [(r, r ^ 1) for r in range(self.rows)])]
    reduce_sum x7 -> x4, other arithmetic: 1.36 us -> 0.05 us  [the longest x1 0.03 us: per_device(): jnp.sum(col_degree[:-1], axis=1).reshape(chip_rows, chip, tile_size)]
    reshape x4 -> x0, local copies, waits for them, and re-layouts: 1.3 us -> none  [the longest x2 1.29 us: to_field(): return value.transpose(1, 0, 2).reshape(task_count, piece_len)]
    pallas_call x6 -> x8, Pallas kernels: 33 us -> 34.3 us  [the longest x4 16.9 us: next_product(): pl.pallas_call(functools.partial(next_kernel, blocks.shape[1] // blocks.s...]
    ppermute x27 -> x30, waiting for transfers between devices: 13.3 us -> 14.5 us  [send(): return lax.ppermute(value, MESH_AXES, self.pairs(by_core))]
    unnamed x39 -> x31, local copies, waits for them, and re-layouts: 1.69 us -> 2.87 us
  transfers between devices with their start and end apart: 45 -> 43, of which waited for: 22 -> 19; matrix products, arithmetic and copies ran while one was open for 5% -> 3% of each run, Pallas kernels for 26% -> 28%
where the time goes in v4:
time: 121 us; the launch traced here: 120 us
  starting transfers between devices  48.4 us (40%)
  Pallas kernels  34.3 us (28%)
  waiting for transfers between devices  26.6 us (22%)
  other arithmetic  5.58 us (5%)
  local copies, waits for them, and re-layouts  3.4 us (3%)
  between operations  2.2 us (2%)
    ppermute x30, starting transfers between devices, send(): return lax.ppermute(value, MESH_AXES, self.pairs(by_core))  41.9 us
    pallas_call x4, Pallas kernels, next_product(): pl.pallas_call(functools.partial(next_kernel, blocks.shape[1] // blocks.s...  16.9 us
    ppermute x30, waiting for transfers between devices, send(): return lax.ppermute(value, MESH_AXES, self.pairs(by_core))  14.5 us
    ppermute x13, waiting for transfers between devices, swap(): return lax.ppermute(value, 'row', [(r, r ^ 1) for r in range(self.rows)])  12 us
    pallas_call x1, Pallas kernels, first_row_product(): pl.pallas_call(functools.partial(first_row_kernel, slots // count), out_s...  8.12 us
    pallas_call x1, Pallas kernels, first_col_product(): pl.pallas_call(functools.partial(first_col_kernel, slots // count), out_s...  7.36 us
    ppermute x13, starting transfers between devices, swap(): return lax.ppermute(value, 'row', [(r, r ^ 1) for r in range(self.rows)])  6.52 us
    unnamed x31, local copies, waits for them, and re-layouts  2.87 us
  transfers between devices with their start and end apart: 43, of which 19 were waited for; matrix products, arithmetic and copies ran while one was open for 3% of the time, Pallas kernels for 28%

profile of v4, /device:TPU:0, one launch (start us, length us, event | category | flops | bytes accessed | tf_op | source)
XLA Modules:
  0.0 120.4 jit_solution(11344025000603119362)
XLA Ops:
  0.6 0.9 copy-done
  1.5 0.5 collective-permute-start
  2.9 0.7 broadcast_select_fusion.3
  3.7 2.6 %collective-permute-start.1 = (bf16[12,32,128]{2,1,0:T(8,128)(2,1)S(1)}, bf16[12,32,128]{2,1,0:T(8,128)(2,1)S(1)}, u32[]{:S(2)}, u32[]{:S(2)}) collective-permute-start(bf16[12,32,128]{2,1,0:T(8,128)(2,1)S(1)} %fusion.14), channel_id=1, source_target_pairs={{0,16},{1,17},{2,18},{3,19},{4,20},{5,21},{6,22},{7,23},{8,9},{9,8... | collective-permute-start | bytes 294920 | tf_op jit(solution)/shard_map/ppermute | solution.py:336
  6.4 0.7 copy-done.1
  7.1 0.7 copy-done.2
  7.8 1.2 %shard_map.86 = (s32[1,256]{1,0:T(1,128)S(1)}, s32[1,256]{1,0:T(1,128)S(1)}, s32[1,256]{1,0:T(1,128)S(1)}, s32[1,256]{1,0:T(1,128)S(1)}, s32[1,256]{1,0:T(1,128)S(1)}) custom-call(s32[11]{0:T(128)S(1)} %pad_add_fusion.here, s32[1,240]{1,0:T(1,128)S(1)} %bitcast.99, s32[1,240]{1,0:T(1,128)S(1)} %bitcast.100), custom_call_target="tpu_custom_call" | custom-call | tf_op jit(solution)/shard_map/pallas_call | solution.py:269
  9.3 3.8 %collective-permute-start.2 = (bf16[12,32,128]{2,1,0:T(8,128)(2,1)S(1)}, bf16[12,32,128]{2,1,0:T(8,128)(2,1)S(1)}, u32[]{:S(2)}, u32[]{:S(2)}) collective-permute-start(bf16[12,32,128]{2,1,0:T(8,128)(2,1)S(1)} %fusion.14), channel_id=1, source_target_pairs={{0,6},{1,7},{2,4},{3,5},{4,2},{5,3},{6,0},{7,1},{8,15},{9,14},{10,... | collective-permute-start | bytes 294920 | tf_op jit(solution)/shard_map/ppermute | solution.py:336
  13.1 0.6 collective-permute-start.4
  14.1 8.1 %shard_map.87 = (bf16[54,32,128]{2,1,0:T(8,128)(2,1)S(1)}, f32[54,8,128]{2,1,0:T(8,128)S(1)}, f32[25,8,128]{2,1,0:T(8,128)S(1)}, f32[32,128]{1,0:T(8,128)S(1)}, bf16[48,640,128]{2,1,0:T(8,128)(2,1)}) custom-call(s32[1,256]{1,0:T(1,128)S(1)} %get-tuple-element.47.col_of, s32[1,256]{1,0:T(1,128)S(1)} %get-tuple-element.48.slots, ...), custom_call_target="tpu_custom_call" | custom-call | flops 5033164800 | bytes 7864320 | tf_op jit(solution)/shard_map/pallas_call | solution.py:191
  22.5 1.7 %collective-permute-start.6 = (bf16[18,32,128]{2,1,0:T(8,128)(2,1)S(1)}, bf16[18,32,128]{2,1,0:T(8,128)(2,1)S(1)}, u32[]{:S(2)}, u32[]{:S(2)}) collective-permute-start(bf16[18,32,128]{2,1,0:T(8,128)(2,1)S(1)} %pad_maximum_fusion.26), channel_id=1, source_target_pairs={{0,8},{8,0},{16,24},{24,16},{1,9},{9,1},{17,25},{25,17},{2,10},{10... | collective-permute-start | bytes 442376 | tf_op jit(solution)/shard_map/ppermute | solution.py:339
  24.5 0.8 collective-permute-done.6
  25.3 0.4 fusion
  25.8 0.4 collective-permute-start.7
  26.3 1.1 collective-permute-done.7
  27.7 3.6 %collective-permute-start.8 = (bf16[15,32,128]{2,1,0:T(8,128)(2,1)S(1)}, bf16[15,32,128]{2,1,0:T(8,128)(2,1)S(1)}, u32[]{:S(2)}, u32[]{:S(2)}) collective-permute-start(bf16[15,32,128]{2,1,0:T(8,128)(2,1)S(1)} %constant_dynamic-update-slice_fusion.15), channel_id=1, source_target_pairs={{0,6},{1,7},{2,4},{3,5},{4,2},{5,3},{6,0},{7,1},{8,15},{9,14},{10,... | collective-permute-start | bytes 368648 | tf_op jit(solution)/shard_map/ppermute | solution.py:336
  31.6 0.9 collective-permute-start.10
  32.5 0.7 collective-permute-start.11
  33.2 7.4 %shard_map.88 = (f32[24,32,128]{2,1,0:T(8,128)S(1)}, bf16[24,1280,128]{2,1,0:T(8,128)(2,1)}) custom-call(s32[1,256]{1,0:T(1,128)S(1)} %get-tuple-element.60.slots, s32[1,256]{1,0:T(1,128)S(1)} %get-tuple-element.61.loads, s32[24]{0:T(128)S(1)} %fusion.62.place, bf16[55,32,128]{2,1,0:T(8,128)(2,1)S(1)} %constant_dynamic-update-slice_fusion.7.field, ...), custom_call_target="tpu_custom_call" | custom-call | flops 2013265920 | bytes 7864320 | tf_op jit(solution)/shard_map/pallas_call | solution.py:168
  40.6 1.6 %collective-permute-start.13 = (bf16[12,32,128]{2,1,0:T(8,128)(2,1)S(1)}, bf16[12,32,128]{2,1,0:T(8,128)(2,1)S(1)}, u32[]{:S(2)}, u32[]{:S(2)}) collective-permute-start(bf16[12,32,128]{2,1,0:T(8,128)(2,1)S(1)} %slice.892), channel_id=1, source_target_pairs={{0,16},{1,17},{2,18},{3,19},{4,20},{5,21},{6,22},{7,23},{8,24},{9,... | collective-permute-start | bytes 294920 | tf_op jit(solution)/shard_map/ppermute | solution.py:336
  42.3 1.1 collective-permute-start.12
  43.5 1.8 %collective-permute-done.13 = bf16[12,32,128]{2,1,0:T(8,128)(2,1)S(1)} collective-permute-done((bf16[12,32,128]{2,1,0:T(8,128)(2,1)S(1)}, bf16[12,32,128]{2,1,0:T(8,128)(2,1)S(1)}, u32[]{:S(2)}, u32[]{:S(2)}) %collective-permute-start.13) | collective-permute-done | bytes 98336 | tf_op jit(solution)/shard_map/ppermute | solution.py:336
  45.4 1.0 collective-permute-done.12
  46.4 1.3 %collective-permute-start.14 = (f32[14,32,128]{2,1,0:T(8,128)S(1)}, f32[14,32,128]{2,1,0:T(8,128)S(1)}, u32[]{:S(2)}, u32[]{:S(2)}) collective-permute-start(f32[14,32,128]{2,1,0:T(8,128)S(1)} %pad_maximum_fusion.21), channel_id=1, source_target_pairs={{0,8},{8,0},{16,24},{24,16},{1,9},{9,1},{17,25},{25,17},{2,10},{10... | collective-permute-start | bytes 688136 | tf_op jit(solution)/shard_map/ppermute | solution.py:339
  47.8 1.1 collective-permute-done.14
  49.2 1.1 collective-permute-start.15
  50.4 3.7 %collective-permute-start.16 = (bf16[12,32,128]{2,1,0:T(8,128)(2,1)S(1)}, bf16[12,32,128]{2,1,0:T(8,128)(2,1)S(1)}, u32[]{:S(2)}, u32[]{:S(2)}) collective-permute-start(bf16[12,32,128]{2,1,0:T(8,128)(2,1)S(1)} %get-tuple-element.94), channel_id=1, source_target_pairs={{0,6},{1,7},{2,4},{3,5},{4,2},{5,3},{6,0},{7,1},{8,15},{9,14},{10,... | collective-permute-start | bytes 294920 | tf_op jit(solution)/shard_map/ppermute | solution.py:336
  54.1 0.8 collective-permute-start.18
  54.8 0.5 collective-permute-start.19
  55.5 0.8 collective-permute-done.19
  56.4 4.2 %shard_map.89 = bf16[54,32,128]{2,1,0:T(8,128)(2,1)S(1)} custom-call(s32[1,256]{1,0:T(1,128)S(1)} %get-tuple-element.49.loads, s32[48]{0:T(128)S(1)} %fusion.61.place, bf16[25,32,128]{2,1,0:T(8,128)(2,1)S(1)} %pad_maximum_fusion.2.field, bf16[48,640,128]{2,1,0:T(8,128)(2,1)} %get-tuple-element.64.source), custom_call_target="tpu_custom_call" | custom-call | flops 2013265920 | bytes 7864320 | tf_op jit(solution)/shard_map/pallas_call | solution.py:214
  60.7 1.3 %collective-permute-done.17 = bf16[12,32,128]{2,1,0:T(8,128)(2,1)S(1)} collective-permute-done((bf16[12,32,128]{2,1,0:T(8,128)(2,1)S(1)}, bf16[12,32,128]{2,1,0:T(8,128)(2,1)S(1)}, u32[]{:S(2)}, u32[]{:S(2)}) %collective-permute-start.17) | collective-permute-done | bytes 98336 | tf_op jit(solution)/shard_map/ppermute | solution.py:336
  62.1 0.4 collective-permute-start.20
  62.6 1.0 collective-permute-done.20
  64.0 0.4 collective-permute-start.21
  64.5 1.1 collective-permute-done.21
  65.7 2.8 %collective-permute-start.22 = (bf16[14,32,128]{2,1,0:T(8,128)(2,1)S(1)}, bf16[14,32,128]{2,1,0:T(8,128)(2,1)S(1)}, u32[]{:S(2)}, u32[]{:S(2)}) collective-permute-start(bf16[14,32,128]{2,1,0:T(8,128)(2,1)S(1)} %get-tuple-element.210), channel_id=1, source_target_pairs={{0,6},{1,7},{2,4},{3,5},{4,2},{5,3},{6,0},{7,1},{8,15},{9,14},{10,... | collective-permute-start | bytes 344072 | tf_op jit(solution)/shard_map/ppermute | solution.py:336
  68.8 1.4 %collective-permute-start.24 = (bf16[14,32,128]{2,1,0:T(8,128)(2,1)S(1)}, bf16[14,32,128]{2,1,0:T(8,128)(2,1)S(1)}, u32[]{:S(2)}, u32[]{:S(2)}) collective-permute-start(bf16[14,32,128]{2,1,0:T(8,128)(2,1)S(1)} %get-tuple-element.212), channel_id=1, source_target_pairs={{0,2},{1,3},{2,0},{3,1},{4,6},{5,7},{6,4},{7,5},{8,11},{9,10},{10,... | collective-permute-start | bytes 344072 | tf_op jit(solution)/shard_map/ppermute | solution.py:336
  70.2 0.8 collective-permute-start.25
  71.0 4.2 %shard_map.90 = f32[24,32,128]{2,1,0:T(8,128)S(1)} custom-call(s32[1,256]{1,0:T(1,128)S(1)} %get-tuple-element.61.loads, s32[24]{0:T(128)S(1)} %fusion.62.place, bf16[55,32,128]{2,1,0:T(8,128)(2,1)S(1)} %constant_dynamic-update-slice_fusion.42.field, bf16[24,1280,128]{2,1,0:T(8,128)(2,1)} %get-tuple-element.71.source), custom_call_target="tpu_custom_call" | custom-call | flops 2013265920 | bytes 7864320 | tf_op jit(solution)/shard_map/pallas_call | solution.py:214
  75.3 1.2 %collective-permute-start.27 = (bf16[12,32,128]{2,1,0:T(8,128)(2,1)S(1)}, bf16[12,32,128]{2,1,0:T(8,128)(2,1)S(1)}, u32[]{:S(2)}, u32[]{:S(2)}) collective-permute-start(bf16[12,32,128]{2,1,0:T(8,128)(2,1)S(1)} %slice.891), channel_id=1, source_target_pairs={{0,16},{1,17},{2,18},{3,19},{4,20},{5,21},{6,22},{7,23},{8,24},{9,... | collective-permute-start | bytes 294920 | tf_op jit(solution)/shard_map/ppermute | solution.py:336
  76.5 3.0 %collective-permute-done.23 = bf16[14,32,128]{2,1,0:T(8,128)(2,1)S(1)} collective-permute-done((bf16[14,32,128]{2,1,0:T(8,128)(2,1)S(1)}, bf16[14,32,128]{2,1,0:T(8,128)(2,1)S(1)}, u32[]{:S(2)}, u32[]{:S(2)}) %collective-permute-start.23) | collective-permute-done | bytes 114720 | tf_op jit(solution)/shard_map/ppermute | solution.py:336
  79.7 1.3 %collective-permute-start.26 = (f32[32,128]{1,0:T(8,128)S(1)}, f32[32,128]{1,0:T(8,128)S(1)}, u32[]{:S(2)}, u32[]{:S(2)}) collective-permute-start(f32[32,128]{1,0:T(8,128)S(1)} %select_add_fusion.2), channel_id=1, source_target_pairs={{0,16},{1,17},{2,18},{3,19},{4,20},{5,21},{6,22},{7,23},{8,24},{9,... | collective-permute-start | bytes 49160 | tf_op jit(solution)/shard_map/ppermute | solution.py:336
  81.0 2.4 %collective-permute-done.26 = f32[32,128]{1,0:T(8,128)S(1)} collective-permute-done((f32[32,128]{1,0:T(8,128)S(1)}, f32[32,128]{1,0:T(8,128)S(1)}, u32[]{:S(2)}, u32[]{:S(2)}) %collective-permute-start.26) | collective-permute-done | bytes 16416 | tf_op jit(solution)/shard_map/ppermute | solution.py:336
  83.6 1.5 %collective-permute-done.28 = f32[13,32,128]{2,1,0:T(8,128)S(1)} collective-permute-done((f32[13,32,128]{2,1,0:T(8,128)S(1)}, f32[13,32,128]{2,1,0:T(8,128)S(1)}, u32[]{:S(2)}, u32[]{:S(2)}) %collective-permute-start.28) | collective-permute-done | bytes 213024 | tf_op jit(solution)/shard_map/ppermute | solution.py:339
  85.4 1.3 %collective-permute-start.29 = (bf16[12,32,128]{2,1,0:T(8,128)(2,1)S(1)}, bf16[12,32,128]{2,1,0:T(8,128)(2,1)S(1)}, u32[]{:S(2)}, u32[]{:S(2)}) collective-permute-start(bf16[12,32,128]{2,1,0:T(8,128)(2,1)S(1)} %get-tuple-element.90), channel_id=1, source_target_pairs={{0,16},{1,17},{2,18},{3,19},{4,20},{5,21},{6,22},{7,23},{8,9},{9,8... | collective-permute-start | bytes 294920 | tf_op jit(solution)/shard_map/ppermute | solution.py:336
  86.7 1.5 %collective-permute-start.30 = (bf16[12,32,128]{2,1,0:T(8,128)(2,1)S(1)}, bf16[12,32,128]{2,1,0:T(8,128)(2,1)S(1)}, u32[]{:S(2)}, u32[]{:S(2)}) collective-permute-start(bf16[12,32,128]{2,1,0:T(8,128)(2,1)S(1)} %get-tuple-element.90), channel_id=1, source_target_pairs={{0,6},{1,7},{2,4},{3,5},{4,2},{5,3},{6,0},{7,1},{8,15},{9,14},{10,... | collective-permute-start | bytes 294920 | tf_op jit(solution)/shard_map/ppermute | solution.py:336
  88.1 3.0 %collective-permute-start.32 = (bf16[12,32,128]{2,1,0:T(8,128)(2,1)S(1)}, bf16[12,32,128]{2,1,0:T(8,128)(2,1)S(1)}, u32[]{:S(2)}, u32[]{:S(2)}) collective-permute-start(bf16[12,32,128]{2,1,0:T(8,128)(2,1)S(1)} %get-tuple-element.90), channel_id=1, source_target_pairs={{0,2},{1,3},{2,0},{3,1},{4,6},{5,7},{6,4},{7,5},{8,11},{9,10},{10,... | collective-permute-start | bytes 294920 | tf_op jit(solution)/shard_map/ppermute | solution.py:336
  91.4 1.0 collective-permute-done.33
  92.5 4.2 %shard_map.91 = bf16[54,32,128]{2,1,0:T(8,128)(2,1)S(1)} custom-call(s32[1,256]{1,0:T(1,128)S(1)} %get-tuple-element.49.loads, s32[48]{0:T(128)S(1)} %fusion.61.place, bf16[25,32,128]{2,1,0:T(8,128)(2,1)S(1)} %pad_maximum_fusion.1.field, bf16[48,640,128]{2,1,0:T(8,128)(2,1)} %get-tuple-element.64.source), custom_call_target="tpu_custom_call" | custom-call | flops 2013265920 | bytes 7864320 | tf_op jit(solution)/shard_map/pallas_call | solution.py:214
  96.8 0.8 collective-permute-done.31
  97.7 0.3 collective-permute-start.34
  98.0 1.1 collective-permute-done.34
  99.9 1.2 collective-permute-done.35
  101.3 1.6 %collective-permute-start.36 = (bf16[14,32,128]{2,1,0:T(8,128)(2,1)S(1)}, bf16[14,32,128]{2,1,0:T(8,128)(2,1)S(1)}, u32[]{:S(2)}, u32[]{:S(2)}) collective-permute-start(bf16[14,32,128]{2,1,0:T(8,128)(2,1)S(1)} %get-tuple-element.206), channel_id=1, source_target_pairs={{0,6},{1,7},{2,4},{3,5},{4,2},{5,3},{6,0},{7,1},{8,15},{9,14},{10,... | collective-permute-start | bytes 344072 | tf_op jit(solution)/shard_map/ppermute | solution.py:336
  102.9 2.8 %collective-permute-start.38 = (bf16[14,32,128]{2,1,0:T(8,128)(2,1)S(1)}, bf16[14,32,128]{2,1,0:T(8,128)(2,1)S(1)}, u32[]{:S(2)}, u32[]{:S(2)}) collective-permute-start(bf16[14,32,128]{2,1,0:T(8,128)(2,1)S(1)} %get-tuple-element.208), channel_id=1, source_target_pairs={{0,2},{1,3},{2,0},{3,1},{4,6},{5,7},{6,4},{7,5},{8,11},{9,10},{10,... | collective-permute-start | bytes 344072 | tf_op jit(solution)/shard_map/ppermute | solution.py:336
  105.8 0.7 collective-permute-start.39
  106.4 4.2 %shard_map.92 = f32[24,32,128]{2,1,0:T(8,128)S(1)} custom-call(s32[1,256]{1,0:T(1,128)S(1)} %get-tuple-element.61.loads, s32[24]{0:T(128)S(1)} %fusion.62.place, bf16[55,32,128]{2,1,0:T(8,128)(2,1)S(1)} %constant_dynamic-update-slice_fusion.57.field, bf16[24,1280,128]{2,1,0:T(8,128)(2,1)} %get-tuple-element.71.source), custom_call_target="tpu_custom_call" | custom-call | flops 2013265920 | bytes 7864320 | tf_op jit(solution)/shard_map/pallas_call | solution.py:214
  110.7 1.3 %collective-permute-start.41 = (bf16[12,32,128]{2,1,0:T(8,128)(2,1)S(1)}, bf16[12,32,128]{2,1,0:T(8,128)(2,1)S(1)}, u32[]{:S(2)}, u32[]{:S(2)}) collective-permute-start(bf16[12,32,128]{2,1,0:T(8,128)(2,1)S(1)} %slice.890), channel_id=1, source_target_pairs={{0,16},{1,17},{2,18},{3,19},{4,20},{5,21},{6,22},{7,23},{8,24},{9,... | collective-permute-start | bytes 294920 | tf_op jit(solution)/shard_map/ppermute | solution.py:336
  112.0 1.9 %collective-permute-done.37 = bf16[14,32,128]{2,1,0:T(8,128)(2,1)S(1)} collective-permute-done((bf16[14,32,128]{2,1,0:T(8,128)(2,1)S(1)}, bf16[14,32,128]{2,1,0:T(8,128)(2,1)S(1)}, u32[]{:S(2)}, u32[]{:S(2)}) %collective-permute-start.37) | collective-permute-done | bytes 114720 | tf_op jit(solution)/shard_map/ppermute | solution.py:336
  114.0 1.3 %collective-permute-start.40 = (f32[32,128]{1,0:T(8,128)S(1)}, f32[32,128]{1,0:T(8,128)S(1)}, u32[]{:S(2)}, u32[]{:S(2)}) collective-permute-start(f32[32,128]{1,0:T(8,128)S(1)} %select_add_fusion), channel_id=1, source_target_pairs={{0,16},{1,17},{2,18},{3,19},{4,20},{5,21},{6,22},{7,23},{8,24},{9,... | collective-permute-start | bytes 49160 | tf_op jit(solution)/shard_map/ppermute | solution.py:336
  115.5 2.3 %collective-permute-done.40 = f32[32,128]{1,0:T(8,128)S(1)} collective-permute-done((f32[32,128]{1,0:T(8,128)S(1)}, f32[32,128]{1,0:T(8,128)S(1)}, u32[]{:S(2)}, u32[]{:S(2)}) %collective-permute-start.40) | collective-permute-done | bytes 16416 | tf_op jit(solution)/shard_map/ppermute | solution.py:336
  117.9 1.5 %collective-permute-done.42 = f32[13,32,128]{2,1,0:T(8,128)S(1)} collective-permute-done((f32[13,32,128]{2,1,0:T(8,128)S(1)}, f32[13,32,128]{2,1,0:T(8,128)S(1)}, u32[]{:S(2)}, u32[]{:S(2)}) %collective-permute-start.42) | collective-permute-done | bytes 213024 | tf_op jit(solution)/shard_map/ppermute | solution.py:339
  119.7 0.7 shard_map.93
  (194 shorter events, 7.0 us)
Async XLA Ops:
  0.6 0.9 copy-start
  1.5 2.2 %collective-permute-start = (f32[6,32,128]{2,1,0:T(8,128)S(1)}, f32[6,32,128]{2,1,0:T(8,128)S(1)}, u32[]{:S(2)}, u32[]{:S(2)}) collective-permute-start(f32[6,32,128]{2,1,0:T(8,128)S(1)} %bitcast_bitcast_fusion), channel_id=1, source_target_pairs={{0,8},{8,0},{16,24},{24,16},{1,9},{9,1},{17,25},{25,17},{2,10},{10... | collective-permute-start | bytes 294920 | tf_op jit(solution)/shard_map/ppermute | solution.py:339
  3.7 5.3 %collective-permute-start.1 = (bf16[12,32,128]{2,1,0:T(8,128)(2,1)S(1)}, bf16[12,32,128]{2,1,0:T(8,128)(2,1)S(1)}, u32[]{:S(2)}, u32[]{:S(2)}) collective-permute-start(bf16[12,32,128]{2,1,0:T(8,128)(2,1)S(1)} %fusion.14), channel_id=1, source_target_pairs={{0,16},{1,17},{2,18},{3,19},{4,20},{5,21},{6,22},{7,23},{8,9},{9,8... | collective-permute-start | bytes 294920 | tf_op jit(solution)/shard_map/ppermute | solution.py:336
  6.4 0.7 copy-start.1
  7.1 0.7 copy-start.2
  9.0 4.7 %collective-permute-start.5 = (bf16[12,32,128]{2,1,0:T(8,128)(2,1)S(1)}, bf16[12,32,128]{2,1,0:T(8,128)(2,1)S(1)}, u32[]{:S(2)}, u32[]{:S(2)}) collective-permute-start(bf16[12,32,128]{2,1,0:T(8,128)(2,1)S(1)} %collective-permute-done.1), channel_id=1, source_target_pairs={{0,8},{8,0},{16,24},{24,16},{1,9},{9,1},{17,25},{25,17},{2,10},{10... | collective-permute-start | bytes 294920 | tf_op jit(solution)/shard_map/ppermute | solution.py:339
  9.3 13.0 %collective-permute-start.2 = (bf16[12,32,128]{2,1,0:T(8,128)(2,1)S(1)}, bf16[12,32,128]{2,1,0:T(8,128)(2,1)S(1)}, u32[]{:S(2)}, u32[]{:S(2)}) collective-permute-start(bf16[12,32,128]{2,1,0:T(8,128)(2,1)S(1)} %fusion.14), channel_id=1, source_target_pairs={{0,6},{1,7},{2,4},{3,5},{4,2},{5,3},{6,0},{7,1},{8,15},{9,14},{10,... | collective-permute-start | bytes 294920 | tf_op jit(solution)/shard_map/ppermute | solution.py:336
  13.1 9.2 %collective-permute-start.3 = (bf16[12,32,128]{2,1,0:T(8,128)(2,1)S(1)}, bf16[12,32,128]{2,1,0:T(8,128)(2,1)S(1)}, u32[]{:S(2)}, u32[]{:S(2)}) collective-permute-start(bf16[12,32,128]{2,1,0:T(8,128)(2,1)S(1)} %fusion.14), channel_id=1, source_target_pairs={{0,4},{1,5},{2,6},{3,7},{4,0},{5,1},{6,2},{7,3},{8,13},{9,12},{10,... | collective-permute-start | bytes 294920 | tf_op jit(solution)/shard_map/ppermute | solution.py:336
  13.1 9.2 %collective-permute-start.4 = (bf16[12,32,128]{2,1,0:T(8,128)(2,1)S(1)}, bf16[12,32,128]{2,1,0:T(8,128)(2,1)S(1)}, u32[]{:S(2)}, u32[]{:S(2)}) collective-permute-start(bf16[12,32,128]{2,1,0:T(8,128)(2,1)S(1)} %fusion.14), channel_id=1, source_target_pairs={{0,2},{1,3},{2,0},{3,1},{4,6},{5,7},{6,4},{7,5},{8,11},{9,10},{10,... | collective-permute-start | bytes 294920 | tf_op jit(solution)/shard_map/ppermute | solution.py:336
  22.2 23.0 %copy-start.3 = (pred[12]{0:T(512)(128)(4,1)S(1)}, pred[12]{0:T(512)(128)(4,1)}, u32[]{:S(2)}) copy-start(pred[12]{0:T(512)(128)(4,1)} %constant.85.clone.1) | copy-start | bytes 40
  22.5 2.7 %collective-permute-start.6 = (bf16[18,32,128]{2,1,0:T(8,128)(2,1)S(1)}, bf16[18,32,128]{2,1,0:T(8,128)(2,1)S(1)}, u32[]{:S(2)}, u32[]{:S(2)}) collective-permute-start(bf16[18,32,128]{2,1,0:T(8,128)(2,1)S(1)} %pad_maximum_fusion.26), channel_id=1, source_target_pairs={{0,8},{8,0},{16,24},{24,16},{1,9},{9,1},{17,25},{25,17},{2,10},{10... | collective-permute-start | bytes 442376 | tf_op jit(solution)/shard_map/ppermute | solution.py:339
  25.8 1.6 %collective-permute-start.7 = (bf16[28,32,128]{2,1,0:T(8,128)(2,1)S(1)}, bf16[28,32,128]{2,1,0:T(8,128)(2,1)S(1)}, u32[]{:S(2)}, u32[]{:S(2)}) collective-permute-start(bf16[28,32,128]{2,1,0:T(8,128)(2,1)S(1)} %pad_maximum_fusion.20), channel_id=1, source_target_pairs={{0,8},{8,0},{16,24},{24,16},{1,9},{9,1},{17,25},{25,17},{2,10},{10... | collective-permute-start | bytes 688136 | tf_op jit(solution)/shard_map/ppermute | solution.py:339
  27.7 14.5 %collective-permute-start.8 = (bf16[15,32,128]{2,1,0:T(8,128)(2,1)S(1)}, bf16[15,32,128]{2,1,0:T(8,128)(2,1)S(1)}, u32[]{:S(2)}, u32[]{:S(2)}) collective-permute-start(bf16[15,32,128]{2,1,0:T(8,128)(2,1)S(1)} %constant_dynamic-update-slice_fusion.15), channel_id=1, source_target_pairs={{0,6},{1,7},{2,4},{3,5},{4,2},{5,3},{6,0},{7,1},{8,15},{9,14},{10,... | collective-permute-start | bytes 368648 | tf_op jit(solution)/shard_map/ppermute | solution.py:336
  31.4 10.7 %collective-permute-start.9 = (bf16[15,32,128]{2,1,0:T(8,128)(2,1)S(1)}, bf16[15,32,128]{2,1,0:T(8,128)(2,1)S(1)}, u32[]{:S(2)}, u32[]{:S(2)}) collective-permute-start(bf16[15,32,128]{2,1,0:T(8,128)(2,1)S(1)} %constant_dynamic-update-slice_fusion.20), channel_id=1, source_target_pairs={{0,4},{1,5},{2,6},{3,7},{4,0},{5,1},{6,2},{7,3},{8,13},{9,12},{10,... | collective-permute-start | bytes 368648 | tf_op jit(solution)/shard_map/ppermute | solution.py:336
  31.6 10.6 %collective-permute-start.10 = (bf16[15,32,128]{2,1,0:T(8,128)(2,1)S(1)}, bf16[15,32,128]{2,1,0:T(8,128)(2,1)S(1)}, u32[]{:S(2)}, u32[]{:S(2)}) collective-permute-start(bf16[15,32,128]{2,1,0:T(8,128)(2,1)S(1)} %constant_dynamic-update-slice_fusion.25), channel_id=1, source_target_pairs={{0,2},{1,3},{2,0},{3,1},{4,6},{5,7},{6,4},{7,5},{8,11},{9,10},{10,... | collective-permute-start | bytes 368648 | tf_op jit(solution)/shard_map/ppermute | solution.py:336
  32.5 9.7 %collective-permute-start.11 = (bf16[15,32,128]{2,1,0:T(8,128)(2,1)S(1)}, bf16[15,32,128]{2,1,0:T(8,128)(2,1)S(1)}, u32[]{:S(2)}, u32[]{:S(2)}) collective-permute-start(bf16[15,32,128]{2,1,0:T(8,128)(2,1)S(1)} %constant_dynamic-update-slice_fusion.30), channel_id=1, source_target_pairs={{8,9},{9,8},{10,11},{11,10},{12,13},{13,12},{14,15},{15,14},{24,25... | collective-permute-start | bytes 368648 | tf_op jit(solution)/shard_map/ppermute | solution.py:336
  40.6 4.7 %collective-permute-start.13 = (bf16[12,32,128]{2,1,0:T(8,128)(2,1)S(1)}, bf16[12,32,128]{2,1,0:T(8,128)(2,1)S(1)}, u32[]{:S(2)}, u32[]{:S(2)}) collective-permute-start(bf16[12,32,128]{2,1,0:T(8,128)(2,1)S(1)} %slice.892), channel_id=1, source_target_pairs={{0,16},{1,17},{2,18},{3,19},{4,20},{5,21},{6,22},{7,23},{8,24},{9,... | collective-permute-start | bytes 294920 | tf_op jit(solution)/shard_map/ppermute | solution.py:336
  42.3 4.0 %collective-permute-start.12 = (f32[44,128]{1,0:T(8,128)S(1)}, f32[44,128]{1,0:T(8,128)S(1)}, u32[]{:S(2)}, u32[]{:S(2)}) collective-permute-start(f32[44,128]{1,0:T(8,128)S(1)} %pad_maximum_fusion.29), channel_id=1, source_target_pairs={{0,16},{1,17},{2,18},{3,19},{4,20},{5,21},{6,22},{7,23},{8,24},{9,... | collective-permute-start | bytes 67592 | tf_op jit(solution)/shard_map/ppermute | solution.py:336
  46.4 2.4 %collective-permute-start.14 = (f32[14,32,128]{2,1,0:T(8,128)S(1)}, f32[14,32,128]{2,1,0:T(8,128)S(1)}, u32[]{:S(2)}, u32[]{:S(2)}) collective-permute-start(f32[14,32,128]{2,1,0:T(8,128)S(1)} %pad_maximum_fusion.21), channel_id=1, source_target_pairs={{0,8},{8,0},{16,24},{24,16},{1,9},{9,1},{17,25},{25,17},{2,10},{10... | collective-permute-start | bytes 688136 | tf_op jit(solution)/shard_map/ppermute | solution.py:339
  49.2 5.6 %collective-permute-start.15 = (bf16[12,32,128]{2,1,0:T(8,128)(2,1)S(1)}, bf16[12,32,128]{2,1,0:T(8,128)(2,1)S(1)}, u32[]{:S(2)}, u32[]{:S(2)}) collective-permute-start(bf16[12,32,128]{2,1,0:T(8,128)(2,1)S(1)} %get-tuple-element.94), channel_id=1, source_target_pairs={{0,16},{1,17},{2,18},{3,19},{4,20},{5,21},{6,22},{7,23},{8,9},{9,8... | collective-permute-start | bytes 294920 | tf_op jit(solution)/shard_map/ppermute | solution.py:336
  50.4 10.3 %collective-permute-start.16 = (bf16[12,32,128]{2,1,0:T(8,128)(2,1)S(1)}, bf16[12,32,128]{2,1,0:T(8,128)(2,1)S(1)}, u32[]{:S(2)}, u32[]{:S(2)}) collective-permute-start(bf16[12,32,128]{2,1,0:T(8,128)(2,1)S(1)} %get-tuple-element.94), channel_id=1, source_target_pairs={{0,6},{1,7},{2,4},{3,5},{4,2},{5,3},{6,0},{7,1},{8,15},{9,14},{10,... | collective-permute-start | bytes 294920 | tf_op jit(solution)/shard_map/ppermute | solution.py:336
  54.1 7.9 %collective-permute-start.17 = (bf16[12,32,128]{2,1,0:T(8,128)(2,1)S(1)}, bf16[12,32,128]{2,1,0:T(8,128)(2,1)S(1)}, u32[]{:S(2)}, u32[]{:S(2)}) collective-permute-start(bf16[12,32,128]{2,1,0:T(8,128)(2,1)S(1)} %get-tuple-element.94), channel_id=1, source_target_pairs={{0,4},{1,5},{2,6},{3,7},{4,0},{5,1},{6,2},{7,3},{8,13},{9,12},{10,... | collective-permute-start | bytes 294920 | tf_op jit(solution)/shard_map/ppermute | solution.py:336
  54.1 7.9 %collective-permute-start.18 = (bf16[12,32,128]{2,1,0:T(8,128)(2,1)S(1)}, bf16[12,32,128]{2,1,0:T(8,128)(2,1)S(1)}, u32[]{:S(2)}, u32[]{:S(2)}) collective-permute-start(bf16[12,32,128]{2,1,0:T(8,128)(2,1)S(1)} %get-tuple-element.94), channel_id=1, source_target_pairs={{0,2},{1,3},{2,0},{3,1},{4,6},{5,7},{6,4},{7,5},{8,11},{9,10},{10,... | collective-permute-start | bytes 294920 | tf_op jit(solution)/shard_map/ppermute | solution.py:336
  54.8 1.5 %collective-permute-start.19 = (bf16[12,32,128]{2,1,0:T(8,128)(2,1)S(1)}, bf16[12,32,128]{2,1,0:T(8,128)(2,1)S(1)}, u32[]{:S(2)}, u32[]{:S(2)}) collective-permute-start(bf16[12,32,128]{2,1,0:T(8,128)(2,1)S(1)} %collective-permute-done.15), channel_id=1, source_target_pairs={{0,8},{8,0},{16,24},{24,16},{1,9},{9,1},{17,25},{25,17},{2,10},{10... | collective-permute-start | bytes 294920 | tf_op jit(solution)/shard_map/ppermute | solution.py:339
  62.1 1.4 %collective-permute-start.20 = (bf16[18,32,128]{2,1,0:T(8,128)(2,1)S(1)}, bf16[18,32,128]{2,1,0:T(8,128)(2,1)S(1)}, u32[]{:S(2)}, u32[]{:S(2)}) collective-permute-start(bf16[18,32,128]{2,1,0:T(8,128)(2,1)S(1)} %pad_maximum_fusion.27), channel_id=1, source_target_pairs={{0,8},{8,0},{16,24},{24,16},{1,9},{9,1},{17,25},{25,17},{2,10},{10... | collective-permute-start | bytes 442376 | tf_op jit(solution)/shard_map/ppermute | solution.py:339
  64.0 1.5 %collective-permute-start.21 = (bf16[26,32,128]{2,1,0:T(8,128)(2,1)S(1)}, bf16[26,32,128]{2,1,0:T(8,128)(2,1)S(1)}, u32[]{:S(2)}, u32[]{:S(2)}) collective-permute-start(bf16[26,32,128]{2,1,0:T(8,128)(2,1)S(1)} %pad_maximum_fusion.22), channel_id=1, source_target_pairs={{0,8},{8,0},{16,24},{24,16},{1,9},{9,1},{17,25},{25,17},{2,10},{10... | collective-permute-start | bytes 638984 | tf_op jit(solution)/shard_map/ppermute | solution.py:339
  65.7 10.8 %collective-permute-start.22 = (bf16[14,32,128]{2,1,0:T(8,128)(2,1)S(1)}, bf16[14,32,128]{2,1,0:T(8,128)(2,1)S(1)}, u32[]{:S(2)}, u32[]{:S(2)}) collective-permute-start(bf16[14,32,128]{2,1,0:T(8,128)(2,1)S(1)} %get-tuple-element.210), channel_id=1, source_target_pairs={{0,6},{1,7},{2,4},{3,5},{4,2},{5,3},{6,0},{7,1},{8,15},{9,14},{10,... | collective-permute-start | bytes 344072 | tf_op jit(solution)/shard_map/ppermute | solution.py:336
  68.5 11.0 %collective-permute-start.23 = (bf16[14,32,128]{2,1,0:T(8,128)(2,1)S(1)}, bf16[14,32,128]{2,1,0:T(8,128)(2,1)S(1)}, u32[]{:S(2)}, u32[]{:S(2)}) collective-permute-start(bf16[14,32,128]{2,1,0:T(8,128)(2,1)S(1)} %get-tuple-element.211), channel_id=1, source_target_pairs={{0,4},{1,5},{2,6},{3,7},{4,0},{5,1},{6,2},{7,3},{8,13},{9,12},{10,... | collective-permute-start | bytes 344072 | tf_op jit(solution)/shard_map/ppermute | solution.py:336
  68.8 10.7 %collective-permute-start.24 = (bf16[14,32,128]{2,1,0:T(8,128)(2,1)S(1)}, bf16[14,32,128]{2,1,0:T(8,128)(2,1)S(1)}, u32[]{:S(2)}, u32[]{:S(2)}) collective-permute-start(bf16[14,32,128]{2,1,0:T(8,128)(2,1)S(1)} %get-tuple-element.212), channel_id=1, source_target_pairs={{0,2},{1,3},{2,0},{3,1},{4,6},{5,7},{6,4},{7,5},{8,11},{9,10},{10,... | collective-permute-start | bytes 344072 | tf_op jit(solution)/shard_map/ppermute | solution.py:336
  70.2 9.3 %collective-permute-start.25 = (bf16[14,32,128]{2,1,0:T(8,128)(2,1)S(1)}, bf16[14,32,128]{2,1,0:T(8,128)(2,1)S(1)}, u32[]{:S(2)}, u32[]{:S(2)}) collective-permute-start(bf16[14,32,128]{2,1,0:T(8,128)(2,1)S(1)} %get-tuple-element.213), channel_id=1, source_target_pairs={{8,9},{9,8},{10,11},{11,10},{12,13},{13,12},{14,15},{15,14},{24,25... | collective-permute-start | bytes 344072 | tf_op jit(solution)/shard_map/ppermute | solution.py:336
  75.3 5.7 %collective-permute-start.27 = (bf16[12,32,128]{2,1,0:T(8,128)(2,1)S(1)}, bf16[12,32,128]{2,1,0:T(8,128)(2,1)S(1)}, u32[]{:S(2)}, u32[]{:S(2)}) collective-permute-start(bf16[12,32,128]{2,1,0:T(8,128)(2,1)S(1)} %slice.891), channel_id=1, source_target_pairs={{0,16},{1,17},{2,18},{3,19},{4,20},{5,21},{6,22},{7,23},{8,24},{9,... | collective-permute-start | bytes 294920 | tf_op jit(solution)/shard_map/ppermute | solution.py:336
  79.7 3.8 %collective-permute-start.26 = (f32[32,128]{1,0:T(8,128)S(1)}, f32[32,128]{1,0:T(8,128)S(1)}, u32[]{:S(2)}, u32[]{:S(2)}) collective-permute-start(f32[32,128]{1,0:T(8,128)S(1)} %select_add_fusion.2), channel_id=1, source_target_pairs={{0,16},{1,17},{2,18},{3,19},{4,20},{5,21},{6,22},{7,23},{8,24},{9,... | collective-permute-start | bytes 49160 | tf_op jit(solution)/shard_map/ppermute | solution.py:336
  83.5 1.5 %collective-permute-start.28 = (f32[13,32,128]{2,1,0:T(8,128)S(1)}, f32[13,32,128]{2,1,0:T(8,128)S(1)}, u32[]{:S(2)}, u32[]{:S(2)}) collective-permute-start(f32[13,32,128]{2,1,0:T(8,128)S(1)} %pad_maximum_fusion.23), channel_id=1, source_target_pairs={{0,8},{8,0},{16,24},{24,16},{1,9},{9,1},{17,25},{25,17},{2,10},{10... | collective-permute-start | bytes 638984 | tf_op jit(solution)/shard_map/ppermute | solution.py:339
  85.4 5.7 %collective-permute-start.29 = (bf16[12,32,128]{2,1,0:T(8,128)(2,1)S(1)}, bf16[12,32,128]{2,1,0:T(8,128)(2,1)S(1)}, u32[]{:S(2)}, u32[]{:S(2)}) collective-permute-start(bf16[12,32,128]{2,1,0:T(8,128)(2,1)S(1)} %get-tuple-element.90), channel_id=1, source_target_pairs={{0,16},{1,17},{2,18},{3,19},{4,20},{5,21},{6,22},{7,23},{8,9},{9,8... | collective-permute-start | bytes 294920 | tf_op jit(solution)/shard_map/ppermute | solution.py:336
  86.7 10.1 %collective-permute-start.30 = (bf16[12,32,128]{2,1,0:T(8,128)(2,1)S(1)}, bf16[12,32,128]{2,1,0:T(8,128)(2,1)S(1)}, u32[]{:S(2)}, u32[]{:S(2)}) collective-permute-start(bf16[12,32,128]{2,1,0:T(8,128)(2,1)S(1)} %get-tuple-element.90), channel_id=1, source_target_pairs={{0,6},{1,7},{2,4},{3,5},{4,2},{5,3},{6,0},{7,1},{8,15},{9,14},{10,... | collective-permute-start | bytes 294920 | tf_op jit(solution)/shard_map/ppermute | solution.py:336
  88.1 9.4 %collective-permute-start.31 = (bf16[12,32,128]{2,1,0:T(8,128)(2,1)S(1)}, bf16[12,32,128]{2,1,0:T(8,128)(2,1)S(1)}, u32[]{:S(2)}, u32[]{:S(2)}) collective-permute-start(bf16[12,32,128]{2,1,0:T(8,128)(2,1)S(1)} %get-tuple-element.90), channel_id=1, source_target_pairs={{0,4},{1,5},{2,6},{3,7},{4,0},{5,1},{6,2},{7,3},{8,13},{9,12},{10,... | collective-permute-start | bytes 294920 | tf_op jit(solution)/shard_map/ppermute | solution.py:336
  88.1 9.4 %collective-permute-start.32 = (bf16[12,32,128]{2,1,0:T(8,128)(2,1)S(1)}, bf16[12,32,128]{2,1,0:T(8,128)(2,1)S(1)}, u32[]{:S(2)}, u32[]{:S(2)}) collective-permute-start(bf16[12,32,128]{2,1,0:T(8,128)(2,1)S(1)} %get-tuple-element.90), channel_id=1, source_target_pairs={{0,2},{1,3},{2,0},{3,1},{4,6},{5,7},{6,4},{7,5},{8,11},{9,10},{10,... | collective-permute-start | bytes 294920 | tf_op jit(solution)/shard_map/ppermute | solution.py:336
  91.1 1.3 %collective-permute-start.33 = (bf16[12,32,128]{2,1,0:T(8,128)(2,1)S(1)}, bf16[12,32,128]{2,1,0:T(8,128)(2,1)S(1)}, u32[]{:S(2)}, u32[]{:S(2)}) collective-permute-start(bf16[12,32,128]{2,1,0:T(8,128)(2,1)S(1)} %collective-permute-done.29), channel_id=1, source_target_pairs={{0,8},{8,0},{16,24},{24,16},{1,9},{9,1},{17,25},{25,17},{2,10},{10... | collective-permute-start | bytes 294920 | tf_op jit(solution)/shard_map/ppermute | solution.py:339
  97.7 1.4 %collective-permute-start.34 = (bf16[18,32,128]{2,1,0:T(8,128)(2,1)S(1)}, bf16[18,32,128]{2,1,0:T(8,128)(2,1)S(1)}, u32[]{:S(2)}, u32[]{:S(2)}) collective-permute-start(bf16[18,32,128]{2,1,0:T(8,128)(2,1)S(1)} %pad_maximum_fusion.28), channel_id=1, source_target_pairs={{0,8},{8,0},{16,24},{24,16},{1,9},{9,1},{17,25},{25,17},{2,10},{10... | collective-permute-start | bytes 442376 | tf_op jit(solution)/shard_map/ppermute | solution.py:339
  99.6 1.5 %collective-permute-start.35 = (bf16[26,32,128]{2,1,0:T(8,128)(2,1)S(1)}, bf16[26,32,128]{2,1,0:T(8,128)(2,1)S(1)}, u32[]{:S(2)}, u32[]{:S(2)}) collective-permute-start(bf16[26,32,128]{2,1,0:T(8,128)(2,1)S(1)} %pad_maximum_fusion.24), channel_id=1, source_target_pairs={{0,8},{8,0},{16,24},{24,16},{1,9},{9,1},{17,25},{25,17},{2,10},{10... | collective-permute-start | bytes 638984 | tf_op jit(solution)/shard_map/ppermute | solution.py:339
  101.3 10.6 %collective-permute-start.36 = (bf16[14,32,128]{2,1,0:T(8,128)(2,1)S(1)}, bf16[14,32,128]{2,1,0:T(8,128)(2,1)S(1)}, u32[]{:S(2)}, u32[]{:S(2)}) collective-permute-start(bf16[14,32,128]{2,1,0:T(8,128)(2,1)S(1)} %get-tuple-element.206), channel_id=1, source_target_pairs={{0,6},{1,7},{2,4},{3,5},{4,2},{5,3},{6,0},{7,1},{8,15},{9,14},{10,... | collective-permute-start | bytes 344072 | tf_op jit(solution)/shard_map/ppermute | solution.py:336
  102.9 10.9 %collective-permute-start.37 = (bf16[14,32,128]{2,1,0:T(8,128)(2,1)S(1)}, bf16[14,32,128]{2,1,0:T(8,128)(2,1)S(1)}, u32[]{:S(2)}, u32[]{:S(2)}) collective-permute-start(bf16[14,32,128]{2,1,0:T(8,128)(2,1)S(1)} %get-tuple-element.207), channel_id=1, source_target_pairs={{0,4},{1,5},{2,6},{3,7},{4,0},{5,1},{6,2},{7,3},{8,13},{9,12},{10,... | collective-permute-start | bytes 344072 | tf_op jit(solution)/shard_map/ppermute | solution.py:336
  102.9 10.9 %collective-permute-start.38 = (bf16[14,32,128]{2,1,0:T(8,128)(2,1)S(1)}, bf16[14,32,128]{2,1,0:T(8,128)(2,1)S(1)}, u32[]{:S(2)}, u32[]{:S(2)}) collective-permute-start(bf16[14,32,128]{2,1,0:T(8,128)(2,1)S(1)} %get-tuple-element.208), channel_id=1, source_target_pairs={{0,2},{1,3},{2,0},{3,1},{4,6},{5,7},{6,4},{7,5},{8,11},{9,10},{10,... | collective-permute-start | bytes 344072 | tf_op jit(solution)/shard_map/ppermute | solution.py:336
  105.8 8.1 %collective-permute-start.39 = (bf16[14,32,128]{2,1,0:T(8,128)(2,1)S(1)}, bf16[14,32,128]{2,1,0:T(8,128)(2,1)S(1)}, u32[]{:S(2)}, u32[]{:S(2)}) collective-permute-start(bf16[14,32,128]{2,1,0:T(8,128)(2,1)S(1)} %get-tuple-element.209), channel_id=1, source_target_pairs={{8,9},{9,8},{10,11},{11,10},{12,13},{13,12},{14,15},{15,14},{24,25... | collective-permute-start | bytes 344072 | tf_op jit(solution)/shard_map/ppermute | solution.py:336
  110.7 4.7 %collective-permute-start.41 = (bf16[12,32,128]{2,1,0:T(8,128)(2,1)S(1)}, bf16[12,32,128]{2,1,0:T(8,128)(2,1)S(1)}, u32[]{:S(2)}, u32[]{:S(2)}) collective-permute-start(bf16[12,32,128]{2,1,0:T(8,128)(2,1)S(1)} %slice.890), channel_id=1, source_target_pairs={{0,16},{1,17},{2,18},{3,19},{4,20},{5,21},{6,22},{7,23},{8,24},{9,... | collective-permute-start | bytes 294920 | tf_op jit(solution)/shard_map/ppermute | solution.py:336
  114.0 3.8 %collective-permute-start.40 = (f32[32,128]{1,0:T(8,128)S(1)}, f32[32,128]{1,0:T(8,128)S(1)}, u32[]{:S(2)}, u32[]{:S(2)}) collective-permute-start(f32[32,128]{1,0:T(8,128)S(1)} %select_add_fusion), channel_id=1, source_target_pairs={{0,16},{1,17},{2,18},{3,19},{4,20},{5,21},{6,22},{7,23},{8,24},{9,... | collective-permute-start | bytes 49160 | tf_op jit(solution)/shard_map/ppermute | solution.py:336
  117.8 1.5 %collective-permute-start.42 = (f32[13,32,128]{2,1,0:T(8,128)S(1)}, f32[13,32,128]{2,1,0:T(8,128)S(1)}, u32[]{:S(2)}, u32[]{:S(2)}) collective-permute-start(f32[13,32,128]{2,1,0:T(8,128)S(1)} %pad_maximum_fusion.25), channel_id=1, source_target_pairs={{0,8},{8,0},{16,24},{24,16},{1,9},{9,1},{17,25},{25,17},{2,10},{10... | collective-permute-start | bytes 638984 | tf_op jit(solution)/shard_map/ppermute | solution.py:339

commit v5 on v4

--- a/solution.py
+++ b/solution.py
@@ -10,6 +10,7 @@
 
 PER_ROW = 5
 ITERS = 3
+DOTS = 3
 MESH_AXES = ("row", "col")
 
 coupling = 0.2
@@ -92,7 +93,7 @@
 
 
 def first_row_kernel(
-    per, col_of, slots, loads, place, field, source, out, degree, col_degree, squares, row_blocks, tiles, blocks,
+    per, col_of, slots, loads, place, field, source, out, degree, col_degree, row_blocks, tiles, blocks,
     semaphores, back_semaphores,
 ):
     copies = start_copies(source, tiles, semaphores)
@@ -102,7 +103,6 @@
     tasks = out.shape[1]
     out[...] = jnp.zeros_like(out)
     degree[...] = jnp.zeros_like(degree)
-    squares[...] = jnp.zeros_like(squares)
     col_degree[...] = jnp.zeros_like(col_degree)
 
     def add_columns(s):
@@ -122,7 +122,6 @@
         total = jnp.dot(held, blocks[i], preferred_element_type=jnp.float32)
         out[place[i]] = total[:tasks].astype(out.dtype)
         degree[place[i]] = total[tasks : tasks + 8]
-        squares[...] += total[tasks + 16 :]
 
     part = count // len(back)
     for g, copy in enumerate(back):
@@ -194,16 +193,15 @@
             jax.ShapeDtypeStruct((out_tiles, tasks, tile_size), field.dtype),
             jax.ShapeDtypeStruct((out_tiles, 8, tile_size), jnp.float32),
             jax.ShapeDtypeStruct((field.shape[0], 8, tile_size), jnp.float32),
-            jax.ShapeDtypeStruct((tasks, tile_size), jnp.float32),
             jax.ShapeDtypeStruct(blocks, tiles.dtype),
         ),
         in_specs=[IN_SMEM] * 4 + [IN_VMEM, IN_HBM],
-        out_specs=(IN_VMEM, IN_VMEM, IN_VMEM, IN_VMEM, IN_HBM),
+        out_specs=(IN_VMEM, IN_VMEM, IN_VMEM, IN_HBM),
         scratch_shapes=[
             pltpu.VMEM(tiles.shape, tiles.dtype),
             pltpu.VMEM(blocks, tiles.dtype),
             pltpu.SemaphoreType.DMA((parts_of(slots, 8),)),
-            pltpu.SemaphoreType.DMA((parts_of(count, 6),)),
+            pltpu.SemaphoreType.DMA((parts_of(count, 12),)),
         ],
         compiler_params=PARAMS,
         cost_estimate=cost(field, tiles),
@@ -225,8 +223,16 @@
     )(*lists[1:], field, blocks)
 
 
-def lists_kernel(own_tiles, row_per, col_per, empty, here, row_ids, col_ids, *rest):
-    by_row, by_row_loads, by_col, by_col_loads, col_of, ids = rest
+def lists_kernel(own_tiles, row_per, col_per, empty, here, row_source, col_source, *rest):
+    by_row, by_row_loads, by_col, by_col_loads, col_of, ids, row_ids, col_ids, semaphores = rest
+    copies = [
+        pltpu.make_async_copy(row_source, row_ids, semaphores.at[0]),
+        pltpu.make_async_copy(col_source, col_ids, semaphores.at[1]),
+    ]
+    for copy in copies:
+        copy.start()
+    for copy in copies:
+        copy.wait()
     slots = row_ids.shape[1]
     size = ids.shape[1]
     lane = lax.broadcasted_iota(jnp.int32, (1, slots), 1)
@@ -269,10 +275,15 @@
     return pl.pallas_call(
         functools.partial(lists_kernel, own_tiles, row_per, col_per, empty),
         out_shape=[jax.ShapeDtypeStruct((1, size), jnp.int32)] * 5,
-        in_specs=[IN_SMEM, IN_VMEM, IN_VMEM],
+        in_specs=[IN_SMEM, IN_HBM, IN_HBM],
         out_specs=[IN_VMEM] * 5,
-        scratch_shapes=[pltpu.VMEM((8, size), jnp.int32)],
-        compiler_params=pltpu.CompilerParams(vmem_limit_bytes=4 * 2**20),
+        scratch_shapes=[
+            pltpu.VMEM((8, size), jnp.int32),
+            pltpu.VMEM(row_ids.shape, jnp.int32),
+            pltpu.VMEM(row_ids.shape, jnp.int32),
+            pltpu.SemaphoreType.DMA((2,)),
+        ],
+        compiler_params=PARAMS,
     )(here, row_ids, col_ids)
 
 
@@ -378,10 +389,8 @@
     def empty_tile(field):
         return jnp.zeros((1,) + field.shape[1:], field.dtype)
 
-    def with_rows(field):
-        ones = jnp.ones((field.shape[0] - 1, 16, tile_size), field.dtype)
-        squares = (field[:-1].astype(jnp.float32) ** 2).astype(field.dtype)
-        field = jnp.concatenate([field[:-1], ones, squares], axis=1)
+    def with_ones(field):
+        field = jnp.pad(field[:-1], ((0, 0), (0, 16), (0, 0)), constant_values=1)
         return jnp.pad(field, ((0, 1), (0, 0), (0, 0)))
 
     def pack(degree):
@@ -389,6 +398,15 @@
 
     def unpack(tiles, count):
         return join(tiles_to_rows(tiles, 2 * count).reshape(2, count, tile_size))
+
+    def pack_dots(dots):
+        parts = addends(dots, 2)
+        return (parts[0] + jnp.pad(parts[1, :, :-DOTS], ((0, 0), (DOTS, 0))))[None]
+
+    def unpack_dots(tile):
+        tile = tile.astype(jnp.float32)
+        tile = tile + jnp.pad(tile[:, DOTS:], ((0, 0), (0, DOTS)))
+        return jnp.where(lax.broadcasted_iota(jnp.int32, tile.shape, 1) < DOTS, tile, 0.0)
 
     def inner(a, b):
         return jnp.sum(a.astype(jnp.float32) * b.astype(jnp.float32), axis=(0, 2))[:, None]
@@ -423,8 +441,8 @@
             col_pieces.append(jnp.where(core == 0, g[own_tiles:], other[:own_tiles]))
         col_field = jnp.concatenate(col_pieces + [empty_tile(pair)])
         if first:
-            forward, row_degree, col_degree, squares, row_blocks = first_row_product(
-                col_of, by_row, with_rows(col_field), tiles, row_pieces, task_count
+            forward, row_degree, col_degree, row_blocks = first_row_product(
+                col_of, by_row, with_ones(col_field), tiles, row_pieces, task_count
             )
         else:
             forward = next_product(by_row, col_field, row_blocks, row_pieces, low)
@@ -442,27 +460,29 @@
             weights = 0.5 * coupling * row_degree[:, None]
             curve_part = coupling * curve_part
             curve_part += inner(row_field[:-1].astype(jnp.float32) ** 2, weights)
-            curve_part += 0.5 * coupling * jnp.sum(squares, axis=1, keepdims=True)
+            col_degree = jnp.sum(col_degree[:-1], axis=1)
+            weights = 0.5 * coupling * col_degree[:, None]
+            curve_part += inner(col_field[:-1].astype(jnp.float32) ** 2, weights)
             dots = as_tile([norm, norm + curve_part])
         else:
             weighted = inner(scale[own] * residual[own], residual[own])
             along = inner(residual[own], image[own])
             dots = as_tile([norm, weighted + coupling * curve_part, along])
 
-        parts = [forward[own_tiles + low_part :], addends(dots, 2)]
-        if first:
-            col_degree = jnp.sum(col_degree[:-1], axis=1).reshape(chip_rows, chip, tile_size)
+        parts = [forward[own_tiles + low_part :], pack_dots(dots)]
+        if first:
+            col_degree = col_degree.reshape(chip_rows, chip, tile_size)
             parts.append(pack(row_degree[own_tiles + low_part :]))
         swapped = plan.swap(jnp.concatenate(parts))
         swapped, row_field = lax.optimization_barrier((swapped, row_field))
         if first:
-            other_degree = unpack(swapped[low_part + 2 :], low_part)
+            other_degree = unpack(swapped[low_part + 1 :], low_part)
         if first:
             backward, col_blocks = first_col_product(by_col, row_field, tiles, col_tiles)
         else:
             backward = next_product(by_col, row_field, col_blocks, col_tiles, jnp.float32)
-        dots = dots + join(swapped[low_part : low_part + 2])
-        dots_low = addends(dots, 2)
+        dots = dots + unpack_dots(swapped[low_part])
+        dots_low = pack_dots(dots)
         mine_products = forward[own]
         messages = []
         order = list(range(plan.count))
@@ -480,7 +500,7 @@
         for m, by_core in enumerate(plan.row_steps, 1):
             returned.append(plan.send(backward[m].astype(low), (by_core,) * 2))
         total = sum(m.astype(jnp.float32) for m in messages)
-        dots = jnp.where(core == 0, dots, 0.0) + jnp.sum(total[chip : chip + 2], axis=0)
+        dots = jnp.where(core == 0, dots, 0.0) + unpack_dots(total[chip])
         dots_mine = dots
         degree_back = col_degree[0] if first else None
         for m, by_core in enumerate(plan.row_steps, 1):
@@ -490,7 +510,7 @@
             if first:
                 degree_back = degree_back + back[task_count:]
         if first:
-            degree = unpack(total[chip + 2 :], chip) + degree_back
+            degree = unpack(total[chip + 1 :], chip) + degree_back
             degree += jnp.pad(row_degree[own], ((0, own_tiles), (0, 0)))
         total = total[:chip] + backward[0]
         total += jnp.pad(mine_products.astype(jnp.float32), ((0, own_tiles), (0, 0), (0, 0)))

time: 121 us -> 119 us (0.983)
  waiting for transfers between devices: 26.6 us -> 24.1 us
    ppermute x30, waiting for transfers between devices: 14.5 us -> 11.5 us  [send(): return lax.ppermute(value, MESH_AXES, self.pairs(by_core))]
    ppermute x30, starting transfers between devices: 41.9 us -> 44.8 us  [send(): return lax.ppermute(value, MESH_AXES, self.pairs(by_core))]
    ppermute x13, starting transfers between devices: 6.52 us -> 4.48 us  [swap(): return lax.ppermute(value, 'row', [(r, r ^ 1) for r in range(self.rows)])]
    unnamed x31 -> x27, local copies, waits for them, and re-layouts: 2.87 us -> 2.8 us
  transfers between devices with their start and end apart: 43 -> 43, of which waited for: 19 -> 21; matrix products, arithmetic and copies ran while one was open for 3% -> 3% of each run, Pallas kernels for 28% -> 28%
where the time goes in v5:
time: 119 us
  starting transfers between devices  49.3 us (41%)
  Pallas kernels  34.2 us (29%)
  waiting for transfers between devices  24.1 us (20%)
  other arithmetic  5.74 us (5%)
  local copies, waits for them, and re-layouts  3.68 us (3%)
  between operations  2.27 us (2%)
    ppermute x30, starting transfers between devices, send(): return lax.ppermute(value, MESH_AXES, self.pairs(by_core))  44.8 us
    pallas_call x4, Pallas kernels, next_product(): pl.pallas_call(functools.partial(next_kernel, blocks.shape[1] // blocks.s...  16.9 us
    ppermute x13, waiting for transfers between devices, swap(): return lax.ppermute(value, 'row', [(r, r ^ 1) for r in range(self.rows)])  12.6 us
    ppermute x30, waiting for transfers between devices, send(): return lax.ppermute(value, MESH_AXES, self.pairs(by_core))  11.5 us
    pallas_call x1, Pallas kernels, first_row_product(): pl.pallas_call(functools.partial(first_row_kernel, slots // count), out_s...  8.04 us
    pallas_call x1, Pallas kernels, first_col_product(): pl.pallas_call(functools.partial(first_col_kernel, slots // count), out_s...  7.3 us
    ppermute x13, starting transfers between devices, swap(): return lax.ppermute(value, 'row', [(r, r ^ 1) for r in range(self.rows)])  4.48 us
    unnamed x27, local copies, waits for them, and re-layouts  2.8 us
  transfers between devices with their start and end apart: 43, of which 21 were waited for; matrix products, arithmetic and copies ran while one was open for 3% of the time, Pallas kernels for 28%

profile of v5, /device:TPU:0, one launch (start us, length us, event | category | flops | bytes accessed | tf_op | source)
XLA Modules:
  0.0 119.2 jit_solution(14898817727029067712)
XLA Ops:
  0.6 0.9 copy-done
  1.5 0.5 collective-permute-start
  2.9 0.7 broadcast_select_fusion.3
  3.7 2.6 %collective-permute-start.1 = (bf16[12,32,128]{2,1,0:T(8,128)(2,1)S(1)}, bf16[12,32,128]{2,1,0:T(8,128)(2,1)S(1)}, u32[]{:S(2)}, u32[]{:S(2)}) collective-permute-start(bf16[12,32,128]{2,1,0:T(8,128)(2,1)S(1)} %fusion.15), channel_id=1, source_target_pairs={{0,16},{1,17},{2,18},{3,19},{4,20},{5,21},{6,22},{7,23},{8,9},{9,8... | collective-permute-start | bytes 294920 | tf_op jit(solution)/shard_map/ppermute | solution.py:347
  6.4 0.7 copy-done.1
  7.0 0.7 copy-done.2
  7.7 1.3 %shard_map.86 = (s32[1,256]{1,0:T(1,128)S(1)}, s32[1,256]{1,0:T(1,128)S(1)}, s32[1,256]{1,0:T(1,128)S(1)}, s32[1,256]{1,0:T(1,128)S(1)}, s32[1,256]{1,0:T(1,128)S(1)}) custom-call(s32[11]{0:T(128)S(1)} %pad_add_fusion.here, s32[1,240]{1,0:T(1,128)S(1)} %bitcast.156, s32[1,240]{1,0:T(1,128)S(1)} %bitcast.157), custom_call_target="tpu_custom_call" | custom-call | tf_op jit(solution)/shard_map/pallas_call | solution.py:275
  9.3 3.8 %collective-permute-start.2 = (bf16[12,32,128]{2,1,0:T(8,128)(2,1)S(1)}, bf16[12,32,128]{2,1,0:T(8,128)(2,1)S(1)}, u32[]{:S(2)}, u32[]{:S(2)}) collective-permute-start(bf16[12,32,128]{2,1,0:T(8,128)(2,1)S(1)} %fusion.15), channel_id=1, source_target_pairs={{0,6},{1,7},{2,4},{3,5},{4,2},{5,3},{6,0},{7,1},{8,15},{9,14},{10,... | collective-permute-start | bytes 294920 | tf_op jit(solution)/shard_map/ppermute | solution.py:347
  13.1 0.7 collective-permute-start.4
  13.8 8.0 %shard_map.87 = (bf16[54,32,128]{2,1,0:T(8,128)(2,1)S(1)}, f32[54,8,128]{2,1,0:T(8,128)S(1)}, f32[25,8,128]{2,1,0:T(8,128)S(1)}, bf16[48,640,128]{2,1,0:T(8,128)(2,1)}) custom-call(s32[1,256]{1,0:T(1,128)S(1)} %get-tuple-element.46.col_of, s32[1,256]{1,0:T(1,128)S(1)} %get-tuple-element.47.slots, s32[1,256]{1,0:T(1,128)S(1)} %get-tuple-element.48.loads, ...), custom_call_target="tpu_custom_call" | custom-call | flops 3019898880 | bytes 7864320 | tf_op jit(solution)/shard_map/pallas_call | solution.py:190
  22.2 1.6 %collective-permute-start.6 = (bf16[18,32,128]{2,1,0:T(8,128)(2,1)S(1)}, bf16[18,32,128]{2,1,0:T(8,128)(2,1)S(1)}, u32[]{:S(2)}, u32[]{:S(2)}) collective-permute-start(bf16[18,32,128]{2,1,0:T(8,128)(2,1)S(1)} %pad_maximum_fusion.22), channel_id=1, source_target_pairs={{0,8},{8,0},{16,24},{24,16},{1,9},{9,1},{17,25},{25,17},{2,10},{10... | collective-permute-start | bytes 442376 | tf_op jit(solution)/shard_map/ppermute | solution.py:350
  24.2 0.6 collective-permute-done.6
  24.9 0.4 fusion
  25.4 0.4 collective-permute-start.7
  25.9 1.1 collective-permute-done.7
  27.7 0.7 collective-permute-start.10
  28.4 0.7 collective-permute-start.11
  29.1 3.0 %collective-permute-start.8 = (bf16[14,32,128]{2,1,0:T(8,128)(2,1)S(1)}, bf16[14,32,128]{2,1,0:T(8,128)(2,1)S(1)}, u32[]{:S(2)}, u32[]{:S(2)}) collective-permute-start(bf16[14,32,128]{2,1,0:T(8,128)(2,1)S(1)} %get-tuple-element.214), channel_id=1, source_target_pairs={{0,6},{1,7},{2,4},{3,5},{4,2},{5,3},{6,0},{7,1},{8,15},{9,14},{10,... | collective-permute-start | bytes 344072 | tf_op jit(solution)/shard_map/ppermute | solution.py:347
  32.1 0.6 collective-permute-start.9
  32.7 7.3 %shard_map.88 = (f32[24,32,128]{2,1,0:T(8,128)S(1)}, bf16[24,1280,128]{2,1,0:T(8,128)(2,1)}) custom-call(s32[1,256]{1,0:T(1,128)S(1)} %get-tuple-element.58.slots, s32[1,256]{1,0:T(1,128)S(1)} %get-tuple-element.59.loads, s32[24]{0:T(128)S(1)} %fusion.83.place, bf16[55,32,128]{2,1,0:T(8,128)(2,1)S(1)} %constant_dynamic-update-slice_fusion.7.field, ...), custom_call_target="tpu_custom_call" | custom-call | flops 2013265920 | bytes 7864320 | tf_op jit(solution)/shard_map/pallas_call | solution.py:167
  40.0 1.6 %collective-permute-start.13 = (bf16[12,32,128]{2,1,0:T(8,128)(2,1)S(1)}, bf16[12,32,128]{2,1,0:T(8,128)(2,1)S(1)}, u32[]{:S(2)}, u32[]{:S(2)}) collective-permute-start(bf16[12,32,128]{2,1,0:T(8,128)(2,1)S(1)} %slice.1022), channel_id=1, source_target_pairs={{0,16},{1,17},{2,18},{3,19},{4,20},{5,21},{6,22},{7,23},{8,24},{9,... | collective-permute-start | bytes 294920 | tf_op jit(solution)/shard_map/ppermute | solution.py:347
  41.6 1.4 %collective-permute-done.9 = bf16[14,32,128]{2,1,0:T(8,128)(2,1)S(1)} collective-permute-done((bf16[14,32,128]{2,1,0:T(8,128)(2,1)S(1)}, bf16[14,32,128]{2,1,0:T(8,128)(2,1)S(1)}, u32[]{:S(2)}, u32[]{:S(2)}) %collective-permute-start.9) | collective-permute-done | bytes 114720 | tf_op jit(solution)/shard_map/ppermute | solution.py:347
  43.2 1.6 %collective-permute-start.12 = (f32[44,128]{1,0:T(8,128)S(1)}, f32[44,128]{1,0:T(8,128)S(1)}, u32[]{:S(2)}, u32[]{:S(2)}) collective-permute-start(f32[44,128]{1,0:T(8,128)S(1)} %pad_maximum_fusion.25), channel_id=1, source_target_pairs={{0,16},{1,17},{2,18},{3,19},{4,20},{5,21},{6,22},{7,23},{8,24},{9,... | collective-permute-start | bytes 67592 | tf_op jit(solution)/shard_map/ppermute | solution.py:347
  45.0 2.3 %collective-permute-done.12 = f32[44,128]{1,0:T(8,128)S(1)} collective-permute-done((f32[44,128]{1,0:T(8,128)S(1)}, f32[44,128]{1,0:T(8,128)S(1)}, u32[]{:S(2)}, u32[]{:S(2)}) %collective-permute-start.12) | collective-permute-done | bytes 22560 | tf_op jit(solution)/shard_map/ppermute | solution.py:347
  47.4 1.5 %collective-permute-done.14 = f32[14,32,128]{2,1,0:T(8,128)S(1)} collective-permute-done((f32[14,32,128]{2,1,0:T(8,128)S(1)}, f32[14,32,128]{2,1,0:T(8,128)S(1)}, u32[]{:S(2)}, u32[]{:S(2)}) %collective-permute-start.14) | collective-permute-done | bytes 229408 | tf_op jit(solution)/shard_map/ppermute | solution.py:350
  49.2 1.6 %collective-permute-start.15 = (bf16[12,32,128]{2,1,0:T(8,128)(2,1)S(1)}, bf16[12,32,128]{2,1,0:T(8,128)(2,1)S(1)}, u32[]{:S(2)}, u32[]{:S(2)}) collective-permute-start(bf16[12,32,128]{2,1,0:T(8,128)(2,1)S(1)} %get-tuple-element.96), channel_id=1, source_target_pairs={{0,16},{1,17},{2,18},{3,19},{4,20},{5,21},{6,22},{7,23},{8,9},{9,8... | collective-permute-start | bytes 294920 | tf_op jit(solution)/shard_map/ppermute | solution.py:347
  50.8 3.4 %collective-permute-start.16 = (bf16[12,32,128]{2,1,0:T(8,128)(2,1)S(1)}, bf16[12,32,128]{2,1,0:T(8,128)(2,1)S(1)}, u32[]{:S(2)}, u32[]{:S(2)}) collective-permute-start(bf16[12,32,128]{2,1,0:T(8,128)(2,1)S(1)} %get-tuple-element.96), channel_id=1, source_target_pairs={{0,6},{1,7},{2,4},{3,5},{4,2},{5,3},{6,0},{7,1},{8,15},{9,14},{10,... | collective-permute-start | bytes 294920 | tf_op jit(solution)/shard_map/ppermute | solution.py:347
  54.2 1.1 collective-permute-start.18
  55.4 1.1 collective-permute-done.19
  56.6 4.2 %shard_map.89 = bf16[54,32,128]{2,1,0:T(8,128)(2,1)S(1)} custom-call(s32[1,256]{1,0:T(1,128)S(1)} %get-tuple-element.48.loads, s32[48]{0:T(128)S(1)} %fusion.82.place, bf16[25,32,128]{2,1,0:T(8,128)(2,1)S(1)} %pad_maximum_fusion.1.field, bf16[48,640,128]{2,1,0:T(8,128)(2,1)} %get-tuple-element.62.source), custom_call_target="tpu_custom_call" | custom-call | flops 2013265920 | bytes 7864320 | tf_op jit(solution)/shard_map/pallas_call | solution.py:212
  60.9 1.1 collective-permute-done.17
  62.2 1.3 %collective-permute-done.20 = bf16[18,32,128]{2,1,0:T(8,128)(2,1)S(1)} collective-permute-done((bf16[18,32,128]{2,1,0:T(8,128)(2,1)S(1)}, bf16[18,32,128]{2,1,0:T(8,128)(2,1)S(1)}, u32[]{:S(2)}, u32[]{:S(2)}) %collective-permute-start.20) | collective-permute-done | bytes 147488 | tf_op jit(solution)/shard_map/ppermute | solution.py:350
  63.6 0.2 multiply_reduce_fusion.1
  64.3 1.3 %collective-permute-done.21 = bf16[25,32,128]{2,1,0:T(8,128)(2,1)S(1)} collective-permute-done((bf16[25,32,128]{2,1,0:T(8,128)(2,1)S(1)}, bf16[25,32,128]{2,1,0:T(8,128)(2,1)S(1)}, u32[]{:S(2)}, u32[]{:S(2)}) %collective-permute-start.21) | collective-permute-done | bytes 204832 | tf_op jit(solution)/shard_map/ppermute | solution.py:350
  65.9 2.5 %collective-permute-start.22 = (bf16[13,32,128]{2,1,0:T(8,128)(2,1)S(1)}, bf16[13,32,128]{2,1,0:T(8,128)(2,1)S(1)}, u32[]{:S(2)}, u32[]{:S(2)}) collective-permute-start(bf16[13,32,128]{2,1,0:T(8,128)(2,1)S(1)} %get-tuple-element.210), channel_id=1, source_target_pairs={{0,6},{1,7},{2,4},{3,5},{4,2},{5,3},{6,0},{7,1},{8,15},{9,14},{10,... | collective-permute-start | bytes 319496 | tf_op jit(solution)/shard_map/ppermute | solution.py:347
  68.4 2.0 %collective-permute-start.24 = (bf16[13,32,128]{2,1,0:T(8,128)(2,1)S(1)}, bf16[13,32,128]{2,1,0:T(8,128)(2,1)S(1)}, u32[]{:S(2)}, u32[]{:S(2)}) collective-permute-start(bf16[13,32,128]{2,1,0:T(8,128)(2,1)S(1)} %get-tuple-element.212), channel_id=1, source_target_pairs={{0,2},{1,3},{2,0},{3,1},{4,6},{5,7},{6,4},{7,5},{8,11},{9,10},{10,... | collective-permute-start | bytes 319496 | tf_op jit(solution)/shard_map/ppermute | solution.py:347
  70.4 0.8 collective-permute-start.25
  71.2 4.2 %shard_map.90 = f32[24,32,128]{2,1,0:T(8,128)S(1)} custom-call(s32[1,256]{1,0:T(1,128)S(1)} %get-tuple-element.59.loads, s32[24]{0:T(128)S(1)} %fusion.83.place, bf16[55,32,128]{2,1,0:T(8,128)(2,1)S(1)} %constant_dynamic-update-slice_fusion.22.field, bf16[24,1280,128]{2,1,0:T(8,128)(2,1)} %get-tuple-element.69.source), custom_call_target="tpu_custom_call" | custom-call | flops 2013265920 | bytes 7864320 | tf_op jit(solution)/shard_map/pallas_call | solution.py:212
  75.5 1.3 %collective-permute-start.27 = (bf16[12,32,128]{2,1,0:T(8,128)(2,1)S(1)}, bf16[12,32,128]{2,1,0:T(8,128)(2,1)S(1)}, u32[]{:S(2)}, u32[]{:S(2)}) collective-permute-start(bf16[12,32,128]{2,1,0:T(8,128)(2,1)S(1)} %slice.1021), channel_id=1, source_target_pairs={{0,16},{1,17},{2,18},{3,19},{4,20},{5,21},{6,22},{7,23},{8,24},{9,... | collective-permute-start | bytes 294920 | tf_op jit(solution)/shard_map/ppermute | solution.py:347
  76.8 1.4 %collective-permute-done.23 = bf16[13,32,128]{2,1,0:T(8,128)(2,1)S(1)} collective-permute-done((bf16[13,32,128]{2,1,0:T(8,128)(2,1)S(1)}, bf16[13,32,128]{2,1,0:T(8,128)(2,1)S(1)}, u32[]{:S(2)}, u32[]{:S(2)}) %collective-permute-start.23) | collective-permute-done | bytes 106528 | tf_op jit(solution)/shard_map/ppermute | solution.py:347
  78.4 2.1 %collective-permute-start.26 = (f32[32,128]{1,0:T(8,128)S(1)}, f32[32,128]{1,0:T(8,128)S(1)}, u32[]{:S(2)}, u32[]{:S(2)}) collective-permute-start(f32[32,128]{1,0:T(8,128)S(1)} %select_add_fusion.3), channel_id=1, source_target_pairs={{0,16},{1,17},{2,18},{3,19},{4,20},{5,21},{6,22},{7,23},{8,24},{9,... | collective-permute-start | bytes 49160 | tf_op jit(solution)/shard_map/ppermute | solution.py:347
  80.5 1.8 %collective-permute-done.26 = f32[32,128]{1,0:T(8,128)S(1)} collective-permute-done((f32[32,128]{1,0:T(8,128)S(1)}, f32[32,128]{1,0:T(8,128)S(1)}, u32[]{:S(2)}, u32[]{:S(2)}) %collective-permute-start.26) | collective-permute-done | bytes 16416 | tf_op jit(solution)/shard_map/ppermute | solution.py:347
  82.5 1.4 %collective-permute-done.28 = f32[13,32,128]{2,1,0:T(8,128)S(1)} collective-permute-done((f32[13,32,128]{2,1,0:T(8,128)S(1)}, f32[13,32,128]{2,1,0:T(8,128)S(1)}, u32[]{:S(2)}, u32[]{:S(2)}) %collective-permute-start.28) | collective-permute-done | bytes 213024 | tf_op jit(solution)/shard_map/ppermute | solution.py:350
  84.2 1.9 %collective-permute-start.29 = (bf16[12,32,128]{2,1,0:T(8,128)(2,1)S(1)}, bf16[12,32,128]{2,1,0:T(8,128)(2,1)S(1)}, u32[]{:S(2)}, u32[]{:S(2)}) collective-permute-start(bf16[12,32,128]{2,1,0:T(8,128)(2,1)S(1)} %get-tuple-element.90), channel_id=1, source_target_pairs={{0,16},{1,17},{2,18},{3,19},{4,20},{5,21},{6,22},{7,23},{8,9},{9,8... | collective-permute-start | bytes 294920 | tf_op jit(solution)/shard_map/ppermute | solution.py:347
  86.2 1.8 %collective-permute-start.30 = (bf16[12,32,128]{2,1,0:T(8,128)(2,1)S(1)}, bf16[12,32,128]{2,1,0:T(8,128)(2,1)S(1)}, u32[]{:S(2)}, u32[]{:S(2)}) collective-permute-start(bf16[12,32,128]{2,1,0:T(8,128)(2,1)S(1)} %get-tuple-element.90), channel_id=1, source_target_pairs={{0,6},{1,7},{2,4},{3,5},{4,2},{5,3},{6,0},{7,1},{8,15},{9,14},{10,... | collective-permute-start | bytes 294920 | tf_op jit(solution)/shard_map/ppermute | solution.py:347
  88.0 2.6 %collective-permute-start.32 = (bf16[12,32,128]{2,1,0:T(8,128)(2,1)S(1)}, bf16[12,32,128]{2,1,0:T(8,128)(2,1)S(1)}, u32[]{:S(2)}, u32[]{:S(2)}) collective-permute-start(bf16[12,32,128]{2,1,0:T(8,128)(2,1)S(1)} %get-tuple-element.90), channel_id=1, source_target_pairs={{0,2},{1,3},{2,0},{3,1},{4,6},{5,7},{6,4},{7,5},{8,11},{9,10},{10,... | collective-permute-start | bytes 294920 | tf_op jit(solution)/shard_map/ppermute | solution.py:347
  90.8 1.1 collective-permute-done.33
  92.0 4.2 %shard_map.91 = bf16[54,32,128]{2,1,0:T(8,128)(2,1)S(1)} custom-call(s32[1,256]{1,0:T(1,128)S(1)} %get-tuple-element.48.loads, s32[48]{0:T(128)S(1)} %fusion.82.place, bf16[25,32,128]{2,1,0:T(8,128)(2,1)S(1)} %pad_maximum_fusion.field, bf16[48,640,128]{2,1,0:T(8,128)(2,1)} %get-tuple-element.62.source), custom_call_target="tpu_custom_call" | custom-call | flops 2013265920 | bytes 7864320 | tf_op jit(solution)/shard_map/pallas_call | solution.py:212
  96.6 0.4 collective-permute-start.34
  97.0 1.0 collective-permute-done.34
  98.1 0.2 multiply_reduce_fusion
  98.6 0.4 collective-permute-start.35
  99.0 1.1 collective-permute-done.35
  100.4 2.2 %collective-permute-start.36 = (bf16[13,32,128]{2,1,0:T(8,128)(2,1)S(1)}, bf16[13,32,128]{2,1,0:T(8,128)(2,1)S(1)}, u32[]{:S(2)}, u32[]{:S(2)}) collective-permute-start(bf16[13,32,128]{2,1,0:T(8,128)(2,1)S(1)} %get-tuple-element.206), channel_id=1, source_target_pairs={{0,6},{1,7},{2,4},{3,5},{4,2},{5,3},{6,0},{7,1},{8,15},{9,14},{10,... | collective-permute-start | bytes 319496 | tf_op jit(solution)/shard_map/ppermute | solution.py:347
  102.7 2.2 %collective-permute-start.38 = (bf16[13,32,128]{2,1,0:T(8,128)(2,1)S(1)}, bf16[13,32,128]{2,1,0:T(8,128)(2,1)S(1)}, u32[]{:S(2)}, u32[]{:S(2)}) collective-permute-start(bf16[13,32,128]{2,1,0:T(8,128)(2,1)S(1)} %get-tuple-element.208), channel_id=1, source_target_pairs={{0,2},{1,3},{2,0},{3,1},{4,6},{5,7},{6,4},{7,5},{8,11},{9,10},{10,... | collective-permute-start | bytes 319496 | tf_op jit(solution)/shard_map/ppermute | solution.py:347
  104.9 0.7 collective-permute-start.39
  105.5 4.2 %shard_map.92 = f32[24,32,128]{2,1,0:T(8,128)S(1)} custom-call(s32[1,256]{1,0:T(1,128)S(1)} %get-tuple-element.59.loads, s32[24]{0:T(128)S(1)} %fusion.83.place, bf16[55,32,128]{2,1,0:T(8,128)(2,1)S(1)} %constant_dynamic-update-slice_fusion.37.field, bf16[24,1280,128]{2,1,0:T(8,128)(2,1)} %get-tuple-element.69.source), custom_call_target="tpu_custom_call" | custom-call | flops 2013265920 | bytes 7864320 | tf_op jit(solution)/shard_map/pallas_call | solution.py:212
  109.8 1.8 %collective-permute-start.41 = (bf16[12,32,128]{2,1,0:T(8,128)(2,1)S(1)}, bf16[12,32,128]{2,1,0:T(8,128)(2,1)S(1)}, u32[]{:S(2)}, u32[]{:S(2)}) collective-permute-start(bf16[12,32,128]{2,1,0:T(8,128)(2,1)S(1)} %slice.1020), channel_id=1, source_target_pairs={{0,16},{1,17},{2,18},{3,19},{4,20},{5,21},{6,22},{7,23},{8,24},{9,... | collective-permute-start | bytes 294920 | tf_op jit(solution)/shard_map/ppermute | solution.py:347
  111.6 1.1 collective-permute-done.37
  112.8 1.6 %collective-permute-start.40 = (f32[32,128]{1,0:T(8,128)S(1)}, f32[32,128]{1,0:T(8,128)S(1)}, u32[]{:S(2)}, u32[]{:S(2)}) collective-permute-start(f32[32,128]{1,0:T(8,128)S(1)} %select_add_fusion), channel_id=1, source_target_pairs={{0,16},{1,17},{2,18},{3,19},{4,20},{5,21},{6,22},{7,23},{8,24},{9,... | collective-permute-start | bytes 49160 | tf_op jit(solution)/shard_map/ppermute | solution.py:347
  114.6 2.1 %collective-permute-done.40 = f32[32,128]{1,0:T(8,128)S(1)} collective-permute-done((f32[32,128]{1,0:T(8,128)S(1)}, f32[32,128]{1,0:T(8,128)S(1)}, u32[]{:S(2)}, u32[]{:S(2)}) %collective-permute-start.40) | collective-permute-done | bytes 16416 | tf_op jit(solution)/shard_map/ppermute | solution.py:347
  116.7 0.4 collective-permute-start.42
  117.1 1.1 collective-permute-done.42
  118.5 0.7 shard_map.93
  (209 shorter events, 6.9 us)
Async XLA Ops:
  0.6 0.9 copy-start
  1.5 2.1 %collective-permute-start = (f32[6,32,128]{2,1,0:T(8,128)S(1)}, f32[6,32,128]{2,1,0:T(8,128)S(1)}, u32[]{:S(2)}, u32[]{:S(2)}) collective-permute-start(f32[6,32,128]{2,1,0:T(8,128)S(1)} %bitcast_bitcast_fusion), channel_id=1, source_target_pairs={{0,8},{8,0},{16,24},{24,16},{1,9},{9,1},{17,25},{25,17},{2,10},{10... | collective-permute-start | bytes 294920 | tf_op jit(solution)/shard_map/ppermute | solution.py:350
  3.7 5.3 %collective-permute-start.1 = (bf16[12,32,128]{2,1,0:T(8,128)(2,1)S(1)}, bf16[12,32,128]{2,1,0:T(8,128)(2,1)S(1)}, u32[]{:S(2)}, u32[]{:S(2)}) collective-permute-start(bf16[12,32,128]{2,1,0:T(8,128)(2,1)S(1)} %fusion.15), channel_id=1, source_target_pairs={{0,16},{1,17},{2,18},{3,19},{4,20},{5,21},{6,22},{7,23},{8,9},{9,8... | collective-permute-start | bytes 294920 | tf_op jit(solution)/shard_map/ppermute | solution.py:347
  6.4 0.7 copy-start.1
  7.0 0.7 copy-start.2
  9.0 4.7 %collective-permute-start.5 = (bf16[12,32,128]{2,1,0:T(8,128)(2,1)S(1)}, bf16[12,32,128]{2,1,0:T(8,128)(2,1)S(1)}, u32[]{:S(2)}, u32[]{:S(2)}) collective-permute-start(bf16[12,32,128]{2,1,0:T(8,128)(2,1)S(1)} %collective-permute-done.1), channel_id=1, source_target_pairs={{0,8},{8,0},{16,24},{24,16},{1,9},{9,1},{17,25},{25,17},{2,10},{10... | collective-permute-start | bytes 294920 | tf_op jit(solution)/shard_map/ppermute | solution.py:350
  9.3 12.7 %collective-permute-start.2 = (bf16[12,32,128]{2,1,0:T(8,128)(2,1)S(1)}, bf16[12,32,128]{2,1,0:T(8,128)(2,1)S(1)}, u32[]{:S(2)}, u32[]{:S(2)}) collective-permute-start(bf16[12,32,128]{2,1,0:T(8,128)(2,1)S(1)} %fusion.15), channel_id=1, source_target_pairs={{0,6},{1,7},{2,4},{3,5},{4,2},{5,3},{6,0},{7,1},{8,15},{9,14},{10,... | collective-permute-start | bytes 294920 | tf_op jit(solution)/shard_map/ppermute | solution.py:347
  13.1 9.0 %collective-permute-start.3 = (bf16[12,32,128]{2,1,0:T(8,128)(2,1)S(1)}, bf16[12,32,128]{2,1,0:T(8,128)(2,1)S(1)}, u32[]{:S(2)}, u32[]{:S(2)}) collective-permute-start(bf16[12,32,128]{2,1,0:T(8,128)(2,1)S(1)} %fusion.15), channel_id=1, source_target_pairs={{0,4},{1,5},{2,6},{3,7},{4,0},{5,1},{6,2},{7,3},{8,13},{9,12},{10,... | collective-permute-start | bytes 294920 | tf_op jit(solution)/shard_map/ppermute | solution.py:347
  13.1 9.0 %collective-permute-start.4 = (bf16[12,32,128]{2,1,0:T(8,128)(2,1)S(1)}, bf16[12,32,128]{2,1,0:T(8,128)(2,1)S(1)}, u32[]{:S(2)}, u32[]{:S(2)}) collective-permute-start(bf16[12,32,128]{2,1,0:T(8,128)(2,1)S(1)} %fusion.15), channel_id=1, source_target_pairs={{0,2},{1,3},{2,0},{3,1},{4,6},{5,7},{6,4},{7,5},{8,11},{9,10},{10,... | collective-permute-start | bytes 294920 | tf_op jit(solution)/shard_map/ppermute | solution.py:347
  22.1 22.7 %copy-start.3 = (pred[12]{0:T(512)(128)(4,1)S(1)}, pred[12]{0:T(512)(128)(4,1)}, u32[]{:S(2)}) copy-start(pred[12]{0:T(512)(128)(4,1)} %constant.88.clone.1) | copy-start | bytes 40
  22.2 2.6 %collective-permute-start.6 = (bf16[18,32,128]{2,1,0:T(8,128)(2,1)S(1)}, bf16[18,32,128]{2,1,0:T(8,128)(2,1)S(1)}, u32[]{:S(2)}, u32[]{:S(2)}) collective-permute-start(bf16[18,32,128]{2,1,0:T(8,128)(2,1)S(1)} %pad_maximum_fusion.22), channel_id=1, source_target_pairs={{0,8},{8,0},{16,24},{24,16},{1,9},{9,1},{17,25},{25,17},{2,10},{10... | collective-permute-start | bytes 442376 | tf_op jit(solution)/shard_map/ppermute | solution.py:350
  25.4 1.5 %collective-permute-start.7 = (bf16[27,32,128]{2,1,0:T(8,128)(2,1)S(1)}, bf16[27,32,128]{2,1,0:T(8,128)(2,1)S(1)}, u32[]{:S(2)}, u32[]{:S(2)}) collective-permute-start(bf16[27,32,128]{2,1,0:T(8,128)(2,1)S(1)} %pad_maximum_fusion.8), channel_id=1, source_target_pairs={{0,8},{8,0},{16,24},{24,16},{1,9},{9,1},{17,25},{25,17},{2,10},{10... | collective-permute-start | bytes 663560 | tf_op jit(solution)/shard_map/ppermute | solution.py:350
  27.7 14.0 %collective-permute-start.10 = (bf16[14,32,128]{2,1,0:T(8,128)(2,1)S(1)}, bf16[14,32,128]{2,1,0:T(8,128)(2,1)S(1)}, u32[]{:S(2)}, u32[]{:S(2)}) collective-permute-start(bf16[14,32,128]{2,1,0:T(8,128)(2,1)S(1)} %get-tuple-element.216), channel_id=1, source_target_pairs={{0,2},{1,3},{2,0},{3,1},{4,6},{5,7},{6,4},{7,5},{8,11},{9,10},{10,... | collective-permute-start | bytes 344072 | tf_op jit(solution)/shard_map/ppermute | solution.py:347
  28.4 13.2 %collective-permute-start.11 = (bf16[14,32,128]{2,1,0:T(8,128)(2,1)S(1)}, bf16[14,32,128]{2,1,0:T(8,128)(2,1)S(1)}, u32[]{:S(2)}, u32[]{:S(2)}) collective-permute-start(bf16[14,32,128]{2,1,0:T(8,128)(2,1)S(1)} %get-tuple-element.217), channel_id=1, source_target_pairs={{8,9},{9,8},{10,11},{11,10},{12,13},{13,12},{14,15},{15,14},{24,25... | collective-permute-start | bytes 344072 | tf_op jit(solution)/shard_map/ppermute | solution.py:347
  29.1 12.6 %collective-permute-start.8 = (bf16[14,32,128]{2,1,0:T(8,128)(2,1)S(1)}, bf16[14,32,128]{2,1,0:T(8,128)(2,1)S(1)}, u32[]{:S(2)}, u32[]{:S(2)}) collective-permute-start(bf16[14,32,128]{2,1,0:T(8,128)(2,1)S(1)} %get-tuple-element.214), channel_id=1, source_target_pairs={{0,6},{1,7},{2,4},{3,5},{4,2},{5,3},{6,0},{7,1},{8,15},{9,14},{10,... | collective-permute-start | bytes 344072 | tf_op jit(solution)/shard_map/ppermute | solution.py:347
  32.1 10.9 %collective-permute-start.9 = (bf16[14,32,128]{2,1,0:T(8,128)(2,1)S(1)}, bf16[14,32,128]{2,1,0:T(8,128)(2,1)S(1)}, u32[]{:S(2)}, u32[]{:S(2)}) collective-permute-start(bf16[14,32,128]{2,1,0:T(8,128)(2,1)S(1)} %get-tuple-element.215), channel_id=1, source_target_pairs={{0,4},{1,5},{2,6},{3,7},{4,0},{5,1},{6,2},{7,3},{8,13},{9,12},{10,... | collective-permute-start | bytes 344072 | tf_op jit(solution)/shard_map/ppermute | solution.py:347
  40.0 4.8 %collective-permute-start.13 = (bf16[12,32,128]{2,1,0:T(8,128)(2,1)S(1)}, bf16[12,32,128]{2,1,0:T(8,128)(2,1)S(1)}, u32[]{:S(2)}, u32[]{:S(2)}) collective-permute-start(bf16[12,32,128]{2,1,0:T(8,128)(2,1)S(1)} %slice.1022), channel_id=1, source_target_pairs={{0,16},{1,17},{2,18},{3,19},{4,20},{5,21},{6,22},{7,23},{8,24},{9,... | collective-permute-start | bytes 294920 | tf_op jit(solution)/shard_map/ppermute | solution.py:347
  43.2 4.0 %collective-permute-start.12 = (f32[44,128]{1,0:T(8,128)S(1)}, f32[44,128]{1,0:T(8,128)S(1)}, u32[]{:S(2)}, u32[]{:S(2)}) collective-permute-start(f32[44,128]{1,0:T(8,128)S(1)} %pad_maximum_fusion.25), channel_id=1, source_target_pairs={{0,16},{1,17},{2,18},{3,19},{4,20},{5,21},{6,22},{7,23},{8,24},{9,... | collective-permute-start | bytes 67592 | tf_op jit(solution)/shard_map/ppermute | solution.py:347
  47.3 1.6 %collective-permute-start.14 = (f32[14,32,128]{2,1,0:T(8,128)S(1)}, f32[14,32,128]{2,1,0:T(8,128)S(1)}, u32[]{:S(2)}, u32[]{:S(2)}) collective-permute-start(f32[14,32,128]{2,1,0:T(8,128)S(1)} %pad_maximum_fusion.7), channel_id=1, source_target_pairs={{0,8},{8,0},{16,24},{24,16},{1,9},{9,1},{17,25},{25,17},{2,10},{10... | collective-permute-start | bytes 688136 | tf_op jit(solution)/shard_map/ppermute | solution.py:350
  49.2 6.1 %collective-permute-start.15 = (bf16[12,32,128]{2,1,0:T(8,128)(2,1)S(1)}, bf16[12,32,128]{2,1,0:T(8,128)(2,1)S(1)}, u32[]{:S(2)}, u32[]{:S(2)}) collective-permute-start(bf16[12,32,128]{2,1,0:T(8,128)(2,1)S(1)} %get-tuple-element.96), channel_id=1, source_target_pairs={{0,16},{1,17},{2,18},{3,19},{4,20},{5,21},{6,22},{7,23},{8,9},{9,8... | collective-permute-start | bytes 294920 | tf_op jit(solution)/shard_map/ppermute | solution.py:347
  50.8 10.1 %collective-permute-start.16 = (bf16[12,32,128]{2,1,0:T(8,128)(2,1)S(1)}, bf16[12,32,128]{2,1,0:T(8,128)(2,1)S(1)}, u32[]{:S(2)}, u32[]{:S(2)}) collective-permute-start(bf16[12,32,128]{2,1,0:T(8,128)(2,1)S(1)} %get-tuple-element.96), channel_id=1, source_target_pairs={{0,6},{1,7},{2,4},{3,5},{4,2},{5,3},{6,0},{7,1},{8,15},{9,14},{10,... | collective-permute-start | bytes 294920 | tf_op jit(solution)/shard_map/ppermute | solution.py:347
  54.1 7.8 %collective-permute-start.17 = (bf16[12,32,128]{2,1,0:T(8,128)(2,1)S(1)}, bf16[12,32,128]{2,1,0:T(8,128)(2,1)S(1)}, u32[]{:S(2)}, u32[]{:S(2)}) collective-permute-start(bf16[12,32,128]{2,1,0:T(8,128)(2,1)S(1)} %get-tuple-element.96), channel_id=1, source_target_pairs={{0,4},{1,5},{2,6},{3,7},{4,0},{5,1},{6,2},{7,3},{8,13},{9,12},{10,... | collective-permute-start | bytes 294920 | tf_op jit(solution)/shard_map/ppermute | solution.py:347
  54.2 7.8 %collective-permute-start.18 = (bf16[12,32,128]{2,1,0:T(8,128)(2,1)S(1)}, bf16[12,32,128]{2,1,0:T(8,128)(2,1)S(1)}, u32[]{:S(2)}, u32[]{:S(2)}) collective-permute-start(bf16[12,32,128]{2,1,0:T(8,128)(2,1)S(1)} %get-tuple-element.96), channel_id=1, source_target_pairs={{0,2},{1,3},{2,0},{3,1},{4,6},{5,7},{6,4},{7,5},{8,11},{9,10},{10,... | collective-permute-start | bytes 294920 | tf_op jit(solution)/shard_map/ppermute | solution.py:347
  55.2 1.3 %collective-permute-start.19 = (bf16[12,32,128]{2,1,0:T(8,128)(2,1)S(1)}, bf16[12,32,128]{2,1,0:T(8,128)(2,1)S(1)}, u32[]{:S(2)}, u32[]{:S(2)}) collective-permute-start(bf16[12,32,128]{2,1,0:T(8,128)(2,1)S(1)} %collective-permute-done.15), channel_id=1, source_target_pairs={{0,8},{8,0},{16,24},{24,16},{1,9},{9,1},{17,25},{25,17},{2,10},{10... | collective-permute-start | bytes 294920 | tf_op jit(solution)/shard_map/ppermute | solution.py:350
  62.1 1.4 %collective-permute-start.20 = (bf16[18,32,128]{2,1,0:T(8,128)(2,1)S(1)}, bf16[18,32,128]{2,1,0:T(8,128)(2,1)S(1)}, u32[]{:S(2)}, u32[]{:S(2)}) collective-permute-start(bf16[18,32,128]{2,1,0:T(8,128)(2,1)S(1)} %pad_maximum_fusion.23), channel_id=1, source_target_pairs={{0,8},{8,0},{16,24},{24,16},{1,9},{9,1},{17,25},{25,17},{2,10},{10... | collective-permute-start | bytes 442376 | tf_op jit(solution)/shard_map/ppermute | solution.py:350
  64.1 1.5 %collective-permute-start.21 = (bf16[25,32,128]{2,1,0:T(8,128)(2,1)S(1)}, bf16[25,32,128]{2,1,0:T(8,128)(2,1)S(1)}, u32[]{:S(2)}, u32[]{:S(2)}) collective-permute-start(bf16[25,32,128]{2,1,0:T(8,128)(2,1)S(1)} %pad_maximum_fusion.19), channel_id=1, source_target_pairs={{0,8},{8,0},{16,24},{24,16},{1,9},{9,1},{17,25},{25,17},{2,10},{10... | collective-permute-start | bytes 614408 | tf_op jit(solution)/shard_map/ppermute | solution.py:350
  65.9 10.8 %collective-permute-start.22 = (bf16[13,32,128]{2,1,0:T(8,128)(2,1)S(1)}, bf16[13,32,128]{2,1,0:T(8,128)(2,1)S(1)}, u32[]{:S(2)}, u32[]{:S(2)}) collective-permute-start(bf16[13,32,128]{2,1,0:T(8,128)(2,1)S(1)} %get-tuple-element.210), channel_id=1, source_target_pairs={{0,6},{1,7},{2,4},{3,5},{4,2},{5,3},{6,0},{7,1},{8,15},{9,14},{10,... | collective-permute-start | bytes 319496 | tf_op jit(solution)/shard_map/ppermute | solution.py:347
  68.4 9.8 %collective-permute-start.23 = (bf16[13,32,128]{2,1,0:T(8,128)(2,1)S(1)}, bf16[13,32,128]{2,1,0:T(8,128)(2,1)S(1)}, u32[]{:S(2)}, u32[]{:S(2)}) collective-permute-start(bf16[13,32,128]{2,1,0:T(8,128)(2,1)S(1)} %get-tuple-element.211), channel_id=1, source_target_pairs={{0,4},{1,5},{2,6},{3,7},{4,0},{5,1},{6,2},{7,3},{8,13},{9,12},{10,... | collective-permute-start | bytes 319496 | tf_op jit(solution)/shard_map/ppermute | solution.py:347
  68.4 9.8 %collective-permute-start.24 = (bf16[13,32,128]{2,1,0:T(8,128)(2,1)S(1)}, bf16[13,32,128]{2,1,0:T(8,128)(2,1)S(1)}, u32[]{:S(2)}, u32[]{:S(2)}) collective-permute-start(bf16[13,32,128]{2,1,0:T(8,128)(2,1)S(1)} %get-tuple-element.212), channel_id=1, source_target_pairs={{0,2},{1,3},{2,0},{3,1},{4,6},{5,7},{6,4},{7,5},{8,11},{9,10},{10,... | collective-permute-start | bytes 319496 | tf_op jit(solution)/shard_map/ppermute | solution.py:347
  70.4 7.8 %collective-permute-start.25 = (bf16[13,32,128]{2,1,0:T(8,128)(2,1)S(1)}, bf16[13,32,128]{2,1,0:T(8,128)(2,1)S(1)}, u32[]{:S(2)}, u32[]{:S(2)}) collective-permute-start(bf16[13,32,128]{2,1,0:T(8,128)(2,1)S(1)} %get-tuple-element.213), channel_id=1, source_target_pairs={{8,9},{9,8},{10,11},{11,10},{12,13},{13,12},{14,15},{15,14},{24,25... | collective-permute-start | bytes 319496 | tf_op jit(solution)/shard_map/ppermute | solution.py:347
  75.5 5.0 %collective-permute-start.27 = (bf16[12,32,128]{2,1,0:T(8,128)(2,1)S(1)}, bf16[12,32,128]{2,1,0:T(8,128)(2,1)S(1)}, u32[]{:S(2)}, u32[]{:S(2)}) collective-permute-start(bf16[12,32,128]{2,1,0:T(8,128)(2,1)S(1)} %slice.1021), channel_id=1, source_target_pairs={{0,16},{1,17},{2,18},{3,19},{4,20},{5,21},{6,22},{7,23},{8,24},{9,... | collective-permute-start | bytes 294920 | tf_op jit(solution)/shard_map/ppermute | solution.py:347
  78.4 3.9 %collective-permute-start.26 = (f32[32,128]{1,0:T(8,128)S(1)}, f32[32,128]{1,0:T(8,128)S(1)}, u32[]{:S(2)}, u32[]{:S(2)}) collective-permute-start(f32[32,128]{1,0:T(8,128)S(1)} %select_add_fusion.3), channel_id=1, source_target_pairs={{0,16},{1,17},{2,18},{3,19},{4,20},{5,21},{6,22},{7,23},{8,24},{9,... | collective-permute-start | bytes 49160 | tf_op jit(solution)/shard_map/ppermute | solution.py:347
  82.3 1.5 %collective-permute-start.28 = (f32[13,32,128]{2,1,0:T(8,128)S(1)}, f32[13,32,128]{2,1,0:T(8,128)S(1)}, u32[]{:S(2)}, u32[]{:S(2)}) collective-permute-start(f32[13,32,128]{2,1,0:T(8,128)S(1)} %pad_maximum_fusion.17), channel_id=1, source_target_pairs={{0,8},{8,0},{16,24},{24,16},{1,9},{9,1},{17,25},{25,17},{2,10},{10... | collective-permute-start | bytes 638984 | tf_op jit(solution)/shard_map/ppermute | solution.py:350
  84.2 6.4 %collective-permute-start.29 = (bf16[12,32,128]{2,1,0:T(8,128)(2,1)S(1)}, bf16[12,32,128]{2,1,0:T(8,128)(2,1)S(1)}, u32[]{:S(2)}, u32[]{:S(2)}) collective-permute-start(bf16[12,32,128]{2,1,0:T(8,128)(2,1)S(1)} %get-tuple-element.90), channel_id=1, source_target_pairs={{0,16},{1,17},{2,18},{3,19},{4,20},{5,21},{6,22},{7,23},{8,9},{9,8... | collective-permute-start | bytes 294920 | tf_op jit(solution)/shard_map/ppermute | solution.py:347
  86.2 10.1 %collective-permute-start.30 = (bf16[12,32,128]{2,1,0:T(8,128)(2,1)S(1)}, bf16[12,32,128]{2,1,0:T(8,128)(2,1)S(1)}, u32[]{:S(2)}, u32[]{:S(2)}) collective-permute-start(bf16[12,32,128]{2,1,0:T(8,128)(2,1)S(1)} %get-tuple-element.90), channel_id=1, source_target_pairs={{0,6},{1,7},{2,4},{3,5},{4,2},{5,3},{6,0},{7,1},{8,15},{9,14},{10,... | collective-permute-start | bytes 294920 | tf_op jit(solution)/shard_map/ppermute | solution.py:347
  88.0 8.5 %collective-permute-start.31 = (bf16[12,32,128]{2,1,0:T(8,128)(2,1)S(1)}, bf16[12,32,128]{2,1,0:T(8,128)(2,1)S(1)}, u32[]{:S(2)}, u32[]{:S(2)}) collective-permute-start(bf16[12,32,128]{2,1,0:T(8,128)(2,1)S(1)} %get-tuple-element.90), channel_id=1, source_target_pairs={{0,4},{1,5},{2,6},{3,7},{4,0},{5,1},{6,2},{7,3},{8,13},{9,12},{10,... | collective-permute-start | bytes 294920 | tf_op jit(solution)/shard_map/ppermute | solution.py:347
  88.0 8.5 %collective-permute-start.32 = (bf16[12,32,128]{2,1,0:T(8,128)(2,1)S(1)}, bf16[12,32,128]{2,1,0:T(8,128)(2,1)S(1)}, u32[]{:S(2)}, u32[]{:S(2)}) collective-permute-start(bf16[12,32,128]{2,1,0:T(8,128)(2,1)S(1)} %get-tuple-element.90), channel_id=1, source_target_pairs={{0,2},{1,3},{2,0},{3,1},{4,6},{5,7},{6,4},{7,5},{8,11},{9,10},{10,... | collective-permute-start | bytes 294920 | tf_op jit(solution)/shard_map/ppermute | solution.py:347
  90.6 1.3 %collective-permute-start.33 = (bf16[12,32,128]{2,1,0:T(8,128)(2,1)S(1)}, bf16[12,32,128]{2,1,0:T(8,128)(2,1)S(1)}, u32[]{:S(2)}, u32[]{:S(2)}) collective-permute-start(bf16[12,32,128]{2,1,0:T(8,128)(2,1)S(1)} %collective-permute-done.29), channel_id=1, source_target_pairs={{0,8},{8,0},{16,24},{24,16},{1,9},{9,1},{17,25},{25,17},{2,10},{10... | collective-permute-start | bytes 294920 | tf_op jit(solution)/shard_map/ppermute | solution.py:350
  96.6 1.4 %collective-permute-start.34 = (bf16[18,32,128]{2,1,0:T(8,128)(2,1)S(1)}, bf16[18,32,128]{2,1,0:T(8,128)(2,1)S(1)}, u32[]{:S(2)}, u32[]{:S(2)}) collective-permute-start(bf16[18,32,128]{2,1,0:T(8,128)(2,1)S(1)} %pad_maximum_fusion.24), channel_id=1, source_target_pairs={{0,8},{8,0},{16,24},{24,16},{1,9},{9,1},{17,25},{25,17},{2,10},{10... | collective-permute-start | bytes 442376 | tf_op jit(solution)/shard_map/ppermute | solution.py:350
  98.6 1.5 %collective-permute-start.35 = (bf16[25,32,128]{2,1,0:T(8,128)(2,1)S(1)}, bf16[25,32,128]{2,1,0:T(8,128)(2,1)S(1)}, u32[]{:S(2)}, u32[]{:S(2)}) collective-permute-start(bf16[25,32,128]{2,1,0:T(8,128)(2,1)S(1)} %pad_maximum_fusion.20), channel_id=1, source_target_pairs={{0,8},{8,0},{16,24},{24,16},{1,9},{9,1},{17,25},{25,17},{2,10},{10... | collective-permute-start | bytes 614408 | tf_op jit(solution)/shard_map/ppermute | solution.py:350
  100.4 11.2 %collective-permute-start.36 = (bf16[13,32,128]{2,1,0:T(8,128)(2,1)S(1)}, bf16[13,32,128]{2,1,0:T(8,128)(2,1)S(1)}, u32[]{:S(2)}, u32[]{:S(2)}) collective-permute-start(bf16[13,32,128]{2,1,0:T(8,128)(2,1)S(1)} %get-tuple-element.206), channel_id=1, source_target_pairs={{0,6},{1,7},{2,4},{3,5},{4,2},{5,3},{6,0},{7,1},{8,15},{9,14},{10,... | collective-permute-start | bytes 319496 | tf_op jit(solution)/shard_map/ppermute | solution.py:347
  102.6 10.0 %collective-permute-start.37 = (bf16[13,32,128]{2,1,0:T(8,128)(2,1)S(1)}, bf16[13,32,128]{2,1,0:T(8,128)(2,1)S(1)}, u32[]{:S(2)}, u32[]{:S(2)}) collective-permute-start(bf16[13,32,128]{2,1,0:T(8,128)(2,1)S(1)} %get-tuple-element.207), channel_id=1, source_target_pairs={{0,4},{1,5},{2,6},{3,7},{4,0},{5,1},{6,2},{7,3},{8,13},{9,12},{10,... | collective-permute-start | bytes 319496 | tf_op jit(solution)/shard_map/ppermute | solution.py:347
  102.7 10.0 %collective-permute-start.38 = (bf16[13,32,128]{2,1,0:T(8,128)(2,1)S(1)}, bf16[13,32,128]{2,1,0:T(8,128)(2,1)S(1)}, u32[]{:S(2)}, u32[]{:S(2)}) collective-permute-start(bf16[13,32,128]{2,1,0:T(8,128)(2,1)S(1)} %get-tuple-element.208), channel_id=1, source_target_pairs={{0,2},{1,3},{2,0},{3,1},{4,6},{5,7},{6,4},{7,5},{8,11},{9,10},{10,... | collective-permute-start | bytes 319496 | tf_op jit(solution)/shard_map/ppermute | solution.py:347
  104.9 7.8 %collective-permute-start.39 = (bf16[13,32,128]{2,1,0:T(8,128)(2,1)S(1)}, bf16[13,32,128]{2,1,0:T(8,128)(2,1)S(1)}, u32[]{:S(2)}, u32[]{:S(2)}) collective-permute-start(bf16[13,32,128]{2,1,0:T(8,128)(2,1)S(1)} %get-tuple-element.209), channel_id=1, source_target_pairs={{8,9},{9,8},{10,11},{11,10},{12,13},{13,12},{14,15},{15,14},{24,25... | collective-permute-start | bytes 319496 | tf_op jit(solution)/shard_map/ppermute | solution.py:347
  109.8 4.7 %collective-permute-start.41 = (bf16[12,32,128]{2,1,0:T(8,128)(2,1)S(1)}, bf16[12,32,128]{2,1,0:T(8,128)(2,1)S(1)}, u32[]{:S(2)}, u32[]{:S(2)}) collective-permute-start(bf16[12,32,128]{2,1,0:T(8,128)(2,1)S(1)} %slice.1020), channel_id=1, source_target_pairs={{0,16},{1,17},{2,18},{3,19},{4,20},{5,21},{6,22},{7,23},{8,24},{9,... | collective-permute-start | bytes 294920 | tf_op jit(solution)/shard_map/ppermute | solution.py:347
  112.8 3.8 %collective-permute-start.40 = (f32[32,128]{1,0:T(8,128)S(1)}, f32[32,128]{1,0:T(8,128)S(1)}, u32[]{:S(2)}, u32[]{:S(2)}) collective-permute-start(f32[32,128]{1,0:T(8,128)S(1)} %select_add_fusion), channel_id=1, source_target_pairs={{0,16},{1,17},{2,18},{3,19},{4,20},{5,21},{6,22},{7,23},{8,24},{9,... | collective-permute-start | bytes 49160 | tf_op jit(solution)/shard_map/ppermute | solution.py:347
  116.7 1.5 %collective-permute-start.42 = (f32[13,32,128]{2,1,0:T(8,128)S(1)}, f32[13,32,128]{2,1,0:T(8,128)S(1)}, u32[]{:S(2)}, u32[]{:S(2)}) collective-permute-start(f32[13,32,128]{2,1,0:T(8,128)S(1)} %pad_maximum_fusion.18), channel_id=1, source_target_pairs={{0,8},{8,0},{16,24},{24,16},{1,9},{9,1},{17,25},{25,17},{2,10},{10... | collective-permute-start | bytes 638984 | tf_op jit(solution)/shard_map/ppermute | solution.py:350

commit v6 on v5

--- a/solution.py
+++ b/solution.py
@@ -116,10 +116,13 @@
 
     def one(i):
         base = i * per
+        turned = []
         for j in range(per):
-            blocks[i, pl.ds(j * tile_size, tile_size)] = tiles[slots[0, base + j]].T
+            turned.append(tiles[slots[0, base + j]].T)
+        turned = jnp.concatenate(turned, axis=0)
+        blocks[i] = turned
         held = gathered(field, loads, base, per)
-        total = jnp.dot(held, blocks[i], preferred_element_type=jnp.float32)
+        total = jnp.dot(held, turned, preferred_element_type=jnp.float32)
         out[place[i]] = total[:tasks].astype(out.dtype)
         degree[place[i]] = total[tasks : tasks + 8]
 

time: 119 us -> 119 us (level)
  no operation moved by 1% of the time
where the time goes in v6:
time: 119 us
  starting transfers between devices  48.7 us (41%)
  Pallas kernels  33.6 us (28%)
  waiting for transfers between devices  24.8 us (21%)
  other arithmetic  5.74 us (5%)
  local copies, waits for them, and re-layouts  3.68 us (3%)
  between operations  2.26 us (2%)
    ppermute x30, starting transfers between devices, send(): return lax.ppermute(value, MESH_AXES, self.pairs(by_core))  44.8 us
    pallas_call x4, Pallas kernels, next_product(): pl.pallas_call(functools.partial(next_kernel, blocks.shape[1] // blocks.s...  16.9 us
    ppermute x13, waiting for transfers between devices, swap(): return lax.ppermute(value, 'row', [(r, r ^ 1) for r in range(self.rows)])  12.7 us
    ppermute x30, waiting for transfers between devices, send(): return lax.ppermute(value, MESH_AXES, self.pairs(by_core))  12.1 us
    pallas_call x1, Pallas kernels, first_row_product(): pl.pallas_call(functools.partial(first_row_kernel, slots // count), out_s...  7.5 us
    pallas_call x1, Pallas kernels, first_col_product(): pl.pallas_call(functools.partial(first_col_kernel, slots // count), out_s...  7.31 us
    ppermute x13, starting transfers between devices, swap(): return lax.ppermute(value, 'row', [(r, r ^ 1) for r in range(self.rows)])  3.88 us
    unnamed x27, local copies, waits for them, and re-layouts  2.8 us
  transfers between devices with their start and end apart: 43, of which 21 were waited for; matrix products, arithmetic and copies ran while one was open for 3% of the time, Pallas kernels for 28%

profile of v6, /device:TPU:0, one launch (start us, length us, event | category | flops | bytes accessed | tf_op | source)
XLA Modules:
  0.0 118.7 jit_solution(7572207414996823147)
XLA Ops:
  0.6 0.9 copy-done
  1.5 0.5 collective-permute-start
  2.9 0.7 broadcast_select_fusion.3
  3.7 2.6 %collective-permute-start.1 = (bf16[12,32,128]{2,1,0:T(8,128)(2,1)S(1)}, bf16[12,32,128]{2,1,0:T(8,128)(2,1)S(1)}, u32[]{:S(2)}, u32[]{:S(2)}) collective-permute-start(bf16[12,32,128]{2,1,0:T(8,128)(2,1)S(1)} %fusion.15), channel_id=1, source_target_pairs={{0,16},{1,17},{2,18},{3,19},{4,20},{5,21},{6,22},{7,23},{8,9},{9,8... | collective-permute-start | bytes 294920 | tf_op jit(solution)/shard_map/ppermute | solution.py:350
  6.4 0.7 copy-done.1
  7.0 0.7 copy-done.2
  7.7 1.3 %shard_map.86 = (s32[1,256]{1,0:T(1,128)S(1)}, s32[1,256]{1,0:T(1,128)S(1)}, s32[1,256]{1,0:T(1,128)S(1)}, s32[1,256]{1,0:T(1,128)S(1)}, s32[1,256]{1,0:T(1,128)S(1)}) custom-call(s32[11]{0:T(128)S(1)} %pad_add_fusion.here, s32[1,240]{1,0:T(1,128)S(1)} %bitcast.156, s32[1,240]{1,0:T(1,128)S(1)} %bitcast.157), custom_call_target="tpu_custom_call" | custom-call | tf_op jit(solution)/shard_map/pallas_call | solution.py:278
  9.3 3.8 %collective-permute-start.2 = (bf16[12,32,128]{2,1,0:T(8,128)(2,1)S(1)}, bf16[12,32,128]{2,1,0:T(8,128)(2,1)S(1)}, u32[]{:S(2)}, u32[]{:S(2)}) collective-permute-start(bf16[12,32,128]{2,1,0:T(8,128)(2,1)S(1)} %fusion.15), channel_id=1, source_target_pairs={{0,6},{1,7},{2,4},{3,5},{4,2},{5,3},{6,0},{7,1},{8,15},{9,14},{10,... | collective-permute-start | bytes 294920 | tf_op jit(solution)/shard_map/ppermute | solution.py:350
  13.1 0.7 collective-permute-start.4
  13.8 7.5 %shard_map.87 = (bf16[54,32,128]{2,1,0:T(8,128)(2,1)S(1)}, f32[54,8,128]{2,1,0:T(8,128)S(1)}, f32[25,8,128]{2,1,0:T(8,128)S(1)}, bf16[48,640,128]{2,1,0:T(8,128)(2,1)}) custom-call(s32[1,256]{1,0:T(1,128)S(1)} %get-tuple-element.46.col_of, s32[1,256]{1,0:T(1,128)S(1)} %get-tuple-element.47.slots, s32[1,256]{1,0:T(1,128)S(1)} %get-tuple-element.48.loads, ...), custom_call_target="tpu_custom_call" | custom-call | flops 3019898880 | bytes 7864320 | tf_op jit(solution)/shard_map/pallas_call | solution.py:193
  21.4 0.7 collective-permute-done.3
  22.2 1.0 collective-permute-start.6
  23.6 0.6 collective-permute-done.6
  24.3 0.4 fusion
  24.9 0.4 collective-permute-start.7
  25.3 1.1 collective-permute-done.7
  27.1 0.8 collective-permute-start.10
  27.9 0.7 collective-permute-start.11
  28.6 3.0 %collective-permute-start.8 = (bf16[14,32,128]{2,1,0:T(8,128)(2,1)S(1)}, bf16[14,32,128]{2,1,0:T(8,128)(2,1)S(1)}, u32[]{:S(2)}, u32[]{:S(2)}) collective-permute-start(bf16[14,32,128]{2,1,0:T(8,128)(2,1)S(1)} %get-tuple-element.214), channel_id=1, source_target_pairs={{0,6},{1,7},{2,4},{3,5},{4,2},{5,3},{6,0},{7,1},{8,15},{9,14},{10,... | collective-permute-start | bytes 344072 | tf_op jit(solution)/shard_map/ppermute | solution.py:350
  31.6 0.6 collective-permute-start.9
  32.2 7.3 %shard_map.88 = (f32[24,32,128]{2,1,0:T(8,128)S(1)}, bf16[24,1280,128]{2,1,0:T(8,128)(2,1)}) custom-call(s32[1,256]{1,0:T(1,128)S(1)} %get-tuple-element.58.slots, s32[1,256]{1,0:T(1,128)S(1)} %get-tuple-element.59.loads, s32[24]{0:T(128)S(1)} %fusion.83.place, bf16[55,32,128]{2,1,0:T(8,128)(2,1)S(1)} %constant_dynamic-update-slice_fusion.7.field, ...), custom_call_target="tpu_custom_call" | custom-call | flops 2013265920 | bytes 7864320 | tf_op jit(solution)/shard_map/pallas_call | solution.py:170
  39.5 1.6 %collective-permute-start.13 = (bf16[12,32,128]{2,1,0:T(8,128)(2,1)S(1)}, bf16[12,32,128]{2,1,0:T(8,128)(2,1)S(1)}, u32[]{:S(2)}, u32[]{:S(2)}) collective-permute-start(bf16[12,32,128]{2,1,0:T(8,128)(2,1)S(1)} %slice.1022), channel_id=1, source_target_pairs={{0,16},{1,17},{2,18},{3,19},{4,20},{5,21},{6,22},{7,23},{8,24},{9,... | collective-permute-start | bytes 294920 | tf_op jit(solution)/shard_map/ppermute | solution.py:350
  41.1 1.4 %collective-permute-done.9 = bf16[14,32,128]{2,1,0:T(8,128)(2,1)S(1)} collective-permute-done((bf16[14,32,128]{2,1,0:T(8,128)(2,1)S(1)}, bf16[14,32,128]{2,1,0:T(8,128)(2,1)S(1)}, u32[]{:S(2)}, u32[]{:S(2)}) %collective-permute-start.9) | collective-permute-done | bytes 114720 | tf_op jit(solution)/shard_map/ppermute | solution.py:350
  42.7 1.6 %collective-permute-start.12 = (f32[44,128]{1,0:T(8,128)S(1)}, f32[44,128]{1,0:T(8,128)S(1)}, u32[]{:S(2)}, u32[]{:S(2)}) collective-permute-start(f32[44,128]{1,0:T(8,128)S(1)} %pad_maximum_fusion.25), channel_id=1, source_target_pairs={{0,16},{1,17},{2,18},{3,19},{4,20},{5,21},{6,22},{7,23},{8,24},{9,... | collective-permute-start | bytes 67592 | tf_op jit(solution)/shard_map/ppermute | solution.py:350
  44.5 2.2 %collective-permute-done.12 = f32[44,128]{1,0:T(8,128)S(1)} collective-permute-done((f32[44,128]{1,0:T(8,128)S(1)}, f32[44,128]{1,0:T(8,128)S(1)}, u32[]{:S(2)}, u32[]{:S(2)}) %collective-permute-start.12) | collective-permute-done | bytes 22560 | tf_op jit(solution)/shard_map/ppermute | solution.py:350
  46.9 1.5 %collective-permute-done.14 = f32[14,32,128]{2,1,0:T(8,128)S(1)} collective-permute-done((f32[14,32,128]{2,1,0:T(8,128)S(1)}, f32[14,32,128]{2,1,0:T(8,128)S(1)}, u32[]{:S(2)}, u32[]{:S(2)}) %collective-permute-start.14) | collective-permute-done | bytes 229408 | tf_op jit(solution)/shard_map/ppermute | solution.py:353
  48.7 1.6 %collective-permute-start.15 = (bf16[12,32,128]{2,1,0:T(8,128)(2,1)S(1)}, bf16[12,32,128]{2,1,0:T(8,128)(2,1)S(1)}, u32[]{:S(2)}, u32[]{:S(2)}) collective-permute-start(bf16[12,32,128]{2,1,0:T(8,128)(2,1)S(1)} %get-tuple-element.96), channel_id=1, source_target_pairs={{0,16},{1,17},{2,18},{3,19},{4,20},{5,21},{6,22},{7,23},{8,9},{9,8... | collective-permute-start | bytes 294920 | tf_op jit(solution)/shard_map/ppermute | solution.py:350
  50.2 3.4 %collective-permute-start.16 = (bf16[12,32,128]{2,1,0:T(8,128)(2,1)S(1)}, bf16[12,32,128]{2,1,0:T(8,128)(2,1)S(1)}, u32[]{:S(2)}, u32[]{:S(2)}) collective-permute-start(bf16[12,32,128]{2,1,0:T(8,128)(2,1)S(1)} %get-tuple-element.96), channel_id=1, source_target_pairs={{0,6},{1,7},{2,4},{3,5},{4,2},{5,3},{6,0},{7,1},{8,15},{9,14},{10,... | collective-permute-start | bytes 294920 | tf_op jit(solution)/shard_map/ppermute | solution.py:350
  53.7 1.0 collective-permute-start.18
  54.9 1.1 collective-permute-done.19
  56.1 4.2 %shard_map.89 = bf16[54,32,128]{2,1,0:T(8,128)(2,1)S(1)} custom-call(s32[1,256]{1,0:T(1,128)S(1)} %get-tuple-element.48.loads, s32[48]{0:T(128)S(1)} %fusion.82.place, bf16[25,32,128]{2,1,0:T(8,128)(2,1)S(1)} %pad_maximum_fusion.1.field, bf16[48,640,128]{2,1,0:T(8,128)(2,1)} %get-tuple-element.62.source), custom_call_target="tpu_custom_call" | custom-call | flops 2013265920 | bytes 7864320 | tf_op jit(solution)/shard_map/pallas_call | solution.py:215
  60.3 1.1 collective-permute-done.17
  61.7 1.3 %collective-permute-done.20 = bf16[18,32,128]{2,1,0:T(8,128)(2,1)S(1)} collective-permute-done((bf16[18,32,128]{2,1,0:T(8,128)(2,1)S(1)}, bf16[18,32,128]{2,1,0:T(8,128)(2,1)S(1)}, u32[]{:S(2)}, u32[]{:S(2)}) %collective-permute-start.20) | collective-permute-done | bytes 147488 | tf_op jit(solution)/shard_map/ppermute | solution.py:353
  63.1 0.2 multiply_reduce_fusion.1
  63.8 1.3 %collective-permute-done.21 = bf16[25,32,128]{2,1,0:T(8,128)(2,1)S(1)} collective-permute-done((bf16[25,32,128]{2,1,0:T(8,128)(2,1)S(1)}, bf16[25,32,128]{2,1,0:T(8,128)(2,1)S(1)}, u32[]{:S(2)}, u32[]{:S(2)}) %collective-permute-start.21) | collective-permute-done | bytes 204832 | tf_op jit(solution)/shard_map/ppermute | solution.py:353
  65.4 2.5 %collective-permute-start.22 = (bf16[13,32,128]{2,1,0:T(8,128)(2,1)S(1)}, bf16[13,32,128]{2,1,0:T(8,128)(2,1)S(1)}, u32[]{:S(2)}, u32[]{:S(2)}) collective-permute-start(bf16[13,32,128]{2,1,0:T(8,128)(2,1)S(1)} %get-tuple-element.210), channel_id=1, source_target_pairs={{0,6},{1,7},{2,4},{3,5},{4,2},{5,3},{6,0},{7,1},{8,15},{9,14},{10,... | collective-permute-start | bytes 319496 | tf_op jit(solution)/shard_map/ppermute | solution.py:350
  67.9 2.0 %collective-permute-start.24 = (bf16[13,32,128]{2,1,0:T(8,128)(2,1)S(1)}, bf16[13,32,128]{2,1,0:T(8,128)(2,1)S(1)}, u32[]{:S(2)}, u32[]{:S(2)}) collective-permute-start(bf16[13,32,128]{2,1,0:T(8,128)(2,1)S(1)} %get-tuple-element.212), channel_id=1, source_target_pairs={{0,2},{1,3},{2,0},{3,1},{4,6},{5,7},{6,4},{7,5},{8,11},{9,10},{10,... | collective-permute-start | bytes 319496 | tf_op jit(solution)/shard_map/ppermute | solution.py:350
  69.9 0.8 collective-permute-start.25
  70.7 4.2 %shard_map.90 = f32[24,32,128]{2,1,0:T(8,128)S(1)} custom-call(s32[1,256]{1,0:T(1,128)S(1)} %get-tuple-element.59.loads, s32[24]{0:T(128)S(1)} %fusion.83.place, bf16[55,32,128]{2,1,0:T(8,128)(2,1)S(1)} %constant_dynamic-update-slice_fusion.22.field, bf16[24,1280,128]{2,1,0:T(8,128)(2,1)} %get-tuple-element.69.source), custom_call_target="tpu_custom_call" | custom-call | flops 2013265920 | bytes 7864320 | tf_op jit(solution)/shard_map/pallas_call | solution.py:215
  75.0 1.3 %collective-permute-start.27 = (bf16[12,32,128]{2,1,0:T(8,128)(2,1)S(1)}, bf16[12,32,128]{2,1,0:T(8,128)(2,1)S(1)}, u32[]{:S(2)}, u32[]{:S(2)}) collective-permute-start(bf16[12,32,128]{2,1,0:T(8,128)(2,1)S(1)} %slice.1021), channel_id=1, source_target_pairs={{0,16},{1,17},{2,18},{3,19},{4,20},{5,21},{6,22},{7,23},{8,24},{9,... | collective-permute-start | bytes 294920 | tf_op jit(solution)/shard_map/ppermute | solution.py:350
  76.3 1.4 %collective-permute-done.23 = bf16[13,32,128]{2,1,0:T(8,128)(2,1)S(1)} collective-permute-done((bf16[13,32,128]{2,1,0:T(8,128)(2,1)S(1)}, bf16[13,32,128]{2,1,0:T(8,128)(2,1)S(1)}, u32[]{:S(2)}, u32[]{:S(2)}) %collective-permute-start.23) | collective-permute-done | bytes 106528 | tf_op jit(solution)/shard_map/ppermute | solution.py:350
  77.9 2.1 %collective-permute-start.26 = (f32[32,128]{1,0:T(8,128)S(1)}, f32[32,128]{1,0:T(8,128)S(1)}, u32[]{:S(2)}, u32[]{:S(2)}) collective-permute-start(f32[32,128]{1,0:T(8,128)S(1)} %select_add_fusion.3), channel_id=1, source_target_pairs={{0,16},{1,17},{2,18},{3,19},{4,20},{5,21},{6,22},{7,23},{8,24},{9,... | collective-permute-start | bytes 49160 | tf_op jit(solution)/shard_map/ppermute | solution.py:350
  80.1 1.7 %collective-permute-done.26 = f32[32,128]{1,0:T(8,128)S(1)} collective-permute-done((f32[32,128]{1,0:T(8,128)S(1)}, f32[32,128]{1,0:T(8,128)S(1)}, u32[]{:S(2)}, u32[]{:S(2)}) %collective-permute-start.26) | collective-permute-done | bytes 16416 | tf_op jit(solution)/shard_map/ppermute | solution.py:350
  81.9 1.4 %collective-permute-done.28 = f32[13,32,128]{2,1,0:T(8,128)S(1)} collective-permute-done((f32[13,32,128]{2,1,0:T(8,128)S(1)}, f32[13,32,128]{2,1,0:T(8,128)S(1)}, u32[]{:S(2)}, u32[]{:S(2)}) %collective-permute-start.28) | collective-permute-done | bytes 213024 | tf_op jit(solution)/shard_map/ppermute | solution.py:353
  83.7 2.0 %collective-permute-start.29 = (bf16[12,32,128]{2,1,0:T(8,128)(2,1)S(1)}, bf16[12,32,128]{2,1,0:T(8,128)(2,1)S(1)}, u32[]{:S(2)}, u32[]{:S(2)}) collective-permute-start(bf16[12,32,128]{2,1,0:T(8,128)(2,1)S(1)} %get-tuple-element.90), channel_id=1, source_target_pairs={{0,16},{1,17},{2,18},{3,19},{4,20},{5,21},{6,22},{7,23},{8,9},{9,8... | collective-permute-start | bytes 294920 | tf_op jit(solution)/shard_map/ppermute | solution.py:350
  85.7 1.8 %collective-permute-start.30 = (bf16[12,32,128]{2,1,0:T(8,128)(2,1)S(1)}, bf16[12,32,128]{2,1,0:T(8,128)(2,1)S(1)}, u32[]{:S(2)}, u32[]{:S(2)}) collective-permute-start(bf16[12,32,128]{2,1,0:T(8,128)(2,1)S(1)} %get-tuple-element.90), channel_id=1, source_target_pairs={{0,6},{1,7},{2,4},{3,5},{4,2},{5,3},{6,0},{7,1},{8,15},{9,14},{10,... | collective-permute-start | bytes 294920 | tf_op jit(solution)/shard_map/ppermute | solution.py:350
  87.5 2.6 %collective-permute-start.32 = (bf16[12,32,128]{2,1,0:T(8,128)(2,1)S(1)}, bf16[12,32,128]{2,1,0:T(8,128)(2,1)S(1)}, u32[]{:S(2)}, u32[]{:S(2)}) collective-permute-start(bf16[12,32,128]{2,1,0:T(8,128)(2,1)S(1)} %get-tuple-element.90), channel_id=1, source_target_pairs={{0,2},{1,3},{2,0},{3,1},{4,6},{5,7},{6,4},{7,5},{8,11},{9,10},{10,... | collective-permute-start | bytes 294920 | tf_op jit(solution)/shard_map/ppermute | solution.py:350
  90.3 1.1 collective-permute-done.33
  91.5 4.2 %shard_map.91 = bf16[54,32,128]{2,1,0:T(8,128)(2,1)S(1)} custom-call(s32[1,256]{1,0:T(1,128)S(1)} %get-tuple-element.48.loads, s32[48]{0:T(128)S(1)} %fusion.82.place, bf16[25,32,128]{2,1,0:T(8,128)(2,1)S(1)} %pad_maximum_fusion.field, bf16[48,640,128]{2,1,0:T(8,128)(2,1)} %get-tuple-element.62.source), custom_call_target="tpu_custom_call" | custom-call | flops 2013265920 | bytes 7864320 | tf_op jit(solution)/shard_map/pallas_call | solution.py:215
  96.1 0.4 collective-permute-start.34
  96.5 1.0 collective-permute-done.34
  98.1 0.4 collective-permute-start.35
  98.5 1.1 collective-permute-done.35
  99.9 2.2 %collective-permute-start.36 = (bf16[13,32,128]{2,1,0:T(8,128)(2,1)S(1)}, bf16[13,32,128]{2,1,0:T(8,128)(2,1)S(1)}, u32[]{:S(2)}, u32[]{:S(2)}) collective-permute-start(bf16[13,32,128]{2,1,0:T(8,128)(2,1)S(1)} %get-tuple-element.206), channel_id=1, source_target_pairs={{0,6},{1,7},{2,4},{3,5},{4,2},{5,3},{6,0},{7,1},{8,15},{9,14},{10,... | collective-permute-start | bytes 319496 | tf_op jit(solution)/shard_map/ppermute | solution.py:350
  102.1 2.2 %collective-permute-start.38 = (bf16[13,32,128]{2,1,0:T(8,128)(2,1)S(1)}, bf16[13,32,128]{2,1,0:T(8,128)(2,1)S(1)}, u32[]{:S(2)}, u32[]{:S(2)}) collective-permute-start(bf16[13,32,128]{2,1,0:T(8,128)(2,1)S(1)} %get-tuple-element.208), channel_id=1, source_target_pairs={{0,2},{1,3},{2,0},{3,1},{4,6},{5,7},{6,4},{7,5},{8,11},{9,10},{10,... | collective-permute-start | bytes 319496 | tf_op jit(solution)/shard_map/ppermute | solution.py:350
  104.4 0.7 collective-permute-start.39
  105.1 4.2 %shard_map.92 = f32[24,32,128]{2,1,0:T(8,128)S(1)} custom-call(s32[1,256]{1,0:T(1,128)S(1)} %get-tuple-element.59.loads, s32[24]{0:T(128)S(1)} %fusion.83.place, bf16[55,32,128]{2,1,0:T(8,128)(2,1)S(1)} %constant_dynamic-update-slice_fusion.37.field, bf16[24,1280,128]{2,1,0:T(8,128)(2,1)} %get-tuple-element.69.source), custom_call_target="tpu_custom_call" | custom-call | flops 2013265920 | bytes 7864320 | tf_op jit(solution)/shard_map/pallas_call | solution.py:215
  109.3 1.8 %collective-permute-start.41 = (bf16[12,32,128]{2,1,0:T(8,128)(2,1)S(1)}, bf16[12,32,128]{2,1,0:T(8,128)(2,1)S(1)}, u32[]{:S(2)}, u32[]{:S(2)}) collective-permute-start(bf16[12,32,128]{2,1,0:T(8,128)(2,1)S(1)} %slice.1020), channel_id=1, source_target_pairs={{0,16},{1,17},{2,18},{3,19},{4,20},{5,21},{6,22},{7,23},{8,24},{9,... | collective-permute-start | bytes 294920 | tf_op jit(solution)/shard_map/ppermute | solution.py:350
  111.1 1.1 collective-permute-done.37
  112.3 1.5 %collective-permute-start.40 = (f32[32,128]{1,0:T(8,128)S(1)}, f32[32,128]{1,0:T(8,128)S(1)}, u32[]{:S(2)}, u32[]{:S(2)}) collective-permute-start(f32[32,128]{1,0:T(8,128)S(1)} %select_add_fusion), channel_id=1, source_target_pairs={{0,16},{1,17},{2,18},{3,19},{4,20},{5,21},{6,22},{7,23},{8,24},{9,... | collective-permute-start | bytes 49160 | tf_op jit(solution)/shard_map/ppermute | solution.py:350
  114.1 2.0 %collective-permute-done.40 = f32[32,128]{1,0:T(8,128)S(1)} collective-permute-done((f32[32,128]{1,0:T(8,128)S(1)}, f32[32,128]{1,0:T(8,128)S(1)}, u32[]{:S(2)}, u32[]{:S(2)}) %collective-permute-start.40) | collective-permute-done | bytes 16416 | tf_op jit(solution)/shard_map/ppermute | solution.py:350
  116.2 0.4 collective-permute-start.42
  116.6 1.1 collective-permute-done.42
  118.0 0.7 shard_map.93
  (209 shorter events, 7.1 us)
Async XLA Ops:
  0.6 0.9 copy-start
  1.5 2.1 %collective-permute-start = (f32[6,32,128]{2,1,0:T(8,128)S(1)}, f32[6,32,128]{2,1,0:T(8,128)S(1)}, u32[]{:S(2)}, u32[]{:S(2)}) collective-permute-start(f32[6,32,128]{2,1,0:T(8,128)S(1)} %bitcast_bitcast_fusion), channel_id=1, source_target_pairs={{0,8},{8,0},{16,24},{24,16},{1,9},{9,1},{17,25},{25,17},{2,10},{10... | collective-permute-start | bytes 294920 | tf_op jit(solution)/shard_map/ppermute | solution.py:353
  3.7 5.3 %collective-permute-start.1 = (bf16[12,32,128]{2,1,0:T(8,128)(2,1)S(1)}, bf16[12,32,128]{2,1,0:T(8,128)(2,1)S(1)}, u32[]{:S(2)}, u32[]{:S(2)}) collective-permute-start(bf16[12,32,128]{2,1,0:T(8,128)(2,1)S(1)} %fusion.15), channel_id=1, source_target_pairs={{0,16},{1,17},{2,18},{3,19},{4,20},{5,21},{6,22},{7,23},{8,9},{9,8... | collective-permute-start | bytes 294920 | tf_op jit(solution)/shard_map/ppermute | solution.py:350
  6.4 0.7 copy-start.1
  7.0 0.7 copy-start.2
  9.0 4.7 %collective-permute-start.5 = (bf16[12,32,128]{2,1,0:T(8,128)(2,1)S(1)}, bf16[12,32,128]{2,1,0:T(8,128)(2,1)S(1)}, u32[]{:S(2)}, u32[]{:S(2)}) collective-permute-start(bf16[12,32,128]{2,1,0:T(8,128)(2,1)S(1)} %collective-permute-done.1), channel_id=1, source_target_pairs={{0,8},{8,0},{16,24},{24,16},{1,9},{9,1},{17,25},{25,17},{2,10},{10... | collective-permute-start | bytes 294920 | tf_op jit(solution)/shard_map/ppermute | solution.py:353
  9.3 12.1 %collective-permute-start.2 = (bf16[12,32,128]{2,1,0:T(8,128)(2,1)S(1)}, bf16[12,32,128]{2,1,0:T(8,128)(2,1)S(1)}, u32[]{:S(2)}, u32[]{:S(2)}) collective-permute-start(bf16[12,32,128]{2,1,0:T(8,128)(2,1)S(1)} %fusion.15), channel_id=1, source_target_pairs={{0,6},{1,7},{2,4},{3,5},{4,2},{5,3},{6,0},{7,1},{8,15},{9,14},{10,... | collective-permute-start | bytes 294920 | tf_op jit(solution)/shard_map/ppermute | solution.py:350
  13.1 9.0 %collective-permute-start.3 = (bf16[12,32,128]{2,1,0:T(8,128)(2,1)S(1)}, bf16[12,32,128]{2,1,0:T(8,128)(2,1)S(1)}, u32[]{:S(2)}, u32[]{:S(2)}) collective-permute-start(bf16[12,32,128]{2,1,0:T(8,128)(2,1)S(1)} %fusion.15), channel_id=1, source_target_pairs={{0,4},{1,5},{2,6},{3,7},{4,0},{5,1},{6,2},{7,3},{8,13},{9,12},{10,... | collective-permute-start | bytes 294920 | tf_op jit(solution)/shard_map/ppermute | solution.py:350
  13.1 9.0 %collective-permute-start.4 = (bf16[12,32,128]{2,1,0:T(8,128)(2,1)S(1)}, bf16[12,32,128]{2,1,0:T(8,128)(2,1)S(1)}, u32[]{:S(2)}, u32[]{:S(2)}) collective-permute-start(bf16[12,32,128]{2,1,0:T(8,128)(2,1)S(1)} %fusion.15), channel_id=1, source_target_pairs={{0,2},{1,3},{2,0},{3,1},{4,6},{5,7},{6,4},{7,5},{8,11},{9,10},{10,... | collective-permute-start | bytes 294920 | tf_op jit(solution)/shard_map/ppermute | solution.py:350
  22.1 22.2 %copy-start.3 = (pred[12]{0:T(512)(128)(4,1)S(1)}, pred[12]{0:T(512)(128)(4,1)}, u32[]{:S(2)}) copy-start(pred[12]{0:T(512)(128)(4,1)} %constant.88.clone.1) | copy-start | bytes 40
  22.2 2.0 %collective-permute-start.6 = (bf16[18,32,128]{2,1,0:T(8,128)(2,1)S(1)}, bf16[18,32,128]{2,1,0:T(8,128)(2,1)S(1)}, u32[]{:S(2)}, u32[]{:S(2)}) collective-permute-start(bf16[18,32,128]{2,1,0:T(8,128)(2,1)S(1)} %pad_maximum_fusion.22), channel_id=1, source_target_pairs={{0,8},{8,0},{16,24},{24,16},{1,9},{9,1},{17,25},{25,17},{2,10},{10... | collective-permute-start | bytes 442376 | tf_op jit(solution)/shard_map/ppermute | solution.py:353
  24.9 1.5 %collective-permute-start.7 = (bf16[27,32,128]{2,1,0:T(8,128)(2,1)S(1)}, bf16[27,32,128]{2,1,0:T(8,128)(2,1)S(1)}, u32[]{:S(2)}, u32[]{:S(2)}) collective-permute-start(bf16[27,32,128]{2,1,0:T(8,128)(2,1)S(1)} %pad_maximum_fusion.8), channel_id=1, source_target_pairs={{0,8},{8,0},{16,24},{24,16},{1,9},{9,1},{17,25},{25,17},{2,10},{10... | collective-permute-start | bytes 663560 | tf_op jit(solution)/shard_map/ppermute | solution.py:353
  27.1 14.0 %collective-permute-start.10 = (bf16[14,32,128]{2,1,0:T(8,128)(2,1)S(1)}, bf16[14,32,128]{2,1,0:T(8,128)(2,1)S(1)}, u32[]{:S(2)}, u32[]{:S(2)}) collective-permute-start(bf16[14,32,128]{2,1,0:T(8,128)(2,1)S(1)} %get-tuple-element.216), channel_id=1, source_target_pairs={{0,2},{1,3},{2,0},{3,1},{4,6},{5,7},{6,4},{7,5},{8,11},{9,10},{10,... | collective-permute-start | bytes 344072 | tf_op jit(solution)/shard_map/ppermute | solution.py:350
  27.9 13.2 %collective-permute-start.11 = (bf16[14,32,128]{2,1,0:T(8,128)(2,1)S(1)}, bf16[14,32,128]{2,1,0:T(8,128)(2,1)S(1)}, u32[]{:S(2)}, u32[]{:S(2)}) collective-permute-start(bf16[14,32,128]{2,1,0:T(8,128)(2,1)S(1)} %get-tuple-element.217), channel_id=1, source_target_pairs={{8,9},{9,8},{10,11},{11,10},{12,13},{13,12},{14,15},{15,14},{24,25... | collective-permute-start | bytes 344072 | tf_op jit(solution)/shard_map/ppermute | solution.py:350
  28.6 12.6 %collective-permute-start.8 = (bf16[14,32,128]{2,1,0:T(8,128)(2,1)S(1)}, bf16[14,32,128]{2,1,0:T(8,128)(2,1)S(1)}, u32[]{:S(2)}, u32[]{:S(2)}) collective-permute-start(bf16[14,32,128]{2,1,0:T(8,128)(2,1)S(1)} %get-tuple-element.214), channel_id=1, source_target_pairs={{0,6},{1,7},{2,4},{3,5},{4,2},{5,3},{6,0},{7,1},{8,15},{9,14},{10,... | collective-permute-start | bytes 344072 | tf_op jit(solution)/shard_map/ppermute | solution.py:350
  31.6 10.9 %collective-permute-start.9 = (bf16[14,32,128]{2,1,0:T(8,128)(2,1)S(1)}, bf16[14,32,128]{2,1,0:T(8,128)(2,1)S(1)}, u32[]{:S(2)}, u32[]{:S(2)}) collective-permute-start(bf16[14,32,128]{2,1,0:T(8,128)(2,1)S(1)} %get-tuple-element.215), channel_id=1, source_target_pairs={{0,4},{1,5},{2,6},{3,7},{4,0},{5,1},{6,2},{7,3},{8,13},{9,12},{10,... | collective-permute-start | bytes 344072 | tf_op jit(solution)/shard_map/ppermute | solution.py:350
  39.5 4.8 %collective-permute-start.13 = (bf16[12,32,128]{2,1,0:T(8,128)(2,1)S(1)}, bf16[12,32,128]{2,1,0:T(8,128)(2,1)S(1)}, u32[]{:S(2)}, u32[]{:S(2)}) collective-permute-start(bf16[12,32,128]{2,1,0:T(8,128)(2,1)S(1)} %slice.1022), channel_id=1, source_target_pairs={{0,16},{1,17},{2,18},{3,19},{4,20},{5,21},{6,22},{7,23},{8,24},{9,... | collective-permute-start | bytes 294920 | tf_op jit(solution)/shard_map/ppermute | solution.py:350
  42.7 4.0 %collective-permute-start.12 = (f32[44,128]{1,0:T(8,128)S(1)}, f32[44,128]{1,0:T(8,128)S(1)}, u32[]{:S(2)}, u32[]{:S(2)}) collective-permute-start(f32[44,128]{1,0:T(8,128)S(1)} %pad_maximum_fusion.25), channel_id=1, source_target_pairs={{0,16},{1,17},{2,18},{3,19},{4,20},{5,21},{6,22},{7,23},{8,24},{9,... | collective-permute-start | bytes 67592 | tf_op jit(solution)/shard_map/ppermute | solution.py:350
  46.8 1.6 %collective-permute-start.14 = (f32[14,32,128]{2,1,0:T(8,128)S(1)}, f32[14,32,128]{2,1,0:T(8,128)S(1)}, u32[]{:S(2)}, u32[]{:S(2)}) collective-permute-start(f32[14,32,128]{2,1,0:T(8,128)S(1)} %pad_maximum_fusion.7), channel_id=1, source_target_pairs={{0,8},{8,0},{16,24},{24,16},{1,9},{9,1},{17,25},{25,17},{2,10},{10... | collective-permute-start | bytes 688136 | tf_op jit(solution)/shard_map/ppermute | solution.py:353
  48.7 6.0 %collective-permute-start.15 = (bf16[12,32,128]{2,1,0:T(8,128)(2,1)S(1)}, bf16[12,32,128]{2,1,0:T(8,128)(2,1)S(1)}, u32[]{:S(2)}, u32[]{:S(2)}) collective-permute-start(bf16[12,32,128]{2,1,0:T(8,128)(2,1)S(1)} %get-tuple-element.96), channel_id=1, source_target_pairs={{0,16},{1,17},{2,18},{3,19},{4,20},{5,21},{6,22},{7,23},{8,9},{9,8... | collective-permute-start | bytes 294920 | tf_op jit(solution)/shard_map/ppermute | solution.py:350
  50.2 10.1 %collective-permute-start.16 = (bf16[12,32,128]{2,1,0:T(8,128)(2,1)S(1)}, bf16[12,32,128]{2,1,0:T(8,128)(2,1)S(1)}, u32[]{:S(2)}, u32[]{:S(2)}) collective-permute-start(bf16[12,32,128]{2,1,0:T(8,128)(2,1)S(1)} %get-tuple-element.96), channel_id=1, source_target_pairs={{0,6},{1,7},{2,4},{3,5},{4,2},{5,3},{6,0},{7,1},{8,15},{9,14},{10,... | collective-permute-start | bytes 294920 | tf_op jit(solution)/shard_map/ppermute | solution.py:350
  53.7 7.8 %collective-permute-start.17 = (bf16[12,32,128]{2,1,0:T(8,128)(2,1)S(1)}, bf16[12,32,128]{2,1,0:T(8,128)(2,1)S(1)}, u32[]{:S(2)}, u32[]{:S(2)}) collective-permute-start(bf16[12,32,128]{2,1,0:T(8,128)(2,1)S(1)} %get-tuple-element.96), channel_id=1, source_target_pairs={{0,4},{1,5},{2,6},{3,7},{4,0},{5,1},{6,2},{7,3},{8,13},{9,12},{10,... | collective-permute-start | bytes 294920 | tf_op jit(solution)/shard_map/ppermute | solution.py:350
  53.7 7.8 %collective-permute-start.18 = (bf16[12,32,128]{2,1,0:T(8,128)(2,1)S(1)}, bf16[12,32,128]{2,1,0:T(8,128)(2,1)S(1)}, u32[]{:S(2)}, u32[]{:S(2)}) collective-permute-start(bf16[12,32,128]{2,1,0:T(8,128)(2,1)S(1)} %get-tuple-element.96), channel_id=1, source_target_pairs={{0,2},{1,3},{2,0},{3,1},{4,6},{5,7},{6,4},{7,5},{8,11},{9,10},{10,... | collective-permute-start | bytes 294920 | tf_op jit(solution)/shard_map/ppermute | solution.py:350
  54.7 1.3 %collective-permute-start.19 = (bf16[12,32,128]{2,1,0:T(8,128)(2,1)S(1)}, bf16[12,32,128]{2,1,0:T(8,128)(2,1)S(1)}, u32[]{:S(2)}, u32[]{:S(2)}) collective-permute-start(bf16[12,32,128]{2,1,0:T(8,128)(2,1)S(1)} %collective-permute-done.15), channel_id=1, source_target_pairs={{0,8},{8,0},{16,24},{24,16},{1,9},{9,1},{17,25},{25,17},{2,10},{10... | collective-permute-start | bytes 294920 | tf_op jit(solution)/shard_map/ppermute | solution.py:353
  61.6 1.4 %collective-permute-start.20 = (bf16[18,32,128]{2,1,0:T(8,128)(2,1)S(1)}, bf16[18,32,128]{2,1,0:T(8,128)(2,1)S(1)}, u32[]{:S(2)}, u32[]{:S(2)}) collective-permute-start(bf16[18,32,128]{2,1,0:T(8,128)(2,1)S(1)} %pad_maximum_fusion.23), channel_id=1, source_target_pairs={{0,8},{8,0},{16,24},{24,16},{1,9},{9,1},{17,25},{25,17},{2,10},{10... | collective-permute-start | bytes 442376 | tf_op jit(solution)/shard_map/ppermute | solution.py:353
  63.5 1.5 %collective-permute-start.21 = (bf16[25,32,128]{2,1,0:T(8,128)(2,1)S(1)}, bf16[25,32,128]{2,1,0:T(8,128)(2,1)S(1)}, u32[]{:S(2)}, u32[]{:S(2)}) collective-permute-start(bf16[25,32,128]{2,1,0:T(8,128)(2,1)S(1)} %pad_maximum_fusion.19), channel_id=1, source_target_pairs={{0,8},{8,0},{16,24},{24,16},{1,9},{9,1},{17,25},{25,17},{2,10},{10... | collective-permute-start | bytes 614408 | tf_op jit(solution)/shard_map/ppermute | solution.py:353
  65.4 10.8 %collective-permute-start.22 = (bf16[13,32,128]{2,1,0:T(8,128)(2,1)S(1)}, bf16[13,32,128]{2,1,0:T(8,128)(2,1)S(1)}, u32[]{:S(2)}, u32[]{:S(2)}) collective-permute-start(bf16[13,32,128]{2,1,0:T(8,128)(2,1)S(1)} %get-tuple-element.210), channel_id=1, source_target_pairs={{0,6},{1,7},{2,4},{3,5},{4,2},{5,3},{6,0},{7,1},{8,15},{9,14},{10,... | collective-permute-start | bytes 319496 | tf_op jit(solution)/shard_map/ppermute | solution.py:350
  67.9 9.8 %collective-permute-start.23 = (bf16[13,32,128]{2,1,0:T(8,128)(2,1)S(1)}, bf16[13,32,128]{2,1,0:T(8,128)(2,1)S(1)}, u32[]{:S(2)}, u32[]{:S(2)}) collective-permute-start(bf16[13,32,128]{2,1,0:T(8,128)(2,1)S(1)} %get-tuple-element.211), channel_id=1, source_target_pairs={{0,4},{1,5},{2,6},{3,7},{4,0},{5,1},{6,2},{7,3},{8,13},{9,12},{10,... | collective-permute-start | bytes 319496 | tf_op jit(solution)/shard_map/ppermute | solution.py:350
  67.9 9.8 %collective-permute-start.24 = (bf16[13,32,128]{2,1,0:T(8,128)(2,1)S(1)}, bf16[13,32,128]{2,1,0:T(8,128)(2,1)S(1)}, u32[]{:S(2)}, u32[]{:S(2)}) collective-permute-start(bf16[13,32,128]{2,1,0:T(8,128)(2,1)S(1)} %get-tuple-element.212), channel_id=1, source_target_pairs={{0,2},{1,3},{2,0},{3,1},{4,6},{5,7},{6,4},{7,5},{8,11},{9,10},{10,... | collective-permute-start | bytes 319496 | tf_op jit(solution)/shard_map/ppermute | solution.py:350
  69.9 7.8 %collective-permute-start.25 = (bf16[13,32,128]{2,1,0:T(8,128)(2,1)S(1)}, bf16[13,32,128]{2,1,0:T(8,128)(2,1)S(1)}, u32[]{:S(2)}, u32[]{:S(2)}) collective-permute-start(bf16[13,32,128]{2,1,0:T(8,128)(2,1)S(1)} %get-tuple-element.213), channel_id=1, source_target_pairs={{8,9},{9,8},{10,11},{11,10},{12,13},{13,12},{14,15},{15,14},{24,25... | collective-permute-start | bytes 319496 | tf_op jit(solution)/shard_map/ppermute | solution.py:350
  75.0 5.0 %collective-permute-start.27 = (bf16[12,32,128]{2,1,0:T(8,128)(2,1)S(1)}, bf16[12,32,128]{2,1,0:T(8,128)(2,1)S(1)}, u32[]{:S(2)}, u32[]{:S(2)}) collective-permute-start(bf16[12,32,128]{2,1,0:T(8,128)(2,1)S(1)} %slice.1021), channel_id=1, source_target_pairs={{0,16},{1,17},{2,18},{3,19},{4,20},{5,21},{6,22},{7,23},{8,24},{9,... | collective-permute-start | bytes 294920 | tf_op jit(solution)/shard_map/ppermute | solution.py:350
  77.9 3.9 %collective-permute-start.26 = (f32[32,128]{1,0:T(8,128)S(1)}, f32[32,128]{1,0:T(8,128)S(1)}, u32[]{:S(2)}, u32[]{:S(2)}) collective-permute-start(f32[32,128]{1,0:T(8,128)S(1)} %select_add_fusion.3), channel_id=1, source_target_pairs={{0,16},{1,17},{2,18},{3,19},{4,20},{5,21},{6,22},{7,23},{8,24},{9,... | collective-permute-start | bytes 49160 | tf_op jit(solution)/shard_map/ppermute | solution.py:350
  81.8 1.5 %collective-permute-start.28 = (f32[13,32,128]{2,1,0:T(8,128)S(1)}, f32[13,32,128]{2,1,0:T(8,128)S(1)}, u32[]{:S(2)}, u32[]{:S(2)}) collective-permute-start(f32[13,32,128]{2,1,0:T(8,128)S(1)} %pad_maximum_fusion.17), channel_id=1, source_target_pairs={{0,8},{8,0},{16,24},{24,16},{1,9},{9,1},{17,25},{25,17},{2,10},{10... | collective-permute-start | bytes 638984 | tf_op jit(solution)/shard_map/ppermute | solution.py:353
  83.7 6.4 %collective-permute-start.29 = (bf16[12,32,128]{2,1,0:T(8,128)(2,1)S(1)}, bf16[12,32,128]{2,1,0:T(8,128)(2,1)S(1)}, u32[]{:S(2)}, u32[]{:S(2)}) collective-permute-start(bf16[12,32,128]{2,1,0:T(8,128)(2,1)S(1)} %get-tuple-element.90), channel_id=1, source_target_pairs={{0,16},{1,17},{2,18},{3,19},{4,20},{5,21},{6,22},{7,23},{8,9},{9,8... | collective-permute-start | bytes 294920 | tf_op jit(solution)/shard_map/ppermute | solution.py:350
  85.7 10.1 %collective-permute-start.30 = (bf16[12,32,128]{2,1,0:T(8,128)(2,1)S(1)}, bf16[12,32,128]{2,1,0:T(8,128)(2,1)S(1)}, u32[]{:S(2)}, u32[]{:S(2)}) collective-permute-start(bf16[12,32,128]{2,1,0:T(8,128)(2,1)S(1)} %get-tuple-element.90), channel_id=1, source_target_pairs={{0,6},{1,7},{2,4},{3,5},{4,2},{5,3},{6,0},{7,1},{8,15},{9,14},{10,... | collective-permute-start | bytes 294920 | tf_op jit(solution)/shard_map/ppermute | solution.py:350
  87.5 8.5 %collective-permute-start.31 = (bf16[12,32,128]{2,1,0:T(8,128)(2,1)S(1)}, bf16[12,32,128]{2,1,0:T(8,128)(2,1)S(1)}, u32[]{:S(2)}, u32[]{:S(2)}) collective-permute-start(bf16[12,32,128]{2,1,0:T(8,128)(2,1)S(1)} %get-tuple-element.90), channel_id=1, source_target_pairs={{0,4},{1,5},{2,6},{3,7},{4,0},{5,1},{6,2},{7,3},{8,13},{9,12},{10,... | collective-permute-start | bytes 294920 | tf_op jit(solution)/shard_map/ppermute | solution.py:350
  87.5 8.5 %collective-permute-start.32 = (bf16[12,32,128]{2,1,0:T(8,128)(2,1)S(1)}, bf16[12,32,128]{2,1,0:T(8,128)(2,1)S(1)}, u32[]{:S(2)}, u32[]{:S(2)}) collective-permute-start(bf16[12,32,128]{2,1,0:T(8,128)(2,1)S(1)} %get-tuple-element.90), channel_id=1, source_target_pairs={{0,2},{1,3},{2,0},{3,1},{4,6},{5,7},{6,4},{7,5},{8,11},{9,10},{10,... | collective-permute-start | bytes 294920 | tf_op jit(solution)/shard_map/ppermute | solution.py:350
  90.1 1.3 %collective-permute-start.33 = (bf16[12,32,128]{2,1,0:T(8,128)(2,1)S(1)}, bf16[12,32,128]{2,1,0:T(8,128)(2,1)S(1)}, u32[]{:S(2)}, u32[]{:S(2)}) collective-permute-start(bf16[12,32,128]{2,1,0:T(8,128)(2,1)S(1)} %collective-permute-done.29), channel_id=1, source_target_pairs={{0,8},{8,0},{16,24},{24,16},{1,9},{9,1},{17,25},{25,17},{2,10},{10... | collective-permute-start | bytes 294920 | tf_op jit(solution)/shard_map/ppermute | solution.py:353
  96.1 1.4 %collective-permute-start.34 = (bf16[18,32,128]{2,1,0:T(8,128)(2,1)S(1)}, bf16[18,32,128]{2,1,0:T(8,128)(2,1)S(1)}, u32[]{:S(2)}, u32[]{:S(2)}) collective-permute-start(bf16[18,32,128]{2,1,0:T(8,128)(2,1)S(1)} %pad_maximum_fusion.24), channel_id=1, source_target_pairs={{0,8},{8,0},{16,24},{24,16},{1,9},{9,1},{17,25},{25,17},{2,10},{10... | collective-permute-start | bytes 442376 | tf_op jit(solution)/shard_map/ppermute | solution.py:353
  98.1 1.5 %collective-permute-start.35 = (bf16[25,32,128]{2,1,0:T(8,128)(2,1)S(1)}, bf16[25,32,128]{2,1,0:T(8,128)(2,1)S(1)}, u32[]{:S(2)}, u32[]{:S(2)}) collective-permute-start(bf16[25,32,128]{2,1,0:T(8,128)(2,1)S(1)} %pad_maximum_fusion.20), channel_id=1, source_target_pairs={{0,8},{8,0},{16,24},{24,16},{1,9},{9,1},{17,25},{25,17},{2,10},{10... | collective-permute-start | bytes 614408 | tf_op jit(solution)/shard_map/ppermute | solution.py:353
  99.9 11.1 %collective-permute-start.36 = (bf16[13,32,128]{2,1,0:T(8,128)(2,1)S(1)}, bf16[13,32,128]{2,1,0:T(8,128)(2,1)S(1)}, u32[]{:S(2)}, u32[]{:S(2)}) collective-permute-start(bf16[13,32,128]{2,1,0:T(8,128)(2,1)S(1)} %get-tuple-element.206), channel_id=1, source_target_pairs={{0,6},{1,7},{2,4},{3,5},{4,2},{5,3},{6,0},{7,1},{8,15},{9,14},{10,... | collective-permute-start | bytes 319496 | tf_op jit(solution)/shard_map/ppermute | solution.py:350
  102.1 10.0 %collective-permute-start.37 = (bf16[13,32,128]{2,1,0:T(8,128)(2,1)S(1)}, bf16[13,32,128]{2,1,0:T(8,128)(2,1)S(1)}, u32[]{:S(2)}, u32[]{:S(2)}) collective-permute-start(bf16[13,32,128]{2,1,0:T(8,128)(2,1)S(1)} %get-tuple-element.207), channel_id=1, source_target_pairs={{0,4},{1,5},{2,6},{3,7},{4,0},{5,1},{6,2},{7,3},{8,13},{9,12},{10,... | collective-permute-start | bytes 319496 | tf_op jit(solution)/shard_map/ppermute | solution.py:350
  102.1 10.0 %collective-permute-start.38 = (bf16[13,32,128]{2,1,0:T(8,128)(2,1)S(1)}, bf16[13,32,128]{2,1,0:T(8,128)(2,1)S(1)}, u32[]{:S(2)}, u32[]{:S(2)}) collective-permute-start(bf16[13,32,128]{2,1,0:T(8,128)(2,1)S(1)} %get-tuple-element.208), channel_id=1, source_target_pairs={{0,2},{1,3},{2,0},{3,1},{4,6},{5,7},{6,4},{7,5},{8,11},{9,10},{10,... | collective-permute-start | bytes 319496 | tf_op jit(solution)/shard_map/ppermute | solution.py:350
  104.4 7.8 %collective-permute-start.39 = (bf16[13,32,128]{2,1,0:T(8,128)(2,1)S(1)}, bf16[13,32,128]{2,1,0:T(8,128)(2,1)S(1)}, u32[]{:S(2)}, u32[]{:S(2)}) collective-permute-start(bf16[13,32,128]{2,1,0:T(8,128)(2,1)S(1)} %get-tuple-element.209), channel_id=1, source_target_pairs={{8,9},{9,8},{10,11},{11,10},{12,13},{13,12},{14,15},{15,14},{24,25... | collective-permute-start | bytes 319496 | tf_op jit(solution)/shard_map/ppermute | solution.py:350
  109.3 4.7 %collective-permute-start.41 = (bf16[12,32,128]{2,1,0:T(8,128)(2,1)S(1)}, bf16[12,32,128]{2,1,0:T(8,128)(2,1)S(1)}, u32[]{:S(2)}, u32[]{:S(2)}) collective-permute-start(bf16[12,32,128]{2,1,0:T(8,128)(2,1)S(1)} %slice.1020), channel_id=1, source_target_pairs={{0,16},{1,17},{2,18},{3,19},{4,20},{5,21},{6,22},{7,23},{8,24},{9,... | collective-permute-start | bytes 294920 | tf_op jit(solution)/shard_map/ppermute | solution.py:350
  112.3 3.8 %collective-permute-start.40 = (f32[32,128]{1,0:T(8,128)S(1)}, f32[32,128]{1,0:T(8,128)S(1)}, u32[]{:S(2)}, u32[]{:S(2)}) collective-permute-start(f32[32,128]{1,0:T(8,128)S(1)} %select_add_fusion), channel_id=1, source_target_pairs={{0,16},{1,17},{2,18},{3,19},{4,20},{5,21},{6,22},{7,23},{8,24},{9,... | collective-permute-start | bytes 49160 | tf_op jit(solution)/shard_map/ppermute | solution.py:350
  116.2 1.5 %collective-permute-start.42 = (f32[13,32,128]{2,1,0:T(8,128)S(1)}, f32[13,32,128]{2,1,0:T(8,128)S(1)}, u32[]{:S(2)}, u32[]{:S(2)}) collective-permute-start(f32[13,32,128]{2,1,0:T(8,128)S(1)} %pad_maximum_fusion.18), channel_id=1, source_target_pairs={{0,8},{8,0},{16,24},{24,16},{1,9},{9,1},{17,25},{25,17},{2,10},{10... | collective-permute-start | bytes 638984 | tf_op jit(solution)/shard_map/ppermute | solution.py:353

commit v7 on v6

--- a/solution.py
+++ b/solution.py
@@ -318,7 +318,7 @@
         self.rows, self.cols = rows, cols
         self.row_steps = [("row", m) for m in range(1, rows // 2)]
         first = self.row_steps + [("col", k) for k in range(cols - 2, 0, -2)]
-        second = [("col", 1)] + [("col", k) for k in range(cols - 1, 1, -2)]
+        second = [("col", k) for k in range(cols - 1, 0, -2)]
         while len(first) > len(second) + 1:
             second.append(first.pop())
         first += [None] * (len(second) - len(first))

time: 119 us -> 120 us (level)
    ppermute x13, starting transfers between devices: 3.88 us -> 7.89 us  [swap(): return lax.ppermute(value, 'row', [(r, r ^ 1) for r in range(self.rows)])]
    ppermute x30, starting transfers between devices: 44.8 us -> 41.1 us  [send(): return lax.ppermute(value, MESH_AXES, self.pairs(by_core))]
    ppermute x30, waiting for transfers between devices: 12.1 us -> 13.6 us  [send(): return lax.ppermute(value, MESH_AXES, self.pairs(by_core))]
  transfers between devices with their start and end apart: 43 -> 43, of which waited for: 21 -> 21; matrix products, arithmetic and copies ran while one was open for 3% -> 2% of each run, Pallas kernels for 28% -> 27%
where the time goes in v7:
time: 120 us
  starting transfers between devices  49 us (41%)
  Pallas kernels  33.7 us (28%)
  waiting for transfers between devices  25.6 us (21%)
  other arithmetic  5.73 us (5%)
  local copies, waits for them, and re-layouts  3.69 us (3%)
  between operations  2.26 us (2%)
    ppermute x30, starting transfers between devices, send(): return lax.ppermute(value, MESH_AXES, self.pairs(by_core))  41.1 us
    pallas_call x4, Pallas kernels, next_product(): pl.pallas_call(functools.partial(next_kernel, blocks.shape[1] // blocks.s...  16.9 us
    ppermute x30, waiting for transfers between devices, send(): return lax.ppermute(value, MESH_AXES, self.pairs(by_core))  13.6 us
    ppermute x13, waiting for transfers between devices, swap(): return lax.ppermute(value, 'row', [(r, r ^ 1) for r in range(self.rows)])  12 us
    ppermute x13, starting transfers between devices, swap(): return lax.ppermute(value, 'row', [(r, r ^ 1) for r in range(self.rows)])  7.89 us
    pallas_call x1, Pallas kernels, first_row_product(): pl.pallas_call(functools.partial(first_row_kernel, slots // count), out_s...  7.53 us
    pallas_call x1, Pallas kernels, first_col_product(): pl.pallas_call(functools.partial(first_col_kernel, slots // count), out_s...  7.31 us
    unnamed x27, local copies, waits for them, and re-layouts  2.81 us
  transfers between devices with their start and end apart: 43, of which 21 were waited for; matrix products, arithmetic and copies ran while one was open for 2% of the time, Pallas kernels for 27%

profile of v7, /device:TPU:0, one launch (start us, length us, event | category | flops | bytes accessed | tf_op | source)
XLA Modules:
  0.0 119.9 jit_solution(13162711388264733516)
XLA Ops:
  0.6 0.9 copy-done
  1.5 0.5 collective-permute-start
  2.9 0.7 broadcast_select_fusion.3
  3.7 2.6 %collective-permute-start.1 = (bf16[12,32,128]{2,1,0:T(8,128)(2,1)S(1)}, bf16[12,32,128]{2,1,0:T(8,128)(2,1)S(1)}, u32[]{:S(2)}, u32[]{:S(2)}) collective-permute-start(bf16[12,32,128]{2,1,0:T(8,128)(2,1)S(1)} %fusion.15), channel_id=1, source_target_pairs={{0,16},{1,17},{2,18},{3,19},{4,20},{5,21},{6,22},{7,23},{8,15},{9,... | collective-permute-start | bytes 294920 | tf_op jit(solution)/shard_map/ppermute | solution.py:350
  6.4 0.7 copy-done.1
  7.0 0.7 copy-done.2
  7.7 1.3 %shard_map.86 = (s32[1,256]{1,0:T(1,128)S(1)}, s32[1,256]{1,0:T(1,128)S(1)}, s32[1,256]{1,0:T(1,128)S(1)}, s32[1,256]{1,0:T(1,128)S(1)}, s32[1,256]{1,0:T(1,128)S(1)}) custom-call(s32[11]{0:T(128)S(1)} %pad_add_fusion.here, s32[1,240]{1,0:T(1,128)S(1)} %bitcast.156, s32[1,240]{1,0:T(1,128)S(1)} %bitcast.157), custom_call_target="tpu_custom_call" | custom-call | tf_op jit(solution)/shard_map/pallas_call | solution.py:278
  9.0 3.3 %collective-permute-start.5 = (bf16[12,32,128]{2,1,0:T(8,128)(2,1)S(1)}, bf16[12,32,128]{2,1,0:T(8,128)(2,1)S(1)}, u32[]{:S(2)}, u32[]{:S(2)}) collective-permute-start(bf16[12,32,128]{2,1,0:T(8,128)(2,1)S(1)} %collective-permute-done.1), channel_id=1, source_target_pairs={{0,8},{8,0},{16,24},{24,16},{1,9},{9,1},{17,25},{25,17},{2,10},{10... | collective-permute-start | bytes 294920 | tf_op jit(solution)/shard_map/ppermute | solution.py:353
  12.3 2.8 %collective-permute-start.2 = (bf16[12,32,128]{2,1,0:T(8,128)(2,1)S(1)}, bf16[12,32,128]{2,1,0:T(8,128)(2,1)S(1)}, u32[]{:S(2)}, u32[]{:S(2)}) collective-permute-start(bf16[12,32,128]{2,1,0:T(8,128)(2,1)S(1)} %fusion.15), channel_id=1, source_target_pairs={{0,6},{1,7},{2,4},{3,5},{4,2},{5,3},{6,0},{7,1},{8,13},{9,12},{10,... | collective-permute-start | bytes 294920 | tf_op jit(solution)/shard_map/ppermute | solution.py:350
  15.1 1.7 %collective-permute-start.4 = (bf16[12,32,128]{2,1,0:T(8,128)(2,1)S(1)}, bf16[12,32,128]{2,1,0:T(8,128)(2,1)S(1)}, u32[]{:S(2)}, u32[]{:S(2)}) collective-permute-start(bf16[12,32,128]{2,1,0:T(8,128)(2,1)S(1)} %fusion.15), channel_id=1, source_target_pairs={{0,2},{1,3},{2,0},{3,1},{4,6},{5,7},{6,4},{7,5},{8,9},{9,8},{10,11... | collective-permute-start | bytes 294920 | tf_op jit(solution)/shard_map/ppermute | solution.py:350
  16.9 7.5 %shard_map.87 = (bf16[54,32,128]{2,1,0:T(8,128)(2,1)S(1)}, f32[54,8,128]{2,1,0:T(8,128)S(1)}, f32[25,8,128]{2,1,0:T(8,128)S(1)}, bf16[48,640,128]{2,1,0:T(8,128)(2,1)}) custom-call(s32[1,256]{1,0:T(1,128)S(1)} %get-tuple-element.46.col_of, s32[1,256]{1,0:T(1,128)S(1)} %get-tuple-element.47.slots, s32[1,256]{1,0:T(1,128)S(1)} %get-tuple-element.48.loads, ...), custom_call_target="tpu_custom_call" | custom-call | flops 3019898880 | bytes 7864320 | tf_op jit(solution)/shard_map/pallas_call | solution.py:193
  24.6 0.5 collective-permute-start.6
  25.6 0.6 collective-permute-done.6
  26.2 0.4 fusion
  26.8 0.4 collective-permute-start.7
  27.3 1.1 collective-permute-done.7
  29.4 0.7 collective-permute-start.11
  30.0 2.4 %collective-permute-start.8 = (bf16[14,32,128]{2,1,0:T(8,128)(2,1)S(1)}, bf16[14,32,128]{2,1,0:T(8,128)(2,1)S(1)}, u32[]{:S(2)}, u32[]{:S(2)}) collective-permute-start(bf16[14,32,128]{2,1,0:T(8,128)(2,1)S(1)} %get-tuple-element.214), channel_id=1, source_target_pairs={{0,6},{1,7},{2,4},{3,5},{4,2},{5,3},{6,0},{7,1},{8,13},{9,12},{10,... | collective-permute-start | bytes 344072 | tf_op jit(solution)/shard_map/ppermute | solution.py:350
  32.4 0.9 collective-permute-start.9
  33.3 7.3 %shard_map.88 = (f32[24,32,128]{2,1,0:T(8,128)S(1)}, bf16[24,1280,128]{2,1,0:T(8,128)(2,1)}) custom-call(s32[1,256]{1,0:T(1,128)S(1)} %get-tuple-element.58.slots, s32[1,256]{1,0:T(1,128)S(1)} %get-tuple-element.59.loads, s32[24]{0:T(128)S(1)} %fusion.83.place, bf16[55,32,128]{2,1,0:T(8,128)(2,1)S(1)} %constant_dynamic-update-slice_fusion.7.field, ...), custom_call_target="tpu_custom_call" | custom-call | flops 2013265920 | bytes 7864320 | tf_op jit(solution)/shard_map/pallas_call | solution.py:170
  40.7 1.6 %collective-permute-start.13 = (bf16[12,32,128]{2,1,0:T(8,128)(2,1)S(1)}, bf16[12,32,128]{2,1,0:T(8,128)(2,1)S(1)}, u32[]{:S(2)}, u32[]{:S(2)}) collective-permute-start(bf16[12,32,128]{2,1,0:T(8,128)(2,1)S(1)} %slice.1022), channel_id=1, source_target_pairs={{0,16},{1,17},{2,18},{3,19},{4,20},{5,21},{6,22},{7,23},{8,24},{9,... | collective-permute-start | bytes 294920 | tf_op jit(solution)/shard_map/ppermute | solution.py:350
  42.2 2.2 %collective-permute-done.9 = bf16[14,32,128]{2,1,0:T(8,128)(2,1)S(1)} collective-permute-done((bf16[14,32,128]{2,1,0:T(8,128)(2,1)S(1)}, bf16[14,32,128]{2,1,0:T(8,128)(2,1)S(1)}, u32[]{:S(2)}, u32[]{:S(2)}) %collective-permute-start.9) | collective-permute-done | bytes 114720 | tf_op jit(solution)/shard_map/ppermute | solution.py:350
  44.7 1.6 %collective-permute-start.12 = (f32[44,128]{1,0:T(8,128)S(1)}, f32[44,128]{1,0:T(8,128)S(1)}, u32[]{:S(2)}, u32[]{:S(2)}) collective-permute-start(f32[44,128]{1,0:T(8,128)S(1)} %pad_maximum_fusion.25), channel_id=1, source_target_pairs={{0,16},{1,17},{2,18},{3,19},{4,20},{5,21},{6,22},{7,23},{8,24},{9,... | collective-permute-start | bytes 67592 | tf_op jit(solution)/shard_map/ppermute | solution.py:350
  46.4 2.2 %collective-permute-done.12 = f32[44,128]{1,0:T(8,128)S(1)} collective-permute-done((f32[44,128]{1,0:T(8,128)S(1)}, f32[44,128]{1,0:T(8,128)S(1)}, u32[]{:S(2)}, u32[]{:S(2)}) %collective-permute-start.12) | collective-permute-done | bytes 22560 | tf_op jit(solution)/shard_map/ppermute | solution.py:350
  48.8 1.4 %collective-permute-done.14 = f32[14,32,128]{2,1,0:T(8,128)S(1)} collective-permute-done((f32[14,32,128]{2,1,0:T(8,128)S(1)}, f32[14,32,128]{2,1,0:T(8,128)S(1)}, u32[]{:S(2)}, u32[]{:S(2)}) %collective-permute-start.14) | collective-permute-done | bytes 229408 | tf_op jit(solution)/shard_map/ppermute | solution.py:353
  50.5 1.6 %collective-permute-start.15 = (bf16[12,32,128]{2,1,0:T(8,128)(2,1)S(1)}, bf16[12,32,128]{2,1,0:T(8,128)(2,1)S(1)}, u32[]{:S(2)}, u32[]{:S(2)}) collective-permute-start(bf16[12,32,128]{2,1,0:T(8,128)(2,1)S(1)} %get-tuple-element.96), channel_id=1, source_target_pairs={{0,16},{1,17},{2,18},{3,19},{4,20},{5,21},{6,22},{7,23},{8,15},{9,... | collective-permute-start | bytes 294920 | tf_op jit(solution)/shard_map/ppermute | solution.py:350
  52.2 2.5 %collective-permute-start.16 = (bf16[12,32,128]{2,1,0:T(8,128)(2,1)S(1)}, bf16[12,32,128]{2,1,0:T(8,128)(2,1)S(1)}, u32[]{:S(2)}, u32[]{:S(2)}) collective-permute-start(bf16[12,32,128]{2,1,0:T(8,128)(2,1)S(1)} %get-tuple-element.96), channel_id=1, source_target_pairs={{0,6},{1,7},{2,4},{3,5},{4,2},{5,3},{6,0},{7,1},{8,13},{9,12},{10,... | collective-permute-start | bytes 294920 | tf_op jit(solution)/shard_map/ppermute | solution.py:350
  54.7 2.0 %collective-permute-start.18 = (bf16[12,32,128]{2,1,0:T(8,128)(2,1)S(1)}, bf16[12,32,128]{2,1,0:T(8,128)(2,1)S(1)}, u32[]{:S(2)}, u32[]{:S(2)}) collective-permute-start(bf16[12,32,128]{2,1,0:T(8,128)(2,1)S(1)} %get-tuple-element.96), channel_id=1, source_target_pairs={{0,2},{1,3},{2,0},{3,1},{4,6},{5,7},{6,4},{7,5},{8,9},{9,8},{10,11... | collective-permute-start | bytes 294920 | tf_op jit(solution)/shard_map/ppermute | solution.py:350
  56.6 0.4 collective-permute-start.19
  57.2 0.8 collective-permute-done.19
  58.0 4.2 %shard_map.89 = bf16[54,32,128]{2,1,0:T(8,128)(2,1)S(1)} custom-call(s32[1,256]{1,0:T(1,128)S(1)} %get-tuple-element.48.loads, s32[48]{0:T(128)S(1)} %fusion.82.place, bf16[25,32,128]{2,1,0:T(8,128)(2,1)S(1)} %pad_maximum_fusion.1.field, bf16[48,640,128]{2,1,0:T(8,128)(2,1)} %get-tuple-element.62.source), custom_call_target="tpu_custom_call" | custom-call | flops 2013265920 | bytes 7864320 | tf_op jit(solution)/shard_map/pallas_call | solution.py:215
  62.9 1.2 collective-permute-done.20
  64.9 1.3 %collective-permute-done.21 = bf16[25,32,128]{2,1,0:T(8,128)(2,1)S(1)} collective-permute-done((bf16[25,32,128]{2,1,0:T(8,128)(2,1)S(1)}, bf16[25,32,128]{2,1,0:T(8,128)(2,1)S(1)}, u32[]{:S(2)}, u32[]{:S(2)}) %collective-permute-start.21) | collective-permute-done | bytes 204832 | tf_op jit(solution)/shard_map/ppermute | solution.py:353
  66.5 2.4 %collective-permute-start.22 = (bf16[13,32,128]{2,1,0:T(8,128)(2,1)S(1)}, bf16[13,32,128]{2,1,0:T(8,128)(2,1)S(1)}, u32[]{:S(2)}, u32[]{:S(2)}) collective-permute-start(bf16[13,32,128]{2,1,0:T(8,128)(2,1)S(1)} %get-tuple-element.210), channel_id=1, source_target_pairs={{0,6},{1,7},{2,4},{3,5},{4,2},{5,3},{6,0},{7,1},{8,13},{9,12},{10,... | collective-permute-start | bytes 319496 | tf_op jit(solution)/shard_map/ppermute | solution.py:350
  68.9 2.1 %collective-permute-start.24 = (bf16[13,32,128]{2,1,0:T(8,128)(2,1)S(1)}, bf16[13,32,128]{2,1,0:T(8,128)(2,1)S(1)}, u32[]{:S(2)}, u32[]{:S(2)}) collective-permute-start(bf16[13,32,128]{2,1,0:T(8,128)(2,1)S(1)} %get-tuple-element.212), channel_id=1, source_target_pairs={{0,2},{1,3},{2,0},{3,1},{4,6},{5,7},{6,4},{7,5},{8,9},{9,8},{10,11... | collective-permute-start | bytes 319496 | tf_op jit(solution)/shard_map/ppermute | solution.py:350
  71.0 0.8 collective-permute-start.25
  71.8 4.2 %shard_map.90 = f32[24,32,128]{2,1,0:T(8,128)S(1)} custom-call(s32[1,256]{1,0:T(1,128)S(1)} %get-tuple-element.59.loads, s32[24]{0:T(128)S(1)} %fusion.83.place, bf16[55,32,128]{2,1,0:T(8,128)(2,1)S(1)} %constant_dynamic-update-slice_fusion.22.field, bf16[24,1280,128]{2,1,0:T(8,128)(2,1)} %get-tuple-element.69.source), custom_call_target="tpu_custom_call" | custom-call | flops 2013265920 | bytes 7864320 | tf_op jit(solution)/shard_map/pallas_call | solution.py:215
  76.0 1.3 %collective-permute-start.27 = (bf16[12,32,128]{2,1,0:T(8,128)(2,1)S(1)}, bf16[12,32,128]{2,1,0:T(8,128)(2,1)S(1)}, u32[]{:S(2)}, u32[]{:S(2)}) collective-permute-start(bf16[12,32,128]{2,1,0:T(8,128)(2,1)S(1)} %slice.1021), channel_id=1, source_target_pairs={{0,16},{1,17},{2,18},{3,19},{4,20},{5,21},{6,22},{7,23},{8,24},{9,... | collective-permute-start | bytes 294920 | tf_op jit(solution)/shard_map/ppermute | solution.py:350
  77.4 1.4 %collective-permute-done.23 = bf16[13,32,128]{2,1,0:T(8,128)(2,1)S(1)} collective-permute-done((bf16[13,32,128]{2,1,0:T(8,128)(2,1)S(1)}, bf16[13,32,128]{2,1,0:T(8,128)(2,1)S(1)}, u32[]{:S(2)}, u32[]{:S(2)}) %collective-permute-start.23) | collective-permute-done | bytes 106528 | tf_op jit(solution)/shard_map/ppermute | solution.py:350
  78.9 0.5 collective-permute-start.26
  79.4 1.3 %collective-permute-done.27 = bf16[12,32,128]{2,1,0:T(8,128)(2,1)S(1)} collective-permute-done((bf16[12,32,128]{2,1,0:T(8,128)(2,1)S(1)}, bf16[12,32,128]{2,1,0:T(8,128)(2,1)S(1)}, u32[]{:S(2)}, u32[]{:S(2)}) %collective-permute-start.27) | collective-permute-done | bytes 98336 | tf_op jit(solution)/shard_map/ppermute | solution.py:350
  80.8 1.9 %collective-permute-done.26 = f32[32,128]{1,0:T(8,128)S(1)} collective-permute-done((f32[32,128]{1,0:T(8,128)S(1)}, f32[32,128]{1,0:T(8,128)S(1)}, u32[]{:S(2)}, u32[]{:S(2)}) %collective-permute-start.26) | collective-permute-done | bytes 16416 | tf_op jit(solution)/shard_map/ppermute | solution.py:350
  83.1 1.2 collective-permute-done.28
  84.6 1.6 %collective-permute-start.29 = (bf16[12,32,128]{2,1,0:T(8,128)(2,1)S(1)}, bf16[12,32,128]{2,1,0:T(8,128)(2,1)S(1)}, u32[]{:S(2)}, u32[]{:S(2)}) collective-permute-start(bf16[12,32,128]{2,1,0:T(8,128)(2,1)S(1)} %get-tuple-element.90), channel_id=1, source_target_pairs={{0,16},{1,17},{2,18},{3,19},{4,20},{5,21},{6,22},{7,23},{8,15},{9,... | collective-permute-start | bytes 294920 | tf_op jit(solution)/shard_map/ppermute | solution.py:350
  86.2 2.5 %collective-permute-start.30 = (bf16[12,32,128]{2,1,0:T(8,128)(2,1)S(1)}, bf16[12,32,128]{2,1,0:T(8,128)(2,1)S(1)}, u32[]{:S(2)}, u32[]{:S(2)}) collective-permute-start(bf16[12,32,128]{2,1,0:T(8,128)(2,1)S(1)} %get-tuple-element.90), channel_id=1, source_target_pairs={{0,6},{1,7},{2,4},{3,5},{4,2},{5,3},{6,0},{7,1},{8,13},{9,12},{10,... | collective-permute-start | bytes 294920 | tf_op jit(solution)/shard_map/ppermute | solution.py:350
  88.7 2.0 %collective-permute-start.32 = (bf16[12,32,128]{2,1,0:T(8,128)(2,1)S(1)}, bf16[12,32,128]{2,1,0:T(8,128)(2,1)S(1)}, u32[]{:S(2)}, u32[]{:S(2)}) collective-permute-start(bf16[12,32,128]{2,1,0:T(8,128)(2,1)S(1)} %get-tuple-element.90), channel_id=1, source_target_pairs={{0,2},{1,3},{2,0},{3,1},{4,6},{5,7},{6,4},{7,5},{8,9},{9,8},{10,11... | collective-permute-start | bytes 294920 | tf_op jit(solution)/shard_map/ppermute | solution.py:350
  90.6 0.6 collective-permute-start.33
  91.4 0.8 collective-permute-done.33
  92.3 4.2 %shard_map.91 = bf16[54,32,128]{2,1,0:T(8,128)(2,1)S(1)} custom-call(s32[1,256]{1,0:T(1,128)S(1)} %get-tuple-element.48.loads, s32[48]{0:T(128)S(1)} %fusion.82.place, bf16[25,32,128]{2,1,0:T(8,128)(2,1)S(1)} %pad_maximum_fusion.field, bf16[48,640,128]{2,1,0:T(8,128)(2,1)} %get-tuple-element.62.source), custom_call_target="tpu_custom_call" | custom-call | flops 2013265920 | bytes 7864320 | tf_op jit(solution)/shard_map/pallas_call | solution.py:215
  96.5 0.4 collective-permute-done.31
  97.1 1.3 %collective-permute-done.34 = bf16[18,32,128]{2,1,0:T(8,128)(2,1)S(1)} collective-permute-done((bf16[18,32,128]{2,1,0:T(8,128)(2,1)S(1)}, bf16[18,32,128]{2,1,0:T(8,128)(2,1)S(1)}, u32[]{:S(2)}, u32[]{:S(2)}) %collective-permute-start.34) | collective-permute-done | bytes 147488 | tf_op jit(solution)/shard_map/ppermute | solution.py:353
  99.2 1.3 %collective-permute-done.35 = bf16[25,32,128]{2,1,0:T(8,128)(2,1)S(1)} collective-permute-done((bf16[25,32,128]{2,1,0:T(8,128)(2,1)S(1)}, bf16[25,32,128]{2,1,0:T(8,128)(2,1)S(1)}, u32[]{:S(2)}, u32[]{:S(2)}) %collective-permute-start.35) | collective-permute-done | bytes 204832 | tf_op jit(solution)/shard_map/ppermute | solution.py:353
  100.8 2.6 %collective-permute-start.36 = (bf16[13,32,128]{2,1,0:T(8,128)(2,1)S(1)}, bf16[13,32,128]{2,1,0:T(8,128)(2,1)S(1)}, u32[]{:S(2)}, u32[]{:S(2)}) collective-permute-start(bf16[13,32,128]{2,1,0:T(8,128)(2,1)S(1)} %get-tuple-element.206), channel_id=1, source_target_pairs={{0,6},{1,7},{2,4},{3,5},{4,2},{5,3},{6,0},{7,1},{8,13},{9,12},{10,... | collective-permute-start | bytes 319496 | tf_op jit(solution)/shard_map/ppermute | solution.py:350
  103.4 1.8 %collective-permute-start.38 = (bf16[13,32,128]{2,1,0:T(8,128)(2,1)S(1)}, bf16[13,32,128]{2,1,0:T(8,128)(2,1)S(1)}, u32[]{:S(2)}, u32[]{:S(2)}) collective-permute-start(bf16[13,32,128]{2,1,0:T(8,128)(2,1)S(1)} %get-tuple-element.208), channel_id=1, source_target_pairs={{0,2},{1,3},{2,0},{3,1},{4,6},{5,7},{6,4},{7,5},{8,9},{9,8},{10,11... | collective-permute-start | bytes 319496 | tf_op jit(solution)/shard_map/ppermute | solution.py:350
  105.3 0.7 collective-permute-start.39
  105.9 4.2 %shard_map.92 = f32[24,32,128]{2,1,0:T(8,128)S(1)} custom-call(s32[1,256]{1,0:T(1,128)S(1)} %get-tuple-element.59.loads, s32[24]{0:T(128)S(1)} %fusion.83.place, bf16[55,32,128]{2,1,0:T(8,128)(2,1)S(1)} %constant_dynamic-update-slice_fusion.37.field, bf16[24,1280,128]{2,1,0:T(8,128)(2,1)} %get-tuple-element.69.source), custom_call_target="tpu_custom_call" | custom-call | flops 2013265920 | bytes 7864320 | tf_op jit(solution)/shard_map/pallas_call | solution.py:215
  110.2 1.2 %collective-permute-start.41 = (bf16[12,32,128]{2,1,0:T(8,128)(2,1)S(1)}, bf16[12,32,128]{2,1,0:T(8,128)(2,1)S(1)}, u32[]{:S(2)}, u32[]{:S(2)}) collective-permute-start(bf16[12,32,128]{2,1,0:T(8,128)(2,1)S(1)} %slice.1020), channel_id=1, source_target_pairs={{0,16},{1,17},{2,18},{3,19},{4,20},{5,21},{6,22},{7,23},{8,24},{9,... | collective-permute-start | bytes 294920 | tf_op jit(solution)/shard_map/ppermute | solution.py:350
  111.4 1.3 %collective-permute-done.37 = bf16[13,32,128]{2,1,0:T(8,128)(2,1)S(1)} collective-permute-done((bf16[13,32,128]{2,1,0:T(8,128)(2,1)S(1)}, bf16[13,32,128]{2,1,0:T(8,128)(2,1)S(1)}, u32[]{:S(2)}, u32[]{:S(2)}) %collective-permute-start.37) | collective-permute-done | bytes 106528 | tf_op jit(solution)/shard_map/ppermute | solution.py:350
  112.9 1.0 collective-permute-start.40
  113.9 1.0 collective-permute-done.41
  115.0 1.8 %collective-permute-done.40 = f32[32,128]{1,0:T(8,128)S(1)} collective-permute-done((f32[32,128]{1,0:T(8,128)S(1)}, f32[32,128]{1,0:T(8,128)S(1)}, u32[]{:S(2)}, u32[]{:S(2)}) %collective-permute-start.40) | collective-permute-done | bytes 16416 | tf_op jit(solution)/shard_map/ppermute | solution.py:350
  116.8 1.0 collective-permute-start.42
  117.7 1.1 collective-permute-done.42
  119.2 0.7 shard_map.93
  (209 shorter events, 8.1 us)
Async XLA Ops:
  0.6 0.9 copy-start
  1.5 2.1 %collective-permute-start = (f32[6,32,128]{2,1,0:T(8,128)S(1)}, f32[6,32,128]{2,1,0:T(8,128)S(1)}, u32[]{:S(2)}, u32[]{:S(2)}) collective-permute-start(f32[6,32,128]{2,1,0:T(8,128)S(1)} %bitcast_bitcast_fusion), channel_id=1, source_target_pairs={{0,8},{8,0},{16,24},{24,16},{1,9},{9,1},{17,25},{25,17},{2,10},{10... | collective-permute-start | bytes 294920 | tf_op jit(solution)/shard_map/ppermute | solution.py:353
  3.7 5.3 %collective-permute-start.1 = (bf16[12,32,128]{2,1,0:T(8,128)(2,1)S(1)}, bf16[12,32,128]{2,1,0:T(8,128)(2,1)S(1)}, u32[]{:S(2)}, u32[]{:S(2)}) collective-permute-start(bf16[12,32,128]{2,1,0:T(8,128)(2,1)S(1)} %fusion.15), channel_id=1, source_target_pairs={{0,16},{1,17},{2,18},{3,19},{4,20},{5,21},{6,22},{7,23},{8,15},{9,... | collective-permute-start | bytes 294920 | tf_op jit(solution)/shard_map/ppermute | solution.py:350
  6.4 0.7 copy-start.1
  7.0 0.7 copy-start.2
  9.0 7.8 %collective-permute-start.5 = (bf16[12,32,128]{2,1,0:T(8,128)(2,1)S(1)}, bf16[12,32,128]{2,1,0:T(8,128)(2,1)S(1)}, u32[]{:S(2)}, u32[]{:S(2)}) collective-permute-start(bf16[12,32,128]{2,1,0:T(8,128)(2,1)S(1)} %collective-permute-done.1), channel_id=1, source_target_pairs={{0,8},{8,0},{16,24},{24,16},{1,9},{9,1},{17,25},{25,17},{2,10},{10... | collective-permute-start | bytes 294920 | tf_op jit(solution)/shard_map/ppermute | solution.py:353
  12.3 12.2 %collective-permute-start.2 = (bf16[12,32,128]{2,1,0:T(8,128)(2,1)S(1)}, bf16[12,32,128]{2,1,0:T(8,128)(2,1)S(1)}, u32[]{:S(2)}, u32[]{:S(2)}) collective-permute-start(bf16[12,32,128]{2,1,0:T(8,128)(2,1)S(1)} %fusion.15), channel_id=1, source_target_pairs={{0,6},{1,7},{2,4},{3,5},{4,2},{5,3},{6,0},{7,1},{8,13},{9,12},{10,... | collective-permute-start | bytes 294920 | tf_op jit(solution)/shard_map/ppermute | solution.py:350
  15.1 9.4 %collective-permute-start.3 = (bf16[12,32,128]{2,1,0:T(8,128)(2,1)S(1)}, bf16[12,32,128]{2,1,0:T(8,128)(2,1)S(1)}, u32[]{:S(2)}, u32[]{:S(2)}) collective-permute-start(bf16[12,32,128]{2,1,0:T(8,128)(2,1)S(1)} %fusion.15), channel_id=1, source_target_pairs={{0,4},{1,5},{2,6},{3,7},{4,0},{5,1},{6,2},{7,3},{8,11},{9,10},{10,... | collective-permute-start | bytes 294920 | tf_op jit(solution)/shard_map/ppermute | solution.py:350
  15.1 9.4 %collective-permute-start.4 = (bf16[12,32,128]{2,1,0:T(8,128)(2,1)S(1)}, bf16[12,32,128]{2,1,0:T(8,128)(2,1)S(1)}, u32[]{:S(2)}, u32[]{:S(2)}) collective-permute-start(bf16[12,32,128]{2,1,0:T(8,128)(2,1)S(1)} %fusion.15), channel_id=1, source_target_pairs={{0,2},{1,3},{2,0},{3,1},{4,6},{5,7},{6,4},{7,5},{8,9},{9,8},{10,11... | collective-permute-start | bytes 294920 | tf_op jit(solution)/shard_map/ppermute | solution.py:350
  24.6 21.7 %copy-start.3 = (pred[12]{0:T(512)(128)(4,1)S(1)}, pred[12]{0:T(512)(128)(4,1)}, u32[]{:S(2)}) copy-start(pred[12]{0:T(512)(128)(4,1)} %constant.88.clone.1) | copy-start | bytes 40
  24.6 1.5 %collective-permute-start.6 = (bf16[18,32,128]{2,1,0:T(8,128)(2,1)S(1)}, bf16[18,32,128]{2,1,0:T(8,128)(2,1)S(1)}, u32[]{:S(2)}, u32[]{:S(2)}) collective-permute-start(bf16[18,32,128]{2,1,0:T(8,128)(2,1)S(1)} %pad_maximum_fusion.22), channel_id=1, source_target_pairs={{0,8},{8,0},{16,24},{24,16},{1,9},{9,1},{17,25},{25,17},{2,10},{10... | collective-permute-start | bytes 442376 | tf_op jit(solution)/shard_map/ppermute | solution.py:353
  26.8 1.5 %collective-permute-start.7 = (bf16[27,32,128]{2,1,0:T(8,128)(2,1)S(1)}, bf16[27,32,128]{2,1,0:T(8,128)(2,1)S(1)}, u32[]{:S(2)}, u32[]{:S(2)}) collective-permute-start(bf16[27,32,128]{2,1,0:T(8,128)(2,1)S(1)} %pad_maximum_fusion.8), channel_id=1, source_target_pairs={{0,8},{8,0},{16,24},{24,16},{1,9},{9,1},{17,25},{25,17},{2,10},{10... | collective-permute-start | bytes 663560 | tf_op jit(solution)/shard_map/ppermute | solution.py:353
  29.0 13.2 %collective-permute-start.10 = (bf16[14,32,128]{2,1,0:T(8,128)(2,1)S(1)}, bf16[14,32,128]{2,1,0:T(8,128)(2,1)S(1)}, u32[]{:S(2)}, u32[]{:S(2)}) collective-permute-start(bf16[14,32,128]{2,1,0:T(8,128)(2,1)S(1)} %get-tuple-element.216), channel_id=1, source_target_pairs={{0,2},{1,3},{2,0},{3,1},{4,6},{5,7},{6,4},{7,5},{8,9},{9,8},{10,11... | collective-permute-start | bytes 344072 | tf_op jit(solution)/shard_map/ppermute | solution.py:350
  29.4 12.9 %collective-permute-start.11 = (bf16[14,32,128]{2,1,0:T(8,128)(2,1)S(1)}, bf16[14,32,128]{2,1,0:T(8,128)(2,1)S(1)}, u32[]{:S(2)}, u32[]{:S(2)}) collective-permute-start(bf16[14,32,128]{2,1,0:T(8,128)(2,1)S(1)} %get-tuple-element.217), channel_id=1, source_target_pairs={{8,15},{9,14},{10,13},{11,12},{12,11},{13,10},{14,9},{15,8},{24,31... | collective-permute-start | bytes 344072 | tf_op jit(solution)/shard_map/ppermute | solution.py:350
  30.0 12.2 %collective-permute-start.8 = (bf16[14,32,128]{2,1,0:T(8,128)(2,1)S(1)}, bf16[14,32,128]{2,1,0:T(8,128)(2,1)S(1)}, u32[]{:S(2)}, u32[]{:S(2)}) collective-permute-start(bf16[14,32,128]{2,1,0:T(8,128)(2,1)S(1)} %get-tuple-element.214), channel_id=1, source_target_pairs={{0,6},{1,7},{2,4},{3,5},{4,2},{5,3},{6,0},{7,1},{8,13},{9,12},{10,... | collective-permute-start | bytes 344072 | tf_op jit(solution)/shard_map/ppermute | solution.py:350
  32.4 12.0 %collective-permute-start.9 = (bf16[14,32,128]{2,1,0:T(8,128)(2,1)S(1)}, bf16[14,32,128]{2,1,0:T(8,128)(2,1)S(1)}, u32[]{:S(2)}, u32[]{:S(2)}) collective-permute-start(bf16[14,32,128]{2,1,0:T(8,128)(2,1)S(1)} %get-tuple-element.215), channel_id=1, source_target_pairs={{0,4},{1,5},{2,6},{3,7},{4,0},{5,1},{6,2},{7,3},{8,11},{9,10},{10,... | collective-permute-start | bytes 344072 | tf_op jit(solution)/shard_map/ppermute | solution.py:350
  40.7 5.6 %collective-permute-start.13 = (bf16[12,32,128]{2,1,0:T(8,128)(2,1)S(1)}, bf16[12,32,128]{2,1,0:T(8,128)(2,1)S(1)}, u32[]{:S(2)}, u32[]{:S(2)}) collective-permute-start(bf16[12,32,128]{2,1,0:T(8,128)(2,1)S(1)} %slice.1022), channel_id=1, source_target_pairs={{0,16},{1,17},{2,18},{3,19},{4,20},{5,21},{6,22},{7,23},{8,24},{9,... | collective-permute-start | bytes 294920 | tf_op jit(solution)/shard_map/ppermute | solution.py:350
  44.7 3.9 %collective-permute-start.12 = (f32[44,128]{1,0:T(8,128)S(1)}, f32[44,128]{1,0:T(8,128)S(1)}, u32[]{:S(2)}, u32[]{:S(2)}) collective-permute-start(f32[44,128]{1,0:T(8,128)S(1)} %pad_maximum_fusion.25), channel_id=1, source_target_pairs={{0,16},{1,17},{2,18},{3,19},{4,20},{5,21},{6,22},{7,23},{8,24},{9,... | collective-permute-start | bytes 67592 | tf_op jit(solution)/shard_map/ppermute | solution.py:350
  48.6 1.6 %collective-permute-start.14 = (f32[14,32,128]{2,1,0:T(8,128)S(1)}, f32[14,32,128]{2,1,0:T(8,128)S(1)}, u32[]{:S(2)}, u32[]{:S(2)}) collective-permute-start(f32[14,32,128]{2,1,0:T(8,128)S(1)} %pad_maximum_fusion.7), channel_id=1, source_target_pairs={{0,8},{8,0},{16,24},{24,16},{1,9},{9,1},{17,25},{25,17},{2,10},{10... | collective-permute-start | bytes 688136 | tf_op jit(solution)/shard_map/ppermute | solution.py:353
  50.5 6.1 %collective-permute-start.15 = (bf16[12,32,128]{2,1,0:T(8,128)(2,1)S(1)}, bf16[12,32,128]{2,1,0:T(8,128)(2,1)S(1)}, u32[]{:S(2)}, u32[]{:S(2)}) collective-permute-start(bf16[12,32,128]{2,1,0:T(8,128)(2,1)S(1)} %get-tuple-element.96), channel_id=1, source_target_pairs={{0,16},{1,17},{2,18},{3,19},{4,20},{5,21},{6,22},{7,23},{8,15},{9,... | collective-permute-start | bytes 294920 | tf_op jit(solution)/shard_map/ppermute | solution.py:350
  52.2 10.1 %collective-permute-start.16 = (bf16[12,32,128]{2,1,0:T(8,128)(2,1)S(1)}, bf16[12,32,128]{2,1,0:T(8,128)(2,1)S(1)}, u32[]{:S(2)}, u32[]{:S(2)}) collective-permute-start(bf16[12,32,128]{2,1,0:T(8,128)(2,1)S(1)} %get-tuple-element.96), channel_id=1, source_target_pairs={{0,6},{1,7},{2,4},{3,5},{4,2},{5,3},{6,0},{7,1},{8,13},{9,12},{10,... | collective-permute-start | bytes 294920 | tf_op jit(solution)/shard_map/ppermute | solution.py:350
  54.7 7.8 %collective-permute-start.17 = (bf16[12,32,128]{2,1,0:T(8,128)(2,1)S(1)}, bf16[12,32,128]{2,1,0:T(8,128)(2,1)S(1)}, u32[]{:S(2)}, u32[]{:S(2)}) collective-permute-start(bf16[12,32,128]{2,1,0:T(8,128)(2,1)S(1)} %get-tuple-element.96), channel_id=1, source_target_pairs={{0,4},{1,5},{2,6},{3,7},{4,0},{5,1},{6,2},{7,3},{8,11},{9,10},{10,... | collective-permute-start | bytes 294920 | tf_op jit(solution)/shard_map/ppermute | solution.py:350
  54.7 7.8 %collective-permute-start.18 = (bf16[12,32,128]{2,1,0:T(8,128)(2,1)S(1)}, bf16[12,32,128]{2,1,0:T(8,128)(2,1)S(1)}, u32[]{:S(2)}, u32[]{:S(2)}) collective-permute-start(bf16[12,32,128]{2,1,0:T(8,128)(2,1)S(1)} %get-tuple-element.96), channel_id=1, source_target_pairs={{0,2},{1,3},{2,0},{3,1},{4,6},{5,7},{6,4},{7,5},{8,9},{9,8},{10,11... | collective-permute-start | bytes 294920 | tf_op jit(solution)/shard_map/ppermute | solution.py:350
  56.6 1.3 %collective-permute-start.19 = (bf16[12,32,128]{2,1,0:T(8,128)(2,1)S(1)}, bf16[12,32,128]{2,1,0:T(8,128)(2,1)S(1)}, u32[]{:S(2)}, u32[]{:S(2)}) collective-permute-start(bf16[12,32,128]{2,1,0:T(8,128)(2,1)S(1)} %collective-permute-done.15), channel_id=1, source_target_pairs={{0,8},{8,0},{16,24},{24,16},{1,9},{9,1},{17,25},{25,17},{2,10},{10... | collective-permute-start | bytes 294920 | tf_op jit(solution)/shard_map/ppermute | solution.py:353
  62.7 1.4 %collective-permute-start.20 = (bf16[18,32,128]{2,1,0:T(8,128)(2,1)S(1)}, bf16[18,32,128]{2,1,0:T(8,128)(2,1)S(1)}, u32[]{:S(2)}, u32[]{:S(2)}) collective-permute-start(bf16[18,32,128]{2,1,0:T(8,128)(2,1)S(1)} %pad_maximum_fusion.23), channel_id=1, source_target_pairs={{0,8},{8,0},{16,24},{24,16},{1,9},{9,1},{17,25},{25,17},{2,10},{10... | collective-permute-start | bytes 442376 | tf_op jit(solution)/shard_map/ppermute | solution.py:353
  64.6 1.5 %collective-permute-start.21 = (bf16[25,32,128]{2,1,0:T(8,128)(2,1)S(1)}, bf16[25,32,128]{2,1,0:T(8,128)(2,1)S(1)}, u32[]{:S(2)}, u32[]{:S(2)}) collective-permute-start(bf16[25,32,128]{2,1,0:T(8,128)(2,1)S(1)} %pad_maximum_fusion.19), channel_id=1, source_target_pairs={{0,8},{8,0},{16,24},{24,16},{1,9},{9,1},{17,25},{25,17},{2,10},{10... | collective-permute-start | bytes 614408 | tf_op jit(solution)/shard_map/ppermute | solution.py:353
  66.5 10.9 %collective-permute-start.22 = (bf16[13,32,128]{2,1,0:T(8,128)(2,1)S(1)}, bf16[13,32,128]{2,1,0:T(8,128)(2,1)S(1)}, u32[]{:S(2)}, u32[]{:S(2)}) collective-permute-start(bf16[13,32,128]{2,1,0:T(8,128)(2,1)S(1)} %get-tuple-element.210), channel_id=1, source_target_pairs={{0,6},{1,7},{2,4},{3,5},{4,2},{5,3},{6,0},{7,1},{8,13},{9,12},{10,... | collective-permute-start | bytes 319496 | tf_op jit(solution)/shard_map/ppermute | solution.py:350
  68.9 9.9 %collective-permute-start.23 = (bf16[13,32,128]{2,1,0:T(8,128)(2,1)S(1)}, bf16[13,32,128]{2,1,0:T(8,128)(2,1)S(1)}, u32[]{:S(2)}, u32[]{:S(2)}) collective-permute-start(bf16[13,32,128]{2,1,0:T(8,128)(2,1)S(1)} %get-tuple-element.211), channel_id=1, source_target_pairs={{0,4},{1,5},{2,6},{3,7},{4,0},{5,1},{6,2},{7,3},{8,11},{9,10},{10,... | collective-permute-start | bytes 319496 | tf_op jit(solution)/shard_map/ppermute | solution.py:350
  68.9 9.9 %collective-permute-start.24 = (bf16[13,32,128]{2,1,0:T(8,128)(2,1)S(1)}, bf16[13,32,128]{2,1,0:T(8,128)(2,1)S(1)}, u32[]{:S(2)}, u32[]{:S(2)}) collective-permute-start(bf16[13,32,128]{2,1,0:T(8,128)(2,1)S(1)} %get-tuple-element.212), channel_id=1, source_target_pairs={{0,2},{1,3},{2,0},{3,1},{4,6},{5,7},{6,4},{7,5},{8,9},{9,8},{10,11... | collective-permute-start | bytes 319496 | tf_op jit(solution)/shard_map/ppermute | solution.py:350
  71.0 7.8 %collective-permute-start.25 = (bf16[13,32,128]{2,1,0:T(8,128)(2,1)S(1)}, bf16[13,32,128]{2,1,0:T(8,128)(2,1)S(1)}, u32[]{:S(2)}, u32[]{:S(2)}) collective-permute-start(bf16[13,32,128]{2,1,0:T(8,128)(2,1)S(1)} %get-tuple-element.213), channel_id=1, source_target_pairs={{8,15},{9,14},{10,13},{11,12},{12,11},{13,10},{14,9},{15,8},{24,31... | collective-permute-start | bytes 319496 | tf_op jit(solution)/shard_map/ppermute | solution.py:350
  76.0 4.7 %collective-permute-start.27 = (bf16[12,32,128]{2,1,0:T(8,128)(2,1)S(1)}, bf16[12,32,128]{2,1,0:T(8,128)(2,1)S(1)}, u32[]{:S(2)}, u32[]{:S(2)}) collective-permute-start(bf16[12,32,128]{2,1,0:T(8,128)(2,1)S(1)} %slice.1021), channel_id=1, source_target_pairs={{0,16},{1,17},{2,18},{3,19},{4,20},{5,21},{6,22},{7,23},{8,24},{9,... | collective-permute-start | bytes 294920 | tf_op jit(solution)/shard_map/ppermute | solution.py:350
  78.9 3.8 %collective-permute-start.26 = (f32[32,128]{1,0:T(8,128)S(1)}, f32[32,128]{1,0:T(8,128)S(1)}, u32[]{:S(2)}, u32[]{:S(2)}) collective-permute-start(f32[32,128]{1,0:T(8,128)S(1)} %select_add_fusion.3), channel_id=1, source_target_pairs={{0,16},{1,17},{2,18},{3,19},{4,20},{5,21},{6,22},{7,23},{8,24},{9,... | collective-permute-start | bytes 49160 | tf_op jit(solution)/shard_map/ppermute | solution.py:350
  82.7 1.5 %collective-permute-start.28 = (f32[13,32,128]{2,1,0:T(8,128)S(1)}, f32[13,32,128]{2,1,0:T(8,128)S(1)}, u32[]{:S(2)}, u32[]{:S(2)}) collective-permute-start(f32[13,32,128]{2,1,0:T(8,128)S(1)} %pad_maximum_fusion.17), channel_id=1, source_target_pairs={{0,8},{8,0},{16,24},{24,16},{1,9},{9,1},{17,25},{25,17},{2,10},{10... | collective-permute-start | bytes 638984 | tf_op jit(solution)/shard_map/ppermute | solution.py:353
  84.6 6.0 %collective-permute-start.29 = (bf16[12,32,128]{2,1,0:T(8,128)(2,1)S(1)}, bf16[12,32,128]{2,1,0:T(8,128)(2,1)S(1)}, u32[]{:S(2)}, u32[]{:S(2)}) collective-permute-start(bf16[12,32,128]{2,1,0:T(8,128)(2,1)S(1)} %get-tuple-element.90), channel_id=1, source_target_pairs={{0,16},{1,17},{2,18},{3,19},{4,20},{5,21},{6,22},{7,23},{8,15},{9,... | collective-permute-start | bytes 294920 | tf_op jit(solution)/shard_map/ppermute | solution.py:350
  86.2 10.3 %collective-permute-start.30 = (bf16[12,32,128]{2,1,0:T(8,128)(2,1)S(1)}, bf16[12,32,128]{2,1,0:T(8,128)(2,1)S(1)}, u32[]{:S(2)}, u32[]{:S(2)}) collective-permute-start(bf16[12,32,128]{2,1,0:T(8,128)(2,1)S(1)} %get-tuple-element.90), channel_id=1, source_target_pairs={{0,6},{1,7},{2,4},{3,5},{4,2},{5,3},{6,0},{7,1},{8,13},{9,12},{10,... | collective-permute-start | bytes 294920 | tf_op jit(solution)/shard_map/ppermute | solution.py:350
  88.7 8.2 %collective-permute-start.31 = (bf16[12,32,128]{2,1,0:T(8,128)(2,1)S(1)}, bf16[12,32,128]{2,1,0:T(8,128)(2,1)S(1)}, u32[]{:S(2)}, u32[]{:S(2)}) collective-permute-start(bf16[12,32,128]{2,1,0:T(8,128)(2,1)S(1)} %get-tuple-element.90), channel_id=1, source_target_pairs={{0,4},{1,5},{2,6},{3,7},{4,0},{5,1},{6,2},{7,3},{8,11},{9,10},{10,... | collective-permute-start | bytes 294920 | tf_op jit(solution)/shard_map/ppermute | solution.py:350
  88.7 8.2 %collective-permute-start.32 = (bf16[12,32,128]{2,1,0:T(8,128)(2,1)S(1)}, bf16[12,32,128]{2,1,0:T(8,128)(2,1)S(1)}, u32[]{:S(2)}, u32[]{:S(2)}) collective-permute-start(bf16[12,32,128]{2,1,0:T(8,128)(2,1)S(1)} %get-tuple-element.90), channel_id=1, source_target_pairs={{0,2},{1,3},{2,0},{3,1},{4,6},{5,7},{6,4},{7,5},{8,9},{9,8},{10,11... | collective-permute-start | bytes 294920 | tf_op jit(solution)/shard_map/ppermute | solution.py:350
  90.6 1.5 %collective-permute-start.33 = (bf16[12,32,128]{2,1,0:T(8,128)(2,1)S(1)}, bf16[12,32,128]{2,1,0:T(8,128)(2,1)S(1)}, u32[]{:S(2)}, u32[]{:S(2)}) collective-permute-start(bf16[12,32,128]{2,1,0:T(8,128)(2,1)S(1)} %collective-permute-done.29), channel_id=1, source_target_pairs={{0,8},{8,0},{16,24},{24,16},{1,9},{9,1},{17,25},{25,17},{2,10},{10... | collective-permute-start | bytes 294920 | tf_op jit(solution)/shard_map/ppermute | solution.py:353
  97.0 1.4 %collective-permute-start.34 = (bf16[18,32,128]{2,1,0:T(8,128)(2,1)S(1)}, bf16[18,32,128]{2,1,0:T(8,128)(2,1)S(1)}, u32[]{:S(2)}, u32[]{:S(2)}) collective-permute-start(bf16[18,32,128]{2,1,0:T(8,128)(2,1)S(1)} %pad_maximum_fusion.24), channel_id=1, source_target_pairs={{0,8},{8,0},{16,24},{24,16},{1,9},{9,1},{17,25},{25,17},{2,10},{10... | collective-permute-start | bytes 442376 | tf_op jit(solution)/shard_map/ppermute | solution.py:353
  99.0 1.5 %collective-permute-start.35 = (bf16[25,32,128]{2,1,0:T(8,128)(2,1)S(1)}, bf16[25,32,128]{2,1,0:T(8,128)(2,1)S(1)}, u32[]{:S(2)}, u32[]{:S(2)}) collective-permute-start(bf16[25,32,128]{2,1,0:T(8,128)(2,1)S(1)} %pad_maximum_fusion.20), channel_id=1, source_target_pairs={{0,8},{8,0},{16,24},{24,16},{1,9},{9,1},{17,25},{25,17},{2,10},{10... | collective-permute-start | bytes 614408 | tf_op jit(solution)/shard_map/ppermute | solution.py:353
  100.8 10.6 %collective-permute-start.36 = (bf16[13,32,128]{2,1,0:T(8,128)(2,1)S(1)}, bf16[13,32,128]{2,1,0:T(8,128)(2,1)S(1)}, u32[]{:S(2)}, u32[]{:S(2)}) collective-permute-start(bf16[13,32,128]{2,1,0:T(8,128)(2,1)S(1)} %get-tuple-element.206), channel_id=1, source_target_pairs={{0,6},{1,7},{2,4},{3,5},{4,2},{5,3},{6,0},{7,1},{8,13},{9,12},{10,... | collective-permute-start | bytes 319496 | tf_op jit(solution)/shard_map/ppermute | solution.py:350
  103.4 9.3 %collective-permute-start.37 = (bf16[13,32,128]{2,1,0:T(8,128)(2,1)S(1)}, bf16[13,32,128]{2,1,0:T(8,128)(2,1)S(1)}, u32[]{:S(2)}, u32[]{:S(2)}) collective-permute-start(bf16[13,32,128]{2,1,0:T(8,128)(2,1)S(1)} %get-tuple-element.207), channel_id=1, source_target_pairs={{0,4},{1,5},{2,6},{3,7},{4,0},{5,1},{6,2},{7,3},{8,11},{9,10},{10,... | collective-permute-start | bytes 319496 | tf_op jit(solution)/shard_map/ppermute | solution.py:350
  103.4 9.2 %collective-permute-start.38 = (bf16[13,32,128]{2,1,0:T(8,128)(2,1)S(1)}, bf16[13,32,128]{2,1,0:T(8,128)(2,1)S(1)}, u32[]{:S(2)}, u32[]{:S(2)}) collective-permute-start(bf16[13,32,128]{2,1,0:T(8,128)(2,1)S(1)} %get-tuple-element.208), channel_id=1, source_target_pairs={{0,2},{1,3},{2,0},{3,1},{4,6},{5,7},{6,4},{7,5},{8,9},{9,8},{10,11... | collective-permute-start | bytes 319496 | tf_op jit(solution)/shard_map/ppermute | solution.py:350
  105.3 7.4 %collective-permute-start.39 = (bf16[13,32,128]{2,1,0:T(8,128)(2,1)S(1)}, bf16[13,32,128]{2,1,0:T(8,128)(2,1)S(1)}, u32[]{:S(2)}, u32[]{:S(2)}) collective-permute-start(bf16[13,32,128]{2,1,0:T(8,128)(2,1)S(1)} %get-tuple-element.209), channel_id=1, source_target_pairs={{8,15},{9,14},{10,13},{11,12},{12,11},{13,10},{14,9},{15,8},{24,31... | collective-permute-start | bytes 319496 | tf_op jit(solution)/shard_map/ppermute | solution.py:350
  110.2 4.7 %collective-permute-start.41 = (bf16[12,32,128]{2,1,0:T(8,128)(2,1)S(1)}, bf16[12,32,128]{2,1,0:T(8,128)(2,1)S(1)}, u32[]{:S(2)}, u32[]{:S(2)}) collective-permute-start(bf16[12,32,128]{2,1,0:T(8,128)(2,1)S(1)} %slice.1020), channel_id=1, source_target_pairs={{0,16},{1,17},{2,18},{3,19},{4,20},{5,21},{6,22},{7,23},{8,24},{9,... | collective-permute-start | bytes 294920 | tf_op jit(solution)/shard_map/ppermute | solution.py:350
  112.9 3.9 %collective-permute-start.40 = (f32[32,128]{1,0:T(8,128)S(1)}, f32[32,128]{1,0:T(8,128)S(1)}, u32[]{:S(2)}, u32[]{:S(2)}) collective-permute-start(f32[32,128]{1,0:T(8,128)S(1)} %select_add_fusion), channel_id=1, source_target_pairs={{0,16},{1,17},{2,18},{3,19},{4,20},{5,21},{6,22},{7,23},{8,24},{9,... | collective-permute-start | bytes 49160 | tf_op jit(solution)/shard_map/ppermute | solution.py:350
  116.8 2.1 %collective-permute-start.42 = (f32[13,32,128]{2,1,0:T(8,128)S(1)}, f32[13,32,128]{2,1,0:T(8,128)S(1)}, u32[]{:S(2)}, u32[]{:S(2)}) collective-permute-start(f32[13,32,128]{2,1,0:T(8,128)S(1)} %pad_maximum_fusion.18), channel_id=1, source_target_pairs={{0,8},{8,0},{16,24},{24,16},{1,9},{9,1},{17,25},{25,17},{2,10},{10... | collective-permute-start | bytes 638984 | tf_op jit(solution)/shard_map/ppermute | solution.py:353
